TPU v7x, 32 devices: a whole 2x2x4 slice. The times are simulated.
32 devices in a mesh: dp: 8 (over z, x), tensor: 4 (over y, core).
Axes of the slice: x: 2, y: 2, z: 4, core: 2. Of those that a mesh axis runs over, the one named last changes fastest.
Arguments:
- tokens: bfloat16 [24576, 1024], P(('dp', 'tensor')), may hold values from -6 to 6
- segments: int32 [24, 1024], P('dp'), may hold values from 0 to 3, never falling along the last dimension, each value on 1 to 800 neighbouring positions
- cotangent: bfloat16 [24576, 1024], P(('dp', 'tensor')), may hold values from -6 to 6
- mixer_in: float32 [3, 1024, 1024], P(None, 'dp', 'tensor'), may hold values from -0.1875 to 0.1875
- mixer_out: float32 [1024, 1024], P('tensor', 'dp'), may hold values from -0.1875 to 0.1875
- gate_up: float32 [2, 1024, 4608], P(None, 'dp', 'tensor'), may hold values from -0.1875 to 0.1875
- down_proj: float32 [4608, 1024], P('tensor', 'dp'), may hold values from -0.09375 to 0.09375
- norm_gains: float32 [2, 1024], P(None, ('dp', 'tensor')), may hold values from 0.5 to 1.5
- conv_kernel: float32 [3, 1024], P(None, ('dp', 'tensor')), may hold values from -3 to 3
- first_mixer_in: float32 [3, 1024, 1024], P(None, 'dp', 'tensor'), may hold values from -128 to 128
- second_mixer_in: float32 [3, 1024, 1024], P(None, 'dp', 'tensor'), may hold values from 2457.6 to 9830.4
- first_mixer_out: float32 [1024, 1024], P('tensor', 'dp'), may hold values from -128 to 128
- second_mixer_out: float32 [1024, 1024], P('tensor', 'dp'), may hold values from 2457.6 to 9830.4
- first_gate_up: float32 [2, 1024, 4608], P(None, 'dp', 'tensor'), may hold values from -32 to 32
- second_gate_up: float32 [2, 1024, 4608], P(None, 'dp', 'tensor'), may hold values from 117.9648 to 466.944
- first_down_proj: float32 [4608, 1024], P('tensor', 'dp'), may hold values from -64 to 64
- second_down_proj: float32 [4608, 1024], P('tensor', 'dp'), may hold values from 466.944 to 1867.776
- first_norm_gains: float32 [2, 1024], P(None, ('dp', 'tensor')), may hold values from -128 to 128
- second_norm_gains: float32 [2, 1024], P(None, ('dp', 'tensor')), may hold values from 2457.6 to 9830.4
- first_conv_kernel: float32 [3, 1024], P(None, ('dp', 'tensor')), may hold values from -128 to 128
- second_conv_kernel: float32 [3, 1024], P(None, ('dp', 'tensor')), may hold values from 2457.6 to 9830.4
Outputs:
- block_out: bfloat16 [24576, 1024], P(('dp', 'tensor'))
- grad_input: float32 [24576, 1024], P(('dp', 'tensor'))
- new_mixer_in: float32 [3, 1024, 1024], P(None, 'dp', 'tensor')
- new_first_mixer_in: float32 [3, 1024, 1024], P(None, 'dp', 'tensor')
- new_second_mixer_in: float32 [3, 1024, 1024], P(None, 'dp', 'tensor')
- new_mixer_out: float32 [1024, 1024], P('tensor', 'dp')
- new_first_mixer_out: float32 [1024, 1024], P('tensor', 'dp')
- new_second_mixer_out: float32 [1024, 1024], P('tensor', 'dp')
- new_gate_up: float32 [2, 1024, 4608], P(None, 'dp', 'tensor')
- new_first_gate_up: float32 [2, 1024, 4608], P(None, 'dp', 'tensor')
- new_second_gate_up: float32 [2, 1024, 4608], P(None, 'dp', 'tensor')
- new_down_proj: float32 [4608, 1024], P('tensor', 'dp')
- new_first_down_proj: float32 [4608, 1024], P('tensor', 'dp')
- new_second_down_proj: float32 [4608, 1024], P('tensor', 'dp')
- new_norm_gains: float32 [2, 1024], P(None, ('dp', 'tensor'))
- new_first_norm_gains: float32 [2, 1024], P(None, ('dp', 'tensor'))
- new_second_norm_gains: float32 [2, 1024], P(None, ('dp', 'tensor'))
- new_conv_kernel: float32 [3, 1024], P(None, ('dp', 'tensor'))
- new_first_conv_kernel: float32 [3, 1024], P(None, ('dp', 'tensor'))
- new_second_conv_kernel: float32 [3, 1024], P(None, ('dp', 'tensor'))
Inputs may be any that keep to these rules, and one draw needn't show every extreme that they name: `segments`: within a row the document numbers never fall; a document holds 1 to 800 tokens.
All inputs are finite; a program needn't handle non-finite values.
Results may differ from a plain program's by a relative error of at most 0.019.
Values may be sent and summed in bfloat16 or wider, within the bound.
No kernel may reach another device: no remote copies, remote signals or barrier semaphores. Data moves between devices by JAX's collectives and lax.ppermute only.
A program may use at most 192 MiB of HBM per device.

v0:
```python
import jax
import jax.numpy as jnp
from jax import lax
from jax.sharding import PartitionSpec as P

KW = 3
STEP = 10


EPS_NORM = 1e-05
EPS_ADAM = 1e-08
BETA_FIRST = 0.9
BETA_SECOND = 0.95
RATE_MATRIX = 0.05
RATE_SMALL = 0.5
DECAY = 0.1


def lagged(values, shift):
    return jnp.concatenate(
        [jnp.zeros((shift,) + values.shape[1:], values.dtype), values[:-shift]], 0
    )


def leading(values, shift):
    return jnp.concatenate(
        [values[shift:], jnp.zeros((shift,) + values.shape[1:], values.dtype)], 0
    )


def lag_masks(seg_flat, length):
    positions = jnp.arange(seg_flat.shape[0], dtype=jnp.int32) % length
    masks = [jnp.ones((seg_flat.shape[0], 1), jnp.float32)]
    for shift in range(1, KW):
        same = (positions >= shift) & (seg_flat == lagged(seg_flat, shift))
        masks.append(jnp.where(same, 1.0, 0.0).astype(jnp.float32)[:, None])
    return masks


def rms_scale(values):
    return lax.rsqrt(jnp.mean(values * values, axis=-1, keepdims=True) + EPS_NORM)


def norm_back(values, scale, gain, upstream):
    scaled = upstream * gain
    gain_grad = jnp.sum(upstream * values * scale, axis=0)
    value_grad = scale * scaled - values * scale * scale * scale * jnp.mean(
        scaled * values, axis=-1, keepdims=True
    )
    return (value_grad, gain_grad)


def spread_rows(values):
    return lax.all_gather(values, "tensor", axis=0, tiled=True)


def collect_rows(values):
    return lax.psum_scatter(values, "tensor", scatter_dimension=0, tiled=True)


def adamw(param, grad, first, second, rate, decay):
    first_new = BETA_FIRST * first + (1.0 - BETA_FIRST) * grad
    second_new = BETA_SECOND * second + (1.0 - BETA_SECOND) * grad * grad
    first_hat = first_new / (1.0 - BETA_FIRST**STEP)
    second_hat = second_new / (1.0 - BETA_SECOND**STEP)
    return (
        param - rate * (first_hat / (jnp.sqrt(second_hat) + EPS_ADAM) + decay * param),
        first_new,
        second_new,
    )


def local(
    tokens,
    segments,
    cotangent,
    mixer_in,
    mixer_out,
    gate_up,
    down_proj,
    norm_gains,
    conv_kernel,
    first_mixer_in,
    second_mixer_in,
    first_mixer_out,
    second_mixer_out,
    first_gate_up,
    second_gate_up,
    first_down_proj,
    second_down_proj,
    first_norm_gains,
    second_norm_gains,
    first_conv_kernel,
    second_conv_kernel,
):
    tensor_index = lax.axis_index("tensor")
    work_in, work_out, work_gate_up, work_down = (
        lax.all_gather(mixer_in.astype(jnp.bfloat16), "dp", axis=1, tiled=True),
        lax.all_gather(mixer_out.astype(jnp.bfloat16), "dp", axis=1, tiled=True),
        lax.all_gather(gate_up.astype(jnp.bfloat16), "dp", axis=1, tiled=True),
        lax.all_gather(down_proj.astype(jnp.bfloat16), "dp", axis=1, tiled=True),
    )
    gains, kernel = (
        lax.all_gather(norm_gains, ("dp", "tensor"), axis=1, tiled=True),
        lax.all_gather(conv_kernel, ("dp", "tensor"), axis=1, tiled=True),
    )
    channels = work_in.shape[2]
    kernel_local = lax.dynamic_slice_in_dim(kernel, tensor_index * channels, channels, 1)
    masks = lag_masks(segments.reshape(-1), segments.shape[1])
    values = tokens.astype(jnp.float32)
    scale_one = rms_scale(values)
    normed_one = (values * scale_one * gains[0]).astype(jnp.bfloat16)
    gathered_one = spread_rows(normed_one)
    projected = jnp.einsum("td,kdc->tkc", gathered_one, work_in, preferred_element_type=jnp.float32)
    part_b = projected[:, 0]
    part_c = projected[:, 1]
    part_x = projected[:, 2]
    product = part_b * part_x
    convolved = kernel_local[0] * product
    for shift in range(1, KW):
        convolved = convolved + kernel_local[shift] * masks[shift] * lagged(product, shift)
    gated = (part_c * convolved).astype(jnp.bfloat16)
    partial_mix = jnp.dot(gated, work_out, preferred_element_type=jnp.float32)
    mixed = lax.psum_scatter(partial_mix, "tensor", scatter_dimension=0, tiled=True)
    middle = values + mixed
    scale_two = rms_scale(middle)
    normed_two = (middle * scale_two * gains[1]).astype(jnp.bfloat16)
    gathered_two = spread_rows(normed_two)
    hidden = jnp.einsum(
        "td,kdf->tkf", gathered_two, work_gate_up, preferred_element_type=jnp.float32
    )
    gate_part = hidden[:, 0]
    up_part = hidden[:, 1]
    sigma = jax.nn.sigmoid(gate_part)
    silu_gate = gate_part * sigma
    activated = (silu_gate * up_part).astype(jnp.bfloat16)
    branch = collect_rows(jnp.dot(activated, work_down, preferred_element_type=jnp.float32))
    block_out = (middle + branch).astype(jnp.bfloat16)
    cot_rows = spread_rows(cotangent)
    grad_down = jnp.einsum("tf,td->fd", activated, cot_rows, preferred_element_type=jnp.float32)
    act_grad = jnp.einsum("td,fd->tf", cot_rows, work_down, preferred_element_type=jnp.float32)
    gate_grad = act_grad * up_part * sigma * (1.0 + gate_part * (1.0 - sigma))
    up_grad = act_grad * silu_gate
    hidden_grad = jnp.stack([gate_grad, up_grad], axis=1).astype(jnp.bfloat16)
    grad_gate_up = jnp.einsum(
        "td,tkf->kdf", gathered_two, hidden_grad, preferred_element_type=jnp.float32
    )
    normed_two_grad = collect_rows(
        jnp.einsum("tkf,kdf->td", hidden_grad, work_gate_up, preferred_element_type=jnp.float32)
    )
    middle_norm_grad, gain_two_grad = norm_back(middle, scale_two, gains[1], normed_two_grad)
    middle_grad = cotangent.astype(jnp.float32) + middle_norm_grad
    mixed_grad = middle_grad.astype(jnp.bfloat16)
    mixed_rows = lax.all_gather(mixed_grad, "tensor", axis=0, tiled=True)
    grad_out = jnp.einsum("tc,td->cd", gated, mixed_rows, preferred_element_type=jnp.float32)
    gated_grad = jnp.einsum("td,cd->tc", mixed_rows, work_out, preferred_element_type=jnp.float32)
    c_grad = gated_grad * convolved
    conv_grad = gated_grad * part_c
    kernel_rows = [jnp.sum(conv_grad * product, axis=0)]
    product_grad = kernel_local[0] * conv_grad
    for shift in range(1, KW):
        masked = masks[shift] * conv_grad
        kernel_rows.append(jnp.sum(masked * lagged(product, shift), axis=0))
        product_grad = product_grad + kernel_local[shift] * leading(masked, shift)
    proj_grad = jnp.stack([product_grad * part_x, c_grad, product_grad * part_b], axis=1).astype(
        jnp.bfloat16
    )
    grad_in = jnp.einsum("td,tkc->kdc", gathered_one, proj_grad, preferred_element_type=jnp.float32)
    normed_one_grad = collect_rows(
        jnp.einsum("tkc,kdc->td", proj_grad, work_in, preferred_element_type=jnp.float32)
    )
    input_norm_grad, gain_one_grad = norm_back(values, scale_one, gains[0], normed_one_grad)
    grad_input = middle_grad + input_norm_grad
    grad_in, grad_out, grad_gate_up, grad_down = (
        lax.psum_scatter(
            grad_in.astype(jnp.bfloat16), "dp", scatter_dimension=1, tiled=True
        ).astype(jnp.float32),
        lax.psum_scatter(
            grad_out.astype(jnp.bfloat16), "dp", scatter_dimension=1, tiled=True
        ).astype(jnp.float32),
        lax.psum_scatter(
            grad_gate_up.astype(jnp.bfloat16), "dp", scatter_dimension=1, tiled=True
        ).astype(jnp.float32),
        lax.psum_scatter(
            grad_down.astype(jnp.bfloat16), "dp", scatter_dimension=1, tiled=True
        ).astype(jnp.float32),
    )
    gain_grads = jnp.stack([gain_one_grad, gain_two_grad], axis=0)
    kernel_full = lax.dynamic_update_slice_in_dim(
        jnp.zeros((kernel.shape[0], kernel.shape[1]), jnp.float32),
        jnp.stack(kernel_rows, axis=0),
        tensor_index * channels,
        1,
    )
    gain_grads, kernel_grads = (
        lax.psum_scatter(gain_grads, ("dp", "tensor"), scatter_dimension=1, tiled=True),
        lax.psum_scatter(kernel_full, ("dp", "tensor"), scatter_dimension=1, tiled=True),
    )
    in_new = adamw(mixer_in, grad_in, first_mixer_in, second_mixer_in, RATE_MATRIX, DECAY)
    out_new = adamw(mixer_out, grad_out, first_mixer_out, second_mixer_out, RATE_MATRIX, DECAY)
    gu_new = adamw(gate_up, grad_gate_up, first_gate_up, second_gate_up, RATE_MATRIX, DECAY)
    down_new = adamw(down_proj, grad_down, first_down_proj, second_down_proj, RATE_MATRIX, DECAY)
    gains_new = adamw(norm_gains, gain_grads, first_norm_gains, second_norm_gains, RATE_SMALL, 0.0)
    kernel_new = adamw(
        conv_kernel, kernel_grads, first_conv_kernel, second_conv_kernel, RATE_SMALL, DECAY
    )
    return (
        block_out,
        grad_input,
        in_new[0],
        in_new[1],
        in_new[2],
        out_new[0],
        out_new[1],
        out_new[2],
        gu_new[0],
        gu_new[1],
        gu_new[2],
        down_new[0],
        down_new[1],
        down_new[2],
        gains_new[0],
        gains_new[1],
        gains_new[2],
        kernel_new[0],
        kernel_new[1],
        kernel_new[2],
    )


def solution(mesh):
    return jax.shard_map(
        local,
        mesh=mesh,
        in_specs=(
            P(("dp", "tensor"), None),
            P("dp", None),
            P(("dp", "tensor"), None),
            P(None, "dp", "tensor"),
            P("tensor", "dp"),
            P(None, "dp", "tensor"),
            P("tensor", "dp"),
            P(None, ("dp", "tensor")),
            P(None, ("dp", "tensor")),
            P(None, "dp", "tensor"),
            P(None, "dp", "tensor"),
            P("tensor", "dp"),
            P("tensor", "dp"),
            P(None, "dp", "tensor"),
            P(None, "dp", "tensor"),
            P("tensor", "dp"),
            P("tensor", "dp"),
            P(None, ("dp", "tensor")),
            P(None, ("dp", "tensor")),
            P(None, ("dp", "tensor")),
            P(None, ("dp", "tensor")),
        ),
        out_specs=(
            P(("dp", "tensor"), None),
            P(("dp", "tensor"), None),
            P(None, "dp", "tensor"),
            P(None, "dp", "tensor"),
            P(None, "dp", "tensor"),
            P("tensor", "dp"),
            P("tensor", "dp"),
            P("tensor", "dp"),
            P(None, "dp", "tensor"),
            P(None, "dp", "tensor"),
            P(None, "dp", "tensor"),
            P("tensor", "dp"),
            P("tensor", "dp"),
            P("tensor", "dp"),
            P(None, ("dp", "tensor")),
            P(None, ("dp", "tensor")),
            P(None, ("dp", "tensor")),
            P(None, ("dp", "tensor")),
            P(None, ("dp", "tensor")),
            P(None, ("dp", "tensor")),
        ),
        check_vma=False,
    )
```

profile of v0, /device:TPU:0, one launch (start us, length us, event | category | flops | bytes accessed | tf_op | source)
XLA Modules:
  0.0 1453.2 jit_solution(7179005535418169532)
XLA Ops:
  9.1 43.5 %all-gather = f32[32,32,2]{1,2,0:T(2,128)S(1)} all-gather(f32[1,32,2]{1,2,0:T(2,128)} %bitcast.184), channel_id=1, replica_groups=mesh['dp'=8,'tensor'=4] {'dp','tensor'}, dimensions={0}, use_global_device_ids=true | all-gather | bytes 8448 | tf_op jit(solution)/shard_map/all_gather | solution.py:104
  56.4 37.3 %all-gather.1 = f32[32,32,3]{1,2,0:T(4,128)S(1)} all-gather(f32[1,32,3]{1,2,0:T(4,128)S(1)} %bitcast.180), channel_id=1, replica_groups=mesh['dp'=8,'tensor'=4] {'dp','tensor'}, dimensions={0}, use_global_device_ids=true | all-gather | bytes 12672 | tf_op jit(solution)/shard_map/all_gather | solution.py:105
  93.9 27.7 %all_gather.34 = bf16[256,1024]{1,0:T(8,128)(2,1)S(1)} all-gather(bf16[256,128]{1,0:T(8,128)(2,1)S(1)} %convert_element_type.72), channel_id=1, replica_groups=mesh['dp'=8,'tensor'=4] {'dp'}, dimensions={1}, use_global_device_ids=true | all-gather | bytes 589824 | tf_op jit(solution)/shard_map/all_gather | solution.py:99
  121.7 7.9 fusion.11
  130.0 3.2 copy-done.4
  133.2 3.3 multiply_convert_fusion.7
  137.6 6.4 fusion.78
  146.2 94.5 %reduce-scatter.23.cloned.1.call-done = f32[768,1024]{1,0:T(8,128)} async-done(((f32[3072,1024]{1,0:T(8,128)}), f32[768,1024]{1,0:T(8,128)}) %reduce-scatter.23.cloned.1.call-update) | async-done | bytes 3145744 | tf_op jit(solution)/shard_map/reduce_scatter | solution.py:124
  240.8 2.8 multiply_reduce_fusion.5
  248.5 74.8 %all-gather.16.cloned.1.call-done = bf16[2,1024,1152]{2,1,0:T(8,128)(2,1)} async-done(((bf16[2,128,1152]{2,1,0:T(8,128)(2,1)}), bf16[2,1024,1152]{2,1,0:T(8,128)(2,1)}) %all-gather.16.cloned.1.call-update) | async-done | bytes 4718608 | tf_op jit(solution)/shard_map/all_gather | solution.py:100
  323.3 46.5 %all-gather.14.cloned.1.call-done = bf16[3072,1024]{1,0:T(8,128)(2,1)} async-done(((bf16[768,1024]{1,0:T(8,128)(2,1)}), bf16[3072,1024]{1,0:T(8,128)(2,1)}) %all-gather.14.cloned.1.call-update) | async-done | bytes 6291472 | tf_op jit(solution)/shard_map/all_gather | solution.py:54
  369.8 21.7 %fusion.7 = f32[3072,2,1152]{2,0,1:T(8,128)} fusion(bf16[2,1024,1152]{2,1,0:T(8,128)(2,1)} %all-gather.16.cloned.1.call-done, bf16[3072,1024]{1,0:T(8,128)(2,1)} %all-gather.14.cloned.1.call-done), kind=kOutput, calls=%fused_computation.15 | convolution fusion | flops 14495514624 | bytes 39321600 | tf_op jit(solution)/shard_map/td,kdf->tkf/dot_general | solution.py:129
  391.5 34.6 %all-gather.18.cloned.1.call-done = bf16[1152,1024]{1,0:T(8,128)(2,1)} async-done(((bf16[1152,128]{1,0:T(8,128)(2,1)}), bf16[1152,1024]{1,0:T(8,128)(2,1)}) %all-gather.18.cloned.1.call-update) | async-done | bytes 2359312 | tf_op jit(solution)/shard_map/all_gather | solution.py:101
  426.1 46.2 %all-gather.20.cloned.1.call-done = bf16[3072,1024]{1,0:T(8,128)(2,1)} async-done(((bf16[768,1024]{1,0:T(8,128)(2,1)}), bf16[3072,1024]{1,0:T(8,128)(2,1)}) %all-gather.20.cloned.1.call-update) | async-done | bytes 6291472 | tf_op jit(solution)/shard_map/all_gather | solution.py:54
  472.3 27.1 %fusion.4 = (bf16[3072,1,1152]{2,0,1:T(8,128)(2,1)}, bf16[3072,1,1152]{2,0,1:T(8,128)(2,1)}, bf16[3072,1152]{1,0:T(8,128)(2,1)}) fusion(f32[3072,2,1152]{2,0,1:T(8,128)} %fusion.7, bf16[3072,1024]{1,0:T(8,128)(2,1)} %all-gather.20.cloned.1.call-done, bf16[1152,1024]{1,0:T(8,128)(2,1)} %all-gather.18.cloned.1.call-done), kind=kOutput, calls=%fused_computation.11 | convolution fusion | flops 7300841472 | bytes 58195968 | tf_op jit(solution)/shard_map/td,fd->tf/dot_general | solution.py:141
  499.4 21.0 %fusion.5 = f32[3072,1024]{1,0:T(8,128)} fusion(bf16[2,1024,1152]{2,1,0:T(8,128)(2,1)} %all-gather.16.cloned.1.call-done, bf16[3072,1,1152]{2,0,1:T(8,128)(2,1)} %get-tuple-element.115, bf16[3072,1,1152]{2,0,1:T(8,128)(2,1)} %get-tuple-element.114), kind=kOutput, calls=%fused_computation.13 | convolution fusion | flops 14502592512 | bytes 31457280 | tf_op jit(solution)/shard_map/tkf,kdf->td/dot_general | solution.py:149
  520.7 99.0 %reduce-scatter.27.cloned.1.call-done = f32[768,1024]{1,0:T(8,128)} async-done(((f32[3072,1024]{1,0:T(8,128)}), f32[768,1024]{1,0:T(8,128)}) %reduce-scatter.27.cloned.1.call-update) | async-done | bytes 3145744 | tf_op jit(solution)/shard_map/reduce_scatter | solution.py:58
  619.7 3.4 multiply_reduce_fusion.3
  623.1 2.2 fusion.64
  625.4 11.7 convolution_convert_fusion
  637.2 2.5 copy.101
  639.8 20.9 %fusion.16 = bf16[2,1024,1152]{1,2,0:T(8,128)(2,1)} fusion(bf16[3072,1024]{1,0:T(8,128)(2,1)} %all-gather.14.cloned.1.call-done, bf16[3072,1,1152]{2,0,1:T(8,128)(2,1)} %get-tuple-element.115, bf16[3072,1,1152]{2,0,1:T(8,128)(2,1)} %get-tuple-element.114), kind=kOutput, calls=%fused_computation.28 | convolution fusion | flops 14504951808 | bytes 25165824 | tf_op jit(solution)/shard_map/td,tkf->kdf/dot_general | solution.py:145
  660.7 12.6 copy.99
  673.3 5.3 copy.108
  680.5 8.2 multiply_reduce_fusion.2
  695.4 6.0 fusion.35
  701.4 3.6 fusion.37
  705.1 4.7 convolution_convert_fusion.1
  710.9 10.0 fusion.38
  720.8 2.9 copy.95
  725.4 10.6 convolution_bitcast_fusion
  737.6 13.2 fusion.79
  753.2 2.0 copy.77
  760.9 3.0 multiply_subtract_fusion.1
  763.9 78.3 %reduce-scatter.35.cloned.1.call-done = bf16[128,2304]{1,0:T(8,128)(2,1)} async-done(((bf16[1024,2304]{1,0:T(8,128)(2,1)}), bf16[128,2304]{1,0:T(8,128)(2,1)}) %reduce-scatter.35.cloned.1.call-update) | async-done | bytes 589840
  842.2 2.6 reshape.112
  844.8 2.9 copy.100
  847.7 3.4 multiply_subtract_fusion
  851.2 2.8 copy.90
  856.7 121.0 %reduce-scatter.41.cloned.1.call-done = f32[32,3]{1,0:T(8,128)} async-done(((f32[1024,3]{1,0:T(8,128)}), f32[32,3]{1,0:T(8,128)}) %reduce-scatter.41.cloned.1.call-update) | async-done | bytes 400
  979.9 59.6 %reduce-scatter.33.cloned.1.call-done = bf16[128,256]{1,0:T(8,128)(2,1)} async-done(((bf16[1024,256]{1,0:T(8,128)(2,1)}), bf16[128,256]{1,0:T(8,128)(2,1)}) %reduce-scatter.33.cloned.1.call-update) | async-done | bytes 65552
  1042.2 64.4 %reduce-scatter.31.cloned.1.call-done = bf16[128,768]{1,0:T(8,128)(2,1)} async-done(((bf16[1024,768]{1,0:T(8,128)(2,1)}), bf16[128,768]{1,0:T(8,128)(2,1)}) %reduce-scatter.31.cloned.1.call-update) | async-done | bytes 196624
  1110.8 2.1 copy.89
  1112.8 94.4 %reduce-scatter.29.cloned.1.call-done = f32[768,1024]{1,0:T(8,128)} async-done(((f32[3072,1024]{1,0:T(8,128)}), f32[768,1024]{1,0:T(8,128)}) %reduce-scatter.29.cloned.1.call-update) | async-done | bytes 3145744 | tf_op jit(solution)/shard_map/reduce_scatter | solution.py:58
  1207.3 3.5 fusion.29
  1211.9 97.1 %reduce-scatter.25.cloned.1.call-done = f32[768,1024]{1,0:T(8,128)} async-done(((f32[3072,1024]{1,0:T(8,128)}), f32[768,1024]{1,0:T(8,128)}) %reduce-scatter.25.cloned.1.call-update) | async-done | bytes 3145744 | tf_op jit(solution)/shard_map/reduce_scatter | solution.py:58
  1309.0 7.2 fusion.25
  1316.2 128.7 %reduce-scatter.39.cloned.1.call-done = f32[32,2]{1,0:T(8,128)} async-done(((f32[1024,2]{1,0:T(8,128)}), f32[32,2]{1,0:T(8,128)}) %reduce-scatter.39.cloned.1.call-update) | async-done | bytes 272
  (183 shorter events, 49.8 us)
Async XLA Ops:
  7.2 47.5 %copy-start.5 = (bf16[768,1024]{1,0:T(8,128)(2,1)S(1)}, bf16[768,1024]{1,0:T(8,128)(2,1)}, u32[]{:S(2)}) copy-start(bf16[768,1024]{1,0:T(8,128)(2,1)} %param.21) | copy-start | bytes 4718596
  7.2 114.4 %all-gather.12.cloned.1.call-start = ((), (), s32[]{:S(2)}) async-start(), calls=%async_computation.11 | async-start | bytes 1769472 | tf_op jit(solution)/shard_map/all_gather | solution.py:98
  9.1 112.6 %all-gather.10.cloned.1.call-start = ((), (), s32[]{:S(2)}) async-start(), calls=%async_computation.10 | async-start | bytes 7864320 | tf_op jit(solution)/shard_map/all_gather | solution.py:54
  52.8 41.0 %copy-start.22 = (f32[256,128]{1,0:T(8,128)S(1)}, f32[256,128]{1,0:T(8,128)}, u32[]{:S(2)}) copy-start(f32[256,128]{1,0:T(8,128)} %param.25) | copy-start | bytes 393220
  54.6 74.9 %copy-start.27 = (f32[768]{0:T(1024)}, f32[768]{0:T(1024)S(1)}, u32[]{:S(2)}) copy-start(f32[768]{0:T(1024)S(1)} %add_rsqrt_fusion.1) | copy-start | bytes 9220
  54.6 74.9 %copy-start.29 = (f32[1,1024]{1,0:T(1,128)}, f32[1,1024]{1,0:T(1,128)S(1)}, u32[]{:S(2)}) copy-start(f32[1,1024]{1,0:T(1,128)S(1)} %get-tuple-element.125) | copy-start | bytes 12292
  56.3 184.5 %reduce-scatter.23.cloned.1.call-start = ((), (), s32[]{:S(2)}) async-start(), calls=%async_computation.12 | async-start | bytes 15728640 | tf_op jit(solution)/shard_map/reduce_scatter | solution.py:124
  93.8 36.2 %copy-start.35 = (f32[1,256]{1,0:T(1,128)}, f32[1,256]{1,0:T(1,128)S(1)}, u32[]{:S(2)}) copy-start(f32[1,256]{1,0:T(1,128)S(1)} %get-tuple-element.126) | copy-start | bytes 3076
  93.8 36.2 %copy-start.37 = (f32[1,256]{1,0:T(1,128)}, f32[1,256]{1,0:T(1,128)S(1)}, u32[]{:S(2)}) copy-start(f32[1,256]{1,0:T(1,128)S(1)} %get-tuple-element.127) | copy-start | bytes 3076
  93.8 36.2 %copy-start.39 = (f32[1,256]{1,0:T(1,128)}, f32[1,256]{1,0:T(1,128)S(1)}, u32[]{:S(2)}) copy-start(f32[1,256]{1,0:T(1,128)S(1)} %get-tuple-element.128) | copy-start | bytes 3076
  93.9 36.1 %copy-start.23 = (f32[3072]{0:T(1024)}, f32[3072]{0:T(1024)S(1)}, u32[]{:S(2)}) copy-start(f32[3072]{0:T(1024)S(1)} %get-tuple-element.122) | copy-start | bytes 36868
  93.9 36.1 %copy-start.25 = (f32[3072]{0:T(1024)}, f32[3072]{0:T(1024)S(1)}, u32[]{:S(2)}) copy-start(f32[3072]{0:T(1024)S(1)} %get-tuple-element.123) | copy-start | bytes 36868
  121.6 14.9 %copy-start.12 = (bf16[256,1024]{1,0:T(8,128)(2,1)}, bf16[256,1024]{1,0:T(8,128)(2,1)S(1)}, u32[]{:S(2)}) copy-start(bf16[256,1024]{1,0:T(8,128)(2,1)S(1)} %all_gather.34) | copy-start | bytes 1572868
  129.5 3.7 copy-start.4
  130.0 6.5 copy-start
  144.0 179.2 %all-gather.16.cloned.1.call-start = ((), (), s32[]{:S(2)}) async-start(), calls=%async_computation.14 | async-start | bytes 5308416 | tf_op jit(solution)/shard_map/all_gather | solution.py:100
  146.2 223.6 %all-gather.14.cloned.1.call-start = ((), (), s32[]{:S(2)}) async-start(), calls=%async_computation.13 | async-start | bytes 7864320 | tf_op jit(solution)/shard_map/all_gather | solution.py:54
  243.6 379.5 %copy-start.2 = (f32[768,1024]{1,0:T(8,128)}, f32[768,1024]{1,0:T(8,128)S(1)}, u32[]{:S(2)}) copy-start(f32[768,1024]{1,0:T(8,128)S(1)} %get-tuple-element.111) | copy-start | bytes 9437188
  245.4 180.7 %all-gather.18.cloned.1.call-start = ((), (), s32[]{:S(2)}) async-start(), calls=%async_computation.15 | async-start | bytes 2654208 | tf_op jit(solution)/shard_map/all_gather | solution.py:101
  247.2 225.0 %all-gather.20.cloned.1.call-start = ((), (), s32[]{:S(2)}) async-start(), calls=%async_computation.17 | async-start | bytes 7864320 | tf_op jit(solution)/shard_map/all_gather | solution.py:54
  248.0 371.7 %reduce-scatter.27.cloned.1.call-start = ((), (), s32[]{:S(2)}) async-start(), calls=%async_computation.18 | async-start | bytes 15728640 | tf_op jit(solution)/shard_map/reduce_scatter | solution.py:58
  520.5 158.4 %all-gather.22.cloned.1.call-start = ((), (), s32[]{:S(2)}) async-start(), calls=%async_computation.19 | async-start | bytes 7864320 | tf_op jit(solution)/shard_map/all_gather | solution.py:154
  625.4 133.7 %reduce-scatter.37.cloned.1.call-start = ((), (), s32[]{:S(2)}) async-start(), calls=%async_computation.24 | async-start | bytes 2654208
  639.7 202.5 %reduce-scatter.35.cloned.1.call-start = ((), (), s32[]{:S(2)}) async-start(), calls=%async_computation.23 | async-start | bytes 5308416
  678.6 299.2 %reduce-scatter.41.cloned.1.call-start = ((), (), s32[]{:S(2)}) async-start(), calls=%async_computation.26 | async-start | bytes 540672
  680.5 8.2 copy-start.24
  680.5 8.2 copy-start.26
  701.4 3.7 copy-start.10
  705.0 334.4 %reduce-scatter.33.cloned.1.call-start = ((), (), s32[]{:S(2)}) async-start(), calls=%async_computation.22 | async-start | bytes 589824
  710.8 395.8 %reduce-scatter.31.cloned.1.call-start = ((), (), s32[]{:S(2)}) async-start(), calls=%async_computation.21 | async-start | bytes 1769472
  725.3 482.0 %reduce-scatter.29.cloned.1.call-start = ((), (), s32[]{:S(2)}) async-start(), calls=%async_computation.20 | async-start | bytes 15728640 | tf_op jit(solution)/shard_map/reduce_scatter | solution.py:58
  736.0 573.0 %reduce-scatter.25.cloned.1.call-start = ((), (), s32[]{:S(2)}) async-start(), calls=%async_computation.16 | async-start | bytes 15728640 | tf_op jit(solution)/shard_map/reduce_scatter | solution.py:58
  750.9 6.1 copy-start.21
  750.9 693.9 %reduce-scatter.39.cloned.1.call-start = ((), (), s32[]{:S(2)}) async-start(), calls=%async_computation.25 | async-start | bytes 540672
  851.1 4.2 copy-start.15
  851.1 127.4 %copy-start.42 = (f32[3,32]{1,0:T(4,128)S(1)}, f32[3,32]{1,0:T(4,128)}, u32[]{:S(2)}) copy-start(f32[3,32]{1,0:T(4,128)} %param.29) | copy-start | bytes 1156
  851.1 127.4 %copy-start.44 = (f32[3,32]{1,0:T(4,128)S(1)}, f32[3,32]{1,0:T(4,128)}, u32[]{:S(2)}) copy-start(f32[3,32]{1,0:T(4,128)} %param.40) | copy-start | bytes 1156
  854.0 253.9 %copy-start.18 = (f32[3,128,256]{1,2,0:T(8,128)S(1)}, f32[3,128,256]{1,2,0:T(8,128)}, u32[]{:S(2)}) copy-start(f32[3,128,256]{1,2,0:T(8,128)} %copy.81) | copy-start | bytes 1179652
  854.0 253.9 %copy-start.19 = (f32[3,128,256]{1,2,0:T(8,128)S(1)}, f32[3,128,256]{1,2,0:T(8,128)}, u32[]{:S(2)}) copy-start(f32[3,128,256]{1,2,0:T(8,128)} %copy.77) | copy-start | bytes 1179652
  854.0 253.9 %copy-start.20 = (f32[3,128,256]{1,2,0:T(8,128)S(1)}, f32[3,128,256]{1,2,0:T(8,128)}, u32[]{:S(2)}) copy-start(f32[3,128,256]{1,2,0:T(8,128)} %copy.79) | copy-start | bytes 1179652
  1040.4 166.9 %copy-start.28 = (f32[768]{0:T(1024)S(1)}, f32[768]{0:T(1024)}, u32[]{:S(2)}) copy-start(f32[768]{0:T(1024)} %copy-done.27) | copy-start | bytes 9220
  1040.4 166.9 %copy-start.30 = (f32[1,1024]{1,0:T(1,128)S(1)}, f32[1,1024]{1,0:T(1,128)}, u32[]{:S(2)}) copy-start(f32[1,1024]{1,0:T(1,128)} %copy-done.29) | copy-start | bytes 12292
  1109.9 100.9 %copy-start.33 = (f32[1024]{0:T(1024)S(1)}, f32[1024]{0:T(1024)}, u32[]{:S(2)}) copy-start(f32[1024]{0:T(1024)} %get-tuple-element.80) | copy-start | bytes 12292
  1110.8 198.2 %copy-start.3 = (f32[768,1024]{1,0:T(8,128)S(1)}, f32[768,1024]{1,0:T(8,128)}, u32[]{:S(2)}) copy-start(f32[768,1024]{1,0:T(8,128)} %copy-done.2) | copy-start | bytes 9437188
  1110.8 198.2 %copy-start.32 = (f32[768]{0:T(1024)S(1)}, f32[768]{0:T(1024)}, u32[]{:S(2)}) copy-start(f32[768]{0:T(1024)} %copy-done.31) | copy-start | bytes 9220
  1211.8 233.8 %copy-start.43 = (f32[2,32]{1,0:T(2,128)S(1)}, f32[2,32]{1,0:T(2,128)}, u32[]{:S(2)}) copy-start(f32[2,32]{1,0:T(2,128)} %param.28) | copy-start | bytes 772
  1211.9 233.8 %copy-start.45 = (f32[2,32]{1,0:T(2,128)S(1)}, f32[2,32]{1,0:T(2,128)}, u32[]{:S(2)}) copy-start(f32[2,32]{1,0:T(2,128)} %param.38) | copy-start | bytes 772
  1211.9 233.8 %copy-start.46 = (f32[2,32]{1,0:T(2,128)S(1)}, f32[2,32]{1,0:T(2,128)}, u32[]{:S(2)}) copy-start(f32[2,32]{1,0:T(2,128)} %param.39) | copy-start | bytes 772
  (17 other events, 41.9 us)
Sparse Core Ops, SparseCore 0:
  10.8 46.5 all-gather.11
  59.6 45.6 all-gather.9
  144.2 96.5 reduce-scatter.22
  243.4 79.8 all-gather.15
  325.3 44.5 all-gather.13
  372.3 53.7 all-gather.17
  427.7 44.5 all-gather.19
  520.6 99.0 reduce-scatter.26
  625.5 46.3 all-gather.21
  675.2 68.9 reduce-scatter.36
  747.9 94.2 reduce-scatter.34
  844.3 133.3 reduce-scatter.40
  981.5 57.8 reduce-scatter.32
  1042.7 63.9 reduce-scatter.30
  1109.3 97.9 reduce-scatter.28
  1209.9 99.0 reduce-scatter.24
  1311.2 133.6 reduce-scatter.38
where the time goes:
time: 1460 us; the launch traced here: 1450 us
  waiting for transfers between devices  1040 us (71%)
  matrix products  163 us (11%)
  blocking collectives  109 us (7%)
  local copies, waits for them, and re-layouts  69.2 us (5%)
  other arithmetic  55.1 us (4%)
  between operations  15 us (1%)
    unnamed x23, waiting for transfers between devices  453 us
    reduce_scatter x3, waiting for transfers between devices, collect_rows(): return lax.psum_scatter(values, 'tensor', scatter_dimension=0, tiled=True)  291 us
    reduce_scatter x1, waiting for transfers between devices, local(): lax.psum_scatter(partial_mix, 'tensor', scatter_dimension=0, tiled=True)  94.5 us
    all_gather x3, waiting for transfers between devices, spread_rows(): return lax.all_gather(values, 'tensor', axis=0, tiled=True)  92.7 us
    all_gather x1, waiting for transfers between devices, local(): lax.all_gather(gate_up.astype(jnp.bfloat16), 'dp', axis=1, tiled=True)  74.8 us
    unnamed x126, local copies, waits for them, and re-layouts  65.4 us
    all_gather x1, blocking collectives, local(): lax.all_gather(norm_gains, ('dp', 'tensor'), axis=1, tiled=True)  43.5 us
    all_gather x1, blocking collectives, local(): lax.all_gather(conv_kernel, ('dp', 'tensor'), axis=1, tiled=True)  37.3 us
  transfers between devices with their start and end apart: 17, of which 13 were waited for; matrix products, arithmetic and copies ran while one was open for 14% of the time, Pallas kernels for 0%

commit v1 on v0

v1 whole, which is shorter than its diff:
```python
import jax
import jax.numpy as jnp
from jax import lax
from jax.sharding import PartitionSpec as P

KW = 3
STEP = 10
HALO = 16

EPS_NORM = 1e-05
EPS_ADAM = 1e-08
BETA_FIRST = 0.9
BETA_SECOND = 0.95
RATE_MATRIX = 0.05
RATE_SMALL = 0.5
DECAY = 0.1

BF = jnp.bfloat16
F32 = jnp.float32


def swap(values, axis, bit):
    size = lax.axis_size(axis)
    return lax.ppermute(values, axis, [(i, i ^ bit) for i in range(size)])


def halves(values, axis):
    size = values.shape[axis] // 2
    return (
        lax.slice_in_dim(values, 0, size, axis=axis),
        lax.slice_in_dim(values, size, 2 * size, axis=axis),
    )


def low_bits():
    return (
        [2 << i for i in range((lax.axis_size("dp") // 2).bit_length() - 1)],
        [4 << i for i in range((lax.axis_size("tensor") // 4).bit_length() - 1)],
    )


def gather_weight(shard, wide, cut):
    z_bits, t_bits = low_bits()
    own = shard
    for bit in z_bits:
        own = jnp.concatenate([own, swap(own, "dp", bit)], wide)
    for bit in t_bits:
        own = jnp.concatenate([own, swap(own, "tensor", bit)], cut)
    by_x = swap(own, "dp", 1)
    by_y = swap(own, "tensor", 2)
    near = jnp.concatenate([own, by_x], wide)
    near_core = swap(near, "tensor", 1)
    far_first = swap(halves(by_y, wide)[0], "dp", 1)
    far_second = swap(halves(by_x, wide)[1], "tensor", 2)
    far = jnp.concatenate([by_y, far_first, far_second], wide)
    far_core = swap(far, "tensor", 1)
    return near, near_core, far, far_core


def plus(left, right):
    return (left.astype(F32) + right.astype(F32)).astype(BF)


def scatter_grad(blocks, wide, cut):
    z_bits, t_bits = low_bits()
    near, near_core, far, far_core = blocks
    far_in = swap(far_core, "tensor", 1)
    near_in = swap(near_core, "tensor", 1)
    far_low, far_high = halves(far, wide)
    far_in_low, far_in_high = halves(far_in, wide)
    corner = [plus(a, b) for a, b in zip(halves(far_high, wide), halves(far_in_high, wide))]
    to_x = swap(corner[0], "dp", 1)
    to_y = swap(corner[1], "tensor", 2)
    near_low, near_high = halves(near, wide)
    near_in_low, near_in_high = halves(near_in, wide)
    far_parts = [a.astype(F32) + b.astype(F32) for a, b in zip(halves(far_low, wide), halves(far_in_low, wide))]
    by_y = jnp.concatenate(
        [(far_parts[0] + to_x.astype(F32)).astype(BF), far_parts[1].astype(BF)], wide
    )
    near_parts = [
        a.astype(F32) + b.astype(F32) for a, b in zip(halves(near_high, wide), halves(near_in_high, wide))
    ]
    by_x = jnp.concatenate(
        [near_parts[0].astype(BF), (near_parts[1] + to_y.astype(F32)).astype(BF)], wide
    )
    got_y = swap(by_y, "tensor", 2)
    got_x = swap(by_x, "dp", 1)
    total = (
        near_low.astype(F32) + near_in_low.astype(F32) + got_y.astype(F32) + got_x.astype(F32)
    )
    for bit in reversed(t_bits):
        keep, give = halves(total, cut)
        total = keep + swap(give.astype(BF), "tensor", bit).astype(F32)
    for bit in reversed(z_bits):
        keep, give = halves(total, wide)
        total = keep + swap(give.astype(BF), "dp", bit).astype(F32)
    return total


def rotate_left(values, count):
    bits = count.bit_length() - 1
    return ((values << 1) | (values >> (bits - 1))) & (count - 1)


def rotate_right(values, count):
    bits = count.bit_length() - 1
    return ((values & 1) << (bits - 1)) | (values >> 1)


def to_relative(values, index, count):
    width = values.shape[-1] // count
    axis = values.ndim - 1
    return jnp.concatenate(
        [
            lax.dynamic_slice_in_dim(values, (index ^ rotate_left(j, count)) * width, width, axis)
            for j in range(count)
        ],
        axis,
    )


def to_natural(values, index, count):
    width = values.shape[-1] // count
    axis = values.ndim - 1
    return jnp.concatenate(
        [
            lax.dynamic_slice_in_dim(values, rotate_right(index ^ q, count) * width, width, axis)
            for q in range(count)
        ],
        axis,
    )


def block_codes(count):
    return [base ^ (e << 2) for base in (0, 1, 2, 3) for e in range(count // 4)]


def block_place(code, count):
    return (code & 3) * (count // 4) + (code >> 2)


def shift_rows(values, start, rows):
    return lax.slice_in_dim(values, start, start + rows, axis=0)


def lag_masks(seg_flat, length):
    positions = jnp.arange(seg_flat.shape[0], dtype=jnp.int32) % length
    masks = []
    for shift in range(1, KW):
        before = jnp.concatenate([jnp.zeros((shift,), seg_flat.dtype), seg_flat[:-shift]], 0)
        same = (positions >= shift) & (seg_flat == before)
        masks.append(jnp.where(same, 1.0, 0.0).astype(F32)[:, None])
    return masks


def rms_scale(values):
    return lax.rsqrt(jnp.mean(values * values, axis=-1, keepdims=True) + EPS_NORM)


def norm_back(values, scale, gain, upstream):
    scaled = upstream * gain
    gain_grad = jnp.sum(upstream * values * scale, axis=0)
    value_grad = scale * scaled - values * scale * scale * scale * jnp.mean(
        scaled * values, axis=-1, keepdims=True
    )
    return (value_grad, gain_grad)


def adamw(param, grad, first, second, rate, decay):
    first_new = BETA_FIRST * first + (1.0 - BETA_FIRST) * grad
    second_new = BETA_SECOND * second + (1.0 - BETA_SECOND) * grad * grad
    first_hat = first_new / (1.0 - BETA_FIRST**STEP)
    second_hat = second_new / (1.0 - BETA_SECOND**STEP)
    return (
        param - rate * (first_hat / (jnp.sqrt(second_hat) + EPS_ADAM) + decay * param),
        first_new,
        second_new,
    )


def mm(spec, left, right, out=F32):
    return jnp.einsum(spec, left, right, preferred_element_type=F32).astype(out)


def local(
    tokens,
    segments,
    cotangent,
    mixer_in,
    mixer_out,
    gate_up,
    down_proj,
    norm_gains,
    conv_kernel,
    first_mixer_in,
    second_mixer_in,
    first_mixer_out,
    second_mixer_out,
    first_gate_up,
    second_gate_up,
    first_down_proj,
    second_down_proj,
    first_norm_gains,
    second_norm_gains,
    first_conv_kernel,
    second_conv_kernel,
):
    dp_size, t_size = lax.axis_size("dp"), lax.axis_size("tensor")
    dp_index, t_index = lax.axis_index("dp"), lax.axis_index("tensor")
    rows, length = tokens.shape[0], segments.shape[1]

    small = lax.all_gather(
        jnp.concatenate([norm_gains, conv_kernel], 0), ("dp", "tensor"), axis=1, tiled=True
    )
    before = lax.ppermute(
        tokens[rows - HALO :], "tensor", [(i, i + 1) for i in range(t_size - 1)]
    )
    win = gather_weight(mixer_in.astype(BF), 1, 2)
    wout = gather_weight(mixer_out.astype(BF), 1, 0)
    wgu = gather_weight(gate_up.astype(BF), 1, 2)
    wdown = gather_weight(down_proj.astype(BF), 1, 0)

    gains = to_relative(small[:2], dp_index, dp_size)
    kernel_full = small[2:]
    channels = kernel_full.shape[1] // t_size
    codes = block_codes(t_size)
    kernel = jnp.concatenate(
        [
            lax.dynamic_slice_in_dim(kernel_full, (t_index ^ code) * channels, channels, 1)
            for code in codes
        ],
        1,
    )

    masks = []
    for mask in lag_masks(segments.reshape(-1), length):
        padded = jnp.concatenate([mask, jnp.zeros((HALO, 1), F32)], 0)
        masks.append(lax.dynamic_slice_in_dim(padded, t_index * rows, rows + HALO, 0))

    extended = to_relative(jnp.concatenate([before, tokens], 0), dp_index, dp_size).astype(F32)
    scale_ext = rms_scale(extended)
    normed_ext = (extended * scale_ext * gains[0]).astype(BF)
    values, scale_one, normed_one = extended[HALO:], scale_ext[HALO:], normed_ext[HALO:]
    cot = to_relative(cotangent, dp_index, dp_size)

    win_all = jnp.concatenate(win, 2)
    wout_all = jnp.concatenate(wout, 0)
    projected = mm("td,kdc->ktc", normed_ext, win_all)
    part_b, part_c, part_x = projected[0], projected[1][HALO:], projected[2]
    product_ext = part_b * part_x
    part_b, part_x = part_b[HALO:], part_x[HALO:]
    product = product_ext[HALO:]
    convolved = kernel[0] * product
    for shift in range(1, KW):
        convolved = convolved + kernel[shift] * masks[shift - 1][:rows] * shift_rows(
            product_ext, HALO - shift, rows
        )
    gated = (part_c * convolved).astype(BF)
    middle = values + mm("tc,cd->td", gated, wout_all)
    scale_two = rms_scale(middle)
    normed_two = (middle * scale_two * gains[1]).astype(BF)

    branch = jnp.zeros(middle.shape, F32)
    normed_two_grad = jnp.zeros(middle.shape, F32)
    grads_gu, grads_down = [], []
    for w_gu, w_down in zip(wgu, wdown):
        gate_part = mm("td,df->tf", normed_two, w_gu[0])
        up_part = mm("td,df->tf", normed_two, w_gu[1])
        sigma = jax.nn.sigmoid(gate_part)
        silu_gate = gate_part * sigma
        activated = (silu_gate * up_part).astype(BF)
        grads_down.append(mm("tf,td->fd", activated, cot, BF))
        act_grad = mm("td,fd->tf", cot, w_down)
        gate_grad = (act_grad * up_part * sigma * (1.0 + gate_part * (1.0 - sigma))).astype(BF)
        up_grad = (act_grad * silu_gate).astype(BF)
        grads_gu.append(
            jnp.stack(
                [mm("td,tf->df", normed_two, gate_grad, BF), mm("td,tf->df", normed_two, up_grad, BF)], 0
            )
        )
        branch = branch + mm("tf,fd->td", activated, w_down)
        normed_two_grad = (
            normed_two_grad
            + mm("tf,df->td", gate_grad, w_gu[0])
            + mm("tf,df->td", up_grad, w_gu[1])
        )
    block_out = to_natural((middle + branch).astype(BF), dp_index, dp_size)
    grad_down = scatter_grad(grads_down, 1, 0)
    grad_gate_up = scatter_grad(grads_gu, 1, 2)

    middle_norm_grad, gain_two_grad = norm_back(middle, scale_two, gains[1], normed_two_grad)
    middle_grad = cot.astype(F32) + middle_norm_grad
    mixed_grad = middle_grad.astype(BF)
    gated_grad = mm("td,cd->tc", mixed_grad, wout_all)
    conv_grad = gated_grad * part_c
    after_rel = lax.ppermute(
        conv_grad[:8], "tensor", [(i + 1, i) for i in range(t_size - 1)]
    )
    after = jnp.concatenate(
        [
            lax.dynamic_slice_in_dim(
                after_rel,
                block_place(code ^ t_index ^ (t_index + 1), t_size) % t_size * channels,
                channels,
                1,
            )
            for code in codes
        ],
        1,
    )
    grad_out_all = mm("tc,td->cd", gated, mixed_grad, BF)
    size = channels * (t_size // 4)
    grad_out = scatter_grad([grad_out_all[i * size : (i + 1) * size] for i in range(4)], 1, 0)
    c_grad = gated_grad * convolved
    conv_ext = jnp.concatenate([conv_grad, after], 0)
    kernel_rows = [jnp.sum(conv_grad * product, axis=0)]
    product_grad = kernel[0] * conv_grad
    for shift in range(1, KW):
        masked = masks[shift - 1][: rows + 8] * conv_ext
        kernel_rows.append(
            jnp.sum(masked[:rows] * shift_rows(product_ext, HALO - shift, rows), axis=0)
        )
        product_grad = product_grad + kernel[shift] * shift_rows(masked, shift, rows)
    proj_grad = jnp.stack([product_grad * part_x, c_grad, product_grad * part_b], 0).astype(BF)
    grads_in = [
        mm("td,ktc->kdc", normed_one, proj_grad[:, :, i * size : (i + 1) * size], BF) for i in range(4)
    ]
    grad_in = scatter_grad(grads_in, 1, 2)
    normed_one_grad = mm("ktc,kdc->td", proj_grad, win_all)
    input_norm_grad, gain_one_grad = norm_back(values, scale_one, gains[0], normed_one_grad)
    grad_input = to_natural(middle_grad + input_norm_grad, dp_index, dp_size)

    gain_sums = to_natural(jnp.stack([gain_one_grad, gain_two_grad], 0), dp_index, dp_size)
    kernel_rel = jnp.stack(kernel_rows, 0)
    kernel_sums = jnp.concatenate(
        [
            lax.dynamic_slice_in_dim(
                kernel_rel, block_place(t_index ^ q, t_size) * channels, channels, 1
            )
            for q in range(t_size)
        ],
        1,
    )
    sums = jnp.concatenate([gain_sums, kernel_sums], 0)
    for axis, size_axis in (("tensor", t_size), ("dp", dp_size)):
        for i in range(size_axis.bit_length() - 1):
            sums = sums + swap(sums, axis, 1 << i)
    own_width = norm_gains.shape[1]
    own = lax.dynamic_slice_in_dim(sums, (dp_index * t_size + t_index) * own_width, own_width, 1)

    in_new = adamw(mixer_in, grad_in, first_mixer_in, second_mixer_in, RATE_MATRIX, DECAY)
    out_new = adamw(mixer_out, grad_out, first_mixer_out, second_mixer_out, RATE_MATRIX, DECAY)
    gu_new = adamw(gate_up, grad_gate_up, first_gate_up, second_gate_up, RATE_MATRIX, DECAY)
    down_new = adamw(down_proj, grad_down, first_down_proj, second_down_proj, RATE_MATRIX, DECAY)
    gains_new = adamw(norm_gains, own[:2], first_norm_gains, second_norm_gains, RATE_SMALL, 0.0)
    kernel_new = adamw(conv_kernel, own[2:], first_conv_kernel, second_conv_kernel, RATE_SMALL, DECAY)
    return (block_out, grad_input, *in_new, *out_new, *gu_new, *down_new, *gains_new, *kernel_new)


def solution(mesh):
    rows = P(("dp", "tensor"), None)
    in_w, out_w, small = P(None, "dp", "tensor"), P("tensor", "dp"), P(None, ("dp", "tensor"))
    return jax.shard_map(
        local,
        mesh=mesh,
        in_specs=(
            (rows, P("dp", None), rows, in_w, out_w, in_w, out_w, small, small)
            + (in_w,) * 2
            + (out_w,) * 2
            + (in_w,) * 2
            + (out_w,) * 2
            + (small,) * 4
        ),
        out_specs=(rows, rows)
        + (in_w,) * 3
        + (out_w,) * 3
        + (in_w,) * 3
        + (out_w,) * 3
        + (small,) * 6,
        check_vma=False,
    )
```

time: 1460 us -> 877 us (0.60)
  waiting for transfers between devices: 1040 us -> 401 us
  starting transfers between devices: 1.81 us -> 65.4 us
  blocking collectives: 109 us -> 55.7 us
  matrix products: 163 us -> 207 us
    unnamed x23 -> x0, waiting for transfers between devices: 453 us -> none
    ppermute x0 -> x71, waiting for transfers between devices: none -> 401 us  [the longest x69 401 us: swap(): return lax.ppermute(values, axis, [(i, i ^ bit) for i in range(size)])]
    reduce_scatter x4 -> x0, waiting for transfers between devices: 385 us -> none  [the longest x3 291 us: collect_rows(): return lax.psum_scatter(values, 'tensor', scatter_dimension=0, tiled=True)]
    all_gather x7 -> x0, waiting for transfers between devices: 202 us -> none  [the longest x3 92.7 us: spread_rows(): return lax.all_gather(values, 'tensor', axis=0, tiled=True)]
    ppermute x0 -> x71, starting transfers between devices: none -> 65.4 us  [the longest x69 61.2 us: swap(): return lax.ppermute(values, axis, [(i, i ^ bit) for i in range(size)])]
    all_gather x3 -> x1, blocking collectives: 109 us -> 55.7 us  [local(): lax.all_gather(jnp.concatenate([norm_gains, conv_kernel], 0), ('dp', 'ten...]
    dot_general x12 -> x45, matrix products: 163 us -> 207 us  [mm(): return jnp.einsum(spec, left, right, preferred_element_type=F32).astype(out)]
    unnamed x126 -> x296, local copies, waits for them, and re-layouts: 65.4 us -> 54.2 us
  transfers between devices with their start and end apart: 17 -> 71, of which waited for: 13 -> 28; matrix products, arithmetic and copies ran while one was open for 14% -> 32% of each run, Pallas kernels for 0% -> 0%
where the time goes in v1:
time: 877 us; the launch traced here: 869 us
  waiting for transfers between devices  401 us (46%)
  matrix products  207 us (24%)
  local copies, waits for them, and re-layouts  70.7 us (8%)
  starting transfers between devices  65.4 us (7%)
  other arithmetic  64.5 us (7%)
  blocking collectives  55.7 us (6%)
    ppermute x69, waiting for transfers between devices, swap(): return lax.ppermute(values, axis, [(i, i ^ bit) for i in range(size)])  401 us
    dot_general x45, matrix products, mm(): return jnp.einsum(spec, left, right, preferred_element_type=F32).astype(out)  207 us
    ppermute x69, starting transfers between devices, swap(): return lax.ppermute(values, axis, [(i, i ^ bit) for i in range(size)])  61.2 us
    all_gather x1, blocking collectives, local(): lax.all_gather(jnp.concatenate([norm_gains, conv_kernel], 0), ('dp', 'ten...  55.7 us
    unnamed x296, local copies, waits for them, and re-layouts  54.2 us
  transfers between devices with their start and end apart: 71, of which 28 were waited for; matrix products, arithmetic and copies ran while one was open for 32% of the time, Pallas kernels for 0%

profile of v1, /device:TPU:0, one launch (start us, length us, event | category | flops | bytes accessed | tf_op | source)
XLA Modules:
  0.0 868.6 jit_solution(4247105045141233451)
XLA Ops:
  13.2 55.7 %all-gather = f32[32,32,5]{1,2,0:T(8,128)S(1)} all-gather(f32[1,32,5]{1,2,0:T(8,128)S(1)} %maximum_bitcast_fusion), channel_id=1, replica_groups=mesh['dp'=8,'tensor'=4] {'dp','tensor'}, dimensions={0}, use_global_device_ids=true | all-gather | bytes 21120 | tf_op jit(solution)/shard_map/all_gather | solution.py:212
  103.4 22.1 %collective-permute-done.10 = bf16[256,256]{1,0:T(8,128)(2,1)S(1)} collective-permute-done((bf16[256,256]{1,0:T(8,128)(2,1)S(1)}, bf16[256,256]{1,0:T(8,128)(2,1)S(1)}, u32[]{:S(2)}, u32[]{:S(2)}) %collective-permute-start.10) | collective-permute-done | bytes 131104 | tf_op jit(solution)/shard_map/ppermute | solution.py:24
  125.8 8.2 collective-permute-done.2
  140.6 5.0 collective-permute-done.11
  145.7 26.2 %collective-permute-done.21 = bf16[1152,256]{1,0:T(8,128)(2,1)S(1)} collective-permute-done((bf16[1152,256]{1,0:T(8,128)(2,1)S(1)}, bf16[1152,256]{1,0:T(8,128)(2,1)S(1)}, u32[]{:S(2)}, u32[]{:S(2)}) %collective-permute-start.21) | collective-permute-done | bytes 589856 | tf_op jit(solution)/shard_map/ppermute | solution.py:24
  181.1 27.3 %collective-permute-done.6 = bf16[3,256,256]{2,1,0:T(8,128)(2,1)S(1)} collective-permute-done((bf16[3,256,256]{2,1,0:T(8,128)(2,1)S(1)}, bf16[3,256,256]{2,1,0:T(8,128)(2,1)S(1)}, u32[]{:S(2)}, u32[]{:S(2)}) %collective-permute-start.6) | collective-permute-done | bytes 393248 | tf_op jit(solution)/shard_map/ppermute | solution.py:24
  218.6 10.2 %collective-permute-done.29 = bf16[1152,256]{1,0:T(8,128)(2,1)S(1)} collective-permute-done((bf16[1152,256]{1,0:T(8,128)(2,1)S(1)}, bf16[1152,256]{1,0:T(8,128)(2,1)S(1)}, u32[]{:S(2)}, u32[]{:S(2)}) %collective-permute-start.29) | collective-permute-done | bytes 589856 | tf_op jit(solution)/shard_map/ppermute | solution.py:24
  231.7 6.1 fusion.102
  238.9 5.7 convolution_bitcast_fusion
  253.1 5.6 multiply_reduce_fusion.5
  259.0 24.5 %collective-permute-done.19 = bf16[2,512,1152]{2,1,0:T(8,128)(2,1)S(1)} collective-permute-done((bf16[2,512,1152]{2,1,0:T(8,128)(2,1)}, bf16[2,512,1152]{2,1,0:T(8,128)(2,1)S(1)}, u32[]{:S(2)}, u32[]{:S(2)}) %collective-permute-start.19) | collective-permute-done | bytes 2359328 | tf_op jit(solution)/shard_map/ppermute | solution.py:24
  283.9 4.0 fusion.25
  287.9 4.0 fusion.27
  291.9 8.4 multiply_convert_fusion.6
  300.4 3.9 fusion.24
  310.5 5.2 convolution_convert_fusion.3
  328.8 6.4 fusion.101
  338.8 4.0 fusion.35
  342.8 6.4 multiply_convert_fusion.3
  349.2 5.2 convolution_convert_fusion.1
  361.9 5.7 fusion.32
  367.5 5.6 fusion.34
  373.1 3.9 fusion.100
  380.7 4.4 multiply_convert_fusion.5
  385.1 5.3 convolution_convert_fusion.2
  395.1 3.9 fusion.28
  405.4 5.6 fusion.99
  413.4 4.0 fusion.37
  417.4 6.9 multiply_convert_fusion
  431.8 3.9 fusion.36
  435.7 10.4 %multiply_reduce_fusion.2 = (f32[1024]{0:T(1024)S(1)}, f32[768]{0:T(1024)S(1)}, f32[768,1024]{1,0:T(8,128)S(1)}) fusion(f32[768,1024]{1,0:T(8,128)S(1)} %get-tuple-element.169, f32[768]{0:T(1024)S(1)} %add_rsqrt_fusion, f32[1024]{0:T(1024)S(1)} %bitcast.247, bf16[768,1152]{1,0:T(8,128)(2,1)} %copy-done.38, bf16[2,1024,1152]{2,1,0:T(8,128)(2,1)} %copy-done.48, ...), kind=kOutput, calls=%fused_computation.84 | convolution fusion | flops 1822161152 | bytes 32454656 | tf_op jit(solution)/shard_map/tf,df->td/dot_general | solution.py:182
  446.1 5.2 convolution_convert_fusion
  451.4 6.5 subtract_add_fusion.1
  458.0 4.5 convolution_convert_fusion.12
  462.7 6.0 fusion.41
  478.7 5.1 multiply_reduce_fusion.1
  490.4 9.9 %fusion.21 = (f32[1024]{0:T(1024)S(1)}, f32[768]{0:T(1024)S(1)}, f32[768,1024,1]{1,0,2:T(8,128)}) fusion(f32[784,1024]{1,0:T(8,128)S(1)} %copy-done.6, f32[768]{0:T(1024)S(1)} %copy-done.79, f32[1024]{0:T(1024)S(1)} %bitcast.252, bf16[3,1024,256]{2,1,0:T(8,128)(2,1)} %copy-done.93, bf16[3,1024,256]{2,1,0:T(8,128)(2,1)} %copy-done.62, ...), kind=kOutput, calls=%fused_computation.82 | convolution fusion | flops 4885313536 | bytes 17315840 | tf_op jit(solution)/shard_map/ktc,kdc->td/dot_general | solution.py:182
  543.8 8.3 collective-permute-done.36
  556.9 7.9 collective-permute-done.38
  565.8 13.3 %collective-permute-done.52 = bf16[2,256,1152]{2,1,0:T(8,128)(2,1)S(1)} collective-permute-done((bf16[2,256,1152]{2,1,0:T(8,128)(2,1)S(1)}, bf16[2,256,1152]{2,1,0:T(8,128)(2,1)S(1)}, u32[]{:S(2)}, u32[]{:S(2)}) %collective-permute-start.52) | collective-permute-done | bytes 1179680 | tf_op jit(solution)/shard_map/ppermute | solution.py:24
  582.8 9.8 %collective-permute-done.60 = bf16[1152,256]{0,1:T(8,128)(2,1)S(1)} collective-permute-done((bf16[1152,256]{0,1:T(8,128)(2,1)S(1)}, bf16[1152,256]{0,1:T(8,128)(2,1)S(1)}, u32[]{:S(2)}, u32[]{:S(2)}) %collective-permute-start.60) | collective-permute-done | bytes 589856 | tf_op jit(solution)/shard_map/ppermute | solution.py:24
  595.5 25.9 %collective-permute-done.54 = bf16[2,256,1152]{2,1,0:T(8,128)(2,1)S(1)} collective-permute-done((bf16[2,256,1152]{2,1,0:T(8,128)(2,1)S(1)}, bf16[2,256,1152]{2,1,0:T(8,128)(2,1)S(1)}, u32[]{:S(2)}, u32[]{:S(2)}) %collective-permute-start.54) | collective-permute-done | bytes 1179680 | tf_op jit(solution)/shard_map/ppermute | solution.py:24
  624.6 26.3 %collective-permute-done.62 = bf16[1152,256]{0,1:T(8,128)(2,1)S(1)} collective-permute-done((bf16[1152,256]{0,1:T(8,128)(2,1)S(1)}, bf16[1152,256]{0,1:T(8,128)(2,1)S(1)}, u32[]{:S(2)}, u32[]{:S(2)}) %collective-permute-start.62) | collective-permute-done | bytes 589856 | tf_op jit(solution)/shard_map/ppermute | solution.py:24
  659.2 80.3 %collective-permute-done.39 = bf16[3,512,256]{1,2,0:T(8,128)(2,1)S(1)} collective-permute-done((bf16[3,512,256]{1,2,0:T(8,128)(2,1)S(1)}, bf16[3,512,256]{1,2,0:T(8,128)(2,1)S(1)}, u32[]{:S(2)}, u32[]{:S(2)}) %collective-permute-start.39) | collective-permute-done | bytes 786464 | tf_op jit(solution)/shard_map/ppermute | solution.py:24
  749.5 43.2 %collective-permute-done.40 = bf16[3,256,256]{1,2,0:T(8,128)(2,1)S(1)} collective-permute-done((bf16[3,256,256]{1,2,0:T(8,128)(2,1)S(1)}, bf16[3,256,256]{1,2,0:T(8,128)(2,1)S(1)}, u32[]{:S(2)}, u32[]{:S(2)}) %collective-permute-start.40) | collective-permute-done | bytes 393248 | tf_op jit(solution)/shard_map/ppermute | solution.py:24
  799.4 33.6 %collective-permute-done.41 = bf16[3,128,256]{1,2,0:T(8,128)(2,1)} collective-permute-done((bf16[3,128,256]{1,2,0:T(8,128)(2,1)}, bf16[3,128,256]{1,2,0:T(8,128)(2,1)}, u32[]{:S(2)}, u32[]{:S(2)}) %collective-permute-start.41) | collective-permute-done | bytes 196640 | tf_op jit(solution)/shard_map/ppermute | solution.py:24
  847.5 4.8 collective-permute-done.65
  864.1 4.2 multiply_subtract_fusion
  (567 shorter events, 266.6 us)
Async XLA Ops:
  2.1 94.7 %collective-permute-start = (bf16[16,1024]{1,0:T(8,128)(2,1)}, bf16[16,1024]{1,0:T(8,128)(2,1)}, u32[]{:S(2)}, u32[]{:S(2)}) collective-permute-start(bf16[16,1024]{1,0:T(8,128)(2,1)} %slice.502), channel_id=1, source_target_pairs={{0,1},{1,2},{2,3},{4,5},{5,6},{6,7},{8,9},{9,10},{10,11},{12,13},{... | collective-permute-start | bytes 98312 | tf_op jit(solution)/shard_map/ppermute | solution.py:215
  6.1 94.3 %collective-permute-start.1 = (bf16[3,128,256]{2,1,0:T(8,128)(2,1)S(1)}, bf16[3,128,256]{2,1,0:T(8,128)(2,1)S(1)}, u32[]{:S(2)}, u32[]{:S(2)}) collective-permute-start(bf16[3,128,256]{2,1,0:T(8,128)(2,1)S(1)} %convert_element_type.454), channel_id=1, source_target_pairs={{0,8},{4,12},{8,0},{12,4},{16,24},{20,28},{24,16},{28,20},{1,9},{5... | collective-permute-start | bytes 589832 | tf_op jit(solution)/shard_map/ppermute | solution.py:24
  9.5 90.8 %collective-permute-start.9 = (bf16[256,128]{1,0:T(8,128)(2,1)S(1)}, bf16[256,128]{1,0:T(8,128)(2,1)S(1)}, u32[]{:S(2)}, u32[]{:S(2)}) collective-permute-start(bf16[256,128]{1,0:T(8,128)(2,1)S(1)} %convert_element_type.457), channel_id=1, source_target_pairs={{0,8},{4,12},{8,0},{12,4},{16,24},{20,28},{24,16},{28,20},{1,9},{5... | collective-permute-start | bytes 196616 | tf_op jit(solution)/shard_map/ppermute | solution.py:24
  10.9 127.6 %collective-permute-start.17 = (bf16[2,128,1152]{2,1,0:T(8,128)(2,1)S(1)}, bf16[2,128,1152]{2,1,0:T(8,128)(2,1)S(1)}, u32[]{:S(2)}, u32[]{:S(2)}) collective-permute-start(bf16[2,128,1152]{2,1,0:T(8,128)(2,1)S(1)} %convert_element_type.459), channel_id=1, source_target_pairs={{0,8},{4,12},{8,0},{12,4},{16,24},{20,28},{24,16},{28,20},{1,9},{5... | collective-permute-start | bytes 1769480 | tf_op jit(solution)/shard_map/ppermute | solution.py:24
  13.0 112.7 %collective-permute-start.20 = (bf16[1152,128]{1,0:T(8,128)(2,1)S(1)}, bf16[1152,128]{1,0:T(8,128)(2,1)S(1)}, u32[]{:S(2)}, u32[]{:S(2)}) collective-permute-start(bf16[1152,128]{1,0:T(8,128)(2,1)S(1)} %convert_element_type.461), channel_id=1, source_target_pairs={{0,8},{4,12},{8,0},{12,4},{16,24},{20,28},{24,16},{28,20},{1,9},{5... | collective-permute-start | bytes 884744 | tf_op jit(solution)/shard_map/ppermute | solution.py:24
  100.5 33.5 %collective-permute-start.2 = (bf16[3,256,256]{2,1,0:T(8,128)(2,1)S(1)}, bf16[3,256,256]{2,1,0:T(8,128)(2,1)S(1)}, u32[]{:S(2)}, u32[]{:S(2)}) collective-permute-start(bf16[3,256,256]{2,1,0:T(8,128)(2,1)S(1)} %pad_maximum_fusion.22), channel_id=1, source_target_pairs={{0,16},{4,20},{8,24},{12,28},{16,0},{20,4},{24,8},{28,12},{1,17},{... | collective-permute-start | bytes 1179656 | tf_op jit(solution)/shard_map/ppermute | solution.py:24
  125.8 46.2 %collective-permute-start.21 = (bf16[1152,256]{1,0:T(8,128)(2,1)S(1)}, bf16[1152,256]{1,0:T(8,128)(2,1)S(1)}, u32[]{:S(2)}, u32[]{:S(2)}) collective-permute-start(bf16[1152,256]{1,0:T(8,128)(2,1)S(1)} %pad_maximum_fusion.20), channel_id=1, source_target_pairs={{0,16},{4,20},{8,24},{12,28},{16,0},{20,4},{24,8},{28,12},{1,17},{... | collective-permute-start | bytes 1769480 | tf_op jit(solution)/shard_map/ppermute | solution.py:24
  134.1 40.7 %collective-permute-start.5 = (bf16[3,512,256]{2,1,0:T(8,128)(2,1)S(1)}, bf16[3,512,256]{2,1,0:T(8,128)(2,1)S(1)}, u32[]{:S(2)}, u32[]{:S(2)}) collective-permute-start(bf16[3,512,256]{2,1,0:T(8,128)(2,1)S(1)} %pad_maximum_fusion.17), channel_id=1, source_target_pairs={{0,2},{1,3},{2,0},{3,1},{4,6},{5,7},{6,4},{7,5},{8,10},{9,11},{10,... | collective-permute-start | bytes 2359304 | tf_op jit(solution)/shard_map/ppermute | solution.py:24
  138.4 33.6 %collective-permute-start.14 = (bf16[256,256]{1,0:T(8,128)(2,1)S(1)}, bf16[256,256]{1,0:T(8,128)(2,1)S(1)}, u32[]{:S(2)}, u32[]{:S(2)}) collective-permute-start(bf16[256,256]{1,0:T(8,128)(2,1)S(1)} %slice.648), channel_id=1, source_target_pairs={{0,4},{4,0},{8,12},{12,8},{16,20},{20,16},{24,28},{28,24},{1,5},{5... | collective-permute-start | bytes 393224 | tf_op jit(solution)/shard_map/ppermute | solution.py:24
  138.5 41.0 %collective-permute-start.3 = (bf16[3,512,256]{2,1,0:T(8,128)(2,1)S(1)}, bf16[3,512,256]{2,1,0:T(8,128)(2,1)S(1)}, u32[]{:S(2)}, u32[]{:S(2)}) collective-permute-start(bf16[3,512,256]{2,1,0:T(8,128)(2,1)S(1)} %pad_maximum_fusion.17), channel_id=1, source_target_pairs={{0,4},{4,0},{8,12},{12,8},{16,20},{20,16},{24,28},{28,24},{1,5},{5... | collective-permute-start | bytes 2359304 | tf_op jit(solution)/shard_map/ppermute | solution.py:24
  145.6 65.4 %collective-permute-start.18 = (bf16[2,256,1152]{2,1,0:T(8,128)(2,1)S(1)}, bf16[2,256,1152]{2,1,0:T(8,128)(2,1)S(1)}, u32[]{:S(2)}, u32[]{:S(2)}) collective-permute-start(bf16[2,256,1152]{2,1,0:T(8,128)(2,1)S(1)} %pad_maximum_fusion.13), channel_id=1, source_target_pairs={{0,16},{4,20},{8,24},{12,28},{16,0},{20,4},{24,8},{28,12},{1,17},{... | collective-permute-start | bytes 3538952 | tf_op jit(solution)/shard_map/ppermute | solution.py:24
  172.0 42.5 %collective-permute-start.22 = (bf16[1152,512]{1,0:T(8,128)(2,1)S(1)}, bf16[1152,512]{1,0:T(8,128)(2,1)S(1)}, u32[]{:S(2)}, u32[]{:S(2)}) collective-permute-start(bf16[1152,512]{1,0:T(8,128)(2,1)S(1)} %pad_maximum_fusion.14), channel_id=1, source_target_pairs={{0,4},{4,0},{8,12},{12,8},{16,20},{20,16},{24,28},{28,24},{1,5},{5... | collective-permute-start | bytes 3538952 | tf_op jit(solution)/shard_map/ppermute | solution.py:24
  174.7 38.5 %collective-permute-start.28 = (bf16[1152,512]{1,0:T(8,128)(2,1)S(1)}, bf16[1152,512]{1,0:T(8,128)(2,1)S(1)}, u32[]{:S(2)}, u32[]{:S(2)}) collective-permute-start(bf16[1152,512]{1,0:T(8,128)(2,1)S(1)} %pad_maximum_fusion.14), channel_id=1, source_target_pairs={{0,2},{1,3},{2,0},{3,1},{4,6},{5,7},{6,4},{7,5},{8,10},{9,11},{10,... | collective-permute-start | bytes 3538952 | tf_op jit(solution)/shard_map/ppermute | solution.py:24
  178.3 30.1 %collective-permute-start.6 = (bf16[3,256,256]{2,1,0:T(8,128)(2,1)S(1)}, bf16[3,256,256]{2,1,0:T(8,128)(2,1)S(1)}, u32[]{:S(2)}, u32[]{:S(2)}) collective-permute-start(bf16[3,256,256]{2,1,0:T(8,128)(2,1)S(1)} %slice.637), channel_id=1, source_target_pairs={{0,4},{4,0},{8,12},{12,8},{16,20},{20,16},{24,28},{28,24},{1,5},{5... | collective-permute-start | bytes 1179656 | tf_op jit(solution)/shard_map/ppermute | solution.py:24
  179.5 31.5 %collective-permute-start.7 = (bf16[3,256,256]{2,1,0:T(8,128)(2,1)S(1)}, bf16[3,256,256]{2,1,0:T(8,128)(2,1)S(1)}, u32[]{:S(2)}, u32[]{:S(2)}) collective-permute-start(bf16[3,256,256]{2,1,0:T(8,128)(2,1)S(1)} %slice.638), channel_id=1, source_target_pairs={{0,2},{1,3},{2,0},{3,1},{4,6},{5,7},{6,4},{7,5},{8,10},{9,11},{10,... | collective-permute-start | bytes 1179656 | tf_op jit(solution)/shard_map/ppermute | solution.py:24
  208.4 43.0 %collective-permute-start.12 = (bf16[256,1024]{1,0:T(8,128)(2,1)S(1)}, bf16[256,1024]{1,0:T(8,128)(2,1)S(1)}, u32[]{:S(2)}, u32[]{:S(2)}) collective-permute-start(bf16[256,1024]{1,0:T(8,128)(2,1)S(1)} %pad_maximum_fusion.21), channel_id=1, source_target_pairs={{0,1},{1,0},{2,3},{3,2},{4,5},{5,4},{6,7},{7,6},{8,9},{9,8},{10,11... | collective-permute-start | bytes 1572872 | tf_op jit(solution)/shard_map/ppermute | solution.py:24
  211.1 27.8 %collective-permute-start.8 = (bf16[3,1024,256]{2,1,0:T(8,128)(2,1)S(1)}, bf16[3,1024,256]{2,1,0:T(8,128)(2,1)S(1)}, u32[]{:S(2)}, u32[]{:S(2)}) collective-permute-start(bf16[3,1024,256]{2,1,0:T(8,128)(2,1)S(1)} %constant_dynamic-update-slice_fusion.10), channel_id=1, source_target_pairs={{0,1},{1,0},{2,3},{3,2},{4,5},{5,4},{6,7},{7,6},{8,9},{9,8},{10,11... | collective-permute-start | bytes 4718600 | tf_op jit(solution)/shard_map/ppermute | solution.py:24
  229.8 53.8 %collective-permute-start.19 = (bf16[2,512,1152]{2,1,0:T(8,128)(2,1)}, bf16[2,512,1152]{2,1,0:T(8,128)(2,1)S(1)}, u32[]{:S(2)}, u32[]{:S(2)}) collective-permute-start(bf16[2,512,1152]{2,1,0:T(8,128)(2,1)} %pad_maximum_fusion.5), channel_id=1, source_target_pairs={{0,4},{4,0},{8,12},{12,8},{16,20},{20,16},{24,28},{28,24},{1,5},{5... | collective-permute-start | bytes 7077896 | tf_op jit(solution)/shard_map/ppermute | solution.py:24
  237.9 70.1 %collective-permute-start.25 = (bf16[2,512,1152]{2,1,0:T(8,128)(2,1)}, bf16[2,512,1152]{2,1,0:T(8,128)(2,1)S(1)}, u32[]{:S(2)}, u32[]{:S(2)}) collective-permute-start(bf16[2,512,1152]{2,1,0:T(8,128)(2,1)} %pad_maximum_fusion.5), channel_id=1, source_target_pairs={{0,2},{1,3},{2,0},{3,1},{4,6},{5,7},{6,4},{7,5},{8,10},{9,11},{10,... | collective-permute-start | bytes 7077896 | tf_op jit(solution)/shard_map/ppermute | solution.py:24
  238.9 89.9 %collective-permute-start.24 = (bf16[1152,1024]{1,0:T(8,128)(2,1)}, bf16[1152,1024]{1,0:T(8,128)(2,1)}, u32[]{:S(2)}, u32[]{:S(2)}) collective-permute-start(bf16[1152,1024]{1,0:T(8,128)(2,1)} %pad_maximum_fusion.6), channel_id=1, source_target_pairs={{0,1},{1,0},{2,3},{3,2},{4,5},{5,4},{6,7},{7,6},{8,9},{9,8},{10,11... | collective-permute-start | bytes 7077896 | tf_op jit(solution)/shard_map/ppermute | solution.py:24
  251.4 166.0 %collective-permute-start.32 = (bf16[1152,1024]{1,0:T(8,128)(2,1)}, bf16[1152,1024]{1,0:T(8,128)(2,1)S(1)}, u32[]{:S(2)}, u32[]{:S(2)}) collective-permute-start(bf16[1152,1024]{1,0:T(8,128)(2,1)} %constant_dynamic-update-slice_fusion.19), channel_id=1, source_target_pairs={{0,1},{1,0},{2,3},{3,2},{4,5},{5,4},{6,7},{7,6},{8,9},{9,8},{10,11... | collective-permute-start | bytes 7077896 | tf_op jit(solution)/shard_map/ppermute | solution.py:24
  291.9 85.1 %collective-permute-start.23 = (bf16[2,1024,1152]{2,1,0:T(8,128)(2,1)S(1)}, bf16[2,1024,1152]{2,1,0:T(8,128)(2,1)S(1)}, u32[]{:S(2)}, u32[]{:S(2)}) collective-permute-start(bf16[2,1024,1152]{2,1,0:T(8,128)(2,1)S(1)} %pad_maximum_fusion.1), channel_id=1, source_target_pairs={{0,1},{1,0},{2,3},{3,2},{4,5},{5,4},{6,7},{7,6},{8,9},{9,8},{10,11... | collective-permute-start | bytes 14155784 | tf_op jit(solution)/shard_map/ppermute | solution.py:24
  308.1 28.4 %collective-permute-start.26 = (bf16[2,256,1152]{2,1,0:T(8,128)(2,1)S(1)}, bf16[2,256,1152]{2,1,0:T(8,128)(2,1)S(1)}, u32[]{:S(2)}, u32[]{:S(2)}) collective-permute-start(bf16[2,256,1152]{2,1,0:T(8,128)(2,1)S(1)} %slice.655), channel_id=1, source_target_pairs={{0,4},{4,0},{8,12},{12,8},{16,20},{20,16},{24,28},{28,24},{1,5},{5... | collective-permute-start | bytes 3538952 | tf_op jit(solution)/shard_map/ppermute | solution.py:24
  309.5 28.2 %collective-permute-start.27 = (bf16[2,256,1152]{2,1,0:T(8,128)(2,1)S(1)}, bf16[2,256,1152]{2,1,0:T(8,128)(2,1)S(1)}, u32[]{:S(2)}, u32[]{:S(2)}) collective-permute-start(bf16[2,256,1152]{2,1,0:T(8,128)(2,1)S(1)} %slice.656), channel_id=1, source_target_pairs={{0,2},{1,3},{2,0},{3,1},{4,6},{5,7},{6,4},{7,5},{8,10},{9,11},{10,... | collective-permute-start | bytes 3538952 | tf_op jit(solution)/shard_map/ppermute | solution.py:24
  338.8 72.2 %collective-permute-start.31 = (bf16[2,1024,1152]{2,1,0:T(8,128)(2,1)}, bf16[2,1024,1152]{2,1,0:T(8,128)(2,1)S(1)}, u32[]{:S(2)}, u32[]{:S(2)}) collective-permute-start(bf16[2,1024,1152]{2,1,0:T(8,128)(2,1)} %constant_dynamic-update-slice_fusion.16), channel_id=1, source_target_pairs={{0,1},{1,0},{2,3},{3,2},{4,5},{5,4},{6,7},{7,6},{8,9},{9,8},{10,11... | collective-permute-start | bytes 14155784 | tf_op jit(solution)/shard_map/ppermute | solution.py:24
  472.6 68.4 %collective-permute-start.51 = (bf16[2,1024,1152]{2,1,0:T(8,128)(2,1)}, bf16[2,1024,1152]{2,1,0:T(8,128)(2,1)}, u32[]{:S(2)}, u32[]{:S(2)}) collective-permute-start(bf16[2,1024,1152]{2,1,0:T(8,128)(2,1)} %pad_maximum_fusion.4), channel_id=1, source_target_pairs={{0,1},{1,0},{2,3},{3,2},{4,5},{5,4},{6,7},{7,6},{8,9},{9,8},{10,11... | collective-permute-start | bytes 14155784 | tf_op jit(solution)/shard_map/ppermute | solution.py:24
  474.9 34.2 %collective-permute-start.43 = (bf16[256,1024]{0,1:T(8,128)(2,1)}, bf16[256,1024]{0,1:T(8,128)(2,1)}, u32[]{:S(2)}, u32[]{:S(2)}) collective-permute-start(bf16[256,1024]{0,1:T(8,128)(2,1)} %get-tuple-element.150), channel_id=1, source_target_pairs={{0,1},{1,0},{2,3},{3,2},{4,5},{5,4},{6,7},{7,6},{8,9},{9,8},{10,11... | collective-permute-start | bytes 1572872 | tf_op jit(solution)/shard_map/ppermute | solution.py:24
  474.9 47.8 %collective-permute-start.42 = (bf16[256,1024]{0,1:T(8,128)(2,1)}, bf16[256,1024]{0,1:T(8,128)(2,1)}, u32[]{:S(2)}, u32[]{:S(2)}) collective-permute-start(bf16[256,1024]{0,1:T(8,128)(2,1)} %get-tuple-element.149), channel_id=1, source_target_pairs={{0,1},{1,0},{2,3},{3,2},{4,5},{5,4},{6,7},{7,6},{8,9},{9,8},{10,11... | collective-permute-start | bytes 1572872 | tf_op jit(solution)/shard_map/ppermute | solution.py:24
  504.0 36.3 %collective-permute-start.35 = (bf16[3,1024,256]{1,2,0:T(8,128)(2,1)S(1)}, bf16[3,1024,256]{1,2,0:T(8,128)(2,1)S(1)}, u32[]{:S(2)}, u32[]{:S(2)}) collective-permute-start(bf16[3,1024,256]{1,2,0:T(8,128)(2,1)S(1)} %fusion.47), channel_id=1, source_target_pairs={{0,1},{1,0},{2,3},{3,2},{4,5},{5,4},{6,7},{7,6},{8,9},{9,8},{10,11... | collective-permute-start | bytes 4718600 | tf_op jit(solution)/shard_map/ppermute | solution.py:24
  516.3 38.3 %collective-permute-start.59 = (bf16[1152,1024]{0,1:T(8,128)(2,1)S(1)}, bf16[1152,1024]{0,1:T(8,128)(2,1)S(1)}, u32[]{:S(2)}, u32[]{:S(2)}) collective-permute-start(bf16[1152,1024]{0,1:T(8,128)(2,1)S(1)} %copy-done.91), channel_id=1, source_target_pairs={{0,1},{1,0},{2,3},{3,2},{4,5},{5,4},{6,7},{7,6},{8,9},{9,8},{10,11... | collective-permute-start | bytes 7077896 | tf_op jit(solution)/shard_map/ppermute | solution.py:24
  528.7 66.8 %collective-permute-start.50 = (bf16[2,1024,1152]{2,1,0:T(8,128)(2,1)S(1)}, bf16[2,1024,1152]{2,1,0:T(8,128)(2,1)S(1)}, u32[]{:S(2)}, u32[]{:S(2)}) collective-permute-start(bf16[2,1024,1152]{2,1,0:T(8,128)(2,1)S(1)} %bitcast.219), channel_id=1, source_target_pairs={{0,1},{1,0},{2,3},{3,2},{4,5},{5,4},{6,7},{7,6},{8,9},{9,8},{10,11... | collective-permute-start | bytes 14155784 | tf_op jit(solution)/shard_map/ppermute | solution.py:24
  538.3 86.2 %collective-permute-start.58 = (bf16[1152,1024]{0,1:T(8,128)(2,1)}, bf16[1152,1024]{0,1:T(8,128)(2,1)S(1)}, u32[]{:S(2)}, u32[]{:S(2)}) collective-permute-start(bf16[1152,1024]{0,1:T(8,128)(2,1)} %convolution_convert_fusion.2), channel_id=1, source_target_pairs={{0,1},{1,0},{2,3},{3,2},{4,5},{5,4},{6,7},{7,6},{8,9},{9,8},{10,11... | collective-permute-start | bytes 7077896 | tf_op jit(solution)/shard_map/ppermute | solution.py:24
  552.1 27.0 %collective-permute-start.52 = (bf16[2,256,1152]{2,1,0:T(8,128)(2,1)S(1)}, bf16[2,256,1152]{2,1,0:T(8,128)(2,1)S(1)}, u32[]{:S(2)}, u32[]{:S(2)}) collective-permute-start(bf16[2,256,1152]{2,1,0:T(8,128)(2,1)S(1)} %add_convert_fusion.6), channel_id=1, source_target_pairs={{0,4},{4,0},{8,12},{12,8},{16,20},{20,16},{24,28},{28,24},{1,5},{5... | collective-permute-start | bytes 3538952 | tf_op jit(solution)/shard_map/ppermute | solution.py:24
  556.8 95.8 %collective-permute-start.70 = (f32[5,1024]{1,0:T(8,128)S(1)}, f32[5,1024]{1,0:T(8,128)S(1)}, u32[]{:S(2)}, u32[]{:S(2)}) collective-permute-start(f32[5,1024]{1,0:T(8,128)S(1)} %add.705), channel_id=1, source_target_pairs={{0,16},{4,20},{8,24},{12,28},{16,0},{20,4},{24,8},{28,12},{1,17},{... | collective-permute-start | bytes 61448 | tf_op jit(solution)/shard_map/ppermute | solution.py:24
  564.8 90.0 %collective-permute-start.48 = (bf16[256,256]{0,1:T(8,128)(2,1)}, bf16[256,256]{0,1:T(8,128)(2,1)}, u32[]{:S(2)}, u32[]{:S(2)}) collective-permute-start(bf16[256,256]{0,1:T(8,128)(2,1)} %slice.976), channel_id=1, source_target_pairs={{0,16},{4,20},{8,24},{12,28},{16,0},{20,4},{24,8},{28,12},{1,17},{... | collective-permute-start | bytes 393224 | tf_op jit(solution)/shard_map/ppermute | solution.py:24
  592.6 28.9 %collective-permute-start.54 = (bf16[2,256,1152]{2,1,0:T(8,128)(2,1)S(1)}, bf16[2,256,1152]{2,1,0:T(8,128)(2,1)S(1)}, u32[]{:S(2)}, u32[]{:S(2)}) collective-permute-start(bf16[2,256,1152]{2,1,0:T(8,128)(2,1)S(1)} %get-tuple-element.112), channel_id=1, source_target_pairs={{0,2},{1,3},{2,0},{3,1},{4,6},{5,7},{6,4},{7,5},{8,10},{9,11},{10,... | collective-permute-start | bytes 3538952 | tf_op jit(solution)/shard_map/ppermute | solution.py:24
  595.5 60.2 %collective-permute-start.37 = (bf16[3,512,256]{1,2,0:T(8,128)(2,1)}, bf16[3,512,256]{1,2,0:T(8,128)(2,1)S(1)}, u32[]{:S(2)}, u32[]{:S(2)}) collective-permute-start(bf16[3,512,256]{1,2,0:T(8,128)(2,1)} %pad_maximum_fusion.18), channel_id=1, source_target_pairs={{0,2},{1,3},{2,0},{3,1},{4,6},{5,7},{6,4},{7,5},{8,10},{9,11},{10,... | collective-permute-start | bytes 2359304 | tf_op jit(solution)/shard_map/ppermute | solution.py:24
  621.5 29.5 %collective-permute-start.62 = (bf16[1152,256]{0,1:T(8,128)(2,1)S(1)}, bf16[1152,256]{0,1:T(8,128)(2,1)S(1)}, u32[]{:S(2)}, u32[]{:S(2)}) collective-permute-start(bf16[1152,256]{0,1:T(8,128)(2,1)S(1)} %get-tuple-element.129), channel_id=1, source_target_pairs={{0,2},{1,3},{2,0},{3,1},{4,6},{5,7},{6,4},{7,5},{8,10},{9,11},{10,... | collective-permute-start | bytes 1769480 | tf_op jit(solution)/shard_map/ppermute | solution.py:24
  624.6 120.0 %collective-permute-start.53 = (bf16[2,512,1152]{2,1,0:T(8,128)(2,1)S(1)}, bf16[2,512,1152]{2,1,0:T(8,128)(2,1)S(1)}, u32[]{:S(2)}, u32[]{:S(2)}) collective-permute-start(bf16[2,512,1152]{2,1,0:T(8,128)(2,1)S(1)} %pad_maximum_fusion.7), channel_id=1, source_target_pairs={{0,2},{1,3},{2,0},{3,1},{4,6},{5,7},{6,4},{7,5},{8,10},{9,11},{10,... | collective-permute-start | bytes 7077896 | tf_op jit(solution)/shard_map/ppermute | solution.py:24
  651.0 93.5 %collective-permute-start.55 = (bf16[2,512,1152]{2,1,0:T(8,128)(2,1)S(1)}, bf16[2,512,1152]{2,1,0:T(8,128)(2,1)S(1)}, u32[]{:S(2)}, u32[]{:S(2)}) collective-permute-start(bf16[2,512,1152]{2,1,0:T(8,128)(2,1)S(1)} %pad_maximum_fusion.8), channel_id=1, source_target_pairs={{0,4},{4,0},{8,12},{12,8},{16,20},{20,16},{24,28},{28,24},{1,5},{5... | collective-permute-start | bytes 7077896 | tf_op jit(solution)/shard_map/ppermute | solution.py:24
  652.7 87.4 %collective-permute-start.61 = (bf16[1152,512]{0,1:T(8,128)(2,1)S(1)}, bf16[1152,512]{0,1:T(8,128)(2,1)S(1)}, u32[]{:S(2)}, u32[]{:S(2)}) collective-permute-start(bf16[1152,512]{0,1:T(8,128)(2,1)S(1)} %pad_maximum_fusion.15), channel_id=1, source_target_pairs={{0,2},{1,3},{2,0},{3,1},{4,6},{5,7},{6,4},{7,5},{8,10},{9,11},{10,... | collective-permute-start | bytes 3538952 | tf_op jit(solution)/shard_map/ppermute | solution.py:24
  654.7 87.7 %collective-permute-start.63 = (bf16[1152,512]{0,1:T(8,128)(2,1)S(1)}, bf16[1152,512]{0,1:T(8,128)(2,1)S(1)}, u32[]{:S(2)}, u32[]{:S(2)}) collective-permute-start(bf16[1152,512]{0,1:T(8,128)(2,1)S(1)} %pad_maximum_fusion.16), channel_id=1, source_target_pairs={{0,4},{4,0},{8,12},{12,8},{16,20},{20,16},{24,28},{28,24},{1,5},{5... | collective-permute-start | bytes 3538952 | tf_op jit(solution)/shard_map/ppermute | solution.py:24
  655.7 83.8 %collective-permute-start.39 = (bf16[3,512,256]{1,2,0:T(8,128)(2,1)S(1)}, bf16[3,512,256]{1,2,0:T(8,128)(2,1)S(1)}, u32[]{:S(2)}, u32[]{:S(2)}) collective-permute-start(bf16[3,512,256]{1,2,0:T(8,128)(2,1)S(1)} %pad_maximum_fusion.19), channel_id=1, source_target_pairs={{0,4},{4,0},{8,12},{12,8},{16,20},{20,16},{24,28},{28,24},{1,5},{5... | collective-permute-start | bytes 2359304 | tf_op jit(solution)/shard_map/ppermute | solution.py:24
  739.5 54.1 %collective-permute-start.49 = (bf16[256,128]{0,1:T(8,128)(2,1)S(1)}, bf16[256,128]{0,1:T(8,128)(2,1)S(1)}, u32[]{:S(2)}, u32[]{:S(2)}) collective-permute-start(bf16[256,128]{0,1:T(8,128)(2,1)S(1)} %slice.977), channel_id=1, source_target_pairs={{0,8},{4,12},{8,0},{12,4},{16,24},{20,28},{24,16},{28,20},{1,9},{5... | collective-permute-start | bytes 196616 | tf_op jit(solution)/shard_map/ppermute | solution.py:24
  740.1 52.6 %collective-permute-start.40 = (bf16[3,256,256]{1,2,0:T(8,128)(2,1)S(1)}, bf16[3,256,256]{1,2,0:T(8,128)(2,1)S(1)}, u32[]{:S(2)}, u32[]{:S(2)}) collective-permute-start(bf16[3,256,256]{1,2,0:T(8,128)(2,1)S(1)} %slice.973), channel_id=1, source_target_pairs={{0,16},{4,20},{8,24},{12,28},{16,0},{20,4},{24,8},{28,12},{1,17},{... | collective-permute-start | bytes 1179656 | tf_op jit(solution)/shard_map/ppermute | solution.py:24
  743.9 97.2 %collective-permute-start.64 = (bf16[1152,256]{0,1:T(8,128)(2,1)}, bf16[1152,256]{0,1:T(8,128)(2,1)}, u32[]{:S(2)}, u32[]{:S(2)}) collective-permute-start(bf16[1152,256]{0,1:T(8,128)(2,1)} %slice.971), channel_id=1, source_target_pairs={{0,16},{4,20},{8,24},{12,28},{16,0},{20,4},{24,8},{28,12},{1,17},{... | collective-permute-start | bytes 1769480 | tf_op jit(solution)/shard_map/ppermute | solution.py:24
  747.2 95.2 %collective-permute-start.56 = (bf16[2,256,1152]{2,1,0:T(8,128)(2,1)}, bf16[2,256,1152]{2,1,0:T(8,128)(2,1)}, u32[]{:S(2)}, u32[]{:S(2)}) collective-permute-start(bf16[2,256,1152]{2,1,0:T(8,128)(2,1)} %slice.970), channel_id=1, source_target_pairs={{0,16},{4,20},{8,24},{12,28},{16,0},{20,4},{24,8},{28,12},{1,17},{... | collective-permute-start | bytes 3538952 | tf_op jit(solution)/shard_map/ppermute | solution.py:24
  793.6 39.4 %collective-permute-start.41 = (bf16[3,128,256]{1,2,0:T(8,128)(2,1)}, bf16[3,128,256]{1,2,0:T(8,128)(2,1)}, u32[]{:S(2)}, u32[]{:S(2)}) collective-permute-start(bf16[3,128,256]{1,2,0:T(8,128)(2,1)} %slice.975), channel_id=1, source_target_pairs={{0,8},{4,12},{8,0},{12,4},{16,24},{20,28},{24,16},{28,20},{1,9},{5... | collective-permute-start | bytes 589832 | tf_op jit(solution)/shard_map/ppermute | solution.py:24
  (139 other events, 2825.4 us)

commit v2 on v1

v2 whole, which is shorter than its diff:
```python
import functools

import jax
import jax.numpy as jnp
from jax import lax
from jax.experimental import pallas as pl
from jax.experimental.pallas import tpu as pltpu
from jax.sharding import PartitionSpec as P

KW = 3
STEP = 10
HALO = 16
PARTS = 3

EPS_NORM = 1e-05
EPS_ADAM = 1e-08
BETA_FIRST = 0.9
BETA_SECOND = 0.95
RATE_MATRIX = 0.05
RATE_SMALL = 0.5
DECAY = 0.1

BF = jnp.bfloat16
F32 = jnp.float32


def swap(values, axis, bit):
    size = lax.axis_size(axis)
    return lax.ppermute(values, axis, [(i, i ^ bit) for i in range(size)])


def halves(values, axis):
    size = values.shape[axis] // 2
    return (
        lax.slice_in_dim(values, 0, size, axis=axis),
        lax.slice_in_dim(values, size, 2 * size, axis=axis),
    )


def low_bits():
    return (
        [2 << i for i in range((lax.axis_size("dp") // 2).bit_length() - 1)],
        [4 << i for i in range((lax.axis_size("tensor") // 4).bit_length() - 1)],
    )


def gather_weight(shard, wide, cut):
    z_bits, t_bits = low_bits()
    own = shard
    for bit in z_bits:
        own = jnp.concatenate([own, swap(own, "dp", bit)], wide)
    for bit in t_bits:
        own = jnp.concatenate([own, swap(own, "tensor", bit)], cut)
    by_x = swap(own, "dp", 1)
    by_y = swap(own, "tensor", 2)
    near = jnp.concatenate([own, by_x], wide)
    near_core = swap(near, "tensor", 1)
    far_first = swap(halves(by_y, wide)[0], "dp", 1)
    far_second = swap(halves(by_x, wide)[1], "tensor", 2)
    far = jnp.concatenate([by_y, far_first, far_second], wide)
    far_core = swap(far, "tensor", 1)
    return near, near_core, far, far_core


def plus(left, right):
    return (left.astype(F32) + right.astype(F32)).astype(BF)


def scatter_corner(far, far_in, wide):
    far_high, far_in_high = halves(far, wide)[1], halves(far_in, wide)[1]
    corner = [plus(a, b) for a, b in zip(halves(far_high, wide), halves(far_in_high, wide))]
    return swap(corner[0], "dp", 1), swap(corner[1], "tensor", 2)


def scatter_sides(near, near_in, far, far_in, to_x, to_y, wide):
    far_low, far_in_low = halves(far, wide)[0], halves(far_in, wide)[0]
    near_high, near_in_high = halves(near, wide)[1], halves(near_in, wide)[1]
    far_parts = [a.astype(F32) + b.astype(F32) for a, b in zip(halves(far_low, wide), halves(far_in_low, wide))]
    near_parts = [
        a.astype(F32) + b.astype(F32) for a, b in zip(halves(near_high, wide), halves(near_in_high, wide))
    ]
    by_y = jnp.concatenate(
        [(far_parts[0] + to_x.astype(F32)).astype(BF), far_parts[1].astype(BF)], wide
    )
    by_x = jnp.concatenate(
        [near_parts[0].astype(BF), (near_parts[1] + to_y.astype(F32)).astype(BF)], wide
    )
    return swap(by_x, "dp", 1), swap(by_y, "tensor", 2)


def scatter_rest(near, near_in, got_x, got_y, wide, cut):
    z_bits, t_bits = low_bits()
    terms = [halves(near, wide)[0], halves(near_in, wide)[0], got_x, got_y]
    total = None
    for axis, bits, name in ((cut, t_bits, "tensor"), (wide, z_bits, "dp")):
        for bit in reversed(bits):
            parts = [halves(term, axis) for term in terms]
            give = functools.reduce(jnp.add, [part[1].astype(F32) for part in parts]).astype(BF)
            terms = [part[0] for part in parts] + [swap(give, name, bit)]
    return functools.reduce(jnp.add, [term.astype(F32) for term in terms])


def rotate_left(values, count):
    bits = count.bit_length() - 1
    return ((values << 1) | (values >> (bits - 1))) & (count - 1)


def rotate_right(values, count):
    bits = count.bit_length() - 1
    return ((values & 1) << (bits - 1)) | (values >> 1)


def block_codes(count):
    return [base ^ (e << 2) for base in (0, 1, 2, 3) for e in range(count // 4)]


def block_place(code, count):
    return (code & 3) * (count // 4) + (code >> 2)


def shift_rows(values, start, rows):
    return lax.slice_in_dim(values, start, start + rows, axis=0)


def lag_masks(seg_flat, length):
    positions = jnp.arange(seg_flat.shape[0], dtype=jnp.int32) % length
    masks = []
    for shift in range(1, KW):
        before = jnp.concatenate([jnp.zeros((shift,), seg_flat.dtype), seg_flat[:-shift]], 0)
        same = (positions >= shift) & (seg_flat == before)
        masks.append(jnp.where(same, 1.0, 0.0).astype(F32)[:, None])
    return masks


def rms_scale(values):
    return lax.rsqrt(jnp.mean(values * values, axis=-1, keepdims=True) + EPS_NORM)


def adamw(param, grad, first, second, rate, decay):
    first_new = BETA_FIRST * first + (1.0 - BETA_FIRST) * grad
    second_new = BETA_SECOND * second + (1.0 - BETA_SECOND) * grad * grad
    first_hat = first_new / (1.0 - BETA_FIRST**STEP)
    second_hat = second_new / (1.0 - BETA_SECOND**STEP)
    return (
        param - rate * (first_hat / (jnp.sqrt(second_hat) + EPS_ADAM) + decay * param),
        first_new,
        second_new,
    )


def mm(spec, left, right, out=F32):
    return jnp.einsum(spec, left, right, preferred_element_type=F32).astype(out)


ANY = pl.BlockSpec(memory_space=pl.ANY)
LIMIT = 44 * 1024 * 1024


def params(count=1):
    return pltpu.CompilerParams(
        vmem_limit_bytes=LIMIT, dimension_semantics=("arbitrary",) * count
    )


def whole(shape):
    return pl.BlockSpec(shape, lambda *_: (0,) * len(shape), pipeline_mode=pl.Buffered(1))


def arrange_kernel(order, tokens, before, cot, x_out, cot_out):
    count = order.shape[0]
    width = tokens.shape[1] // count
    for j in range(count):
        spot = pl.ds(pl.multiple_of(order[j] * width, width), width)
        own = pl.ds(j * width, width)
        x_out[:HALO, own] = before[:, spot]
        x_out[HALO:, own] = tokens[:, spot]
        cot_out[:, own] = cot[:, spot]


def pick_blocks(values, places):
    count = places.shape[0]
    width = values.shape[1] // count
    return jnp.concatenate(
        [lax.dynamic_slice_in_dim(values, places[j] * width, width, 1) for j in range(count)], 1
    )


def narrow(order, width):
    return (width // order.shape[0]) % 128 != 0


def to_natural(values, order):
    if not narrow(order, values.shape[1]):
        return values
    return pick_blocks(values, jnp.argsort(order))


def arrange(order, tokens, before, cot):
    rows, width = tokens.shape
    if narrow(order, width):
        extended = jnp.concatenate([before, tokens], 0)
        return pick_blocks(extended, order), pick_blocks(cot, order)
    vmem = pl.BlockSpec(memory_space=pltpu.VMEM)
    return pl.pallas_call(
        arrange_kernel,
        out_shape=(
            jax.ShapeDtypeStruct((rows + HALO, width), BF),
            jax.ShapeDtypeStruct((rows, width), BF),
        ),
        in_specs=[pl.BlockSpec(memory_space=pltpu.SMEM), vmem, vmem, vmem],
        out_specs=(vmem, vmem),
        compiler_params=pltpu.CompilerParams(vmem_limit_bytes=LIMIT),
        name="arrange",
    )(order, tokens, before, cot)


def nt(left, right):
    return lax.dot_general(left, right, (((1,), (1,)), ((), ())), preferred_element_type=F32)


def nn(left, right):
    return jnp.dot(left, right, preferred_element_type=F32)


def ffn_kernel(h, ht, c, ct, wa, wb, *rest):
    ga, gb, branch, back, branch_sum, back_sum = rest[-6:]
    step = pl.program_id(0)
    half = wa.shape[2]
    wg, wu, wd = [jnp.concatenate([wa[k], wb[k]], 1) for k in range(3)]
    gate = nn(h[...], wg)
    up = nn(h[...], wu)
    da = nn(c[...], wd)
    sigma = 1.0 / (1.0 + jnp.exp(-gate))
    silu = gate * sigma
    act = (silu * up).astype(BF)
    dgate = (da * up * sigma * (1.0 + gate * (1.0 - sigma))).astype(BF)
    dup = (da * silu).astype(BF)
    for k, (left, right) in enumerate(((ht, dgate), (ht, dup), (ct, act))):
        grad = nn(left[...], right).astype(BF)
        ga[k] = grad[:, :half]
        gb[k] = grad[:, half:]
    out = nt(act, wd)
    into = nt(jnp.concatenate([dgate, dup], 1), jnp.concatenate([wg, wu], 1))

    @pl.when(step == 0)
    def _():
        branch_sum[...] = out
        back_sum[...] = into

    @pl.when(step > 0)
    def _():
        branch_sum[...] += out
        back_sum[...] += into

    @pl.when(step == pl.num_programs(0) - 1)
    def _():
        branch[...] = branch_sum[...].astype(BF)
        back[...] = back_sum[...].astype(BF)


def ffn(h, ht, c, ct, wa, wb, deps):
    rows, width = h.shape
    cols = wa.shape[2]
    tile = 128
    block = pl.BlockSpec((3, width, tile), lambda j: (0, 0, j))
    grad = jax.ShapeDtypeStruct(wa.shape, BF)
    part = jax.ShapeDtypeStruct((rows, width), BF)
    return pl.pallas_call(
        ffn_kernel,
        grid=(cols // tile,),
        out_shape=(grad, grad, part, part),
        in_specs=[whole((rows, width)), whole((width, rows)), whole((rows, width)), whole((width, rows))]
        + [block, block]
        + [ANY] * len(deps),
        out_specs=(block, block, whole((rows, width)), whole((rows, width))),
        scratch_shapes=[pltpu.VMEM((rows, width), F32)] * 2,
        compiler_params=params(),
        cost_estimate=pl.CostEstimate(
            flops=36 * rows * width * cols,
            bytes_accessed=12 * rows * width + 24 * width * cols,
            transcendentals=2 * rows * cols,
        ),
        name="ffn",
    )(h, ht, c, ct, wa, wb, *deps)


def middle_kernel(order, middle, scale, gain, cot, *rest):
    block_out, grad, grad_low, gain_grad = rest[-4:]
    half = (len(rest) - 4) // 2
    branches, backs = rest[:half], rest[half : 2 * half]
    x2, r2, up = middle[...], scale[...], backs[0][...].astype(F32)
    for ref in backs[1:]:
        up = up + ref[...].astype(F32)
    total = x2
    for ref in branches:
        total = total + ref[...].astype(F32)
    store_natural(order, block_out, total.astype(BF))
    norm_back(x2, r2, gain, up, cot[...].astype(F32), grad, gain_grad)
    grad_low[...] = grad[...].astype(BF)


def store_natural(order, out, total):
    count = order.shape[0]
    if narrow(order, total.shape[1]):
        out[...] = total
        return
    width = total.shape[1] // count
    for j in range(count):
        spot = pl.ds(pl.multiple_of(order[j] * width, width), width)
        out[:, spot] = total[:, j * width : (j + 1) * width]


def norm_back(values, scale, gain, upstream, carried, out, gain_grad, order=None):
    scaled = upstream * gain[...]
    mean = jnp.mean(scaled * values, axis=-1, keepdims=True)
    total = carried + scale * scaled - values * (scale * scale * scale * mean)
    if order is None:
        out[...] = total
    else:
        store_natural(order, out, total)
    sums = jnp.sum(upstream * values * scale, axis=0, keepdims=True)

    @pl.when(pl.program_id(0) == 0)
    def _():
        gain_grad[...] = sums

    @pl.when(pl.program_id(0) > 0)
    def _():
        gain_grad[...] += sums


def row_specs(tile, width):
    return (
        pl.BlockSpec(memory_space=pltpu.SMEM),
        pl.BlockSpec((tile, width), lambda i: (i, 0)),
        pl.BlockSpec((tile, 1), lambda i: (i, 0)),
        pl.BlockSpec((1, width), lambda i: (0, 0)),
    )


def middle_back(order, middle, scale, gain, cot, branches, backs, deps):
    rows, width = middle.shape
    tile = 128
    smem, row, column, single = row_specs(tile, width)
    count = len(branches)

    def kernel(*refs):
        middle_kernel(*refs[: 5 + 2 * count], *refs[5 + 2 * count + len(deps) :])

    return pl.pallas_call(
        kernel,
        grid=(rows // tile,),
        out_shape=(
            jax.ShapeDtypeStruct((rows, width), BF),
            jax.ShapeDtypeStruct((rows, width), F32),
            jax.ShapeDtypeStruct((rows, width), BF),
            jax.ShapeDtypeStruct((1, width), F32),
        ),
        in_specs=[smem, row, column, single, row] + [row] * (2 * count) + [ANY] * len(deps),
        out_specs=(row, row, row, single),
        compiler_params=params(),
        cost_estimate=pl.CostEstimate(
            flops=30 * rows * width, bytes_accessed=(14 + 4 * count) * rows * width, transcendentals=0
        ),
        name="middle_back",
    )(order, middle, scale, gain, cot, *branches, *backs, *deps)


def input_kernel(order, values, scale, gain, carried, upstream, out, gain_grad):
    norm_back(
        values[...].astype(F32), scale[...], gain, upstream[...], carried[...], out, gain_grad, order
    )


def input_back(order, values, scale, gain, carried, upstream):
    rows, width = values.shape
    tile = 128
    smem, row, column, single = row_specs(tile, width)
    return pl.pallas_call(
        input_kernel,
        grid=(rows // tile,),
        out_shape=(
            jax.ShapeDtypeStruct((rows, width), F32),
            jax.ShapeDtypeStruct((1, width), F32),
        ),
        in_specs=[smem, row, column, single, row, row],
        out_specs=(row, single),
        compiler_params=params(),
        cost_estimate=pl.CostEstimate(
            flops=20 * rows * width, bytes_accessed=14 * rows * width, transcendentals=0
        ),
        name="input_back",
    )(order, values, scale, gain, carried, upstream)


def mixer_grad_kernel(ht, dt, pa, pb, ya, yb, *rest):
    ga, gb = rest[-2:]
    step = pl.program_id(0)

    @pl.when(step < 3)
    def _():
        ga[0] = nn(ht[...], pa[0]).astype(BF)
        gb[0] = nn(ht[...], pb[0]).astype(BF)

    @pl.when(step == 3)
    def _():
        ga[0] = nn(dt[...], ya[...]).astype(BF)
        gb[0] = nn(dt[...], yb[...]).astype(BF)


def mixer_grad(ht, dt, proj_grad, gated, first, second, deps):
    width, rows = ht.shape
    cols = gated.shape[1] // 4

    def column(block):
        return pl.BlockSpec((1, rows, cols), lambda k: (jnp.minimum(k, 2), 0, block))

    def gated_column(block):
        return pl.BlockSpec((rows, cols), lambda k: (0, block))

    out = pl.BlockSpec((1, width, cols), lambda k: (k, 0, 0))
    grad = jax.ShapeDtypeStruct((4, width, cols), BF)
    return pl.pallas_call(
        mixer_grad_kernel,
        grid=(4,),
        out_shape=(grad, grad),
        in_specs=[
            whole((width, rows)),
            whole((width, rows)),
            column(first),
            column(second),
            gated_column(first),
            gated_column(second),
        ]
        + [ANY] * len(deps),
        out_specs=(out, out),
        compiler_params=params(),
        cost_estimate=pl.CostEstimate(
            flops=16 * rows * width * cols,
            bytes_accessed=4 * rows * width + 16 * width * cols + 16 * rows * cols,
            transcendentals=0,
        ),
        name="mixer_grad",
    )(ht, dt, proj_grad, proj_grad, gated, gated, *deps)


def update_kernel(*refs):
    count = (len(refs) - 12)
    totals, rest = refs[:count], refs[count:]
    wide, tall, wide_new, tall_new = rest[:3], rest[3:6], rest[6:9], rest[9:]
    for i, total in enumerate(totals):

        @pl.when(pl.program_id(0) == i)
        def _():
            last = total.shape[0] - 1
            new = adamw(wide[0][...], total[:last], wide[1][...], wide[2][...], RATE_MATRIX, DECAY)
            for ref, value in zip(wide_new, new):
                ref[...] = value
            grad = jnp.transpose(total[last])
            new = adamw(tall[0][...], grad, tall[1][...], tall[2][...], RATE_MATRIX, DECAY)
            for ref, value in zip(tall_new, new):
                ref[...] = value


def update(totals, wide, tall):
    if (wide[0].shape[2] // len(totals)) % 128:
        totals = [jnp.concatenate(totals, 2)]
    count = len(totals)
    planes, deep, cols = wide[0].shape
    part = cols // count
    wide_spec = pl.BlockSpec((planes, deep, part), lambda i: (0, 0, i))
    tall_spec = pl.BlockSpec((part, deep), lambda i: (i, 0))
    return pl.pallas_call(
        update_kernel,
        grid=(count,),
        out_shape=tuple(jax.ShapeDtypeStruct(a.shape, F32) for a in wide + tall),
        in_specs=[whole(total.shape) for total in totals] + [wide_spec] * 3 + [tall_spec] * 3,
        out_specs=(wide_spec,) * 3 + (tall_spec,) * 3,
        compiler_params=params(),
        cost_estimate=pl.CostEstimate(
            flops=20 * (planes + 1) * deep * cols,
            bytes_accessed=28 * (planes + 1) * deep * cols,
            transcendentals=(planes + 1) * deep * cols,
        ),
        name="update",
    )(*totals, *wide, *tall)


def local(
    tokens,
    segments,
    cotangent,
    mixer_in,
    mixer_out,
    gate_up,
    down_proj,
    norm_gains,
    conv_kernel,
    first_mixer_in,
    second_mixer_in,
    first_mixer_out,
    second_mixer_out,
    first_gate_up,
    second_gate_up,
    first_down_proj,
    second_down_proj,
    first_norm_gains,
    second_norm_gains,
    first_conv_kernel,
    second_conv_kernel,
):
    dp_size, t_size = lax.axis_size("dp"), lax.axis_size("tensor")
    dp_index, t_index = lax.axis_index("dp"), lax.axis_index("tensor")
    rows, length = tokens.shape[0], segments.shape[1]
    order = dp_index ^ jnp.array([rotate_left(j, dp_size) for j in range(dp_size)], jnp.int32)

    before = lax.ppermute(
        tokens[rows - HALO :], "tensor", [(i, i + 1) for i in range(t_size - 1)]
    )
    wm = gather_weight(
        jnp.concatenate([mixer_in.astype(BF), mixer_out.T.astype(BF)[None]], 0), 1, 2
    )
    ffn_cols = gate_up.shape[2] // PARTS
    wf = []
    for i in range(PARTS):
        cols = slice(i * ffn_cols, (i + 1) * ffn_cols)
        packed = jnp.concatenate(
            [gate_up[:, :, cols].astype(BF), down_proj[cols].T.astype(BF)[None]], 0
        )
        wf.append(gather_weight(packed, 1, 2))

    small = jnp.concatenate([norm_gains, conv_kernel], 0)[:, None, :]
    for axis, size_axis in (("tensor", t_size), ("dp", dp_size)):
        for i in range(size_axis.bit_length() - 1):
            small = jnp.concatenate([small, swap(small, axis, 1 << i)], 1)
    small = small.reshape(small.shape[0], dp_size, t_size, small.shape[2])
    for axis, index, size_axis in ((1, dp_index, dp_size), (2, t_index, t_size)):
        for i in range(size_axis.bit_length() - 1):
            shape = small.shape
            split = small.reshape(shape[:axis] + (size_axis >> (i + 1), 2, 1 << i) + shape[axis + 1 :])
            flipped = jnp.flip(split, axis + 1)
            small = jnp.where((index >> i) & 1 == 1, flipped, split).reshape(shape)
    small = small.reshape(small.shape[0], -1)
    wide = small.shape[1] // dp_size
    gains = jnp.concatenate(
        [lax.dynamic_slice_in_dim(small[:2], order[j] * wide, wide, 1) for j in range(dp_size)], 1
    )
    channels = small.shape[1] // t_size
    codes = block_codes(t_size)
    kernel = jnp.concatenate(
        [
            lax.dynamic_slice_in_dim(small[2:], (t_index ^ code) * channels, channels, 1)
            for code in codes
        ],
        1,
    )

    masks = []
    for mask in lag_masks(segments.reshape(-1), length):
        padded = jnp.concatenate([mask, jnp.zeros((HALO, 1), F32)], 0)
        masks.append(lax.dynamic_slice_in_dim(padded, t_index * rows, rows + HALO, 0))

    x_ext, cot = arrange(order, tokens, before, cotangent)
    extended = x_ext.astype(F32)
    scale_ext = rms_scale(extended)
    normed_ext = (extended * scale_ext * gains[0]).astype(BF)
    values, scale_one, normed_one = extended[HALO:], scale_ext[HALO:], normed_ext[HALO:]
    wm_all = jnp.concatenate(wm, 2)
    win_all, wout_all = wm_all[:3], wm_all[3]
    projected = mm("td,kdc->ktc", normed_ext, win_all)
    part_b, part_c, part_x = projected[0], projected[1][HALO:], projected[2]
    product_ext = part_b * part_x
    part_b, part_x = part_b[HALO:], part_x[HALO:]
    product = product_ext[HALO:]
    convolved = kernel[0] * product
    for shift in range(1, KW):
        convolved = convolved + kernel[shift] * masks[shift - 1][:rows] * shift_rows(
            product_ext, HALO - shift, rows
        )
    gated = (part_c * convolved).astype(BF)
    middle = values + mm("tc,dc->td", gated, wout_all)
    scale_two = rms_scale(middle)
    normed_two = (middle * scale_two * gains[1]).astype(BF)

    norm_t, cot_t = normed_two.T, cot.T
    branches, backs, grads = [], [], []
    near_in, far_in, corner, sides = [], [], [], []
    for i in range(PARTS):
        near, near_core, far, far_core = wf[i]
        deps = []
        if i >= 1:
            deps.append(near_in[i - 1])
        if i >= 2:
            deps += corner[i - 2]
        g_near, g_near_core, branch, back = ffn(normed_two, norm_t, cot, cot_t, near, near_core, deps)
        branches.append(branch)
        backs.append(back)
        near_in.append(swap(g_near_core, "tensor", 1))
        if i >= 2:
            sides.append(scatter_sides(*grads[i - 2][:1], near_in[i - 2], grads[i - 2][1], far_in[i - 2], *corner[i - 2], 1))
        deps = [far_in[i - 1]] if i >= 1 else []
        g_far, g_far_core, branch, back = ffn(normed_two, norm_t, cot, cot_t, far, far_core, deps)
        branches.append(branch)
        backs.append(back)
        far_in.append(swap(g_far_core, "tensor", 1))
        grads.append((g_near, g_far))
        if i >= 1:
            corner.append(scatter_corner(grads[i - 1][1], far_in[i - 1], 1))

    def finish_sides(i):
        return scatter_sides(grads[i][0], near_in[i], grads[i][1], far_in[i], *corner[i], 1)

    block_out, middle_grad, mixed_grad, gain_two_grad = middle_back(
        order, middle, scale_two, gains[1:2], cot, branches, backs, [near_in[-1], *corner[-1]]
    )
    corner.append(scatter_corner(grads[-1][1], far_in[-1], 1))
    while len(sides) < PARTS - 1:
        sides.append(finish_sides(len(sides)))

    gated_grad = mm("td,dc->tc", mixed_grad, wout_all)
    conv_grad = gated_grad * part_c
    after_rel = lax.ppermute(
        conv_grad[:8], "tensor", [(i + 1, i) for i in range(t_size - 1)]
    )
    after = jnp.concatenate(
        [
            lax.dynamic_slice_in_dim(
                after_rel,
                block_place(code ^ t_index ^ (t_index + 1), t_size) % t_size * channels,
                channels,
                1,
            )
            for code in codes
        ],
        1,
    )
    c_grad = gated_grad * convolved
    conv_ext = jnp.concatenate([conv_grad, after], 0)
    kernel_rows = [jnp.sum(conv_grad * product, axis=0)]
    product_grad = kernel[0] * conv_grad
    for shift in range(1, KW):
        masked = masks[shift - 1][: rows + 8] * conv_ext
        kernel_rows.append(
            jnp.sum(masked[:rows] * shift_rows(product_ext, HALO - shift, rows), axis=0)
        )
        product_grad = product_grad + kernel[shift] * shift_rows(masked, shift, rows)
    proj_grad = jnp.stack([product_grad * part_x, c_grad, product_grad * part_b], 0).astype(BF)
    one_t, mixed_t = normed_one.T, mixed_grad.T
    m_near_core, m_far_core = mixer_grad(
        one_t, mixed_t, proj_grad, gated, 1, 3, [*sides[0], *corner[-1]]
    )
    m_far_in, m_near_in = swap(m_far_core, "tensor", 1), swap(m_near_core, "tensor", 1)
    sides.append(finish_sides(PARTS - 1))
    m_near, m_far = mixer_grad(one_t, mixed_t, proj_grad, gated, 0, 2, [])
    m_corner = scatter_corner(m_far, m_far_in, 1)
    normed_one_grad = mm("ktc,kdc->td", proj_grad, win_all)
    grad_input, gain_one_grad = input_back(
        order, x_ext[HALO:], scale_one, gains[:1], middle_grad, normed_one_grad
    )
    m_sides = scatter_sides(m_near, m_near_in, m_far, m_far_in, *m_corner, 1)

    gain_rel = jnp.concatenate([gain_one_grad, gain_two_grad], 0)
    kernel_rel = jnp.stack(kernel_rows, 0)
    gain_sums = jnp.concatenate(
        [
            lax.dynamic_slice_in_dim(gain_rel, rotate_right(dp_index ^ q, dp_size) * wide, wide, 1)
            for q in range(dp_size)
        ],
        1,
    )
    kernel_sums = jnp.concatenate(
        [
            lax.dynamic_slice_in_dim(
                kernel_rel, block_place(t_index ^ q, t_size) * channels, channels, 1
            )
            for q in range(t_size)
        ],
        1,
    )
    sums = jnp.concatenate([gain_sums, kernel_sums], 0)
    for axis, size_axis in (("tensor", t_size), ("dp", dp_size)):
        for i in range(size_axis.bit_length() - 1):
            sums = sums + swap(sums, axis, 1 << i)
    own_width = norm_gains.shape[1]
    own = lax.dynamic_slice_in_dim(sums, (dp_index * t_size + t_index) * own_width, own_width, 1)

    totals = [
        scatter_rest(grads[i][0], near_in[i], *sides[i], 1, 2) for i in range(PARTS)
    ]
    ffn_new = update(
        totals, (gate_up, first_gate_up, second_gate_up), (down_proj, first_down_proj, second_down_proj)
    )
    total = scatter_rest(m_near, m_near_in, *m_sides, 1, 2)
    mix_new = update(
        [total], (mixer_in, first_mixer_in, second_mixer_in), (mixer_out, first_mixer_out, second_mixer_out)
    )
    gains_new = adamw(norm_gains, own[:2], first_norm_gains, second_norm_gains, RATE_SMALL, 0.0)
    kernel_new = adamw(conv_kernel, own[2:], first_conv_kernel, second_conv_kernel, RATE_SMALL, DECAY)
    block_out, grad_input = to_natural(block_out, order), to_natural(grad_input, order)
    return (block_out, grad_input, *mix_new, *ffn_new, *gains_new, *kernel_new)


def solution(mesh):
    rows = P(("dp", "tensor"), None)
    in_w, out_w, small = P(None, "dp", "tensor"), P("tensor", "dp"), P(None, ("dp", "tensor"))
    return jax.shard_map(
        local,
        mesh=mesh,
        in_specs=(
            (rows, P("dp", None), rows, in_w, out_w, in_w, out_w, small, small)
            + (in_w,) * 2
            + (out_w,) * 2
            + (in_w,) * 2
            + (out_w,) * 2
            + (small,) * 4
        ),
        out_specs=(rows, rows)
        + (in_w,) * 3
        + (out_w,) * 3
        + (in_w,) * 3
        + (out_w,) * 3
        + (small,) * 6,
        check_vma=False,
    )
```

time: 877 us -> 695 us (0.79)
  matrix products: 207 us -> 23.6 us
  Pallas kernels: 0 us -> 148 us
  waiting for transfers between devices: 401 us -> 280 us
  blocking collectives: 55.7 us -> 0 us
  other arithmetic: 64.5 us -> 98 us
    dot_general x45 -> x4, matrix products: 207 us -> 23.6 us  [mm(): return jnp.einsum(spec, left, right, preferred_element_type=F32).astype(out)]
    pallas_call x0 -> x13, Pallas kernels: none -> 148 us  [the longest x6 114 us: ffn(): pl.pallas_call(ffn_kernel, grid=(cols // tile,), out_shape=(grad, grad, p...]
    ppermute x69 -> x74, waiting for transfers between devices: 401 us -> 280 us  [swap(): return lax.ppermute(values, axis, [(i, i ^ bit) for i in range(size)])]
    all_gather x1 -> x0, blocking collectives: 55.7 us -> none  [local(): lax.all_gather(jnp.concatenate([norm_gains, conv_kernel], 0), ('dp', 'ten...]
    unnamed x296 -> x293, local copies, waits for them, and re-layouts: 54.2 us -> 28 us
    convert_element_type x13 -> x18, other arithmetic: 11.6 us -> 30.8 us  [the longest x8 12.4 us: scatter_rest(): functools.reduce(jnp.add, [part[1].astype(F32) for part in parts])]
    concatenate x9 -> x17, other arithmetic: 1.67 us -> 14 us  [the longest x1 4.54 us: local(): wm_all = jnp.concatenate(wm, 2)]
    concatenate x4, other arithmetic: 2.35 us -> 12.1 us  [gather_weight(): near = jnp.concatenate([own, by_x], wide)]
  transfers between devices with their start and end apart: 71 -> 76, of which waited for: 28 -> 28; matrix products, arithmetic and copies ran while one was open for 32% -> 25% of each run, Pallas kernels for 0% -> 21%
where the time goes in v2:
time: 695 us; the launch traced here: 690 us
  waiting for transfers between devices  280 us (40%)
  Pallas kernels  148 us (21%)
  other arithmetic  98 us (14%)
  local copies, waits for them, and re-layouts  67.1 us (10%)
  starting transfers between devices  65.7 us (9%)
  matrix products  23.6 us (3%)
  between operations  7.97 us (1%)
    ppermute x74, waiting for transfers between devices, swap(): return lax.ppermute(values, axis, [(i, i ^ bit) for i in range(size)])  280 us
    pallas_call x6, Pallas kernels, ffn(): pl.pallas_call(ffn_kernel, grid=(cols // tile,), out_shape=(grad, grad, p...  114 us
    ppermute x74, starting transfers between devices, swap(): return lax.ppermute(values, axis, [(i, i ^ bit) for i in range(size)])  62.3 us
    unnamed x293, local copies, waits for them, and re-layouts  28 us
    dot_general x4, matrix products, mm(): return jnp.einsum(spec, left, right, preferred_element_type=F32).astype(out)  23.6 us
  transfers between devices with their start and end apart: 76, of which 28 were waited for; matrix products, arithmetic and copies ran while one was open for 25% of the time, Pallas kernels for 21%

profile of v2, /device:TPU:0, one launch (start us, length us, event | category | flops | bytes accessed | tf_op | source)
XLA Modules:
  0.0 690.2 jit_solution(12476891776172890313)
XLA Ops:
  23.0 11.1 %collective-permute-done.12 = f32[5,8,32]{2,0,1:T(8,128)S(1)} collective-permute-done((f32[5,8,32]{2,0,1:T(8,128)S(1)}, f32[5,8,32]{2,0,1:T(8,128)S(1)}, u32[]{:S(2)}, u32[]{:S(2)}) %collective-permute-start.12) | collective-permute-done | bytes 5152 | tf_op jit(solution)/shard_map/ppermute | solution.py:29
  46.3 25.0 %collective-permute-done.2 = bf16[4,256,256]{2,1,0:T(8,128)(2,1)S(1)} collective-permute-done((bf16[4,256,256]{2,1,0:T(8,128)(2,1)S(1)}, bf16[4,256,256]{2,1,0:T(8,128)(2,1)S(1)}, u32[]{:S(2)}, u32[]{:S(2)}) %collective-permute-start.2) | collective-permute-done | bytes 524320 | tf_op jit(solution)/shard_map/ppermute | solution.py:29
  74.7 2.9 collective-permute-start.23
  77.6 36.4 %collective-permute-done.15 = bf16[3,256,384]{2,1,0:T(8,128)(2,1)S(1)} collective-permute-done((bf16[3,256,384]{2,1,0:T(8,128)(2,1)S(1)}, bf16[3,256,384]{2,1,0:T(8,128)(2,1)S(1)}, u32[]{:S(2)}, u32[]{:S(2)}) %collective-permute-start.15) | collective-permute-done | bytes 589856 | tf_op jit(solution)/shard_map/ppermute | solution.py:29
  118.9 20.5 %collective-permute-done.23 = bf16[3,256,384]{2,1,0:T(8,128)(2,1)S(1)} collective-permute-done((bf16[3,256,384]{2,1,0:T(8,128)(2,1)S(1)}, bf16[3,256,384]{2,1,0:T(8,128)(2,1)S(1)}, u32[]{:S(2)}, u32[]{:S(2)}) %collective-permute-start.23) | collective-permute-done | bytes 589856 | tf_op jit(solution)/shard_map/ppermute | solution.py:29
  145.0 12.4 %collective-permute-done.7 = bf16[4,256,256]{2,1,0:T(8,128)(2,1)S(1)} collective-permute-done((bf16[4,256,256]{2,1,0:T(8,128)(2,1)S(1)}, bf16[4,256,256]{2,1,0:T(8,128)(2,1)S(1)}, u32[]{:S(2)}, u32[]{:S(2)}) %collective-permute-start.7) | collective-permute-done | bytes 524320 | tf_op jit(solution)/shard_map/ppermute | solution.py:29
  164.1 2.8 copy.57
  177.1 8.4 %collective-permute-done.27 = bf16[3,512,384]{2,1,0:T(8,128)(2,1)} collective-permute-done((bf16[3,512,384]{2,1,0:T(8,128)(2,1)}, bf16[3,512,384]{2,1,0:T(8,128)(2,1)}, u32[]{:S(2)}, u32[]{:S(2)}) %collective-permute-start.27) | collective-permute-done | bytes 1179680 | tf_op jit(solution)/shard_map/ppermute | solution.py:29
  185.8 3.4 pad_maximum_fusion.2.wa
  191.3 6.8 collective-permute-done.24
  203.0 3.5 pad_maximum_fusion.3.wa
  206.6 4.1 collective-permute-done.19
  215.0 4.5 pad_maximum_fusion
  219.6 6.5 convolution_bitcast_fusion
  227.1 3.5 multiply_convert_fusion.3
  242.2 18.7 %ffn.6 = (bf16[3,1024,384]{2,1,0:T(8,128)(2,1)}, bf16[3,1024,384]{2,1,0:T(8,128)(2,1)}, bf16[768,1024]{1,0:T(8,128)(2,1)S(1)}, bf16[768,1024]{1,0:T(8,128)(2,1)S(1)}) custom-call(bf16[768,1024]{1,0:T(8,128)(2,1)S(1)} %copy-done.35, bf16[1024,768]{1,0:T(8,128)(2,1)S(1)} %fusion.51.ht, bf16[768,1024]{1,0:T(8,128)(2,1)S(1)} %get-tuple-element.69.c.refs_4_, ...), custom_call_target="tpu_custom_call" | custom-call | flops 10871635968 | bytes 18874368 | tf_op jit(solution)/shard_map/ffn/pallas_call | solution.py:268
  262.2 18.9 %ffn.7 = (bf16[3,1024,384]{2,1,0:T(8,128)(2,1)}, bf16[3,1024,384]{2,1,0:T(8,128)(2,1)}, bf16[768,1024]{1,0:T(8,128)(2,1)S(1)}, bf16[768,1024]{1,0:T(8,128)(2,1)S(1)}) custom-call(bf16[768,1024]{1,0:T(8,128)(2,1)S(1)} %copy-done.35, bf16[1024,768]{1,0:T(8,128)(2,1)S(1)} %fusion.51.ht, bf16[768,1024]{1,0:T(8,128)(2,1)S(1)} %get-tuple-element.69.c.refs_4_, ...), custom_call_target="tpu_custom_call" | custom-call | flops 10871635968 | bytes 18874368 | tf_op jit(solution)/shard_map/ffn/pallas_call | solution.py:268
  281.4 3.7 constant_dynamic-update-slice_fusion.27
  289.7 3.6 pad_maximum_fusion.4.wa
  293.5 18.7 %ffn.8 = (bf16[3,1024,384]{2,1,0:T(8,128)(2,1)}, bf16[3,1024,384]{2,1,0:T(8,128)(2,1)}, bf16[768,1024]{1,0:T(8,128)(2,1)S(1)}, bf16[768,1024]{1,0:T(8,128)(2,1)S(1)}) custom-call(bf16[768,1024]{1,0:T(8,128)(2,1)S(1)} %copy-done.35, bf16[1024,768]{1,0:T(8,128)(2,1)S(1)} %fusion.51.ht, bf16[768,1024]{1,0:T(8,128)(2,1)S(1)} %get-tuple-element.69.c.refs_4_, ...), custom_call_target="tpu_custom_call" | custom-call | flops 10871635968 | bytes 18874368 | tf_op jit(solution)/shard_map/ffn/pallas_call | solution.py:268
  316.5 19.0 %ffn.9 = (bf16[3,1024,384]{2,1,0:T(8,128)(2,1)}, bf16[3,1024,384]{2,1,0:T(8,128)(2,1)}, bf16[768,1024]{1,0:T(8,128)(2,1)S(1)}, bf16[768,1024]{1,0:T(8,128)(2,1)S(1)}) custom-call(bf16[768,1024]{1,0:T(8,128)(2,1)S(1)} %copy-done.35, bf16[1024,768]{1,0:T(8,128)(2,1)S(1)} %fusion.51.ht, bf16[768,1024]{1,0:T(8,128)(2,1)S(1)} %get-tuple-element.69.c.refs_4_, ...), custom_call_target="tpu_custom_call" | custom-call | flops 10871635968 | bytes 18874368 | tf_op jit(solution)/shard_map/ffn/pallas_call | solution.py:268
  336.3 3.4 slice.881
  342.8 8.6 %collective-permute-done.40 = bf16[3,256,384]{2,1,0:T(8,128)(2,1)S(1)} collective-permute-done((bf16[3,256,384]{2,1,0:T(8,128)(2,1)S(1)}, bf16[3,256,384]{2,1,0:T(8,128)(2,1)S(1)}, u32[]{:S(2)}, u32[]{:S(2)}) %collective-permute-start.40) | collective-permute-done | bytes 589856 | tf_op jit(solution)/shard_map/ppermute | solution.py:29
  359.9 7.8 %collective-permute-done.38.rest_2_ = bf16[3,256,384]{2,1,0:T(8,128)(2,1)} collective-permute-done((bf16[3,256,384]{2,1,0:T(8,128)(2,1)}, bf16[3,256,384]{2,1,0:T(8,128)(2,1)}, u32[]{:S(2)}, u32[]{:S(2)}) %collective-permute-start.38) | collective-permute-done | bytes 589856 | tf_op jit(solution)/shard_map/ppermute | solution.py:29
  367.7 19.4 %ffn.10 = (bf16[3,1024,384]{2,1,0:T(8,128)(2,1)}, bf16[3,1024,384]{2,1,0:T(8,128)(2,1)}, bf16[768,1024]{1,0:T(8,128)(2,1)S(1)}, bf16[768,1024]{1,0:T(8,128)(2,1)S(1)}) custom-call(bf16[768,1024]{1,0:T(8,128)(2,1)S(1)} %copy-done.36, bf16[1024,768]{1,0:T(8,128)(2,1)S(1)} %copy-done.41, bf16[768,1024]{1,0:T(8,128)(2,1)S(1)} %get-tuple-element.69.c.refs_4_, ...), custom_call_target="tpu_custom_call" | custom-call | flops 10871635968 | bytes 18874368 | tf_op jit(solution)/shard_map/ffn/pallas_call | solution.py:268
  387.3 3.2 add_convert_fusion.18
  394.5 3.6 copy.70.refs_1_
  406.5 3.2 add_convert_fusion.7
  410.3 19.0 %ffn.11 = (bf16[3,1024,384]{2,1,0:T(8,128)(2,1)}, bf16[3,1024,384]{2,1,0:T(8,128)(2,1)}, bf16[768,1024]{1,0:T(8,128)(2,1)S(1)}, bf16[768,1024]{1,0:T(8,128)(2,1)S(1)}) custom-call(bf16[768,1024]{1,0:T(8,128)(2,1)S(1)} %copy-done.37, bf16[1024,768]{1,0:T(8,128)(2,1)S(1)} %copy-done.42, bf16[768,1024]{1,0:T(8,128)(2,1)S(1)} %copy-done.4, ...), custom_call_target="tpu_custom_call" | custom-call | flops 10871635968 | bytes 18874368 | tf_op jit(solution)/shard_map/ffn/pallas_call | solution.py:268
  435.2 5.5 collective-permute-done.46.refs_19_
  440.7 10.9 %middle_back.1 = (bf16[768,1024]{1,0:T(8,128)(2,1)}, f32[768,1024]{1,0:T(8,128)}, bf16[768,1024]{1,0:T(8,128)(2,1)S(1)}, f32[1,1024]{1,0:T(1,128)S(1)}) custom-call(s32[8]{0:T(128)S(1)} %broadcast_xor_fusion.order.refs_0_, f32[768,1024]{1,0:T(8,128)} %copy.70.refs_1_, f32[768,1]{1,0:T(8,128)S(1)} %copy-done.43, f32[1,1024]{1,0:T(1,128)S(1)} %get-tuple-element.180.refs_3_, ...), custom_call_target="tpu_custom_call" | custom-call | flops 23592960 | bytes 29884416 | tf_op jit(solution)/shard_map/middle_back/pallas_call | solution.py:350
  451.6 7.2 %fusion.17 = (bf16[1,768,1024]{2,1,0:T(8,128)(2,1)}, f32[768,1024]{1,0:T(8,128)}) fusion(f32[768,1024]{1,0:T(8,128)S(1)} %copy-done.63, f32[3,784,1024]{2,1,0:T(8,128)} %copy-done.59, bf16[768,1024]{1,0:T(8,128)(2,1)S(1)} %get-tuple-element.91, bf16[4,1024,1024]{2,1,0:T(8,128)(2,1)} %copy-done.62), kind=kOutput, calls=%fused_computation.46 | convolution fusion | flops 1612972032 | bytes 14680064 | tf_op jit(solution)/shard_map/td,dc->tc/dot_general | solution.py:152
  464.3 2.8 copy.73
  470.7 4.5 multiply_reduce_fusion.1
  480.4 8.0 %fusion.11.upstream = f32[768,1024]{1,0:T(8,128)S(1)} fusion(bf16[4,1024,1024]{2,1,0:T(8,128)(2,1)} %copy-done.62, bf16[1,768,1024]{2,1,0:T(8,128)(2,1)S(1)} %fusion.19, bf16[1,768,1024]{2,1,0:T(8,128)(2,1)S(1)} %copy-done.68, bf16[1,768,1024]{2,1,0:T(8,128)(2,1)S(1)} %get-tuple-element.129), kind=kOutput, calls=%fused_computation.40 | convolution fusion | flops 4836556800 | bytes 14155776 | tf_op jit(solution)/shard_map/ktc,kdc->td/dot_general | solution.py:152
  488.5 4.6 input_back.1
  502.5 10.7 %collective-permute-done.52.rest_3_ = bf16[3,256,384]{2,1,0:T(8,128)(2,1)S(1)} collective-permute-done((bf16[3,256,384]{2,1,0:T(8,128)(2,1)S(1)}, bf16[3,256,384]{2,1,0:T(8,128)(2,1)S(1)}, u32[]{:S(2)}, u32[]{:S(2)}) %collective-permute-start.52) | collective-permute-done | bytes 589856 | tf_op jit(solution)/shard_map/ppermute | solution.py:29
  513.2 6.3 mixer_grad.3
  527.0 23.4 %collective-permute-done.72 = f32[5,1024]{1,0:T(8,128)S(1)} collective-permute-done((f32[5,1024]{1,0:T(8,128)S(1)}, f32[5,1024]{1,0:T(8,128)S(1)}, u32[]{:S(2)}, u32[]{:S(2)}) %collective-permute-start.72) | collective-permute-done | bytes 20512 | tf_op jit(solution)/shard_map/ppermute | solution.py:29
  559.5 5.5 mixer_grad.2
  572.6 22.2 %collective-permute-done.57 = bf16[4,256,256]{2,1,0:T(8,128)(2,1)S(1)} collective-permute-done((bf16[4,256,256]{2,1,0:T(8,128)(2,1)S(1)}, bf16[4,256,256]{2,1,0:T(8,128)(2,1)S(1)}, u32[]{:S(2)}, u32[]{:S(2)}) %collective-permute-start.57) | collective-permute-done | bytes 524320 | tf_op jit(solution)/shard_map/ppermute | solution.py:29
  604.0 6.5 collective-permute-done.68
  610.5 13.2 %collective-permute-done.67 = bf16[3,512,384]{2,1,0:T(8,128)(2,1)S(1)} collective-permute-done((bf16[3,512,384]{2,1,0:T(8,128)(2,1)S(1)}, bf16[3,512,384]{2,1,0:T(8,128)(2,1)S(1)}, u32[]{:S(2)}, u32[]{:S(2)}) %collective-permute-start.67) | collective-permute-done | bytes 1179680 | tf_op jit(solution)/shard_map/ppermute | solution.py:29
  625.8 14.2 %collective-permute-done.65 = bf16[3,256,384]{2,1,0:T(8,128)(2,1)S(1)} collective-permute-done((bf16[3,256,384]{2,1,0:T(8,128)(2,1)S(1)}, bf16[3,256,384]{2,1,0:T(8,128)(2,1)S(1)}, u32[]{:S(2)}, u32[]{:S(2)}) %collective-permute-start.65) | collective-permute-done | bytes 589856 | tf_op jit(solution)/shard_map/ppermute | solution.py:29
  644.8 19.2 %collective-permute-done.69 = bf16[3,256,384]{2,1,0:T(8,128)(2,1)S(1)} collective-permute-done((bf16[3,256,384]{2,1,0:T(8,128)(2,1)S(1)}, bf16[3,256,384]{2,1,0:T(8,128)(2,1)S(1)}, u32[]{:S(2)}, u32[]{:S(2)}) %collective-permute-start.69) | collective-permute-done | bytes 589856 | tf_op jit(solution)/shard_map/ppermute | solution.py:29
  666.6 8.6 %collective-permute-done.59 = bf16[4,256,256]{2,1,0:T(8,128)(2,1)S(1)} collective-permute-done((bf16[4,256,256]{2,1,0:T(8,128)(2,1)S(1)}, bf16[4,256,256]{2,1,0:T(8,128)(2,1)S(1)}, u32[]{:S(2)}, u32[]{:S(2)}) %collective-permute-start.59) | collective-permute-done | bytes 524320 | tf_op jit(solution)/shard_map/ppermute | solution.py:29
  676.4 5.1 collective-permute-done.70
  682.8 4.3 update.3
  (553 shorter events, 196.8 us)
Async XLA Ops:
  4.7 41.0 %collective-permute-start.1 = (bf16[4,128,256]{2,1,0:T(8,128)(2,1)}, bf16[4,128,256]{2,1,0:T(8,128)(2,1)S(1)}, u32[]{:S(2)}, u32[]{:S(2)}) collective-permute-start(bf16[4,128,256]{2,1,0:T(8,128)(2,1)} %pad_maximum_fusion.25), channel_id=1, source_target_pairs={{0,8},{4,12},{8,0},{12,4},{16,24},{20,28},{24,16},{28,20},{1,9},{5... | collective-permute-start | bytes 786440 | tf_op jit(solution)/shard_map/ppermute | solution.py:29
  9.7 64.7 %collective-permute-start.14 = (bf16[3,128,384]{2,1,0:T(8,128)(2,1)}, bf16[3,128,384]{2,1,0:T(8,128)(2,1)S(1)}, u32[]{:S(2)}, u32[]{:S(2)}) collective-permute-start(bf16[3,128,384]{2,1,0:T(8,128)(2,1)} %pad_maximum_fusion.22), channel_id=1, source_target_pairs={{0,8},{4,12},{8,0},{12,4},{16,24},{20,28},{24,16},{28,20},{1,9},{5... | collective-permute-start | bytes 884744 | tf_op jit(solution)/shard_map/ppermute | solution.py:29
  10.4 64.2 %collective-permute-start.22 = (bf16[3,128,384]{2,1,0:T(8,128)(2,1)}, bf16[3,128,384]{2,1,0:T(8,128)(2,1)S(1)}, u32[]{:S(2)}, u32[]{:S(2)}) collective-permute-start(bf16[3,128,384]{2,1,0:T(8,128)(2,1)} %pad_maximum_fusion.23), channel_id=1, source_target_pairs={{0,8},{4,12},{8,0},{12,4},{16,24},{20,28},{24,16},{28,20},{1,9},{5... | collective-permute-start | bytes 884744 | tf_op jit(solution)/shard_map/ppermute | solution.py:29
  13.2 104.8 %collective-permute-start.32 = (bf16[3,128,384]{2,1,0:T(8,128)(2,1)}, bf16[3,128,384]{2,1,0:T(8,128)(2,1)S(1)}, u32[]{:S(2)}, u32[]{:S(2)}) collective-permute-start(bf16[3,128,384]{2,1,0:T(8,128)(2,1)} %pad_maximum_fusion.24), channel_id=1, source_target_pairs={{0,8},{4,12},{8,0},{12,4},{16,24},{20,28},{24,16},{28,20},{1,9},{5... | collective-permute-start | bytes 884744 | tf_op jit(solution)/shard_map/ppermute | solution.py:29
  71.3 46.1 %collective-permute-start.5 = (bf16[4,512,256]{2,1,0:T(8,128)(2,1)S(1)}, bf16[4,512,256]{2,1,0:T(8,128)(2,1)S(1)}, u32[]{:S(2)}, u32[]{:S(2)}) collective-permute-start(bf16[4,512,256]{2,1,0:T(8,128)(2,1)S(1)} %pad_maximum_fusion.15), channel_id=1, source_target_pairs={{0,2},{1,3},{2,0},{3,1},{4,6},{5,7},{6,4},{7,5},{8,10},{9,11},{10,... | collective-permute-start | bytes 3145736 | tf_op jit(solution)/shard_map/ppermute | solution.py:29
  72.9 45.8 %collective-permute-start.3 = (bf16[4,512,256]{2,1,0:T(8,128)(2,1)S(1)}, bf16[4,512,256]{2,1,0:T(8,128)(2,1)S(1)}, u32[]{:S(2)}, u32[]{:S(2)}) collective-permute-start(bf16[4,512,256]{2,1,0:T(8,128)(2,1)S(1)} %pad_maximum_fusion.15), channel_id=1, source_target_pairs={{0,4},{4,0},{8,12},{12,8},{16,20},{20,16},{24,28},{28,24},{1,5},{5... | collective-permute-start | bytes 3145736 | tf_op jit(solution)/shard_map/ppermute | solution.py:29
  74.5 39.6 %collective-permute-start.15 = (bf16[3,256,384]{2,1,0:T(8,128)(2,1)S(1)}, bf16[3,256,384]{2,1,0:T(8,128)(2,1)S(1)}, u32[]{:S(2)}, u32[]{:S(2)}) collective-permute-start(bf16[3,256,384]{2,1,0:T(8,128)(2,1)S(1)} %pad_maximum_fusion.18), channel_id=1, source_target_pairs={{0,16},{4,20},{8,24},{12,28},{16,0},{20,4},{24,8},{28,12},{1,17},{... | collective-permute-start | bytes 1769480 | tf_op jit(solution)/shard_map/ppermute | solution.py:29
  74.7 64.7 %collective-permute-start.23 = (bf16[3,256,384]{2,1,0:T(8,128)(2,1)S(1)}, bf16[3,256,384]{2,1,0:T(8,128)(2,1)S(1)}, u32[]{:S(2)}, u32[]{:S(2)}) collective-permute-start(bf16[3,256,384]{2,1,0:T(8,128)(2,1)S(1)} %pad_maximum_fusion.19), channel_id=1, source_target_pairs={{0,16},{4,20},{8,24},{12,28},{16,0},{20,4},{24,8},{28,12},{1,17},{... | collective-permute-start | bytes 1769480 | tf_op jit(solution)/shard_map/ppermute | solution.py:29
  114.1 44.4 %collective-permute-start = (bf16[16,1024]{1,0:T(8,128)(2,1)}, bf16[16,1024]{1,0:T(8,128)(2,1)S(1)}, u32[]{:S(2)}, u32[]{:S(2)}) collective-permute-start(bf16[16,1024]{1,0:T(8,128)(2,1)} %slice.681), channel_id=1, source_target_pairs={{0,1},{1,2},{2,3},{4,5},{5,6},{6,7},{8,9},{9,10},{10,11},{12,13},{... | collective-permute-start | bytes 98312 | tf_op jit(solution)/shard_map/ppermute | solution.py:517
  117.4 41.8 %collective-permute-start.18 = (bf16[3,512,384]{2,1,0:T(8,128)(2,1)}, bf16[3,512,384]{2,1,0:T(8,128)(2,1)}, u32[]{:S(2)}, u32[]{:S(2)}) collective-permute-start(bf16[3,512,384]{2,1,0:T(8,128)(2,1)} %pad_maximum_fusion.6), channel_id=1, source_target_pairs={{0,2},{1,3},{2,0},{3,1},{4,6},{5,7},{6,4},{7,5},{8,10},{9,11},{10,... | collective-permute-start | bytes 3538952 | tf_op jit(solution)/shard_map/ppermute | solution.py:29
  118.8 39.7 %collective-permute-start.33 = (bf16[3,256,384]{2,1,0:T(8,128)(2,1)S(1)}, bf16[3,256,384]{2,1,0:T(8,128)(2,1)S(1)}, u32[]{:S(2)}, u32[]{:S(2)}) collective-permute-start(bf16[3,256,384]{2,1,0:T(8,128)(2,1)S(1)} %pad_maximum_fusion.20), channel_id=1, source_target_pairs={{0,16},{4,20},{8,24},{12,28},{16,0},{20,4},{24,8},{28,12},{1,17},{... | collective-permute-start | bytes 1769480 | tf_op jit(solution)/shard_map/ppermute | solution.py:29
  143.6 30.8 %collective-permute-start.16 = (bf16[3,512,384]{2,1,0:T(8,128)(2,1)}, bf16[3,512,384]{2,1,0:T(8,128)(2,1)}, u32[]{:S(2)}, u32[]{:S(2)}) collective-permute-start(bf16[3,512,384]{2,1,0:T(8,128)(2,1)} %pad_maximum_fusion.6), channel_id=1, source_target_pairs={{0,4},{4,0},{8,12},{12,8},{16,20},{20,16},{24,28},{28,24},{1,5},{5... | collective-permute-start | bytes 3538952 | tf_op jit(solution)/shard_map/ppermute | solution.py:29
  157.4 28.1 %collective-permute-start.27 = (bf16[3,512,384]{2,1,0:T(8,128)(2,1)}, bf16[3,512,384]{2,1,0:T(8,128)(2,1)}, u32[]{:S(2)}, u32[]{:S(2)}) collective-permute-start(bf16[3,512,384]{2,1,0:T(8,128)(2,1)} %pad_maximum_fusion.7), channel_id=1, source_target_pairs={{0,2},{1,3},{2,0},{3,1},{4,6},{5,7},{6,4},{7,5},{8,10},{9,11},{10,... | collective-permute-start | bytes 3538952 | tf_op jit(solution)/shard_map/ppermute | solution.py:29
  158.5 56.0 %collective-permute-start.4 = (bf16[4,1024,256]{2,1,0:T(8,128)(2,1)}, bf16[4,1024,256]{2,1,0:T(8,128)(2,1)}, u32[]{:S(2)}, u32[]{:S(2)}) collective-permute-start(bf16[4,1024,256]{2,1,0:T(8,128)(2,1)} %pad_maximum_fusion.5), channel_id=1, source_target_pairs={{0,1},{1,0},{2,3},{3,2},{4,5},{5,4},{6,7},{7,6},{8,9},{9,8},{10,11... | collective-permute-start | bytes 6291464 | tf_op jit(solution)/shard_map/ppermute | solution.py:29
  158.5 56.0 %collective-permute-start.8 = (bf16[4,1024,256]{2,1,0:T(8,128)(2,1)}, bf16[4,1024,256]{2,1,0:T(8,128)(2,1)}, u32[]{:S(2)}, u32[]{:S(2)}) collective-permute-start(bf16[4,1024,256]{2,1,0:T(8,128)(2,1)} %constant_dynamic-update-slice_fusion), channel_id=1, source_target_pairs={{0,1},{1,0},{2,3},{3,2},{4,5},{5,4},{6,7},{7,6},{8,9},{9,8},{10,11... | collective-permute-start | bytes 6291464 | tf_op jit(solution)/shard_map/ppermute | solution.py:29
  159.2 38.9 %collective-permute-start.24 = (bf16[3,512,384]{2,1,0:T(8,128)(2,1)}, bf16[3,512,384]{2,1,0:T(8,128)(2,1)}, u32[]{:S(2)}, u32[]{:S(2)}) collective-permute-start(bf16[3,512,384]{2,1,0:T(8,128)(2,1)} %pad_maximum_fusion.7), channel_id=1, source_target_pairs={{0,4},{4,0},{8,12},{12,8},{16,20},{20,16},{24,28},{28,24},{1,5},{5... | collective-permute-start | bytes 3538952 | tf_op jit(solution)/shard_map/ppermute | solution.py:29
  174.4 36.2 %collective-permute-start.19 = (bf16[3,256,384]{2,1,0:T(8,128)(2,1)S(1)}, bf16[3,256,384]{2,1,0:T(8,128)(2,1)S(1)}, u32[]{:S(2)}, u32[]{:S(2)}) collective-permute-start(bf16[3,256,384]{2,1,0:T(8,128)(2,1)S(1)} %slice.870), channel_id=1, source_target_pairs={{0,4},{4,0},{8,12},{12,8},{16,20},{20,16},{24,28},{28,24},{1,5},{5... | collective-permute-start | bytes 1769480 | tf_op jit(solution)/shard_map/ppermute | solution.py:29
  198.1 91.1 %collective-permute-start.34 = (bf16[3,512,384]{2,1,0:T(8,128)(2,1)}, bf16[3,512,384]{2,1,0:T(8,128)(2,1)}, u32[]{:S(2)}, u32[]{:S(2)}) collective-permute-start(bf16[3,512,384]{2,1,0:T(8,128)(2,1)} %pad_maximum_fusion.8), channel_id=1, source_target_pairs={{0,4},{4,0},{8,12},{12,8},{16,20},{20,16},{24,28},{28,24},{1,5},{5... | collective-permute-start | bytes 3538952 | tf_op jit(solution)/shard_map/ppermute | solution.py:29
  210.6 70.5 %collective-permute-start.28 = (bf16[3,256,384]{2,1,0:T(8,128)(2,1)}, bf16[3,256,384]{2,1,0:T(8,128)(2,1)}, u32[]{:S(2)}, u32[]{:S(2)}) collective-permute-start(bf16[3,256,384]{2,1,0:T(8,128)(2,1)} %slice.874), channel_id=1, source_target_pairs={{0,4},{4,0},{8,12},{12,8},{16,20},{20,16},{24,28},{28,24},{1,5},{5... | collective-permute-start | bytes 1769480 | tf_op jit(solution)/shard_map/ppermute | solution.py:29
  212.1 75.0 %collective-permute-start.29 = (bf16[3,256,384]{2,1,0:T(8,128)(2,1)}, bf16[3,256,384]{2,1,0:T(8,128)(2,1)}, u32[]{:S(2)}, u32[]{:S(2)}) collective-permute-start(bf16[3,256,384]{2,1,0:T(8,128)(2,1)} %slice.875), channel_id=1, source_target_pairs={{0,2},{1,3},{2,0},{3,1},{4,6},{5,7},{6,4},{7,5},{8,10},{9,11},{10,... | collective-permute-start | bytes 1769480 | tf_op jit(solution)/shard_map/ppermute | solution.py:29
  214.5 27.3 %collective-permute-start.17 = (bf16[3,1024,384]{2,1,0:T(8,128)(2,1)}, bf16[3,1024,384]{2,1,0:T(8,128)(2,1)}, u32[]{:S(2)}, u32[]{:S(2)}) collective-permute-start(bf16[3,1024,384]{2,1,0:T(8,128)(2,1)} %pad_maximum_fusion.2.wa), channel_id=1, source_target_pairs={{0,1},{1,0},{2,3},{3,2},{4,5},{5,4},{6,7},{7,6},{8,9},{9,8},{10,11... | collective-permute-start | bytes 7077896 | tf_op jit(solution)/shard_map/ppermute | solution.py:29
  214.5 47.6 %collective-permute-start.21 = (bf16[3,1024,384]{2,1,0:T(8,128)(2,1)}, bf16[3,1024,384]{2,1,0:T(8,128)(2,1)}, u32[]{:S(2)}, u32[]{:S(2)}) collective-permute-start(bf16[3,1024,384]{2,1,0:T(8,128)(2,1)} %constant_dynamic-update-slice_fusion.22.wa), channel_id=1, source_target_pairs={{0,1},{1,0},{2,3},{3,2},{4,5},{5,4},{6,7},{7,6},{8,9},{9,8},{10,11... | collective-permute-start | bytes 7077896 | tf_op jit(solution)/shard_map/ppermute | solution.py:29
  241.8 51.6 %collective-permute-start.25 = (bf16[3,1024,384]{2,1,0:T(8,128)(2,1)}, bf16[3,1024,384]{2,1,0:T(8,128)(2,1)}, u32[]{:S(2)}, u32[]{:S(2)}) collective-permute-start(bf16[3,1024,384]{2,1,0:T(8,128)(2,1)} %pad_maximum_fusion.3.wa), channel_id=1, source_target_pairs={{0,1},{1,0},{2,3},{3,2},{4,5},{5,4},{6,7},{7,6},{8,9},{9,8},{10,11... | collective-permute-start | bytes 7077896 | tf_op jit(solution)/shard_map/ppermute | solution.py:29
  262.1 31.4 %collective-permute-start.26 = (bf16[3,1024,384]{2,1,0:T(8,128)(2,1)}, bf16[3,1024,384]{2,1,0:T(8,128)(2,1)}, u32[]{:S(2)}, u32[]{:S(2)}) collective-permute-start(bf16[3,1024,384]{2,1,0:T(8,128)(2,1)} %get-tuple-element.72), channel_id=1, source_target_pairs={{0,1},{1,0},{2,3},{3,2},{4,5},{5,4},{6,7},{7,6},{8,9},{9,8},{10,11... | collective-permute-start | bytes 7077896 | tf_op jit(solution)/shard_map/ppermute | solution.py:29
  281.2 32.7 %collective-permute-start.31 = (bf16[3,1024,384]{2,1,0:T(8,128)(2,1)}, bf16[3,1024,384]{2,1,0:T(8,128)(2,1)S(1)}, u32[]{:S(2)}, u32[]{:S(2)}) collective-permute-start(bf16[3,1024,384]{2,1,0:T(8,128)(2,1)} %get-tuple-element.74), channel_id=1, source_target_pairs={{0,1},{1,0},{2,3},{3,2},{4,5},{5,4},{6,7},{7,6},{8,9},{9,8},{10,11... | collective-permute-start | bytes 7077896 | tf_op jit(solution)/shard_map/ppermute | solution.py:29
  289.0 27.4 %collective-permute-start.30 = (bf16[3,1024,384]{2,1,0:T(8,128)(2,1)}, bf16[3,1024,384]{2,1,0:T(8,128)(2,1)}, u32[]{:S(2)}, u32[]{:S(2)}) collective-permute-start(bf16[3,1024,384]{2,1,0:T(8,128)(2,1)} %constant_dynamic-update-slice_fusion.25.wa), channel_id=1, source_target_pairs={{0,1},{1,0},{2,3},{3,2},{4,5},{5,4},{6,7},{7,6},{8,9},{9,8},{10,11... | collective-permute-start | bytes 7077896 | tf_op jit(solution)/shard_map/ppermute | solution.py:29
  289.2 46.4 %collective-permute-start.39 = (bf16[3,512,384]{2,1,0:T(8,128)(2,1)}, bf16[3,512,384]{2,1,0:T(8,128)(2,1)S(1)}, u32[]{:S(2)}, u32[]{:S(2)}) collective-permute-start(bf16[3,512,384]{2,1,0:T(8,128)(2,1)} %pad_maximum_fusion.8), channel_id=1, source_target_pairs={{0,2},{1,3},{2,0},{3,1},{4,6},{5,7},{6,4},{7,5},{8,10},{9,11},{10,... | collective-permute-start | bytes 3538952 | tf_op jit(solution)/shard_map/ppermute | solution.py:29
  293.4 66.5 %collective-permute-start.35 = (bf16[3,1024,384]{2,1,0:T(8,128)(2,1)}, bf16[3,1024,384]{2,1,0:T(8,128)(2,1)}, u32[]{:S(2)}, u32[]{:S(2)}) collective-permute-start(bf16[3,1024,384]{2,1,0:T(8,128)(2,1)} %pad_maximum_fusion.4.wa), channel_id=1, source_target_pairs={{0,1},{1,0},{2,3},{3,2},{4,5},{5,4},{6,7},{7,6},{8,9},{9,8},{10,11... | collective-permute-start | bytes 7077896 | tf_op jit(solution)/shard_map/ppermute | solution.py:29
  313.4 54.3 %collective-permute-start.36 = (bf16[3,1024,384]{2,1,0:T(8,128)(2,1)}, bf16[3,1024,384]{2,1,0:T(8,128)(2,1)}, u32[]{:S(2)}, u32[]{:S(2)}) collective-permute-start(bf16[3,1024,384]{2,1,0:T(8,128)(2,1)} %get-tuple-element.76), channel_id=1, source_target_pairs={{0,1},{1,0},{2,3},{3,2},{4,5},{5,4},{6,7},{7,6},{8,9},{9,8},{10,11... | collective-permute-start | bytes 7077896 | tf_op jit(solution)/shard_map/ppermute | solution.py:29
  335.5 51.8 %collective-permute-start.43 = (bf16[3,1024,384]{2,1,0:T(8,128)(2,1)}, bf16[3,1024,384]{2,1,0:T(8,128)(2,1)}, u32[]{:S(2)}, u32[]{:S(2)}) collective-permute-start(bf16[3,1024,384]{2,1,0:T(8,128)(2,1)} %get-tuple-element.79), channel_id=1, source_target_pairs={{0,1},{1,0},{2,3},{3,2},{4,5},{5,4},{6,7},{7,6},{8,9},{9,8},{10,11... | collective-permute-start | bytes 7077896 | tf_op jit(solution)/shard_map/ppermute | solution.py:29
  359.9 50.4 %collective-permute-start.42 = (bf16[3,1024,384]{2,1,0:T(8,128)(2,1)}, bf16[3,1024,384]{2,1,0:T(8,128)(2,1)}, u32[]{:S(2)}, u32[]{:S(2)}) collective-permute-start(bf16[3,1024,384]{2,1,0:T(8,128)(2,1)} %constant_dynamic-update-slice_fusion.28.wa), channel_id=1, source_target_pairs={{0,1},{1,0},{2,3},{3,2},{4,5},{5,4},{6,7},{7,6},{8,9},{9,8},{10,11... | collective-permute-start | bytes 7077896 | tf_op jit(solution)/shard_map/ppermute | solution.py:29
  387.2 53.5 %collective-permute-start.44 = (bf16[3,1024,384]{2,1,0:T(8,128)(2,1)}, bf16[3,1024,384]{2,1,0:T(8,128)(2,1)}, u32[]{:S(2)}, u32[]{:S(2)}) collective-permute-start(bf16[3,1024,384]{2,1,0:T(8,128)(2,1)} %get-tuple-element.87), channel_id=1, source_target_pairs={{0,1},{1,0},{2,3},{3,2},{4,5},{5,4},{6,7},{7,6},{8,9},{9,8},{10,11... | collective-permute-start | bytes 7077896 | tf_op jit(solution)/shard_map/ppermute | solution.py:29
  400.6 29.9 %collective-permute-start.49 = (bf16[3,512,384]{2,1,0:T(8,128)(2,1)}, bf16[3,512,384]{2,1,0:T(8,128)(2,1)S(1)}, u32[]{:S(2)}, u32[]{:S(2)}) collective-permute-start(bf16[3,512,384]{2,1,0:T(8,128)(2,1)} %pad_maximum_fusion.10), channel_id=1, source_target_pairs={{0,2},{1,3},{2,0},{3,1},{4,6},{5,7},{6,4},{7,5},{8,10},{9,11},{10,... | collective-permute-start | bytes 3538952 | tf_op jit(solution)/shard_map/ppermute | solution.py:29
  409.8 30.9 %collective-permute-start.46 = (bf16[3,256,384]{2,1,0:T(8,128)(2,1)S(1)}, bf16[3,256,384]{2,1,0:T(8,128)(2,1)S(1)}, u32[]{:S(2)}, u32[]{:S(2)}) collective-permute-start(bf16[3,256,384]{2,1,0:T(8,128)(2,1)S(1)} %get-tuple-element.140), channel_id=1, source_target_pairs={{0,2},{1,3},{2,0},{3,1},{4,6},{5,7},{6,4},{7,5},{8,10},{9,11},{10,... | collective-permute-start | bytes 1769480 | tf_op jit(solution)/shard_map/ppermute | solution.py:29
  430.5 47.3 %collective-permute-start.50 = (bf16[3,1024,384]{2,1,0:T(8,128)(2,1)}, bf16[3,1024,384]{2,1,0:T(8,128)(2,1)}, u32[]{:S(2)}, u32[]{:S(2)}) collective-permute-start(bf16[3,1024,384]{2,1,0:T(8,128)(2,1)} %get-tuple-element.96), channel_id=1, source_target_pairs={{0,1},{1,0},{2,3},{3,2},{4,5},{5,4},{6,7},{7,6},{8,9},{9,8},{10,11... | collective-permute-start | bytes 7077896 | tf_op jit(solution)/shard_map/ppermute | solution.py:29
  464.2 61.4 %collective-permute-start.62 = (bf16[3,128,384]{2,1,0:T(8,128)(2,1)}, bf16[3,128,384]{2,1,0:T(8,128)(2,1)}, u32[]{:S(2)}, u32[]{:S(2)}) collective-permute-start(bf16[3,128,384]{2,1,0:T(8,128)(2,1)} %add_convert_fusion.30), channel_id=1, source_target_pairs={{0,8},{4,12},{8,0},{12,4},{16,24},{20,28},{24,16},{28,20},{1,9},{5... | collective-permute-start | bytes 884744 | tf_op jit(solution)/shard_map/ppermute | solution.py:29
  519.5 45.5 %collective-permute-start.54 = (bf16[4,1024,256]{2,1,0:T(8,128)(2,1)}, bf16[4,1024,256]{2,1,0:T(8,128)(2,1)}, u32[]{:S(2)}, u32[]{:S(2)}) collective-permute-start(bf16[4,1024,256]{2,1,0:T(8,128)(2,1)} %get-tuple-element.99), channel_id=1, source_target_pairs={{0,1},{1,0},{2,3},{3,2},{4,5},{5,4},{6,7},{7,6},{8,9},{9,8},{10,11... | collective-permute-start | bytes 6291464 | tf_op jit(solution)/shard_map/ppermute | solution.py:29
  521.6 79.5 %collective-permute-start.64 = (bf16[3,512,384]{2,1,0:T(8,128)(2,1)}, bf16[3,512,384]{2,1,0:T(8,128)(2,1)S(1)}, u32[]{:S(2)}, u32[]{:S(2)}) collective-permute-start(bf16[3,512,384]{2,1,0:T(8,128)(2,1)} %pad_maximum_fusion.12), channel_id=1, source_target_pairs={{0,2},{1,3},{2,0},{3,1},{4,6},{5,7},{6,4},{7,5},{8,10},{9,11},{10,... | collective-permute-start | bytes 3538952 | tf_op jit(solution)/shard_map/ppermute | solution.py:29
  523.3 48.9 %collective-permute-start.53 = (bf16[4,1024,256]{2,1,0:T(8,128)(2,1)S(1)}, bf16[4,1024,256]{2,1,0:T(8,128)(2,1)}, u32[]{:S(2)}, u32[]{:S(2)}) collective-permute-start(bf16[4,1024,256]{2,1,0:T(8,128)(2,1)S(1)} %get-tuple-element.97), channel_id=1, source_target_pairs={{0,1},{1,0},{2,3},{3,2},{4,5},{5,4},{6,7},{7,6},{8,9},{9,8},{10,11... | collective-permute-start | bytes 6291464 | tf_op jit(solution)/shard_map/ppermute | solution.py:29
  557.2 44.7 %collective-permute-start.63 = (bf16[3,512,384]{2,1,0:T(8,128)(2,1)}, bf16[3,512,384]{2,1,0:T(8,128)(2,1)S(1)}, u32[]{:S(2)}, u32[]{:S(2)}) collective-permute-start(bf16[3,512,384]{2,1,0:T(8,128)(2,1)} %pad_maximum_fusion.11), channel_id=1, source_target_pairs={{0,4},{4,0},{8,12},{12,8},{16,20},{20,16},{24,28},{28,24},{1,5},{5... | collective-permute-start | bytes 3538952 | tf_op jit(solution)/shard_map/ppermute | solution.py:29
  566.9 27.9 %collective-permute-start.57 = (bf16[4,256,256]{2,1,0:T(8,128)(2,1)S(1)}, bf16[4,256,256]{2,1,0:T(8,128)(2,1)S(1)}, u32[]{:S(2)}, u32[]{:S(2)}) collective-permute-start(bf16[4,256,256]{2,1,0:T(8,128)(2,1)S(1)} %get-tuple-element.150), channel_id=1, source_target_pairs={{0,4},{4,0},{8,12},{12,8},{16,20},{20,16},{24,28},{28,24},{1,5},{5... | collective-permute-start | bytes 1572872 | tf_op jit(solution)/shard_map/ppermute | solution.py:29
  572.3 38.3 %collective-permute-start.68 = (bf16[3,512,384]{2,1,0:T(8,128)(2,1)S(1)}, bf16[3,512,384]{2,1,0:T(8,128)(2,1)S(1)}, u32[]{:S(2)}, u32[]{:S(2)}) collective-permute-start(bf16[3,512,384]{2,1,0:T(8,128)(2,1)S(1)} %pad_maximum_fusion.14), channel_id=1, source_target_pairs={{0,2},{1,3},{2,0},{3,1},{4,6},{5,7},{6,4},{7,5},{8,10},{9,11},{10,... | collective-permute-start | bytes 3538952 | tf_op jit(solution)/shard_map/ppermute | solution.py:29
  594.8 28.9 %collective-permute-start.67 = (bf16[3,512,384]{2,1,0:T(8,128)(2,1)S(1)}, bf16[3,512,384]{2,1,0:T(8,128)(2,1)S(1)}, u32[]{:S(2)}, u32[]{:S(2)}) collective-permute-start(bf16[3,512,384]{2,1,0:T(8,128)(2,1)S(1)} %pad_maximum_fusion.13), channel_id=1, source_target_pairs={{0,4},{4,0},{8,12},{12,8},{16,20},{20,16},{24,28},{28,24},{1,5},{5... | collective-permute-start | bytes 3538952 | tf_op jit(solution)/shard_map/ppermute | solution.py:29
  597.4 43.9 %collective-permute-start.58 = (bf16[4,512,256]{2,1,0:T(8,128)(2,1)S(1)}, bf16[4,512,256]{2,1,0:T(8,128)(2,1)S(1)}, u32[]{:S(2)}, u32[]{:S(2)}) collective-permute-start(bf16[4,512,256]{2,1,0:T(8,128)(2,1)S(1)} %pad_maximum_fusion.17), channel_id=1, source_target_pairs={{0,2},{1,3},{2,0},{3,1},{4,6},{5,7},{6,4},{7,5},{8,10},{9,11},{10,... | collective-permute-start | bytes 3145736 | tf_op jit(solution)/shard_map/ppermute | solution.py:29
  601.1 41.0 %collective-permute-start.56 = (bf16[4,512,256]{2,1,0:T(8,128)(2,1)S(1)}, bf16[4,512,256]{2,1,0:T(8,128)(2,1)S(1)}, u32[]{:S(2)}, u32[]{:S(2)}) collective-permute-start(bf16[4,512,256]{2,1,0:T(8,128)(2,1)S(1)} %pad_maximum_fusion.16), channel_id=1, source_target_pairs={{0,4},{4,0},{8,12},{12,8},{16,20},{20,16},{24,28},{28,24},{1,5},{5... | collective-permute-start | bytes 3145736 | tf_op jit(solution)/shard_map/ppermute | solution.py:29
  603.3 36.8 %collective-permute-start.65 = (bf16[3,256,384]{2,1,0:T(8,128)(2,1)S(1)}, bf16[3,256,384]{2,1,0:T(8,128)(2,1)S(1)}, u32[]{:S(2)}, u32[]{:S(2)}) collective-permute-start(bf16[3,256,384]{2,1,0:T(8,128)(2,1)S(1)} %add_convert_fusion.5), channel_id=1, source_target_pairs={{0,16},{4,20},{8,24},{12,28},{16,0},{20,4},{24,8},{28,12},{1,17},{... | collective-permute-start | bytes 1769480 | tf_op jit(solution)/shard_map/ppermute | solution.py:29
  625.1 38.9 %collective-permute-start.69 = (bf16[3,256,384]{2,1,0:T(8,128)(2,1)S(1)}, bf16[3,256,384]{2,1,0:T(8,128)(2,1)S(1)}, u32[]{:S(2)}, u32[]{:S(2)}) collective-permute-start(bf16[3,256,384]{2,1,0:T(8,128)(2,1)S(1)} %add_convert_fusion), channel_id=1, source_target_pairs={{0,16},{4,20},{8,24},{12,28},{16,0},{20,4},{24,8},{28,12},{1,17},{... | collective-permute-start | bytes 1769480 | tf_op jit(solution)/shard_map/ppermute | solution.py:29
  643.4 31.9 %collective-permute-start.59 = (bf16[4,256,256]{2,1,0:T(8,128)(2,1)S(1)}, bf16[4,256,256]{2,1,0:T(8,128)(2,1)S(1)}, u32[]{:S(2)}, u32[]{:S(2)}) collective-permute-start(bf16[4,256,256]{2,1,0:T(8,128)(2,1)S(1)} %add_convert_fusion.21), channel_id=1, source_target_pairs={{0,16},{4,20},{8,24},{12,28},{16,0},{20,4},{24,8},{28,12},{1,17},{... | collective-permute-start | bytes 1572872 | tf_op jit(solution)/shard_map/ppermute | solution.py:29
  (165 other events, 3123.6 us)

commit v3 on v2

--- a/solution.py
+++ b/solution.py
@@ -44,22 +44,50 @@
     )
 
 
-def gather_weight(shard, wide, cut):
+def ordered(value, *others):
+    return lax.optimization_barrier((value, *others))[0]
+
+
+def gather_weights(shards, wide, cut, between):
     z_bits, t_bits = low_bits()
-    own = shard
-    for bit in z_bits:
-        own = jnp.concatenate([own, swap(own, "dp", bit)], wide)
-    for bit in t_bits:
-        own = jnp.concatenate([own, swap(own, "tensor", bit)], cut)
-    by_x = swap(own, "dp", 1)
-    by_y = swap(own, "tensor", 2)
-    near = jnp.concatenate([own, by_x], wide)
-    near_core = swap(near, "tensor", 1)
-    far_first = swap(halves(by_y, wide)[0], "dp", 1)
-    far_second = swap(halves(by_x, wide)[1], "tensor", 2)
-    far = jnp.concatenate([by_y, far_first, far_second], wide)
-    far_core = swap(far, "tensor", 1)
-    return near, near_core, far, far_core
+    done, corners = {}, []
+
+    def step(name, value, axis, bit):
+        if name in done:
+            value = ordered(value, *done[name])
+        got = swap(value, axis, bit)
+        done[name] = (got,)
+        return got
+
+    results = []
+    for place, own in enumerate(shards):
+        for bit in z_bits:
+            if place >= 2 and bit == z_bits[-1]:
+                own = ordered(own, *corners[place - 2])
+            own = jnp.concatenate([own, step(("z", bit), own, "dp", bit)], wide)
+        for bit in t_bits:
+            own = jnp.concatenate([own, step(("t", bit), own, "tensor", bit)], cut)
+        if place == 1:
+            own = ordered(own, *corners[0])
+        if place == 2:
+            own = ordered(own, result)
+        by_x = step("x", own, "dp", 1)
+        by_y = step("y", own, "tensor", 2)
+        if place == 1:
+            by_x, by_y = ordered(by_x, result), ordered(by_y, result)
+        near = jnp.concatenate([own, by_x], wide)
+        near_core = swap(near, "tensor", 1)
+        far_first, far_second = halves(by_y, wide)[0], halves(by_x, wide)[1]
+        if place == 1:
+            far_first, far_second = ordered(far_first, result), ordered(far_second, result)
+        far_first, far_second = swap(far_first, "dp", 1), swap(far_second, "tensor", 2)
+        corners.append((far_first, far_second))
+        far = jnp.concatenate([by_y, far_first, far_second], wide)
+        far_core = swap(far, "tensor", 1)
+        results.append((near, near_core, far, far_core))
+        if place == 0:
+            result = between(results[0])
+    return results
 
 
 def plus(left, right):
@@ -153,7 +181,7 @@
 
 
 ANY = pl.BlockSpec(memory_space=pl.ANY)
-LIMIT = 44 * 1024 * 1024
+LIMIT = 26 * 1024 * 1024
 
 
 def params(count=1):
@@ -222,66 +250,61 @@
     return jnp.dot(left, right, preferred_element_type=F32)
 
 
-def ffn_kernel(h, ht, c, ct, wa, wb, *rest):
-    ga, gb, branch, back, branch_sum, back_sum = rest[-6:]
-    step = pl.program_id(0)
+def ffn_kernel(first, h, ht, c, ct, wa, wb, *rest):
+    ga, gb, branch, back, act, dgate, dup = rest[-7:]
     half = wa.shape[2]
     wg, wu, wd = [jnp.concatenate([wa[k], wb[k]], 1) for k in range(3)]
-    gate = nn(h[...], wg)
-    up = nn(h[...], wu)
-    da = nn(c[...], wd)
-    sigma = 1.0 / (1.0 + jnp.exp(-gate))
-    silu = gate * sigma
-    act = (silu * up).astype(BF)
-    dgate = (da * up * sigma * (1.0 + gate * (1.0 - sigma))).astype(BF)
-    dup = (da * silu).astype(BF)
+    rows = h.shape[0]
+    tall = rows // 2
+    if first:
+
+        @pl.when(pl.program_id(0) == 0)
+        def _():
+            branch[...] = jnp.zeros_like(branch)
+            back[...] = jnp.zeros_like(back)
+
+    for start in range(0, rows, tall):
+        span = pl.ds(start, tall)
+        gate = nn(h[span, :], wg)
+        up = nn(h[span, :], wu)
+        da = nn(c[span, :], wd)
+        sigma = 1.0 / (1.0 + jnp.exp(-gate))
+        silu = gate * sigma
+        act[span, :] = (silu * up).astype(BF)
+        dup[span, :] = (da * silu).astype(BF)
+        dgate[span, :] = (da * up * (sigma + silu * (1.0 - sigma))).astype(BF)
     for k, (left, right) in enumerate(((ht, dgate), (ht, dup), (ct, act))):
-        grad = nn(left[...], right).astype(BF)
+        grad = nn(left[...], right[...]).astype(BF)
         ga[k] = grad[:, :half]
         gb[k] = grad[:, half:]
-    out = nt(act, wd)
-    into = nt(jnp.concatenate([dgate, dup], 1), jnp.concatenate([wg, wu], 1))
-
-    @pl.when(step == 0)
-    def _():
-        branch_sum[...] = out
-        back_sum[...] = into
-
-    @pl.when(step > 0)
-    def _():
-        branch_sum[...] += out
-        back_sum[...] += into
-
-    @pl.when(step == pl.num_programs(0) - 1)
-    def _():
-        branch[...] = branch_sum[...].astype(BF)
-        back[...] = back_sum[...].astype(BF)
-
-
-def ffn(h, ht, c, ct, wa, wb, deps):
+    branch[...] += nt(act[...], wd)
+    back[...] += nt(dgate[...], wg) + nt(dup[...], wu)
+
+
+def ffn(h, ht, c, ct, wa, wb, sums, deps):
     rows, width = h.shape
     cols = wa.shape[2]
     tile = 128
     block = pl.BlockSpec((3, width, tile), lambda j: (0, 0, j))
+    vmem = pl.BlockSpec(memory_space=pltpu.VMEM)
     grad = jax.ShapeDtypeStruct(wa.shape, BF)
-    part = jax.ShapeDtypeStruct((rows, width), BF)
+    part = jax.ShapeDtypeStruct((rows, width), F32)
     return pl.pallas_call(
-        ffn_kernel,
+        functools.partial(ffn_kernel, not sums),
         grid=(cols // tile,),
         out_shape=(grad, grad, part, part),
-        in_specs=[whole((rows, width)), whole((width, rows)), whole((rows, width)), whole((width, rows))]
-        + [block, block]
-        + [ANY] * len(deps),
-        out_specs=(block, block, whole((rows, width)), whole((rows, width))),
-        scratch_shapes=[pltpu.VMEM((rows, width), F32)] * 2,
+        in_specs=[vmem] * 4 + [block, block] + [vmem] * len(sums) + [ANY] * len(deps),
+        out_specs=(block, block, vmem, vmem),
+        input_output_aliases={6: 2, 7: 3} if sums else {},
+        scratch_shapes=[pltpu.VMEM((rows, 2 * tile), BF)] * 3,
         compiler_params=params(),
         cost_estimate=pl.CostEstimate(
             flops=36 * rows * width * cols,
-            bytes_accessed=12 * rows * width + 24 * width * cols,
+            bytes_accessed=24 * width * cols,
             transcendentals=2 * rows * cols,
         ),
         name="ffn",
-    )(h, ht, c, ct, wa, wb, *deps)
+    )(h, ht, c, ct, wa, wb, *sums, *deps)
 
 
 def middle_kernel(order, middle, scale, gain, cot, *rest):
@@ -360,7 +383,7 @@
         out_specs=(row, row, row, single),
         compiler_params=params(),
         cost_estimate=pl.CostEstimate(
-            flops=30 * rows * width, bytes_accessed=(14 + 4 * count) * rows * width, transcendentals=0
+            flops=30 * rows * width, bytes_accessed=(14 + 8 * count) * rows * width, transcendentals=0
         ),
         name="middle_back",
     )(order, middle, scale, gain, cot, *branches, *backs, *deps)
@@ -517,17 +540,13 @@
     before = lax.ppermute(
         tokens[rows - HALO :], "tensor", [(i, i + 1) for i in range(t_size - 1)]
     )
-    wm = gather_weight(
-        jnp.concatenate([mixer_in.astype(BF), mixer_out.T.astype(BF)[None]], 0), 1, 2
-    )
     ffn_cols = gate_up.shape[2] // PARTS
-    wf = []
+    shards = [jnp.concatenate([mixer_in.astype(BF), mixer_out.T.astype(BF)[None]], 0)]
     for i in range(PARTS):
         cols = slice(i * ffn_cols, (i + 1) * ffn_cols)
-        packed = jnp.concatenate(
-            [gate_up[:, :, cols].astype(BF), down_proj[cols].T.astype(BF)[None]], 0
+        shards.append(
+            jnp.concatenate([gate_up[:, :, cols].astype(BF), down_proj[cols].T.astype(BF)[None]], 0)
         )
-        wf.append(gather_weight(packed, 1, 2))
 
     small = jnp.concatenate([norm_gains, conv_kernel], 0)[:, None, :]
     for axis, size_axis in (("tensor", t_size), ("dp", dp_size)):
@@ -565,25 +584,39 @@
     scale_ext = rms_scale(extended)
     normed_ext = (extended * scale_ext * gains[0]).astype(BF)
     values, scale_one, normed_one = extended[HALO:], scale_ext[HALO:], normed_ext[HALO:]
-    wm_all = jnp.concatenate(wm, 2)
-    win_all, wout_all = wm_all[:3], wm_all[3]
-    projected = mm("td,kdc->ktc", normed_ext, win_all)
-    part_b, part_c, part_x = projected[0], projected[1][HALO:], projected[2]
-    product_ext = part_b * part_x
-    part_b, part_x = part_b[HALO:], part_x[HALO:]
-    product = product_ext[HALO:]
-    convolved = kernel[0] * product
-    for shift in range(1, KW):
-        convolved = convolved + kernel[shift] * masks[shift - 1][:rows] * shift_rows(
-            product_ext, HALO - shift, rows
-        )
-    gated = (part_c * convolved).astype(BF)
-    middle = values + mm("tc,dc->td", gated, wout_all)
-    scale_two = rms_scale(middle)
-    normed_two = (middle * scale_two * gains[1]).astype(BF)
+    kept = {}
+
+    def mixer_forward(wm):
+        wm_all = jnp.concatenate(wm, 2)
+        win_all, wout_all = wm_all[:3], wm_all[3]
+        projected = mm("td,kdc->ktc", normed_ext, win_all)
+        part_b, part_c, part_x = projected[0], projected[1][HALO:], projected[2]
+        product_ext = part_b * part_x
+        part_b, part_x = part_b[HALO:], part_x[HALO:]
+        product = product_ext[HALO:]
+        convolved = kernel[0] * product
+        for shift in range(1, KW):
+            convolved = convolved + kernel[shift] * masks[shift - 1][:rows] * shift_rows(
+                product_ext, HALO - shift, rows
+            )
+        gated = (part_c * convolved).astype(BF)
+        middle = values + mm("tc,dc->td", gated, wout_all)
+        scale_two = rms_scale(middle)
+        normed_two = (middle * scale_two * gains[1]).astype(BF)
+        kept.update(locals())
+        return normed_two
+
+    _, *wf = gather_weights(shards, 1, 2, mixer_forward)
+    win_all, wout_all, part_b, part_c, part_x = [
+        kept[name] for name in ("win_all", "wout_all", "part_b", "part_c", "part_x")
+    ]
+    product_ext, product, convolved, gated, middle, scale_two, normed_two = [
+        kept[name]
+        for name in ("product_ext", "product", "convolved", "gated", "middle", "scale_two", "normed_two")
+    ]
 
     norm_t, cot_t = normed_two.T, cot.T
-    branches, backs, grads = [], [], []
+    sums, grads = [], []
     near_in, far_in, corner, sides = [], [], [], []
     for i in range(PARTS):
         near, near_core, far, far_core = wf[i]
@@ -592,16 +625,12 @@
             deps.append(near_in[i - 1])
         if i >= 2:
             deps += corner[i - 2]
-        g_near, g_near_core, branch, back = ffn(normed_two, norm_t, cot, cot_t, near, near_core, deps)
-        branches.append(branch)
-        backs.append(back)
+        g_near, g_near_core, *sums = ffn(normed_two, norm_t, cot, cot_t, near, near_core, sums, deps)
         near_in.append(swap(g_near_core, "tensor", 1))
         if i >= 2:
             sides.append(scatter_sides(*grads[i - 2][:1], near_in[i - 2], grads[i - 2][1], far_in[i - 2], *corner[i - 2], 1))
         deps = [far_in[i - 1]] if i >= 1 else []
-        g_far, g_far_core, branch, back = ffn(normed_two, norm_t, cot, cot_t, far, far_core, deps)
-        branches.append(branch)
-        backs.append(back)
+        g_far, g_far_core, *sums = ffn(normed_two, norm_t, cot, cot_t, far, far_core, sums, deps)
         far_in.append(swap(g_far_core, "tensor", 1))
         grads.append((g_near, g_far))
         if i >= 1:
@@ -611,7 +640,7 @@
         return scatter_sides(grads[i][0], near_in[i], grads[i][1], far_in[i], *corner[i], 1)
 
     block_out, middle_grad, mixed_grad, gain_two_grad = middle_back(
-        order, middle, scale_two, gains[1:2], cot, branches, backs, [near_in[-1], *corner[-1]]
+        order, middle, scale_two, gains[1:2], cot, sums[:1], sums[1:], [near_in[-1], *corner[-1]]
     )
     corner.append(scatter_corner(grads[-1][1], far_in[-1], 1))
     while len(sides) < PARTS - 1:
@@ -653,7 +682,7 @@
     sides.append(finish_sides(PARTS - 1))
     m_near, m_far = mixer_grad(one_t, mixed_t, proj_grad, gated, 0, 2, [])
     m_corner = scatter_corner(m_far, m_far_in, 1)
-    normed_one_grad = mm("ktc,kdc->td", proj_grad, win_all)
+    normed_one_grad = mm("ktc,kdc->td", ordered(proj_grad, m_far), win_all)
     grad_input, gain_one_grad = input_back(
         order, x_ext[HALO:], scale_one, gains[:1], middle_grad, normed_one_grad
     )
@@ -677,7 +706,7 @@
         ],
         1,
     )
-    sums = jnp.concatenate([gain_sums, kernel_sums], 0)
+    sums = ordered(jnp.concatenate([gain_sums, kernel_sums], 0), *m_corner)
     for axis, size_axis in (("tensor", t_size), ("dp", dp_size)):
         for i in range(size_axis.bit_length() - 1):
             sums = sums + swap(sums, axis, 1 << i)

time: 695 us -> 678 us (0.976)
  Pallas kernels: 148 us -> 113 us
  waiting for transfers between devices: 280 us -> 314 us
  other arithmetic: 98 us -> 79.8 us
  local copies, waits for them, and re-layouts: 67.1 us -> 80.5 us
  starting transfers between devices: 65.7 us -> 54.4 us
    ppermute x74, waiting for transfers between devices: 280 us -> 314 us  [swap(): return lax.ppermute(values, axis, [(i, i ^ bit) for i in range(size)])]
    pallas_call x6, Pallas kernels: 114 us -> 87.8 us  [ffn(): pl.pallas_call(functools.partial(ffn_kernel, not sums), grid=(cols // til...]
    unnamed x293 -> x251, local copies, waits for them, and re-layouts: 28 us -> 42.8 us
    ppermute x74, starting transfers between devices: 62.3 us -> 51.1 us  [swap(): return lax.ppermute(values, axis, [(i, i ^ bit) for i in range(size)])]
    concatenate x14 -> x10, other arithmetic: 20.4 us -> 11.8 us  [the longest x7 6.28 us: gather_weights(): own = jnp.concatenate([own, step(('z', bit), own, 'dp', bit)], wide)]
  transfers between devices with their start and end apart: 76 -> 76, of which waited for: 28 -> 27; matrix products, arithmetic and copies ran while one was open for 25% -> 23% of each run, Pallas kernels for 21% -> 17%
where the time goes in v3:
time: 678 us; the launch traced here: 672 us
  waiting for transfers between devices  314 us (46%)
  Pallas kernels  113 us (17%)
  local copies, waits for them, and re-layouts  80.5 us (12%)
  other arithmetic  79.8 us (12%)
  starting transfers between devices  54.4 us (8%)
  matrix products  23 us (3%)
  between operations  7.86 us (1%)
    ppermute x74, waiting for transfers between devices, swap(): return lax.ppermute(values, axis, [(i, i ^ bit) for i in range(size)])  314 us
    pallas_call x6, Pallas kernels, ffn(): pl.pallas_call(functools.partial(ffn_kernel, not sums), grid=(cols // til...  87.8 us
    ppermute x74, starting transfers between devices, swap(): return lax.ppermute(values, axis, [(i, i ^ bit) for i in range(size)])  51.1 us
    unnamed x251, local copies, waits for them, and re-layouts  42.8 us
    dot_general x4, matrix products, mm(): return jnp.einsum(spec, left, right, preferred_element_type=F32).astype(out)  23 us
  transfers between devices with their start and end apart: 76, of which 27 were waited for; matrix products, arithmetic and copies ran while one was open for 23% of the time, Pallas kernels for 17%

profile of v3, /device:TPU:0, one launch (start us, length us, event | category | flops | bytes accessed | tf_op | source)
XLA Modules:
  0.0 672.3 jit_solution(9224551154969035762)
XLA Ops:
  7.3 3.1 collective-permute-start.1
  25.1 11.0 %collective-permute-done.12 = f32[5,8,32]{2,0,1:T(8,128)S(1)} collective-permute-done((f32[5,8,32]{2,0,1:T(8,128)S(1)}, f32[5,8,32]{2,0,1:T(8,128)S(1)}, u32[]{:S(2)}, u32[]{:S(2)}) %collective-permute-start.12) | collective-permute-done | bytes 5152 | tf_op jit(solution)/shard_map/ppermute | solution.py:29
  43.9 6.2 collective-permute-done.13
  52.6 23.9 %collective-permute-done.5 = bf16[4,512,256]{2,1,0:T(8,128)(2,1)S(1)} collective-permute-done((bf16[4,512,256]{2,1,0:T(8,128)(2,1)}, bf16[4,512,256]{2,1,0:T(8,128)(2,1)S(1)}, u32[]{:S(2)}, u32[]{:S(2)}) %collective-permute-start.5) | collective-permute-done | bytes 1048608 | tf_op jit(solution)/shard_map/ppermute | solution.py:29
  81.0 8.6 %collective-permute-done.6 = bf16[4,256,256]{2,1,0:T(8,128)(2,1)S(1)} collective-permute-done((bf16[4,256,256]{2,1,0:T(8,128)(2,1)S(1)}, bf16[4,256,256]{2,1,0:T(8,128)(2,1)S(1)}, u32[]{:S(2)}, u32[]{:S(2)}) %collective-permute-start.6) | collective-permute-done | bytes 524320 | tf_op jit(solution)/shard_map/ppermute | solution.py:29
  95.6 3.0 copy.67
  106.5 24.3 %collective-permute-done.17 = bf16[3,256,384]{2,1,0:T(8,128)(2,1)S(1)} collective-permute-done((bf16[3,256,384]{2,1,0:T(8,128)(2,1)S(1)}, bf16[3,256,384]{2,1,0:T(8,128)(2,1)S(1)}, u32[]{:S(2)}, u32[]{:S(2)}) %collective-permute-start.17) | collective-permute-done | bytes 589856 | tf_op jit(solution)/shard_map/ppermute | solution.py:29
  134.5 4.0 pad_maximum_fusion
  138.5 6.5 convolution_bitcast_fusion
  146.1 2.8 copy-done.65
  148.8 3.0 multiply_convert_fusion.3
  155.9 3.9 collective-permute-done.20
  165.6 11.3 %collective-permute-done.19 = bf16[3,256,384]{2,1,0:T(8,128)(2,1)S(1)} collective-permute-done((bf16[3,256,384]{2,1,0:T(8,128)(2,1)S(1)}, bf16[3,256,384]{2,1,0:T(8,128)(2,1)S(1)}, u32[]{:S(2)}, u32[]{:S(2)}) %collective-permute-start.19) | collective-permute-done | bytes 589856 | tf_op jit(solution)/shard_map/ppermute | solution.py:29
  178.6 10.4 %collective-permute-done.22 = bf16[3,256,384]{2,1,0:T(8,128)(2,1)S(1)} collective-permute-done((bf16[3,256,384]{2,1,0:T(8,128)(2,1)S(1)}, bf16[3,256,384]{2,1,0:T(8,128)(2,1)S(1)}, u32[]{:S(2)}, u32[]{:S(2)}) %collective-permute-start.22) | collective-permute-done | bytes 589856 | tf_op jit(solution)/shard_map/ppermute | solution.py:29
  204.2 22.6 %collective-permute-done.23 = bf16[3,256,384]{2,1,0:T(8,128)(2,1)S(1)} collective-permute-done((bf16[3,256,384]{2,1,0:T(8,128)(2,1)}, bf16[3,256,384]{2,1,0:T(8,128)(2,1)S(1)}, u32[]{:S(2)}, u32[]{:S(2)}) %collective-permute-start.23) | collective-permute-done | bytes 589856 | tf_op jit(solution)/shard_map/ppermute | solution.py:29
  235.9 14.8 %ffn.6 = (bf16[3,1024,384]{2,1,0:T(8,128)(2,1)S(1)}, bf16[3,1024,384]{2,1,0:T(8,128)(2,1)S(1)}, f32[768,1024]{1,0:T(8,128)S(1)}, f32[768,1024]{1,0:T(8,128)S(1)}) custom-call(bf16[768,1024]{1,0:T(8,128)(2,1)S(1)} %copy-done.41, bf16[1024,768]{1,0:T(8,128)(2,1)S(1)} %fusion.51.ht, bf16[768,1024]{1,0:T(8,128)(2,1)S(1)} %copy-done.3, ...), custom_call_target="tpu_custom_call" | custom-call | flops 10871635968 | bytes 9437184 | tf_op jit(solution)/shard_map/ffn/pallas_call | solution.py:292
  253.1 14.3 %ffn.7 = (bf16[3,1024,384]{2,1,0:T(8,128)(2,1)S(1)}, bf16[3,1024,384]{2,1,0:T(8,128)(2,1)S(1)}, f32[768,1024]{1,0:T(8,128)S(1)}, f32[768,1024]{1,0:T(8,128)S(1)}) custom-call(bf16[768,1024]{1,0:T(8,128)(2,1)S(1)} %copy-done.41, bf16[1024,768]{1,0:T(8,128)(2,1)S(1)} %fusion.51.ht, ...), custom_call_target="tpu_custom_call", output_to_operand_aliasing={{2}: (6, {}), {3}: (7, {})} | custom-call | flops 10871635968 | bytes 9437184 | tf_op jit(solution)/shard_map/ffn/pallas_call | solution.py:292
  267.4 7.3 %collective-permute-done.25 = bf16[3,512,384]{2,1,0:T(8,128)(2,1)S(1)} collective-permute-done((bf16[3,512,384]{2,1,0:T(8,128)(2,1)}, bf16[3,512,384]{2,1,0:T(8,128)(2,1)S(1)}, u32[]{:S(2)}, u32[]{:S(2)}) %collective-permute-start.25) | collective-permute-done | bytes 1179680 | tf_op jit(solution)/shard_map/ppermute | solution.py:29
  281.4 11.0 %collective-permute-done.26 = bf16[3,256,384]{2,1,0:T(8,128)(2,1)S(1)} collective-permute-done((bf16[3,256,384]{2,1,0:T(8,128)(2,1)S(1)}, bf16[3,256,384]{2,1,0:T(8,128)(2,1)S(1)}, u32[]{:S(2)}, u32[]{:S(2)}) %collective-permute-start.26) | collective-permute-done | bytes 589856 | tf_op jit(solution)/shard_map/ppermute | solution.py:29
  297.9 9.5 %collective-permute-done.29 = bf16[3,256,384]{2,1,0:T(8,128)(2,1)S(1)} collective-permute-done((bf16[3,256,384]{2,1,0:T(8,128)(2,1)S(1)}, bf16[3,256,384]{2,1,0:T(8,128)(2,1)S(1)}, u32[]{:S(2)}, u32[]{:S(2)}) %collective-permute-start.29) | collective-permute-done | bytes 589856 | tf_op jit(solution)/shard_map/ppermute | solution.py:29
  312.8 14.1 %ffn.8 = (bf16[3,1024,384]{2,1,0:T(8,128)(2,1)S(1)}, bf16[3,1024,384]{2,1,0:T(8,128)(2,1)}, f32[768,1024]{1,0:T(8,128)S(1)}, f32[768,1024]{1,0:T(8,128)S(1)}) custom-call(bf16[768,1024]{1,0:T(8,128)(2,1)S(1)} %copy-done.41, bf16[1024,768]{1,0:T(8,128)(2,1)S(1)} %fusion.51.ht, ...), custom_call_target="tpu_custom_call", output_to_operand_aliasing={{2}: (6, {}), {3}: (7, {})} | custom-call | flops 10871635968 | bytes 9437184 | tf_op jit(solution)/shard_map/ffn/pallas_call | solution.py:292
  329.5 15.0 %ffn.9 = (bf16[3,1024,384]{2,1,0:T(8,128)(2,1)S(1)}, bf16[3,1024,384]{2,1,0:T(8,128)(2,1)}, f32[768,1024]{1,0:T(8,128)S(1)}, f32[768,1024]{1,0:T(8,128)S(1)}) custom-call(bf16[768,1024]{1,0:T(8,128)(2,1)S(1)} %copy-done.41, bf16[1024,768]{1,0:T(8,128)(2,1)S(1)} %fusion.51.ht, ...), custom_call_target="tpu_custom_call", output_to_operand_aliasing={{2}: (6, {}), {3}: (7, {})} | custom-call | flops 10871635968 | bytes 9437184 | tf_op jit(solution)/shard_map/ffn/pallas_call | solution.py:292
  355.6 10.2 %collective-permute-done.42.rest_4_ = bf16[3,256,384]{2,1,0:T(8,128)(2,1)} collective-permute-done((bf16[3,256,384]{2,1,0:T(8,128)(2,1)}, bf16[3,256,384]{2,1,0:T(8,128)(2,1)}, u32[]{:S(2)}, u32[]{:S(2)}) %collective-permute-start.42) | collective-permute-done | bytes 589856 | tf_op jit(solution)/shard_map/ppermute | solution.py:29
  373.3 14.8 %ffn.10 = (bf16[3,1024,384]{2,1,0:T(8,128)(2,1)S(1)}, bf16[3,1024,384]{2,1,0:T(8,128)(2,1)}, f32[768,1024]{1,0:T(8,128)S(1)}, f32[768,1024]{1,0:T(8,128)S(1)}) custom-call(bf16[768,1024]{1,0:T(8,128)(2,1)S(1)} %copy-done.42, bf16[1024,768]{1,0:T(8,128)(2,1)S(1)} %copy-done.47, ...), custom_call_target="tpu_custom_call", output_to_operand_aliasing={{2}: (6, {}), {3}: (7, {})} | custom-call | flops 10871635968 | bytes 9437184 | tf_op jit(solution)/shard_map/ffn/pallas_call | solution.py:292
  392.0 14.8 %ffn.11 = (bf16[3,1024,384]{2,1,0:T(8,128)(2,1)S(1)}, bf16[3,1024,384]{2,1,0:T(8,128)(2,1)}, f32[768,1024]{1,0:T(8,128)S(1)}, f32[768,1024]{1,0:T(8,128)S(1)}) custom-call(bf16[768,1024]{1,0:T(8,128)(2,1)S(1)} %copy-done.43, bf16[1024,768]{1,0:T(8,128)(2,1)S(1)} %copy-done.47, ...), custom_call_target="tpu_custom_call", output_to_operand_aliasing={{2}: (6, {}), {3}: (7, {})} | custom-call | flops 10871635968 | bytes 9437184 | tf_op jit(solution)/shard_map/ffn/pallas_call | solution.py:292
  408.5 3.2 add_convert_fusion.10
  411.8 3.1 add_convert_fusion.7
  416.7 3.6 copy.80.refs_1_
  424.7 15.8 %collective-permute-done.61 = bf16[3,256,384]{2,1,0:T(8,128)(2,1)} collective-permute-done((bf16[3,256,384]{2,1,0:T(8,128)(2,1)}, bf16[3,256,384]{2,1,0:T(8,128)(2,1)}, u32[]{:S(2)}, u32[]{:S(2)}) %collective-permute-start.61) | collective-permute-done | bytes 589856 | tf_op jit(solution)/shard_map/ppermute | solution.py:29
  447.5 4.3 middle_back.1
  451.8 7.2 %fusion.17 = (bf16[1,768,1024]{2,1,0:T(8,128)(2,1)}, f32[768,1024]{1,0:T(8,128)S(1)}) fusion(f32[768,1024]{1,0:T(8,128)S(1)} %copy-done.71, f32[3,784,1024]{2,1,0:T(8,128)} %copy-done.65, bf16[768,1024]{1,0:T(8,128)(2,1)S(1)} %get-tuple-element.133, bf16[4,1024,1024]{2,1,0:T(8,128)(2,1)} %copy-done.70), kind=kOutput, calls=%fused_computation.43 | convolution fusion | flops 1612972032 | bytes 14680064 | tf_op jit(solution)/shard_map/td,dc->tc/dot_general | solution.py:180
  464.6 2.8 copy.82
  468.2 2.8 broadcast_multiply_fusion.1
  474.9 4.0 multiply_reduce_fusion.1
  481.5 23.8 %collective-permute-done.51.rest_2_ = bf16[3,256,384]{2,1,0:T(8,128)(2,1)S(1)} collective-permute-done((bf16[3,256,384]{2,1,0:T(8,128)(2,1)}, bf16[3,256,384]{2,1,0:T(8,128)(2,1)S(1)}, u32[]{:S(2)}, u32[]{:S(2)}) %collective-permute-start.51) | collective-permute-done | bytes 589856 | tf_op jit(solution)/shard_map/ppermute | solution.py:29
  510.1 4.5 mixer_grad.2
  514.6 8.1 %collective-permute-done.52.rest_3_ = bf16[3,256,384]{2,1,0:T(8,128)(2,1)S(1)} collective-permute-done((bf16[3,256,384]{2,1,0:T(8,128)(2,1)S(1)}, bf16[3,256,384]{2,1,0:T(8,128)(2,1)S(1)}, u32[]{:S(2)}, u32[]{:S(2)}) %collective-permute-start.52) | collective-permute-done | bytes 589856 | tf_op jit(solution)/shard_map/ppermute | solution.py:29
  522.7 4.5 mixer_grad.3
  527.3 7.3 %fusion.11.upstream = f32[768,1024]{1,0:T(8,128)S(1)} fusion(bf16[3,768,1024]{2,1,0:T(8,128)(2,1)S(1)} %pad_maximum_fusion.1.pa.pb, bf16[4,1024,1024]{2,1,0:T(8,128)(2,1)} %copy-done.70), kind=kOutput, calls=%fused_computation.37 | convolution fusion | flops 4831838208 | bytes 14155776 | tf_op jit(solution)/shard_map/ktc,kdc->td/dot_general | solution.py:180
  534.7 4.9 input_back.1
  549.1 30.8 %collective-permute-done.55 = bf16[4,256,256]{2,1,0:T(8,128)(2,1)S(1)} collective-permute-done((bf16[4,256,256]{2,1,0:T(8,128)(2,1)S(1)}, bf16[4,256,256]{2,1,0:T(8,128)(2,1)S(1)}, u32[]{:S(2)}, u32[]{:S(2)}) %collective-permute-start.55) | collective-permute-done | bytes 524320 | tf_op jit(solution)/shard_map/ppermute | solution.py:29
  580.4 3.4 collective-permute-done.57
  590.1 29.9 %collective-permute-done.65 = bf16[3,256,384]{2,1,0:T(8,128)(2,1)S(1)} collective-permute-done((bf16[3,256,384]{2,1,0:T(8,128)(2,1)S(1)}, bf16[3,256,384]{2,1,0:T(8,128)(2,1)S(1)}, u32[]{:S(2)}, u32[]{:S(2)}) %collective-permute-start.65) | collective-permute-done | bytes 589856 | tf_op jit(solution)/shard_map/ppermute | solution.py:29
  622.2 10.3 %collective-permute-done.69 = bf16[3,256,384]{2,1,0:T(8,128)(2,1)S(1)} collective-permute-done((bf16[3,256,384]{2,1,0:T(8,128)(2,1)S(1)}, bf16[3,256,384]{2,1,0:T(8,128)(2,1)S(1)}, u32[]{:S(2)}, u32[]{:S(2)}) %collective-permute-start.69) | collective-permute-done | bytes 589856 | tf_op jit(solution)/shard_map/ppermute | solution.py:29
  640.3 10.0 %collective-permute-done.74 = f32[5,1024]{1,0:T(8,128)S(1)} collective-permute-done((f32[5,1024]{1,0:T(8,128)S(1)}, f32[5,1024]{1,0:T(8,128)S(1)}, u32[]{:S(2)}, u32[]{:S(2)}) %collective-permute-start.74) | collective-permute-done | bytes 20512 | tf_op jit(solution)/shard_map/ppermute | solution.py:29
  651.6 4.3 update.3
  655.9 7.2 %collective-permute-done.75 = f32[5,1024]{1,0:T(8,128)S(1)} collective-permute-done((f32[5,1024]{1,0:T(8,128)S(1)}, f32[5,1024]{1,0:T(8,128)S(1)}, u32[]{:S(2)}, u32[]{:S(2)}) %collective-permute-start.75) | collective-permute-done | bytes 20512 | tf_op jit(solution)/shard_map/ppermute | solution.py:29
  664.7 5.5 collective-permute-done.60
  (509 shorter events, 192.8 us)
Async XLA Ops:
  3.3 88.4 %collective-permute-start = (bf16[16,1024]{1,0:T(8,128)(2,1)}, bf16[16,1024]{1,0:T(8,128)(2,1)S(1)}, u32[]{:S(2)}, u32[]{:S(2)}) collective-permute-start(bf16[16,1024]{1,0:T(8,128)(2,1)} %slice.681), channel_id=1, source_target_pairs={{0,1},{1,2},{2,3},{4,5},{5,6},{6,7},{8,9},{9,10},{10,11},{12,13},{... | collective-permute-start | bytes 98312 | tf_op jit(solution)/shard_map/ppermute | solution.py:540
  21.9 28.2 %collective-permute-start.2 = (bf16[4,256,256]{2,1,0:T(8,128)(2,1)S(1)}, bf16[4,256,256]{2,1,0:T(8,128)(2,1)S(1)}, u32[]{:S(2)}, u32[]{:S(2)}) collective-permute-start(bf16[4,256,256]{2,1,0:T(8,128)(2,1)S(1)} %pad_maximum_fusion.17), channel_id=1, source_target_pairs={{0,16},{4,20},{8,24},{12,28},{16,0},{20,4},{24,8},{28,12},{1,17},{... | collective-permute-start | bytes 1572872 | tf_op jit(solution)/shard_map/ppermute | solution.py:29
  51.2 25.3 %collective-permute-start.5 = (bf16[4,512,256]{2,1,0:T(8,128)(2,1)}, bf16[4,512,256]{2,1,0:T(8,128)(2,1)S(1)}, u32[]{:S(2)}, u32[]{:S(2)}) collective-permute-start(bf16[4,512,256]{2,1,0:T(8,128)(2,1)} %pad_maximum_fusion.11), channel_id=1, source_target_pairs={{0,2},{1,3},{2,0},{3,1},{4,6},{5,7},{6,4},{7,5},{8,10},{9,11},{10,... | collective-permute-start | bytes 3145736 | tf_op jit(solution)/shard_map/ppermute | solution.py:29
  51.5 25.6 %collective-permute-start.3 = (bf16[4,512,256]{2,1,0:T(8,128)(2,1)}, bf16[4,512,256]{2,1,0:T(8,128)(2,1)S(1)}, u32[]{:S(2)}, u32[]{:S(2)}) collective-permute-start(bf16[4,512,256]{2,1,0:T(8,128)(2,1)} %pad_maximum_fusion.11), channel_id=1, source_target_pairs={{0,4},{4,0},{8,12},{12,8},{16,20},{20,16},{24,28},{28,24},{1,5},{5... | collective-permute-start | bytes 3145736 | tf_op jit(solution)/shard_map/ppermute | solution.py:29
  79.9 54.5 %collective-permute-start.4 = (bf16[4,1024,256]{2,1,0:T(8,128)(2,1)}, bf16[4,1024,256]{2,1,0:T(8,128)(2,1)}, u32[]{:S(2)}, u32[]{:S(2)}) collective-permute-start(bf16[4,1024,256]{2,1,0:T(8,128)(2,1)} %pad_maximum_fusion.2), channel_id=1, source_target_pairs={{0,1},{1,0},{2,3},{3,2},{4,5},{5,4},{6,7},{7,6},{8,9},{9,8},{10,11... | collective-permute-start | bytes 6291464 | tf_op jit(solution)/shard_map/ppermute | solution.py:29
  91.3 43.2 %collective-permute-start.8 = (bf16[4,1024,256]{2,1,0:T(8,128)(2,1)}, bf16[4,1024,256]{2,1,0:T(8,128)(2,1)}, u32[]{:S(2)}, u32[]{:S(2)}) collective-permute-start(bf16[4,1024,256]{2,1,0:T(8,128)(2,1)} %constant_dynamic-update-slice_fusion), channel_id=1, source_target_pairs={{0,1},{1,0},{2,3},{3,2},{4,5},{5,4},{6,7},{7,6},{8,9},{9,8},{10,11... | collective-permute-start | bytes 6291464 | tf_op jit(solution)/shard_map/ppermute | solution.py:29
  102.3 28.5 %collective-permute-start.17 = (bf16[3,256,384]{2,1,0:T(8,128)(2,1)S(1)}, bf16[3,256,384]{2,1,0:T(8,128)(2,1)S(1)}, u32[]{:S(2)}, u32[]{:S(2)}) collective-permute-start(bf16[3,256,384]{2,1,0:T(8,128)(2,1)S(1)} %pad_maximum_fusion.15), channel_id=1, source_target_pairs={{0,16},{4,20},{8,24},{12,28},{16,0},{20,4},{24,8},{28,12},{1,17},{... | collective-permute-start | bytes 1769480 | tf_op jit(solution)/shard_map/ppermute | solution.py:29
  105.6 57.0 %collective-permute-start.15 = (bf16[3,128,384]{2,1,0:T(8,128)(2,1)S(1)}, bf16[3,128,384]{2,1,0:T(8,128)(2,1)S(1)}, u32[]{:S(2)}, u32[]{:S(2)}) collective-permute-start(bf16[3,128,384]{2,1,0:T(8,128)(2,1)S(1)} %copy-done.95), channel_id=1, source_target_pairs={{0,8},{4,12},{8,0},{12,4},{16,24},{20,28},{24,16},{28,20},{1,9},{5... | collective-permute-start | bytes 884744 | tf_op jit(solution)/shard_map/ppermute | solution.py:29
  131.9 28.0 %collective-permute-start.20 = (bf16[3,512,384]{2,1,0:T(8,128)(2,1)S(1)}, bf16[3,512,384]{2,1,0:T(8,128)(2,1)S(1)}, u32[]{:S(2)}, u32[]{:S(2)}) collective-permute-start(bf16[3,512,384]{2,1,0:T(8,128)(2,1)S(1)} %pad_maximum_fusion.3), channel_id=1, source_target_pairs={{0,4},{4,0},{8,12},{12,8},{16,20},{20,16},{24,28},{28,24},{1,5},{5... | collective-permute-start | bytes 3538952 | tf_op jit(solution)/shard_map/ppermute | solution.py:29
  133.0 28.0 %collective-permute-start.18 = (bf16[3,512,384]{2,1,0:T(8,128)(2,1)S(1)}, bf16[3,512,384]{2,1,0:T(8,128)(2,1)S(1)}, u32[]{:S(2)}, u32[]{:S(2)}) collective-permute-start(bf16[3,512,384]{2,1,0:T(8,128)(2,1)S(1)} %pad_maximum_fusion.3), channel_id=1, source_target_pairs={{0,2},{1,3},{2,0},{3,1},{4,6},{5,7},{6,4},{7,5},{8,10},{9,11},{10,... | collective-permute-start | bytes 3538952 | tf_op jit(solution)/shard_map/ppermute | solution.py:29
  161.0 73.8 %collective-permute-start.37 = (bf16[3,1024,384]{2,1,0:T(8,128)(2,1)}, bf16[3,1024,384]{2,1,0:T(8,128)(2,1)}, u32[]{:S(2)}, u32[]{:S(2)}) collective-permute-start(bf16[3,1024,384]{2,1,0:T(8,128)(2,1)} %constant_dynamic-update-slice_fusion.38.wa), channel_id=1, source_target_pairs={{0,1},{1,0},{2,3},{3,2},{4,5},{5,4},{6,7},{7,6},{8,9},{9,8},{10,11... | collective-permute-start | bytes 7077896 | tf_op jit(solution)/shard_map/ppermute | solution.py:29
  162.7 26.3 %collective-permute-start.22 = (bf16[3,256,384]{2,1,0:T(8,128)(2,1)S(1)}, bf16[3,256,384]{2,1,0:T(8,128)(2,1)S(1)}, u32[]{:S(2)}, u32[]{:S(2)}) collective-permute-start(bf16[3,256,384]{2,1,0:T(8,128)(2,1)S(1)} %pad_maximum_fusion.16), channel_id=1, source_target_pairs={{0,16},{4,20},{8,24},{12,28},{16,0},{20,4},{24,8},{28,12},{1,17},{... | collective-permute-start | bytes 1769480 | tf_op jit(solution)/shard_map/ppermute | solution.py:29
  163.5 31.3 %collective-permute-start.16 = (bf16[3,128,384]{2,1,0:T(8,128)(2,1)}, bf16[3,128,384]{2,1,0:T(8,128)(2,1)}, u32[]{:S(2)}, u32[]{:S(2)}) collective-permute-start(bf16[3,128,384]{2,1,0:T(8,128)(2,1)} %pad_maximum_fusion.18), channel_id=1, source_target_pairs={{0,8},{4,12},{8,0},{12,4},{16,24},{20,28},{24,16},{28,20},{1,9},{5... | collective-permute-start | bytes 884744 | tf_op jit(solution)/shard_map/ppermute | solution.py:29
  178.6 74.4 %collective-permute-start.36 = (bf16[3,1024,384]{2,1,0:T(8,128)(2,1)}, bf16[3,1024,384]{2,1,0:T(8,128)(2,1)}, u32[]{:S(2)}, u32[]{:S(2)}) collective-permute-start(bf16[3,1024,384]{2,1,0:T(8,128)(2,1)} %constant_dynamic-update-slice_fusion.35.wa), channel_id=1, source_target_pairs={{0,1},{1,0},{2,3},{3,2},{4,5},{5,4},{6,7},{7,6},{8,9},{9,8},{10,11... | collective-permute-start | bytes 7077896 | tf_op jit(solution)/shard_map/ppermute | solution.py:29
  190.1 37.7 %collective-permute-start.27 = (bf16[3,512,384]{2,1,0:T(8,128)(2,1)}, bf16[3,512,384]{2,1,0:T(8,128)(2,1)}, u32[]{:S(2)}, u32[]{:S(2)}) collective-permute-start(bf16[3,512,384]{2,1,0:T(8,128)(2,1)} %pad_maximum_fusion.4), channel_id=1, source_target_pairs={{0,4},{4,0},{8,12},{12,8},{16,20},{20,16},{24,28},{28,24},{1,5},{5... | collective-permute-start | bytes 3538952 | tf_op jit(solution)/shard_map/ppermute | solution.py:29
  191.8 37.9 %collective-permute-start.24 = (bf16[3,512,384]{2,1,0:T(8,128)(2,1)}, bf16[3,512,384]{2,1,0:T(8,128)(2,1)}, u32[]{:S(2)}, u32[]{:S(2)}) collective-permute-start(bf16[3,512,384]{2,1,0:T(8,128)(2,1)} %pad_maximum_fusion.4), channel_id=1, source_target_pairs={{0,2},{1,3},{2,0},{3,1},{4,6},{5,7},{6,4},{7,5},{8,10},{9,11},{10,... | collective-permute-start | bytes 3538952 | tf_op jit(solution)/shard_map/ppermute | solution.py:29
  199.3 27.5 %collective-permute-start.23 = (bf16[3,256,384]{2,1,0:T(8,128)(2,1)}, bf16[3,256,384]{2,1,0:T(8,128)(2,1)S(1)}, u32[]{:S(2)}, u32[]{:S(2)}) collective-permute-start(bf16[3,256,384]{2,1,0:T(8,128)(2,1)} %pad_maximum_fusion.14), channel_id=1, source_target_pairs={{0,16},{4,20},{8,24},{12,28},{16,0},{20,4},{24,8},{28,12},{1,17},{... | collective-permute-start | bytes 1769480 | tf_op jit(solution)/shard_map/ppermute | solution.py:29
  229.5 78.8 %collective-permute-start.35 = (bf16[3,1024,384]{2,1,0:T(8,128)(2,1)S(1)}, bf16[3,1024,384]{2,1,0:T(8,128)(2,1)S(1)}, u32[]{:S(2)}, u32[]{:S(2)}) collective-permute-start(bf16[3,1024,384]{2,1,0:T(8,128)(2,1)S(1)} %constant_dynamic-update-slice_fusion.33.wa), channel_id=1, source_target_pairs={{0,1},{1,0},{2,3},{3,2},{4,5},{5,4},{6,7},{7,6},{8,9},{9,8},{10,11... | collective-permute-start | bytes 7077896 | tf_op jit(solution)/shard_map/ppermute | solution.py:29
  233.8 42.4 %collective-permute-start.33 = (bf16[3,256,384]{2,1,0:T(8,128)(2,1)}, bf16[3,256,384]{2,1,0:T(8,128)(2,1)}, u32[]{:S(2)}, u32[]{:S(2)}) collective-permute-start(bf16[3,256,384]{2,1,0:T(8,128)(2,1)} %slice.877), channel_id=1, source_target_pairs={{0,2},{1,3},{2,0},{3,1},{4,6},{5,7},{6,4},{7,5},{8,10},{9,11},{10,... | collective-permute-start | bytes 1769480 | tf_op jit(solution)/shard_map/ppermute | solution.py:29
  234.8 39.9 %collective-permute-start.25 = (bf16[3,512,384]{2,1,0:T(8,128)(2,1)}, bf16[3,512,384]{2,1,0:T(8,128)(2,1)S(1)}, u32[]{:S(2)}, u32[]{:S(2)}) collective-permute-start(bf16[3,512,384]{2,1,0:T(8,128)(2,1)} %get-tuple-element.111), channel_id=1, source_target_pairs={{0,2},{1,3},{2,0},{3,1},{4,6},{5,7},{6,4},{7,5},{8,10},{9,11},{10,... | collective-permute-start | bytes 3538952 | tf_op jit(solution)/shard_map/ppermute | solution.py:29
  252.1 28.2 %collective-permute-start.28 = (bf16[3,512,384]{2,1,0:T(8,128)(2,1)}, bf16[3,512,384]{2,1,0:T(8,128)(2,1)}, u32[]{:S(2)}, u32[]{:S(2)}) collective-permute-start(bf16[3,512,384]{2,1,0:T(8,128)(2,1)} %get-tuple-element.111), channel_id=1, source_target_pairs={{0,4},{4,0},{8,12},{12,8},{16,20},{20,16},{24,28},{28,24},{1,5},{5... | collective-permute-start | bytes 3538952 | tf_op jit(solution)/shard_map/ppermute | solution.py:29
  253.1 57.2 %collective-permute-start.38 = (bf16[3,1024,384]{2,1,0:T(8,128)(2,1)S(1)}, bf16[3,1024,384]{2,1,0:T(8,128)(2,1)S(1)}, u32[]{:S(2)}, u32[]{:S(2)}) collective-permute-start(bf16[3,1024,384]{2,1,0:T(8,128)(2,1)S(1)} %get-tuple-element.116), channel_id=1, source_target_pairs={{0,1},{1,0},{2,3},{3,2},{4,5},{5,4},{6,7},{7,6},{8,9},{9,8},{10,11... | collective-permute-start | bytes 7077896 | tf_op jit(solution)/shard_map/ppermute | solution.py:29
  274.7 53.5 %collective-permute-start.39 = (bf16[3,1024,384]{2,1,0:T(8,128)(2,1)S(1)}, bf16[3,1024,384]{2,1,0:T(8,128)(2,1)S(1)}, u32[]{:S(2)}, u32[]{:S(2)}) collective-permute-start(bf16[3,1024,384]{2,1,0:T(8,128)(2,1)S(1)} %get-tuple-element.119), channel_id=1, source_target_pairs={{0,1},{1,0},{2,3},{3,2},{4,5},{5,4},{6,7},{7,6},{8,9},{9,8},{10,11... | collective-permute-start | bytes 7077896 | tf_op jit(solution)/shard_map/ppermute | solution.py:29
  280.3 49.2 %collective-permute-start.34 = (bf16[3,1024,384]{2,1,0:T(8,128)(2,1)S(1)}, bf16[3,1024,384]{2,1,0:T(8,128)(2,1)}, u32[]{:S(2)}, u32[]{:S(2)}) collective-permute-start(bf16[3,1024,384]{2,1,0:T(8,128)(2,1)S(1)} %constant_dynamic-update-slice_fusion.30.wa), channel_id=1, source_target_pairs={{0,1},{1,0},{2,3},{3,2},{4,5},{5,4},{6,7},{7,6},{8,9},{9,8},{10,11... | collective-permute-start | bytes 7077896 | tf_op jit(solution)/shard_map/ppermute | solution.py:29
  307.4 62.1 %collective-permute-start.31 = (bf16[3,1024,384]{2,1,0:T(8,128)(2,1)}, bf16[3,1024,384]{2,1,0:T(8,128)(2,1)}, u32[]{:S(2)}, u32[]{:S(2)}) collective-permute-start(bf16[3,1024,384]{2,1,0:T(8,128)(2,1)} %constant_dynamic-update-slice_fusion.27.wa), channel_id=1, source_target_pairs={{0,1},{1,0},{2,3},{3,2},{4,5},{5,4},{6,7},{7,6},{8,9},{9,8},{10,11... | collective-permute-start | bytes 7077896 | tf_op jit(solution)/shard_map/ppermute | solution.py:29
  309.7 82.3 %collective-permute-start.30 = (bf16[3,1024,384]{2,1,0:T(8,128)(2,1)}, bf16[3,1024,384]{2,1,0:T(8,128)(2,1)}, u32[]{:S(2)}, u32[]{:S(2)}) collective-permute-start(bf16[3,1024,384]{2,1,0:T(8,128)(2,1)} %constant_dynamic-update-slice_fusion.24.wa), channel_id=1, source_target_pairs={{0,1},{1,0},{2,3},{3,2},{4,5},{5,4},{6,7},{7,6},{8,9},{9,8},{10,11... | collective-permute-start | bytes 7077896 | tf_op jit(solution)/shard_map/ppermute | solution.py:29
  328.3 41.7 %collective-permute-start.40 = (bf16[3,1024,384]{2,1,0:T(8,128)(2,1)}, bf16[3,1024,384]{2,1,0:T(8,128)(2,1)}, u32[]{:S(2)}, u32[]{:S(2)}) collective-permute-start(bf16[3,1024,384]{2,1,0:T(8,128)(2,1)} %get-tuple-element.122), channel_id=1, source_target_pairs={{0,1},{1,0},{2,3},{3,2},{4,5},{5,4},{6,7},{7,6},{8,9},{9,8},{10,11... | collective-permute-start | bytes 7077896 | tf_op jit(solution)/shard_map/ppermute | solution.py:29
  346.2 43.3 %collective-permute-start.43 = (bf16[3,1024,384]{2,1,0:T(8,128)(2,1)}, bf16[3,1024,384]{2,1,0:T(8,128)(2,1)}, u32[]{:S(2)}, u32[]{:S(2)}) collective-permute-start(bf16[3,1024,384]{2,1,0:T(8,128)(2,1)} %get-tuple-element.126), channel_id=1, source_target_pairs={{0,1},{1,0},{2,3},{3,2},{4,5},{5,4},{6,7},{7,6},{8,9},{9,8},{10,11... | collective-permute-start | bytes 7077896 | tf_op jit(solution)/shard_map/ppermute | solution.py:29
  365.7 42.8 %collective-permute-start.49 = (bf16[3,512,384]{2,1,0:T(8,128)(2,1)S(1)}, bf16[3,512,384]{2,1,0:T(8,128)(2,1)S(1)}, u32[]{:S(2)}, u32[]{:S(2)}) collective-permute-start(bf16[3,512,384]{2,1,0:T(8,128)(2,1)S(1)} %pad_maximum_fusion.6), channel_id=1, source_target_pairs={{0,2},{1,3},{2,0},{3,1},{4,6},{5,7},{6,4},{7,5},{8,10},{9,11},{10,... | collective-permute-start | bytes 3538952 | tf_op jit(solution)/shard_map/ppermute | solution.py:29
  369.5 39.0 %collective-permute-start.48 = (bf16[3,512,384]{2,1,0:T(8,128)(2,1)S(1)}, bf16[3,512,384]{2,1,0:T(8,128)(2,1)S(1)}, u32[]{:S(2)}, u32[]{:S(2)}) collective-permute-start(bf16[3,512,384]{2,1,0:T(8,128)(2,1)S(1)} %pad_maximum_fusion.5), channel_id=1, source_target_pairs={{0,4},{4,0},{8,12},{12,8},{16,20},{20,16},{24,28},{28,24},{1,5},{5... | collective-permute-start | bytes 3538952 | tf_op jit(solution)/shard_map/ppermute | solution.py:29
  389.5 55.7 %collective-permute-start.44 = (bf16[3,1024,384]{2,1,0:T(8,128)(2,1)}, bf16[3,1024,384]{2,1,0:T(8,128)(2,1)}, u32[]{:S(2)}, u32[]{:S(2)}) collective-permute-start(bf16[3,1024,384]{2,1,0:T(8,128)(2,1)} %get-tuple-element.129), channel_id=1, source_target_pairs={{0,1},{1,0},{2,3},{3,2},{4,5},{5,4},{6,7},{7,6},{8,9},{9,8},{10,11... | collective-permute-start | bytes 7077896 | tf_op jit(solution)/shard_map/ppermute | solution.py:29
  408.3 62.7 %collective-permute-start.50 = (bf16[3,1024,384]{2,1,0:T(8,128)(2,1)}, bf16[3,1024,384]{2,1,0:T(8,128)(2,1)}, u32[]{:S(2)}, u32[]{:S(2)}) collective-permute-start(bf16[3,1024,384]{2,1,0:T(8,128)(2,1)} %get-tuple-element.140), channel_id=1, source_target_pairs={{0,1},{1,0},{2,3},{3,2},{4,5},{5,4},{6,7},{7,6},{8,9},{9,8},{10,11... | collective-permute-start | bytes 7077896 | tf_op jit(solution)/shard_map/ppermute | solution.py:29
  411.8 28.7 %collective-permute-start.61 = (bf16[3,256,384]{2,1,0:T(8,128)(2,1)}, bf16[3,256,384]{2,1,0:T(8,128)(2,1)}, u32[]{:S(2)}, u32[]{:S(2)}) collective-permute-start(bf16[3,256,384]{2,1,0:T(8,128)(2,1)} %add_convert_fusion.10), channel_id=1, source_target_pairs={{0,16},{4,20},{8,24},{12,28},{16,0},{20,4},{24,8},{28,12},{1,17},{... | collective-permute-start | bytes 1769480 | tf_op jit(solution)/shard_map/ppermute | solution.py:29
  415.7 27.2 %collective-permute-start.46 = (bf16[3,256,384]{2,1,0:T(8,128)(2,1)}, bf16[3,256,384]{2,1,0:T(8,128)(2,1)}, u32[]{:S(2)}, u32[]{:S(2)}) collective-permute-start(bf16[3,256,384]{2,1,0:T(8,128)(2,1)} %get-tuple-element.184), channel_id=1, source_target_pairs={{0,2},{1,3},{2,0},{3,1},{4,6},{5,7},{6,4},{7,5},{8,10},{9,11},{10,... | collective-permute-start | bytes 1769480 | tf_op jit(solution)/shard_map/ppermute | solution.py:29
  423.0 122.2 %collective-permute-start.64 = (bf16[3,512,384]{2,1,0:T(8,128)(2,1)}, bf16[3,512,384]{2,1,0:T(8,128)(2,1)}, u32[]{:S(2)}, u32[]{:S(2)}) collective-permute-start(bf16[3,512,384]{2,1,0:T(8,128)(2,1)} %pad_maximum_fusion.8), channel_id=1, source_target_pairs={{0,2},{1,3},{2,0},{3,1},{4,6},{5,7},{6,4},{7,5},{8,10},{9,11},{10,... | collective-permute-start | bytes 3538952 | tf_op jit(solution)/shard_map/ppermute | solution.py:29
  463.7 82.3 %collective-permute-start.63 = (bf16[3,512,384]{2,1,0:T(8,128)(2,1)}, bf16[3,512,384]{2,1,0:T(8,128)(2,1)}, u32[]{:S(2)}, u32[]{:S(2)}) collective-permute-start(bf16[3,512,384]{2,1,0:T(8,128)(2,1)} %pad_maximum_fusion.7), channel_id=1, source_target_pairs={{0,4},{4,0},{8,12},{12,8},{16,20},{20,16},{24,28},{28,24},{1,5},{5... | collective-permute-start | bytes 3538952 | tf_op jit(solution)/shard_map/ppermute | solution.py:29
  473.7 31.6 %collective-permute-start.51 = (bf16[3,256,384]{2,1,0:T(8,128)(2,1)}, bf16[3,256,384]{2,1,0:T(8,128)(2,1)S(1)}, u32[]{:S(2)}, u32[]{:S(2)}) collective-permute-start(bf16[3,256,384]{2,1,0:T(8,128)(2,1)} %add_convert_fusion.12), channel_id=1, source_target_pairs={{0,4},{4,0},{8,12},{12,8},{16,20},{20,16},{24,28},{28,24},{1,5},{5... | collective-permute-start | bytes 1769480 | tf_op jit(solution)/shard_map/ppermute | solution.py:29
  540.7 44.2 %collective-permute-start.68 = (bf16[3,512,384]{2,1,0:T(8,128)(2,1)S(1)}, bf16[3,512,384]{2,1,0:T(8,128)(2,1)S(1)}, u32[]{:S(2)}, u32[]{:S(2)}) collective-permute-start(bf16[3,512,384]{2,1,0:T(8,128)(2,1)S(1)} %pad_maximum_fusion.10), channel_id=1, source_target_pairs={{0,2},{1,3},{2,0},{3,1},{4,6},{5,7},{6,4},{7,5},{8,10},{9,11},{10,... | collective-permute-start | bytes 3538952 | tf_op jit(solution)/shard_map/ppermute | solution.py:29
  543.3 36.6 %collective-permute-start.55 = (bf16[4,256,256]{2,1,0:T(8,128)(2,1)S(1)}, bf16[4,256,256]{2,1,0:T(8,128)(2,1)S(1)}, u32[]{:S(2)}, u32[]{:S(2)}) collective-permute-start(bf16[4,256,256]{2,1,0:T(8,128)(2,1)S(1)} %get-tuple-element.192), channel_id=1, source_target_pairs={{0,2},{1,3},{2,0},{3,1},{4,6},{5,7},{6,4},{7,5},{8,10},{9,11},{10,... | collective-permute-start | bytes 1572872 | tf_op jit(solution)/shard_map/ppermute | solution.py:29
  545.1 40.9 %collective-permute-start.67 = (bf16[3,512,384]{2,1,0:T(8,128)(2,1)S(1)}, bf16[3,512,384]{2,1,0:T(8,128)(2,1)S(1)}, u32[]{:S(2)}, u32[]{:S(2)}) collective-permute-start(bf16[3,512,384]{2,1,0:T(8,128)(2,1)S(1)} %pad_maximum_fusion.9), channel_id=1, source_target_pairs={{0,4},{4,0},{8,12},{12,8},{16,20},{20,16},{24,28},{28,24},{1,5},{5... | collective-permute-start | bytes 3538952 | tf_op jit(solution)/shard_map/ppermute | solution.py:29
  546.1 37.8 %collective-permute-start.57 = (bf16[4,256,256]{2,1,0:T(8,128)(2,1)S(1)}, bf16[4,256,256]{2,1,0:T(8,128)(2,1)S(1)}, u32[]{:S(2)}, u32[]{:S(2)}) collective-permute-start(bf16[4,256,256]{2,1,0:T(8,128)(2,1)S(1)} %get-tuple-element.194), channel_id=1, source_target_pairs={{0,4},{4,0},{8,12},{12,8},{16,20},{20,16},{24,28},{28,24},{1,5},{5... | collective-permute-start | bytes 1572872 | tf_op jit(solution)/shard_map/ppermute | solution.py:29
  549.1 38.5 %collective-permute-start.62 = (bf16[3,128,384]{2,1,0:T(8,128)(2,1)S(1)}, bf16[3,128,384]{2,1,0:T(8,128)(2,1)S(1)}, u32[]{:S(2)}, u32[]{:S(2)}) collective-permute-start(bf16[3,128,384]{2,1,0:T(8,128)(2,1)S(1)} %copy-done.94), channel_id=1, source_target_pairs={{0,8},{4,12},{8,0},{12,4},{16,24},{20,28},{24,16},{28,20},{1,9},{5... | collective-permute-start | bytes 884744 | tf_op jit(solution)/shard_map/ppermute | solution.py:29
  579.9 40.0 %collective-permute-start.65 = (bf16[3,256,384]{2,1,0:T(8,128)(2,1)S(1)}, bf16[3,256,384]{2,1,0:T(8,128)(2,1)S(1)}, u32[]{:S(2)}, u32[]{:S(2)}) collective-permute-start(bf16[3,256,384]{2,1,0:T(8,128)(2,1)S(1)} %add_convert_fusion.5), channel_id=1, source_target_pairs={{0,16},{4,20},{8,24},{12,28},{16,0},{20,4},{24,8},{28,12},{1,17},{... | collective-permute-start | bytes 1769480 | tf_op jit(solution)/shard_map/ppermute | solution.py:29
  583.8 52.1 %collective-permute-start.56 = (bf16[4,512,256]{2,1,0:T(8,128)(2,1)S(1)}, bf16[4,512,256]{2,1,0:T(8,128)(2,1)S(1)}, u32[]{:S(2)}, u32[]{:S(2)}) collective-permute-start(bf16[4,512,256]{2,1,0:T(8,128)(2,1)S(1)} %pad_maximum_fusion.12), channel_id=1, source_target_pairs={{0,4},{4,0},{8,12},{12,8},{16,20},{20,16},{24,28},{28,24},{1,5},{5... | collective-permute-start | bytes 3145736 | tf_op jit(solution)/shard_map/ppermute | solution.py:29
  584.9 51.0 %collective-permute-start.58 = (bf16[4,512,256]{2,1,0:T(8,128)(2,1)S(1)}, bf16[4,512,256]{2,1,0:T(8,128)(2,1)S(1)}, u32[]{:S(2)}, u32[]{:S(2)}) collective-permute-start(bf16[4,512,256]{2,1,0:T(8,128)(2,1)S(1)} %pad_maximum_fusion.13), channel_id=1, source_target_pairs={{0,2},{1,3},{2,0},{3,1},{4,6},{5,7},{6,4},{7,5},{8,10},{9,11},{10,... | collective-permute-start | bytes 3145736 | tf_op jit(solution)/shard_map/ppermute | solution.py:29
  587.4 45.2 %collective-permute-start.69 = (bf16[3,256,384]{2,1,0:T(8,128)(2,1)S(1)}, bf16[3,256,384]{2,1,0:T(8,128)(2,1)S(1)}, u32[]{:S(2)}, u32[]{:S(2)}) collective-permute-start(bf16[3,256,384]{2,1,0:T(8,128)(2,1)S(1)} %add_convert_fusion), channel_id=1, source_target_pairs={{0,16},{4,20},{8,24},{12,28},{16,0},{20,4},{24,8},{28,12},{1,17},{... | collective-permute-start | bytes 1769480 | tf_op jit(solution)/shard_map/ppermute | solution.py:29
  589.0 32.3 %collective-permute-start.72 = (f32[5,1024]{1,0:T(8,128)S(1)}, f32[5,1024]{1,0:T(8,128)S(1)}, u32[]{:S(2)}, u32[]{:S(2)}) collective-permute-start(f32[5,1024]{1,0:T(8,128)S(1)} %add.623), channel_id=1, source_target_pairs={{0,2},{1,3},{2,0},{3,1},{4,6},{5,7},{6,4},{7,5},{8,10},{9,11},{10,... | collective-permute-start | bytes 61448 | tf_op jit(solution)/shard_map/ppermute | solution.py:29
  636.3 26.9 %collective-permute-start.59 = (bf16[4,256,256]{2,1,0:T(8,128)(2,1)S(1)}, bf16[4,256,256]{2,1,0:T(8,128)(2,1)S(1)}, u32[]{:S(2)}, u32[]{:S(2)}) collective-permute-start(bf16[4,256,256]{2,1,0:T(8,128)(2,1)S(1)} %add_convert_fusion.21), channel_id=1, source_target_pairs={{0,16},{4,20},{8,24},{12,28},{16,0},{20,4},{24,8},{28,12},{1,17},{... | collective-permute-start | bytes 1572872 | tf_op jit(solution)/shard_map/ppermute | solution.py:29
  (141 other events, 1747.8 us)

commit v4 on v3

--- a/solution.py
+++ b/solution.py
@@ -44,88 +44,45 @@
     )
 
 
-def ordered(value, *others):
-    return lax.optimization_barrier((value, *others))[0]
-
-
-def gather_weights(shards, wide, cut, between):
-    z_bits, t_bits = low_bits()
-    done, corners = {}, []
-
-    def step(name, value, axis, bit):
-        if name in done:
-            value = ordered(value, *done[name])
-        got = swap(value, axis, bit)
-        done[name] = (got,)
-        return got
-
-    results = []
-    for place, own in enumerate(shards):
-        for bit in z_bits:
-            if place >= 2 and bit == z_bits[-1]:
-                own = ordered(own, *corners[place - 2])
-            own = jnp.concatenate([own, step(("z", bit), own, "dp", bit)], wide)
-        for bit in t_bits:
-            own = jnp.concatenate([own, step(("t", bit), own, "tensor", bit)], cut)
-        if place == 1:
-            own = ordered(own, *corners[0])
-        if place == 2:
-            own = ordered(own, result)
-        by_x = step("x", own, "dp", 1)
-        by_y = step("y", own, "tensor", 2)
-        if place == 1:
-            by_x, by_y = ordered(by_x, result), ordered(by_y, result)
-        near = jnp.concatenate([own, by_x], wide)
-        near_core = swap(near, "tensor", 1)
-        far_first, far_second = halves(by_y, wide)[0], halves(by_x, wide)[1]
-        if place == 1:
-            far_first, far_second = ordered(far_first, result), ordered(far_second, result)
-        far_first, far_second = swap(far_first, "dp", 1), swap(far_second, "tensor", 2)
-        corners.append((far_first, far_second))
-        far = jnp.concatenate([by_y, far_first, far_second], wide)
-        far_core = swap(far, "tensor", 1)
-        results.append((near, near_core, far, far_core))
-        if place == 0:
-            result = between(results[0])
-    return results
+def ordered(values, others):
+    values = list(values)
+    return list(lax.optimization_barrier((*values, *others)))[: len(values)]
+
+
+def phase(others, sends):
+    values = ordered([send[0] for send in sends], others)
+    return [swap(value, axis, bit) for value, (_, axis, bit) in zip(values, sends)]
+
+
+def join(parts, axis):
+    return jnp.concatenate(parts, axis)
+
+
+def fold(parts, wide):
+    return functools.reduce(jnp.add, [halves(part, wide)[1].astype(F32) for part in parts]).astype(BF)
 
 
 def plus(left, right):
     return (left.astype(F32) + right.astype(F32)).astype(BF)
 
 
-def scatter_corner(far, far_in, wide):
+def corner_sends(far, far_in, wide):
     far_high, far_in_high = halves(far, wide)[1], halves(far_in, wide)[1]
-    corner = [plus(a, b) for a, b in zip(halves(far_high, wide), halves(far_in_high, wide))]
-    return swap(corner[0], "dp", 1), swap(corner[1], "tensor", 2)
-
-
-def scatter_sides(near, near_in, far, far_in, to_x, to_y, wide):
+    first, second = [plus(a, b) for a, b in zip(halves(far_high, wide), halves(far_in_high, wide))]
+    return [(first, "dp", 1), (second, "tensor", 2)]
+
+
+def side_sends(near, near_in, far, far_in, corner, wide):
+    to_x, to_y = corner
     far_low, far_in_low = halves(far, wide)[0], halves(far_in, wide)[0]
     near_high, near_in_high = halves(near, wide)[1], halves(near_in, wide)[1]
     far_parts = [a.astype(F32) + b.astype(F32) for a, b in zip(halves(far_low, wide), halves(far_in_low, wide))]
     near_parts = [
         a.astype(F32) + b.astype(F32) for a, b in zip(halves(near_high, wide), halves(near_in_high, wide))
     ]
-    by_y = jnp.concatenate(
-        [(far_parts[0] + to_x.astype(F32)).astype(BF), far_parts[1].astype(BF)], wide
-    )
-    by_x = jnp.concatenate(
-        [near_parts[0].astype(BF), (near_parts[1] + to_y.astype(F32)).astype(BF)], wide
-    )
-    return swap(by_x, "dp", 1), swap(by_y, "tensor", 2)
-
-
-def scatter_rest(near, near_in, got_x, got_y, wide, cut):
-    z_bits, t_bits = low_bits()
-    terms = [halves(near, wide)[0], halves(near_in, wide)[0], got_x, got_y]
-    total = None
-    for axis, bits, name in ((cut, t_bits, "tensor"), (wide, z_bits, "dp")):
-        for bit in reversed(bits):
-            parts = [halves(term, axis) for term in terms]
-            give = functools.reduce(jnp.add, [part[1].astype(F32) for part in parts]).astype(BF)
-            terms = [part[0] for part in parts] + [swap(give, name, bit)]
-    return functools.reduce(jnp.add, [term.astype(F32) for term in terms])
+    by_y = join([(far_parts[0] + to_x.astype(F32)).astype(BF), far_parts[1].astype(BF)], wide)
+    by_x = join([near_parts[0].astype(BF), (near_parts[1] + to_y.astype(F32)).astype(BF)], wide)
+    return [(by_x, "dp", 1), (by_y, "tensor", 2)]
 
 
 def rotate_left(values, count):
@@ -537,21 +494,61 @@
     rows, length = tokens.shape[0], segments.shape[1]
     order = dp_index ^ jnp.array([rotate_left(j, dp_size) for j in range(dp_size)], jnp.int32)
 
+    z_bits, t_bits = low_bits()
+    wide, cut = 1, 2
+    ffn_cols = gate_up.shape[2] // PARTS
+    own = [join([mixer_in.astype(BF), mixer_out.T.astype(BF)[None]], 0)]
+    for i in range(PARTS):
+        cols = slice(i * ffn_cols, (i + 1) * ffn_cols)
+        own.append(join([gate_up[:, :, cols].astype(BF), down_proj[cols].T.astype(BF)[None]], 0))
+
+    def deepen(places, others, axis="dp", bit=None, along=wide):
+        got = phase(others, [(own[i], axis, bit) for i in places])
+        for i, part in zip(places, got):
+            own[i] = join([own[i], part], along)
+        return got
+
+    def near_block(i, side):
+        return join([own[i], side[0]], wide)
+
+    def corner_of(side):
+        by_x, by_y = side
+        return [(halves(by_y, wide)[0], "dp", 1), (halves(by_x, wide)[1], "tensor", 2)]
+
+    def far_block(side, corner):
+        return join([side[1], *corner], wide)
+
+    def sides_of(i):
+        return [(own[i], "dp", 1), (own[i], "tensor", 2)]
+
+    def other_core(value):
+        return swap(value, "tensor", 1)
+
+    small = jnp.concatenate([norm_gains, conv_kernel], 0)[:, None, :]
     before = lax.ppermute(
         tokens[rows - HALO :], "tensor", [(i, i + 1) for i in range(t_size - 1)]
     )
-    ffn_cols = gate_up.shape[2] // PARTS
-    shards = [jnp.concatenate([mixer_in.astype(BF), mixer_out.T.astype(BF)[None]], 0)]
-    for i in range(PARTS):
-        cols = slice(i * ffn_cols, (i + 1) * ffn_cols)
-        shards.append(
-            jnp.concatenate([gate_up[:, :, cols].astype(BF), down_proj[cols].T.astype(BF)[None]], 0)
-        )
-
-    small = jnp.concatenate([norm_gains, conv_kernel], 0)[:, None, :]
-    for axis, size_axis in (("tensor", t_size), ("dp", dp_size)):
-        for i in range(size_axis.bit_length() - 1):
-            small = jnp.concatenate([small, swap(small, axis, 1 << i)], 1)
+    small_t = phase([], [(small, "tensor", code) for code in range(1, t_size)])
+    last = []
+    for bit in z_bits[:-1]:
+        last = deepen([0, 1], last, bit=bit)
+    small = join([small, *small_t], 1)
+    small_x = phase([*last, small], [(small, "dp", 1)])
+    later = last
+    last = deepen([0], last, bit=z_bits[-1])
+    for bit in z_bits[:-1]:
+        later = deepen(range(2, PARTS + 1), later, bit=bit)
+    for bit in t_bits:
+        last = deepen([0], last, "tensor", bit, cut)
+    small = join([small, *small_x], 1)
+    small_z = phase([*last, small], [(small, "dp", code) for code in range(2, dp_size, 2)])
+    side = {0: None}
+    side[0] = phase([*last, *later], sides_of(0))
+    last = deepen([1], [*last, *later], bit=z_bits[-1])
+    for bit in t_bits:
+        last = deepen(range(1, PARTS + 1), last, "tensor", bit, cut)
+    small = join([small, *small_z], 1)
+
     small = small.reshape(small.shape[0], dp_size, t_size, small.shape[2])
     for axis, index, size_axis in ((1, dp_index, dp_size), (2, t_index, t_size)):
         for i in range(size_axis.bit_length() - 1):
@@ -560,9 +557,9 @@
             flipped = jnp.flip(split, axis + 1)
             small = jnp.where((index >> i) & 1 == 1, flipped, split).reshape(shape)
     small = small.reshape(small.shape[0], -1)
-    wide = small.shape[1] // dp_size
+    block = small.shape[1] // dp_size
     gains = jnp.concatenate(
-        [lax.dynamic_slice_in_dim(small[:2], order[j] * wide, wide, 1) for j in range(dp_size)], 1
+        [lax.dynamic_slice_in_dim(small[:2], order[j] * block, block, 1) for j in range(dp_size)], 1
     )
     channels = small.shape[1] // t_size
     codes = block_codes(t_size)
@@ -584,67 +581,112 @@
     scale_ext = rms_scale(extended)
     normed_ext = (extended * scale_ext * gains[0]).astype(BF)
     values, scale_one, normed_one = extended[HALO:], scale_ext[HALO:], normed_ext[HALO:]
-    kept = {}
-
-    def mixer_forward(wm):
-        wm_all = jnp.concatenate(wm, 2)
-        win_all, wout_all = wm_all[:3], wm_all[3]
-        projected = mm("td,kdc->ktc", normed_ext, win_all)
-        part_b, part_c, part_x = projected[0], projected[1][HALO:], projected[2]
-        product_ext = part_b * part_x
-        part_b, part_x = part_b[HALO:], part_x[HALO:]
-        product = product_ext[HALO:]
-        convolved = kernel[0] * product
-        for shift in range(1, KW):
-            convolved = convolved + kernel[shift] * masks[shift - 1][:rows] * shift_rows(
-                product_ext, HALO - shift, rows
-            )
-        gated = (part_c * convolved).astype(BF)
-        middle = values + mm("tc,dc->td", gated, wout_all)
-        scale_two = rms_scale(middle)
-        normed_two = (middle * scale_two * gains[1]).astype(BF)
-        kept.update(locals())
-        return normed_two
-
-    _, *wf = gather_weights(shards, 1, 2, mixer_forward)
-    win_all, wout_all, part_b, part_c, part_x = [
-        kept[name] for name in ("win_all", "wout_all", "part_b", "part_c", "part_x")
-    ]
-    product_ext, product, convolved, gated, middle, scale_two, normed_two = [
-        kept[name]
-        for name in ("product_ext", "product", "convolved", "gated", "middle", "scale_two", "normed_two")
-    ]
+    corner = {0: phase([*side[0], *last], corner_of(side[0]))}
+    near = near_block(0, side[0])
+    near_core = other_core(near)
+    later = phase([*side[0], *last], [(own[2], "dp", z_bits[-1])])
+    side[1] = phase(corner[0], sides_of(1))
+    far = far_block(side[0], corner[0])
+    wm = [near, near_core, far, other_core(far)]
+    wm_all = jnp.concatenate(wm, 2)
+    win_all, wout_all = wm_all[:3], wm_all[3]
+    projected = mm("td,kdc->ktc", normed_ext, win_all)
+    part_b, part_c, part_x = projected[0], projected[1][HALO:], projected[2]
+    product_ext = part_b * part_x
+    part_b, part_x = part_b[HALO:], part_x[HALO:]
+    product = product_ext[HALO:]
+    convolved = kernel[0] * product
+    for shift in range(1, KW):
+        convolved = convolved + kernel[shift] * masks[shift - 1][:rows] * shift_rows(
+            product_ext, HALO - shift, rows
+        )
+    gated = (part_c * convolved).astype(BF)
+    middle = values + mm("tc,dc->td", gated, wout_all)
+    scale_two = rms_scale(middle)
+    normed_two = (middle * scale_two * gains[1]).astype(BF)
 
     norm_t, cot_t = normed_two.T, cot.T
-    sums, grads = [], []
-    near_in, far_in, corner, sides = [], [], [], []
-    for i in range(PARTS):
-        near, near_core, far, far_core = wf[i]
-        deps = []
-        if i >= 1:
-            deps.append(near_in[i - 1])
-        if i >= 2:
-            deps += corner[i - 2]
-        g_near, g_near_core, *sums = ffn(normed_two, norm_t, cot, cot_t, near, near_core, sums, deps)
-        near_in.append(swap(g_near_core, "tensor", 1))
-        if i >= 2:
-            sides.append(scatter_sides(*grads[i - 2][:1], near_in[i - 2], grads[i - 2][1], far_in[i - 2], *corner[i - 2], 1))
-        deps = [far_in[i - 1]] if i >= 1 else []
-        g_far, g_far_core, *sums = ffn(normed_two, norm_t, cot, cot_t, far, far_core, sums, deps)
-        far_in.append(swap(g_far_core, "tensor", 1))
-        grads.append((g_near, g_far))
-        if i >= 1:
-            corner.append(scatter_corner(grads[i - 1][1], far_in[i - 1], 1))
-
-    def finish_sides(i):
-        return scatter_sides(grads[i][0], near_in[i], grads[i][1], far_in[i], *corner[i], 1)
-
+    sums = []
+    grads, core_grads, near_in, far_in = {}, {}, {}, {}
+
+    def run(weights, other):
+        nonlocal sums
+        grad, grad_core, *sums = ffn(normed_two, norm_t, cot, cot_t, weights, other, sums, [])
+        return grad, grad_core
+
+    *side[1], later = ordered([*side[1], *later], [normed_two])
+    own[2] = join([own[2], later], wide)
+    last = [own[2]]
+    w_far = {}
+    for i in range(1, PARTS + 1):
+        sends = corner_of(side[i])
+        if i < PARTS:
+            sends += sides_of(i + 1)
+        else:
+            sends += corner_sends(grads[1][1], far_in[1], wide)
+        if i + 2 <= PARTS:
+            sends.append((own[i + 2], "dp", z_bits[-1]))
+        if i > 2:
+            last = [*last, near_in[i - 2]]
+        got = phase(last, sends)
+        near = near_block(i, side[i])
+        near_core = other_core(near)
+        corner[i] = got[:2]
+        if i > 1:
+            g_far, g_far_core = run(*w_far[i - 1])
+            far_in[i - 1] = other_core(g_far_core)
+            grads[i - 1] = (g_near, g_far)
+            corner[i] = ordered(corner[i], [g_far])
+        far = far_block(side[i], corner[i])
+        w_far[i] = (far, other_core(far))
+        (near,) = ordered([near], corner[i])
+        g_near, g_near_core = run(near, near_core)
+        near_in[i] = other_core(g_near_core)
+        rest = ordered(got[2:], [g_near])
+        last = [*corner[i], *rest]
+        if i < PARTS:
+            side[i + 1] = rest[:2]
+        else:
+            back_corner = {1: rest[:2]}
+        if i + 2 <= PARTS:
+            own[i + 2] = join([own[i + 2], rest[2]], wide)
+
+    def back_sides(i):
+        return side_sends(grads[i][0], near_in[i], grads[i][1], far_in[i], back_corner[i], wide)
+
+    def back_corners(i):
+        return corner_sends(grads[i][1], far_in[i], wide)
+
+    got = phase([*last, near_in[PARTS - 1]], back_sides(1) + back_corners(2))
+    g_far, g_far_core = run(*w_far[PARTS])
+    far_in[PARTS] = other_core(g_far_core)
+    grads[PARTS] = (g_near, g_far)
     block_out, middle_grad, mixed_grad, gain_two_grad = middle_back(
-        order, middle, scale_two, gains[1:2], cot, sums[:1], sums[1:], [near_in[-1], *corner[-1]]
-    )
-    corner.append(scatter_corner(grads[-1][1], far_in[-1], 1))
-    while len(sides) < PARTS - 1:
-        sides.append(finish_sides(len(sides)))
+        order, middle, scale_two, gains[1:2], cot, sums[:1], sums[1:], []
+    )
+    back_side = {1: got[:2]}
+    back_corner[2] = got[2:]
+
+    terms = {}
+
+    def last_terms(i):
+        terms[i] = [halves(grads[i][0], wide)[0], halves(near_in[i], wide)[0], *back_side[i]]
+
+    def fold_send(i, axis, bit, along):
+        return (fold(terms[i], along), axis, bit)
+
+    def folded(i, got, along):
+        terms[i] = [halves(term, along)[0] for term in terms[i]] + [got]
+
+    steps = [("tensor", bit, cut) for bit in reversed(t_bits)]
+    steps += [("dp", bit, wide) for bit in reversed(z_bits)]
+
+    def advance(work, others, extra=()):
+        sends = [fold_send(i, *steps[step]) for i, step in work]
+        got = phase(others, [*extra, *sends])
+        for (i, step), value in zip(work, got[len(extra) :]):
+            folded(i, value, steps[step][2])
+        return got
 
     gated_grad = mm("td,dc->tc", mixed_grad, wout_all)
     conv_grad = gated_grad * part_c
@@ -674,25 +716,39 @@
         )
         product_grad = product_grad + kernel[shift] * shift_rows(masked, shift, rows)
     proj_grad = jnp.stack([product_grad * part_x, c_grad, product_grad * part_b], 0).astype(BF)
+    last_terms(1)
+    (proj_grad,) = ordered([proj_grad], got)
+    last = [*got, mixed_grad, near_in[PARTS]]
+    extra = back_sides(2) + back_corners(3)
+    for i in range(4, PARTS + 1):
+        extra += back_corners(i)
+    got = advance([(1, 0)], last, extra)
+    back_side[2], back_corner[3] = got[:2], got[2:4]
+    last_terms(2)
+    last = got
+
     one_t, mixed_t = normed_one.T, mixed_grad.T
-    m_near_core, m_far_core = mixer_grad(
-        one_t, mixed_t, proj_grad, gated, 1, 3, [*sides[0], *corner[-1]]
-    )
-    m_far_in, m_near_in = swap(m_far_core, "tensor", 1), swap(m_near_core, "tensor", 1)
-    sides.append(finish_sides(PARTS - 1))
+    m_near_core, m_far_core = mixer_grad(one_t, mixed_t, proj_grad, gated, 1, 3, [])
+    far_in[0], near_in[0] = other_core(m_far_core), other_core(m_near_core)
     m_near, m_far = mixer_grad(one_t, mixed_t, proj_grad, gated, 0, 2, [])
-    m_corner = scatter_corner(m_far, m_far_in, 1)
-    normed_one_grad = mm("ktc,kdc->td", ordered(proj_grad, m_far), win_all)
+    grads[0] = (m_near, m_far)
+    got = advance([(1, 1), (2, 0)], [*last, m_far], back_sides(3))
+    back_side[3] = got[:2]
+    last_terms(3)
+    back_corner[0] = phase([*last, m_far], back_corners(0))
+    last = [*got, *back_corner[0]]
+
+    (late,) = ordered([proj_grad], [m_far])
+    normed_one_grad = mm("ktc,kdc->td", late, win_all)
     grad_input, gain_one_grad = input_back(
         order, x_ext[HALO:], scale_one, gains[:1], middle_grad, normed_one_grad
     )
-    m_sides = scatter_sides(m_near, m_near_in, m_far, m_far_in, *m_corner, 1)
 
     gain_rel = jnp.concatenate([gain_one_grad, gain_two_grad], 0)
     kernel_rel = jnp.stack(kernel_rows, 0)
     gain_sums = jnp.concatenate(
         [
-            lax.dynamic_slice_in_dim(gain_rel, rotate_right(dp_index ^ q, dp_size) * wide, wide, 1)
+            lax.dynamic_slice_in_dim(gain_rel, rotate_right(dp_index ^ q, dp_size) * block, block, 1)
             for q in range(dp_size)
         ],
         1,
@@ -706,25 +762,40 @@
         ],
         1,
     )
-    sums = ordered(jnp.concatenate([gain_sums, kernel_sums], 0), *m_corner)
-    for axis, size_axis in (("tensor", t_size), ("dp", dp_size)):
-        for i in range(size_axis.bit_length() - 1):
-            sums = sums + swap(sums, axis, 1 << i)
+    total_small = jnp.concatenate([gain_sums, kernel_sums], 0)
+
+    def small_step(value, others, axis, codes):
+        return functools.reduce(jnp.add, [value, *phase(others, [(value, axis, code) for code in codes])])
+
+    stages = len(steps)
+    total_small = small_step(total_small, last, "tensor", range(1, t_size))
+    work = [(1, 2), (2, 1), (3, 0)]
+    got = advance([(i, step) for i, step in work if step < stages], last, back_sides(0))
+    back_side[0] = got[:2]
+    last_terms(0)
+    total_small = small_step(total_small, got, "dp", [1])
+    for late_step in range(stages):
+        work = [(1, 3 + late_step), (2, 2 + late_step), (3, 1 + late_step), (0, late_step)]
+        got = advance([(i, step) for i, step in work if step < stages], got)
+    total_small = small_step(total_small, got[:1], "dp", range(2, dp_size, 2))
     own_width = norm_gains.shape[1]
-    own = lax.dynamic_slice_in_dim(sums, (dp_index * t_size + t_index) * own_width, own_width, 1)
-
-    totals = [
-        scatter_rest(grads[i][0], near_in[i], *sides[i], 1, 2) for i in range(PARTS)
-    ]
+    own_small = lax.dynamic_slice_in_dim(
+        total_small, (dp_index * t_size + t_index) * own_width, own_width, 1
+    )
+
+    def total(i):
+        return functools.reduce(jnp.add, [term.astype(F32) for term in terms[i]])
+
     ffn_new = update(
-        totals, (gate_up, first_gate_up, second_gate_up), (down_proj, first_down_proj, second_down_proj)
-    )
-    total = scatter_rest(m_near, m_near_in, *m_sides, 1, 2)
+        [total(i) for i in range(1, PARTS + 1)],
+        (gate_up, first_gate_up, second_gate_up),
+        (down_proj, first_down_proj, second_down_proj),
+    )
     mix_new = update(
-        [total], (mixer_in, first_mixer_in, second_mixer_in), (mixer_out, first_mixer_out, second_mixer_out)
-    )
-    gains_new = adamw(norm_gains, own[:2], first_norm_gains, second_norm_gains, RATE_SMALL, 0.0)
-    kernel_new = adamw(conv_kernel, own[2:], first_conv_kernel, second_conv_kernel, RATE_SMALL, DECAY)
+        [total(0)], (mixer_in, first_mixer_in, second_mixer_in), (mixer_out, first_mixer_out, second_mixer_out)
+    )
+    gains_new = adamw(norm_gains, own_small[:2], first_norm_gains, second_norm_gains, RATE_SMALL, 0.0)
+    kernel_new = adamw(conv_kernel, own_small[2:], first_conv_kernel, second_conv_kernel, RATE_SMALL, DECAY)
     block_out, grad_input = to_natural(block_out, order), to_natural(grad_input, order)
     return (block_out, grad_input, *mix_new, *ffn_new, *gains_new, *kernel_new)
 

time: 678 us -> 614 us (0.906)
  waiting for transfers between devices: 314 us -> 204 us
  starting transfers between devices: 54.4 us -> 71.5 us
  other arithmetic: 79.8 us -> 95.5 us
  local copies, waits for them, and re-layouts: 80.5 us -> 95.2 us
    ppermute x74 -> x78, waiting for transfers between devices: 314 us -> 204 us  [swap(): return lax.ppermute(values, axis, [(i, i ^ bit) for i in range(size)])]
    unnamed x251 -> x329, local copies, waits for them, and re-layouts: 42.8 us -> 60.9 us
    ppermute x74 -> x78, starting transfers between devices: 51.1 us -> 67.9 us  [swap(): return lax.ppermute(values, axis, [(i, i ^ bit) for i in range(size)])]
    concatenate x25 -> x26, other arithmetic: 20 us -> 32.2 us  [the longest x24 27.9 us: join(): return jnp.concatenate(parts, axis)]
  transfers between devices with their start and end apart: 76 -> 80, of which waited for: 27 -> 24; matrix products, arithmetic and copies ran while one was open for 23% -> 26% of each run, Pallas kernels for 17% -> 18%
where the time goes in v4:
time: 614 us; the launch traced here: 610 us
  waiting for transfers between devices  204 us (33%)
  Pallas kernels  113 us (18%)
  other arithmetic  95.5 us (16%)
  local copies, waits for them, and re-layouts  95.2 us (16%)
  starting transfers between devices  71.5 us (12%)
  matrix products  22.7 us (4%)
  between operations  8.4 us (1%)
    ppermute x78, waiting for transfers between devices, swap(): return lax.ppermute(values, axis, [(i, i ^ bit) for i in range(size)])  204 us
    pallas_call x6, Pallas kernels, ffn(): pl.pallas_call(functools.partial(ffn_kernel, not sums), grid=(cols // til...  87.5 us
    ppermute x78, starting transfers between devices, swap(): return lax.ppermute(values, axis, [(i, i ^ bit) for i in range(size)])  67.9 us
    unnamed x329, local copies, waits for them, and re-layouts  60.9 us
    concatenate x24, other arithmetic, join(): return jnp.concatenate(parts, axis)  27.9 us
    dot_general x4, matrix products, mm(): return jnp.einsum(spec, left, right, preferred_element_type=F32).astype(out)  22.7 us
  transfers between devices with their start and end apart: 80, of which 24 were waited for; matrix products, arithmetic and copies ran while one was open for 26% of the time, Pallas kernels for 18%

profile of v4, /device:TPU:0, one launch (start us, length us, event | category | flops | bytes accessed | tf_op | source)
XLA Modules:
  0.0 610.0 jit_solution(7050616187726289881)
XLA Ops:
  4.2 3.0 collective-permute-start.1
  23.2 3.0 collective-permute-start.3
  34.0 3.8 convert_element_type.481
  41.9 8.1 %collective-permute-done.3 = bf16[4,256,256]{2,1,0:T(8,128)(2,1)} collective-permute-done((bf16[4,256,256]{2,1,0:T(8,128)(2,1)}, bf16[4,256,256]{2,1,0:T(8,128)(2,1)}, u32[]{:S(2)}, u32[]{:S(2)}) %collective-permute-start.3) | collective-permute-done | bytes 524320 | tf_op jit(solution)/shard_map/ppermute | solution.py:29
  51.1 5.6 collective-permute-done.4
  56.8 6.3 %collective-permute-done.5 = bf16[3,128,384]{2,1,0:T(8,128)(2,1)S(1)} collective-permute-done((bf16[3,128,384]{2,1,0:T(8,128)(2,1)S(1)}, bf16[3,128,384]{2,1,0:T(8,128)(2,1)S(1)}, u32[]{:S(2)}, u32[]{:S(2)}) %collective-permute-start.5) | collective-permute-done | bytes 294944 | tf_op jit(solution)/shard_map/ppermute | solution.py:29
  66.0 4.0 collective-permute-start.18
  72.5 3.7 collective-permute-done.19
  76.3 12.0 %collective-permute-done.6 = bf16[4,512,256]{2,1,0:T(8,128)(2,1)S(1)} collective-permute-done((bf16[4,512,256]{2,1,0:T(8,128)(2,1)S(1)}, bf16[4,512,256]{2,1,0:T(8,128)(2,1)S(1)}, u32[]{:S(2)}, u32[]{:S(2)}) %collective-permute-start.6) | collective-permute-done | bytes 1048608 | tf_op jit(solution)/shard_map/ppermute | solution.py:29
  90.7 8.5 %collective-permute-done.9 = bf16[3,256,384]{2,1,0:T(8,128)(2,1)S(1)} collective-permute-done((bf16[3,256,384]{2,1,0:T(8,128)(2,1)S(1)}, bf16[3,256,384]{2,1,0:T(8,128)(2,1)S(1)}, u32[]{:S(2)}, u32[]{:S(2)}) %collective-permute-start.9) | collective-permute-done | bytes 589856 | tf_op jit(solution)/shard_map/ppermute | solution.py:29
  106.2 7.4 %collective-permute-done.10 = bf16[4,256,256]{2,1,0:T(8,128)(2,1)} collective-permute-done((bf16[4,256,256]{2,1,0:T(8,128)(2,1)}, bf16[4,256,256]{2,1,0:T(8,128)(2,1)}, u32[]{:S(2)}, u32[]{:S(2)}) %collective-permute-start.10) | collective-permute-done | bytes 524320 | tf_op jit(solution)/shard_map/ppermute | solution.py:29
  123.6 4.3 pad_maximum_fusion
  127.9 6.5 %convolution_bitcast_fusion = f32[3,784,1024]{2,1,0:T(8,128)S(1)} fusion(bf16[4,1024,1024]{2,1,0:T(8,128)(2,1)S(1)} %pad_maximum_fusion, bf16[784,1024]{0,1:T(8,128)(2,1)S(1)} %multiply_convert_fusion), kind=kOutput, calls=%fused_computation.6 | convolution fusion | flops 4932501504 | bytes 19628032 | tf_op jit(solution)/shard_map/td,kdc->ktc/dot_general | solution.py:137
  135.5 3.1 multiply_convert_fusion.3
  144.9 5.8 collective-permute-done.22
  150.8 4.0 pad_maximum_fusion.2.wa
  167.6 7.4 %collective-permute-done.26 = bf16[3,256,384]{2,1,0:T(8,128)(2,1)} collective-permute-done((bf16[3,256,384]{2,1,0:T(8,128)(2,1)}, bf16[3,256,384]{2,1,0:T(8,128)(2,1)}, u32[]{:S(2)}, u32[]{:S(2)}) %collective-permute-start.26) | collective-permute-done | bytes 589856 | tf_op jit(solution)/shard_map/ppermute | solution.py:29
  190.6 15.4 %ffn.6 = (bf16[3,1024,384]{2,1,0:T(8,128)(2,1)S(1)}, bf16[3,1024,384]{2,1,0:T(8,128)(2,1)}, f32[768,1024]{1,0:T(8,128)S(1)}, f32[768,1024]{1,0:T(8,128)S(1)}) custom-call(bf16[768,1024]{1,0:T(8,128)(2,1)S(1)} %copy-done.45, bf16[1024,768]{1,0:T(8,128)(2,1)S(1)} %copy-done.52, bf16[768,1024]{1,0:T(8,128)(2,1)S(1)} %copy-done.4, ...), custom_call_target="tpu_custom_call" | custom-call | flops 10871635968 | bytes 9437184 | tf_op jit(solution)/shard_map/ffn/pallas_call | solution.py:249
  206.0 6.6 %collective-permute-done.25 = bf16[3,256,384]{2,1,0:T(8,128)(2,1)S(1)} collective-permute-done((bf16[3,256,384]{2,1,0:T(8,128)(2,1)}, bf16[3,256,384]{2,1,0:T(8,128)(2,1)S(1)}, u32[]{:S(2)}, u32[]{:S(2)}) %collective-permute-start.25) | collective-permute-done | bytes 589856 | tf_op jit(solution)/shard_map/ppermute | solution.py:29
  212.7 2.9 pad_maximum_fusion.3.wa
  220.6 14.7 %ffn.7 = (bf16[3,1024,384]{2,1,0:T(8,128)(2,1)S(1)}, bf16[3,1024,384]{2,1,0:T(8,128)(2,1)}, f32[768,1024]{1,0:T(8,128)S(1)}, f32[768,1024]{1,0:T(8,128)S(1)}) custom-call(bf16[768,1024]{1,0:T(8,128)(2,1)S(1)} %copy-done.45, bf16[1024,768]{1,0:T(8,128)(2,1)S(1)} %copy-done.52, ...), custom_call_target="tpu_custom_call", output_to_operand_aliasing={{2}: (6, {}), {3}: (7, {})} | custom-call | flops 10871635968 | bytes 9437184 | tf_op jit(solution)/shard_map/ffn/pallas_call | solution.py:249
  235.3 3.3 constant_dynamic-update-slice_fusion.29
  242.4 13.5 %ffn.8 = (bf16[3,1024,384]{2,1,0:T(8,128)(2,1)S(1)}, bf16[3,1024,384]{2,1,0:T(8,128)(2,1)S(1)}, f32[768,1024]{1,0:T(8,128)S(1)}, f32[768,1024]{1,0:T(8,128)S(1)}) custom-call(bf16[768,1024]{1,0:T(8,128)(2,1)S(1)} %copy-done.45, bf16[1024,768]{1,0:T(8,128)(2,1)S(1)} %copy-done.52, ...), custom_call_target="tpu_custom_call", output_to_operand_aliasing={{2}: (6, {}), {3}: (7, {})} | custom-call | flops 10871635968 | bytes 9437184 | tf_op jit(solution)/shard_map/ffn/pallas_call | solution.py:249
  260.4 8.3 %collective-permute-done.29 = bf16[3,512,384]{2,1,0:T(8,128)(2,1)S(1)} collective-permute-done((bf16[3,512,384]{2,1,0:T(8,128)(2,1)S(1)}, bf16[3,512,384]{2,1,0:T(8,128)(2,1)S(1)}, u32[]{:S(2)}, u32[]{:S(2)}) %collective-permute-start.29) | collective-permute-done | bytes 1179680 | tf_op jit(solution)/shard_map/ppermute | solution.py:29
  269.7 4.1 pad_maximum_fusion.4.wa
  288.6 14.6 %ffn.9 = (bf16[3,1024,384]{2,1,0:T(8,128)(2,1)S(1)}, bf16[3,1024,384]{2,1,0:T(8,128)(2,1)}, f32[768,1024]{1,0:T(8,128)S(1)}, f32[768,1024]{1,0:T(8,128)S(1)}) custom-call(bf16[768,1024]{1,0:T(8,128)(2,1)S(1)} %copy-done.46, bf16[1024,768]{1,0:T(8,128)(2,1)S(1)} %copy-done.53, ...), custom_call_target="tpu_custom_call", output_to_operand_aliasing={{2}: (6, {}), {3}: (7, {})} | custom-call | flops 10871635968 | bytes 9437184 | tf_op jit(solution)/shard_map/ffn/pallas_call | solution.py:249
  310.0 3.5 copy.80.refs_1_
  326.0 15.0 %ffn.10 = (bf16[3,1024,384]{2,1,0:T(8,128)(2,1)S(1)}, bf16[3,1024,384]{2,1,0:T(8,128)(2,1)}, f32[768,1024]{1,0:T(8,128)S(1)}, f32[768,1024]{1,0:T(8,128)S(1)}) custom-call(bf16[768,1024]{1,0:T(8,128)(2,1)S(1)} %copy-done.47, bf16[1024,768]{1,0:T(8,128)(2,1)S(1)} %copy-done.54, ...), custom_call_target="tpu_custom_call", output_to_operand_aliasing={{2}: (6, {}), {3}: (7, {})} | custom-call | flops 10871635968 | bytes 9437184 | tf_op jit(solution)/shard_map/ffn/pallas_call | solution.py:249
  341.1 3.0 add_convert_fusion.16
  348.3 2.8 add_convert_fusion.13
  355.2 14.3 %ffn.11 = (bf16[3,1024,384]{2,1,0:T(8,128)(2,1)S(1)}, bf16[3,1024,384]{2,1,0:T(8,128)(2,1)S(1)}, f32[768,1024]{1,0:T(8,128)S(1)}, f32[768,1024]{1,0:T(8,128)S(1)}) custom-call(bf16[768,1024]{1,0:T(8,128)(2,1)S(1)} %copy-done.48, bf16[1024,768]{1,0:T(8,128)(2,1)S(1)} %copy-done.55, ...), custom_call_target="tpu_custom_call", output_to_operand_aliasing={{2}: (6, {}), {3}: (7, {})} | custom-call | flops 10871635968 | bytes 9437184 | tf_op jit(solution)/shard_map/ffn/pallas_call | solution.py:249
  375.8 4.3 middle_back.1
  382.9 6.5 %fusion.17 = (bf16[1,768,1024]{2,1,0:T(8,128)(2,1)}, f32[768,1024]{1,0:T(8,128)}) fusion(f32[768,1024]{1,0:T(8,128)S(1)} %copy-done.79, f32[3,784,1024]{2,1,0:T(8,128)} %copy-done.73, bf16[768,1024]{1,0:T(8,128)(2,1)S(1)} %get-tuple-element.217, bf16[4,1024,1024]{2,1,0:T(8,128)(2,1)} %copy-done.78), kind=kOutput, calls=%fused_computation.46 | convolution fusion | flops 1612972032 | bytes 14680064 | tf_op jit(solution)/shard_map/td,dc->tc/dot_general | solution.py:137
  403.8 5.1 multiply_reduce_fusion.1
  409.0 3.5 fusion.19
  413.9 4.5 mixer_grad.3
  418.6 4.5 mixer_grad.2
  429.2 7.8 %fusion.11.upstream = f32[768,1024]{1,0:T(8,128)S(1)} fusion(bf16[3,768,1024]{2,1,0:T(8,128)(2,1)S(1)} %pad_maximum_fusion.1.pa.pb, bf16[4,1024,1024]{2,1,0:T(8,128)(2,1)} %copy-done.78), kind=kOutput, calls=%fused_computation.40 | convolution fusion | flops 4831838208 | bytes 14155776 | tf_op jit(solution)/shard_map/ktc,kdc->td/dot_general | solution.py:137
  437.2 4.8 input_back.1
  447.5 24.7 %collective-permute-done.59 = bf16[3,256,384]{2,1,0:T(8,128)(2,1)S(1)} collective-permute-done((bf16[3,256,384]{2,1,0:T(8,128)(2,1)S(1)}, bf16[3,256,384]{2,1,0:T(8,128)(2,1)S(1)}, u32[]{:S(2)}, u32[]{:S(2)}) %collective-permute-start.59) | collective-permute-done | bytes 589856 | tf_op jit(solution)/shard_map/ppermute | solution.py:29
  473.5 10.1 %collective-permute-done.58 = bf16[3,256,384]{2,1,0:T(8,128)(2,1)S(1)} collective-permute-done((bf16[3,256,384]{2,1,0:T(8,128)(2,1)S(1)}, bf16[3,256,384]{2,1,0:T(8,128)(2,1)S(1)}, u32[]{:S(2)}, u32[]{:S(2)}) %collective-permute-start.58) | collective-permute-done | bytes 589856 | tf_op jit(solution)/shard_map/ppermute | solution.py:29
  491.1 9.1 %collective-permute-done.61 = bf16[4,256,256]{2,1,0:T(8,128)(2,1)S(1)} collective-permute-done((bf16[4,256,256]{2,1,0:T(8,128)(2,1)S(1)}, bf16[4,256,256]{2,1,0:T(8,128)(2,1)S(1)}, u32[]{:S(2)}, u32[]{:S(2)}) %collective-permute-start.61) | collective-permute-done | bytes 524320 | tf_op jit(solution)/shard_map/ppermute | solution.py:29
  500.7 3.0 collective-permute-start.65
  503.7 22.9 %collective-permute-done.60 = bf16[4,256,256]{2,1,0:T(8,128)(2,1)S(1)} collective-permute-done((bf16[4,256,256]{2,1,0:T(8,128)(2,1)S(1)}, bf16[4,256,256]{2,1,0:T(8,128)(2,1)S(1)}, u32[]{:S(2)}, u32[]{:S(2)}) %collective-permute-start.60) | collective-permute-done | bytes 524320 | tf_op jit(solution)/shard_map/ppermute | solution.py:29
  533.9 24.1 %collective-permute-done.68 = bf16[3,256,384]{2,1,0:T(8,128)(2,1)S(1)} collective-permute-done((bf16[3,256,384]{2,1,0:T(8,128)(2,1)S(1)}, bf16[3,256,384]{2,1,0:T(8,128)(2,1)S(1)}, u32[]{:S(2)}, u32[]{:S(2)}) %collective-permute-start.68) | collective-permute-done | bytes 589856 | tf_op jit(solution)/shard_map/ppermute | solution.py:29
  560.0 6.9 %collective-permute-done.69 = bf16[3,128,384]{2,1,0:T(8,128)(2,1)S(1)} collective-permute-done((bf16[3,128,384]{2,1,0:T(8,128)(2,1)S(1)}, bf16[3,128,384]{2,1,0:T(8,128)(2,1)S(1)}, u32[]{:S(2)}, u32[]{:S(2)}) %collective-permute-start.69) | collective-permute-done | bytes 294944 | tf_op jit(solution)/shard_map/ppermute | solution.py:29
  572.9 19.2 %collective-permute-done.70 = bf16[4,256,256]{2,1,0:T(8,128)(2,1)S(1)} collective-permute-done((bf16[4,256,256]{2,1,0:T(8,128)(2,1)S(1)}, bf16[4,256,256]{2,1,0:T(8,128)(2,1)S(1)}, u32[]{:S(2)}, u32[]{:S(2)}) %collective-permute-start.70) | collective-permute-done | bytes 524320 | tf_op jit(solution)/shard_map/ppermute | solution.py:29
  593.6 4.3 update.3
  (591 shorter events, 218.0 us)
Async XLA Ops:
  23.2 26.8 %collective-permute-start.3 = (bf16[4,256,256]{2,1,0:T(8,128)(2,1)}, bf16[4,256,256]{2,1,0:T(8,128)(2,1)}, u32[]{:S(2)}, u32[]{:S(2)}) collective-permute-start(bf16[4,256,256]{2,1,0:T(8,128)(2,1)} %pad_maximum_fusion.21), channel_id=1, source_target_pairs={{0,16},{4,20},{8,24},{12,28},{16,0},{20,4},{24,8},{28,12},{1,17},{... | collective-permute-start | bytes 1572872 | tf_op jit(solution)/shard_map/ppermute | solution.py:29
  40.4 24.6 %collective-permute-start.16 = (f32[5,4,32]{2,0,1:T(8,128)S(1)}, f32[5,4,32]{2,0,1:T(8,128)S(1)}, u32[]{:S(2)}, u32[]{:S(2)}) collective-permute-start(f32[5,4,32]{2,0,1:T(8,128)S(1)} %copy-done.142), channel_id=1, source_target_pairs={{0,4},{4,0},{8,12},{12,8},{16,20},{20,16},{24,28},{28,24},{1,5},{5... | collective-permute-start | bytes 7688 | tf_op jit(solution)/shard_map/ppermute | solution.py:29
  63.1 25.3 %collective-permute-start.6 = (bf16[4,512,256]{2,1,0:T(8,128)(2,1)S(1)}, bf16[4,512,256]{2,1,0:T(8,128)(2,1)S(1)}, u32[]{:S(2)}, u32[]{:S(2)}) collective-permute-start(bf16[4,512,256]{2,1,0:T(8,128)(2,1)S(1)} %pad_maximum_fusion.15), channel_id=1, source_target_pairs={{0,4},{4,0},{8,12},{12,8},{16,20},{20,16},{24,28},{28,24},{1,5},{5... | collective-permute-start | bytes 3145736 | tf_op jit(solution)/shard_map/ppermute | solution.py:29
  64.9 24.9 %collective-permute-start.8 = (bf16[4,512,256]{2,1,0:T(8,128)(2,1)S(1)}, bf16[4,512,256]{2,1,0:T(8,128)(2,1)S(1)}, u32[]{:S(2)}, u32[]{:S(2)}) collective-permute-start(bf16[4,512,256]{2,1,0:T(8,128)(2,1)S(1)} %pad_maximum_fusion.15), channel_id=1, source_target_pairs={{0,2},{1,3},{2,0},{3,1},{4,6},{5,7},{6,4},{7,5},{8,10},{9,11},{10,... | collective-permute-start | bytes 3145736 | tf_op jit(solution)/shard_map/ppermute | solution.py:29
  70.4 28.8 %collective-permute-start.9 = (bf16[3,256,384]{2,1,0:T(8,128)(2,1)S(1)}, bf16[3,256,384]{2,1,0:T(8,128)(2,1)S(1)}, u32[]{:S(2)}, u32[]{:S(2)}) collective-permute-start(bf16[3,256,384]{2,1,0:T(8,128)(2,1)S(1)} %pad_maximum_fusion.18), channel_id=1, source_target_pairs={{0,16},{4,20},{8,24},{12,28},{16,0},{20,4},{24,8},{28,12},{1,17},{... | collective-permute-start | bytes 1769480 | tf_op jit(solution)/shard_map/ppermute | solution.py:29
  121.4 29.3 %collective-permute-start.22 = (bf16[3,256,384]{2,1,0:T(8,128)(2,1)S(1)}, bf16[3,256,384]{2,1,0:T(8,128)(2,1)S(1)}, u32[]{:S(2)}, u32[]{:S(2)}) collective-permute-start(bf16[3,256,384]{2,1,0:T(8,128)(2,1)S(1)} %copy-done.126), channel_id=1, source_target_pairs={{0,16},{4,20},{8,24},{12,28},{16,0},{20,4},{24,8},{28,12},{1,17},{... | collective-permute-start | bytes 1769480 | tf_op jit(solution)/shard_map/ppermute | solution.py:29
  121.5 29.3 %collective-permute-start.20 = (bf16[3,512,384]{2,1,0:T(8,128)(2,1)S(1)}, bf16[3,512,384]{2,1,0:T(8,128)(2,1)S(1)}, u32[]{:S(2)}, u32[]{:S(2)}) collective-permute-start(bf16[3,512,384]{2,1,0:T(8,128)(2,1)S(1)} %pad_maximum_fusion.6), channel_id=1, source_target_pairs={{0,4},{4,0},{8,12},{12,8},{16,20},{20,16},{24,28},{28,24},{1,5},{5... | collective-permute-start | bytes 3538952 | tf_op jit(solution)/shard_map/ppermute | solution.py:29
  122.0 28.8 %collective-permute-start.21 = (bf16[3,512,384]{2,1,0:T(8,128)(2,1)S(1)}, bf16[3,512,384]{2,1,0:T(8,128)(2,1)S(1)}, u32[]{:S(2)}, u32[]{:S(2)}) collective-permute-start(bf16[3,512,384]{2,1,0:T(8,128)(2,1)S(1)} %pad_maximum_fusion.6), channel_id=1, source_target_pairs={{0,2},{1,3},{2,0},{3,1},{4,6},{5,7},{6,4},{7,5},{8,10},{9,11},{10,... | collective-permute-start | bytes 3538952 | tf_op jit(solution)/shard_map/ppermute | solution.py:29
  154.7 30.2 %collective-permute-start.28 = (bf16[3,1024,384]{2,1,0:T(8,128)(2,1)}, bf16[3,1024,384]{2,1,0:T(8,128)(2,1)}, u32[]{:S(2)}, u32[]{:S(2)}) collective-permute-start(bf16[3,1024,384]{2,1,0:T(8,128)(2,1)} %pad_maximum_fusion.2.wa), channel_id=1, source_target_pairs={{0,1},{1,0},{2,3},{3,2},{4,5},{5,4},{6,7},{7,6},{8,9},{9,8},{10,11... | collective-permute-start | bytes 7077896 | tf_op jit(solution)/shard_map/ppermute | solution.py:29
  163.7 48.9 %collective-permute-start.23 = (bf16[3,512,384]{2,1,0:T(8,128)(2,1)}, bf16[3,512,384]{2,1,0:T(8,128)(2,1)}, u32[]{:S(2)}, u32[]{:S(2)}) collective-permute-start(bf16[3,512,384]{2,1,0:T(8,128)(2,1)} %pad_maximum_fusion.7), channel_id=1, source_target_pairs={{0,4},{4,0},{8,12},{12,8},{16,20},{20,16},{24,28},{28,24},{1,5},{5... | collective-permute-start | bytes 3538952 | tf_op jit(solution)/shard_map/ppermute | solution.py:29
  164.8 47.8 %collective-permute-start.24 = (bf16[3,512,384]{2,1,0:T(8,128)(2,1)}, bf16[3,512,384]{2,1,0:T(8,128)(2,1)}, u32[]{:S(2)}, u32[]{:S(2)}) collective-permute-start(bf16[3,512,384]{2,1,0:T(8,128)(2,1)} %pad_maximum_fusion.7), channel_id=1, source_target_pairs={{0,2},{1,3},{2,0},{3,1},{4,6},{5,7},{6,4},{7,5},{8,10},{9,11},{10,... | collective-permute-start | bytes 3538952 | tf_op jit(solution)/shard_map/ppermute | solution.py:29
  178.9 41.7 %collective-permute-start.33 = (bf16[3,1024,384]{2,1,0:T(8,128)(2,1)}, bf16[3,1024,384]{2,1,0:T(8,128)(2,1)}, u32[]{:S(2)}, u32[]{:S(2)}) collective-permute-start(bf16[3,1024,384]{2,1,0:T(8,128)(2,1)} %constant_dynamic-update-slice_fusion.24.wa), channel_id=1, source_target_pairs={{0,1},{1,0},{2,3},{3,2},{4,5},{5,4},{6,7},{7,6},{8,9},{9,8},{10,11... | collective-permute-start | bytes 7077896 | tf_op jit(solution)/shard_map/ppermute | solution.py:29
  183.1 29.5 %collective-permute-start.25 = (bf16[3,256,384]{2,1,0:T(8,128)(2,1)}, bf16[3,256,384]{2,1,0:T(8,128)(2,1)S(1)}, u32[]{:S(2)}, u32[]{:S(2)}) collective-permute-start(bf16[3,256,384]{2,1,0:T(8,128)(2,1)} %pad_maximum_fusion.20), channel_id=1, source_target_pairs={{0,16},{4,20},{8,24},{12,28},{16,0},{20,4},{24,8},{28,12},{1,17},{... | collective-permute-start | bytes 1769480 | tf_op jit(solution)/shard_map/ppermute | solution.py:29
  215.5 26.5 %collective-permute-start.34 = (bf16[3,1024,384]{2,1,0:T(8,128)(2,1)S(1)}, bf16[3,1024,384]{2,1,0:T(8,128)(2,1)S(1)}, u32[]{:S(2)}, u32[]{:S(2)}) collective-permute-start(bf16[3,1024,384]{2,1,0:T(8,128)(2,1)S(1)} %pad_maximum_fusion.3.wa), channel_id=1, source_target_pairs={{0,1},{1,0},{2,3},{3,2},{4,5},{5,4},{6,7},{7,6},{8,9},{9,8},{10,11... | collective-permute-start | bytes 7077896 | tf_op jit(solution)/shard_map/ppermute | solution.py:29
  235.3 46.5 %collective-permute-start.35 = (bf16[3,1024,384]{2,1,0:T(8,128)(2,1)}, bf16[3,1024,384]{2,1,0:T(8,128)(2,1)}, u32[]{:S(2)}, u32[]{:S(2)}) collective-permute-start(bf16[3,1024,384]{2,1,0:T(8,128)(2,1)} %get-tuple-element.199), channel_id=1, source_target_pairs={{0,1},{1,0},{2,3},{3,2},{4,5},{5,4},{6,7},{7,6},{8,9},{9,8},{10,11... | collective-permute-start | bytes 7077896 | tf_op jit(solution)/shard_map/ppermute | solution.py:29
  238.6 45.9 %collective-permute-start.36 = (bf16[3,1024,384]{2,1,0:T(8,128)(2,1)}, bf16[3,1024,384]{2,1,0:T(8,128)(2,1)}, u32[]{:S(2)}, u32[]{:S(2)}) collective-permute-start(bf16[3,1024,384]{2,1,0:T(8,128)(2,1)} %get-tuple-element.200), channel_id=1, source_target_pairs={{0,1},{1,0},{2,3},{3,2},{4,5},{5,4},{6,7},{7,6},{8,9},{9,8},{10,11... | collective-permute-start | bytes 7077896 | tf_op jit(solution)/shard_map/ppermute | solution.py:29
  240.4 45.4 %collective-permute-start.39 = (bf16[3,1024,384]{2,1,0:T(8,128)(2,1)}, bf16[3,1024,384]{2,1,0:T(8,128)(2,1)}, u32[]{:S(2)}, u32[]{:S(2)}) collective-permute-start(bf16[3,1024,384]{2,1,0:T(8,128)(2,1)} %constant_dynamic-update-slice_fusion.27.wa), channel_id=1, source_target_pairs={{0,1},{1,0},{2,3},{3,2},{4,5},{5,4},{6,7},{7,6},{8,9},{9,8},{10,11... | collective-permute-start | bytes 7077896 | tf_op jit(solution)/shard_map/ppermute | solution.py:29
  240.9 27.9 %collective-permute-start.29 = (bf16[3,512,384]{2,1,0:T(8,128)(2,1)S(1)}, bf16[3,512,384]{2,1,0:T(8,128)(2,1)S(1)}, u32[]{:S(2)}, u32[]{:S(2)}) collective-permute-start(bf16[3,512,384]{2,1,0:T(8,128)(2,1)S(1)} %pad_maximum_fusion.8), channel_id=1, source_target_pairs={{0,4},{4,0},{8,12},{12,8},{16,20},{20,16},{24,28},{28,24},{1,5},{5... | collective-permute-start | bytes 3538952 | tf_op jit(solution)/shard_map/ppermute | solution.py:29
  242.0 27.7 %collective-permute-start.30 = (bf16[3,512,384]{2,1,0:T(8,128)(2,1)S(1)}, bf16[3,512,384]{2,1,0:T(8,128)(2,1)}, u32[]{:S(2)}, u32[]{:S(2)}) collective-permute-start(bf16[3,512,384]{2,1,0:T(8,128)(2,1)S(1)} %pad_maximum_fusion.8), channel_id=1, source_target_pairs={{0,2},{1,3},{2,0},{3,1},{4,6},{5,7},{6,4},{7,5},{8,10},{9,11},{10,... | collective-permute-start | bytes 3538952 | tf_op jit(solution)/shard_map/ppermute | solution.py:29
  273.8 41.1 %collective-permute-start.41 = (bf16[3,1024,384]{2,1,0:T(8,128)(2,1)}, bf16[3,1024,384]{2,1,0:T(8,128)(2,1)}, u32[]{:S(2)}, u32[]{:S(2)}) collective-permute-start(bf16[3,1024,384]{2,1,0:T(8,128)(2,1)} %pad_maximum_fusion.4.wa), channel_id=1, source_target_pairs={{0,1},{1,0},{2,3},{3,2},{4,5},{5,4},{6,7},{7,6},{8,9},{9,8},{10,11... | collective-permute-start | bytes 7077896 | tf_op jit(solution)/shard_map/ppermute | solution.py:29
  278.9 72.2 %collective-permute-start.46 = (bf16[3,1024,384]{2,1,0:T(8,128)(2,1)}, bf16[3,1024,384]{2,1,0:T(8,128)(2,1)}, u32[]{:S(2)}, u32[]{:S(2)}) collective-permute-start(bf16[3,1024,384]{2,1,0:T(8,128)(2,1)} %copy-done.68), channel_id=1, source_target_pairs={{0,1},{1,0},{2,3},{3,2},{4,5},{5,4},{6,7},{7,6},{8,9},{9,8},{10,11... | collective-permute-start | bytes 7077896 | tf_op jit(solution)/shard_map/ppermute | solution.py:29
  306.5 41.8 %collective-permute-start.45 = (bf16[3,1024,384]{2,1,0:T(8,128)(2,1)}, bf16[3,1024,384]{2,1,0:T(8,128)(2,1)}, u32[]{:S(2)}, u32[]{:S(2)}) collective-permute-start(bf16[3,1024,384]{2,1,0:T(8,128)(2,1)} %get-tuple-element.223), channel_id=1, source_target_pairs={{0,1},{1,0},{2,3},{3,2},{4,5},{5,4},{6,7},{7,6},{8,9},{9,8},{10,11... | collective-permute-start | bytes 7077896 | tf_op jit(solution)/shard_map/ppermute | solution.py:29
  308.4 45.2 %collective-permute-start.40 = (bf16[3,1024,384]{2,1,0:T(8,128)(2,1)}, bf16[3,1024,384]{2,1,0:T(8,128)(2,1)}, u32[]{:S(2)}, u32[]{:S(2)}) collective-permute-start(bf16[3,1024,384]{2,1,0:T(8,128)(2,1)} %constant_dynamic-update-slice_fusion.30.wa), channel_id=1, source_target_pairs={{0,1},{1,0},{2,3},{3,2},{4,5},{5,4},{6,7},{7,6},{8,9},{9,8},{10,11... | collective-permute-start | bytes 7077896 | tf_op jit(solution)/shard_map/ppermute | solution.py:29
  313.7 27.3 %collective-permute-start.43 = (bf16[3,256,384]{2,1,0:T(8,128)(2,1)}, bf16[3,256,384]{2,1,0:T(8,128)(2,1)S(1)}, u32[]{:S(2)}, u32[]{:S(2)}) collective-permute-start(bf16[3,256,384]{2,1,0:T(8,128)(2,1)} %get-tuple-element.218), channel_id=1, source_target_pairs={{0,4},{4,0},{8,12},{12,8},{16,20},{20,16},{24,28},{28,24},{1,5},{5... | collective-permute-start | bytes 1769480 | tf_op jit(solution)/shard_map/ppermute | solution.py:29
  314.9 26.1 %collective-permute-start.44 = (bf16[3,256,384]{2,1,0:T(8,128)(2,1)}, bf16[3,256,384]{2,1,0:T(8,128)(2,1)S(1)}, u32[]{:S(2)}, u32[]{:S(2)}) collective-permute-start(bf16[3,256,384]{2,1,0:T(8,128)(2,1)} %get-tuple-element.219), channel_id=1, source_target_pairs={{0,2},{1,3},{2,0},{3,1},{4,6},{5,7},{6,4},{7,5},{8,10},{9,11},{10,... | collective-permute-start | bytes 1769480 | tf_op jit(solution)/shard_map/ppermute | solution.py:29
  341.1 87.1 %collective-permute-start.54 = (bf16[3,1024,384]{2,1,0:T(8,128)(2,1)}, bf16[3,1024,384]{2,1,0:T(8,128)(2,1)}, u32[]{:S(2)}, u32[]{:S(2)}) collective-permute-start(bf16[3,1024,384]{2,1,0:T(8,128)(2,1)} %get-tuple-element.238), channel_id=1, source_target_pairs={{0,1},{1,0},{2,3},{3,2},{4,5},{5,4},{6,7},{7,6},{8,9},{9,8},{10,11... | collective-permute-start | bytes 7077896 | tf_op jit(solution)/shard_map/ppermute | solution.py:29
  351.1 62.0 %collective-permute-start.47 = (bf16[3,512,384]{2,1,0:T(8,128)(2,1)}, bf16[3,512,384]{2,1,0:T(8,128)(2,1)}, u32[]{:S(2)}, u32[]{:S(2)}) collective-permute-start(bf16[3,512,384]{2,1,0:T(8,128)(2,1)} %pad_maximum_fusion.9), channel_id=1, source_target_pairs={{0,4},{4,0},{8,12},{12,8},{16,20},{20,16},{24,28},{28,24},{1,5},{5... | collective-permute-start | bytes 3538952 | tf_op jit(solution)/shard_map/ppermute | solution.py:29
  352.0 61.1 %collective-permute-start.48 = (bf16[3,512,384]{2,1,0:T(8,128)(2,1)}, bf16[3,512,384]{2,1,0:T(8,128)(2,1)}, u32[]{:S(2)}, u32[]{:S(2)}) collective-permute-start(bf16[3,512,384]{2,1,0:T(8,128)(2,1)} %pad_maximum_fusion.10), channel_id=1, source_target_pairs={{0,2},{1,3},{2,0},{3,1},{4,6},{5,7},{6,4},{7,5},{8,10},{9,11},{10,... | collective-permute-start | bytes 3538952 | tf_op jit(solution)/shard_map/ppermute | solution.py:29
  352.4 40.4 %collective-permute-start.49 = (bf16[3,256,384]{2,1,0:T(8,128)(2,1)}, bf16[3,256,384]{2,1,0:T(8,128)(2,1)}, u32[]{:S(2)}, u32[]{:S(2)}) collective-permute-start(bf16[3,256,384]{2,1,0:T(8,128)(2,1)} %get-tuple-element.227), channel_id=1, source_target_pairs={{0,4},{4,0},{8,12},{12,8},{16,20},{20,16},{24,28},{28,24},{1,5},{5... | collective-permute-start | bytes 1769480 | tf_op jit(solution)/shard_map/ppermute | solution.py:29
  353.5 44.2 %collective-permute-start.50 = (bf16[3,256,384]{2,1,0:T(8,128)(2,1)}, bf16[3,256,384]{2,1,0:T(8,128)(2,1)}, u32[]{:S(2)}, u32[]{:S(2)}) collective-permute-start(bf16[3,256,384]{2,1,0:T(8,128)(2,1)} %get-tuple-element.228), channel_id=1, source_target_pairs={{0,2},{1,3},{2,0},{3,1},{4,6},{5,7},{6,4},{7,5},{8,10},{9,11},{10,... | collective-permute-start | bytes 1769480 | tf_op jit(solution)/shard_map/ppermute | solution.py:29
  397.7 28.1 %collective-permute-start.53 = (bf16[3,1024,384]{2,1,0:T(8,128)(2,1)S(1)}, bf16[3,1024,384]{2,1,0:T(8,128)(2,1)}, u32[]{:S(2)}, u32[]{:S(2)}) collective-permute-start(bf16[3,1024,384]{2,1,0:T(8,128)(2,1)S(1)} %copy-done.70), channel_id=1, source_target_pairs={{0,1},{1,0},{2,3},{3,2},{4,5},{5,4},{6,7},{7,6},{8,9},{9,8},{10,11... | collective-permute-start | bytes 7077896 | tf_op jit(solution)/shard_map/ppermute | solution.py:29
  418.4 25.3 %collective-permute-start.52 = (bf16[4,1024,256]{2,1,0:T(8,128)(2,1)S(1)}, bf16[4,1024,256]{2,1,0:T(8,128)(2,1)S(1)}, u32[]{:S(2)}, u32[]{:S(2)}) collective-permute-start(bf16[4,1024,256]{2,1,0:T(8,128)(2,1)S(1)} %get-tuple-element.235), channel_id=1, source_target_pairs={{0,1},{1,0},{2,3},{3,2},{4,5},{5,4},{6,7},{7,6},{8,9},{9,8},{10,11... | collective-permute-start | bytes 6291464 | tf_op jit(solution)/shard_map/ppermute | solution.py:29
  437.0 63.7 %collective-permute-start.51 = (bf16[4,1024,256]{2,1,0:T(8,128)(2,1)S(1)}, bf16[4,1024,256]{2,1,0:T(8,128)(2,1)S(1)}, u32[]{:S(2)}, u32[]{:S(2)}) collective-permute-start(bf16[4,1024,256]{2,1,0:T(8,128)(2,1)S(1)} %get-tuple-element.234), channel_id=1, source_target_pairs={{0,1},{1,0},{2,3},{3,2},{4,5},{5,4},{6,7},{7,6},{8,9},{9,8},{10,11... | collective-permute-start | bytes 6291464 | tf_op jit(solution)/shard_map/ppermute | solution.py:29
  442.0 43.3 %collective-permute-start.55 = (bf16[3,512,384]{2,1,0:T(8,128)(2,1)S(1)}, bf16[3,512,384]{2,1,0:T(8,128)(2,1)S(1)}, u32[]{:S(2)}, u32[]{:S(2)}) collective-permute-start(bf16[3,512,384]{2,1,0:T(8,128)(2,1)S(1)} %copy-done.125), channel_id=1, source_target_pairs={{0,4},{4,0},{8,12},{12,8},{16,20},{20,16},{24,28},{28,24},{1,5},{5... | collective-permute-start | bytes 3538952 | tf_op jit(solution)/shard_map/ppermute | solution.py:29
  443.2 42.1 %collective-permute-start.56 = (bf16[3,512,384]{2,1,0:T(8,128)(2,1)S(1)}, bf16[3,512,384]{2,1,0:T(8,128)(2,1)S(1)}, u32[]{:S(2)}, u32[]{:S(2)}) collective-permute-start(bf16[3,512,384]{2,1,0:T(8,128)(2,1)S(1)} %copy-done.124), channel_id=1, source_target_pairs={{0,2},{1,3},{2,0},{3,1},{4,6},{5,7},{6,4},{7,5},{8,10},{9,11},{10,... | collective-permute-start | bytes 3538952 | tf_op jit(solution)/shard_map/ppermute | solution.py:29
  443.7 28.5 %collective-permute-start.59 = (bf16[3,256,384]{2,1,0:T(8,128)(2,1)S(1)}, bf16[3,256,384]{2,1,0:T(8,128)(2,1)S(1)}, u32[]{:S(2)}, u32[]{:S(2)}) collective-permute-start(bf16[3,256,384]{2,1,0:T(8,128)(2,1)S(1)} %copy-done.127), channel_id=1, source_target_pairs={{0,16},{4,20},{8,24},{12,28},{16,0},{20,4},{24,8},{28,12},{1,17},{... | collective-permute-start | bytes 1769480 | tf_op jit(solution)/shard_map/ppermute | solution.py:29
  444.2 39.5 %collective-permute-start.58 = (bf16[3,256,384]{2,1,0:T(8,128)(2,1)S(1)}, bf16[3,256,384]{2,1,0:T(8,128)(2,1)S(1)}, u32[]{:S(2)}, u32[]{:S(2)}) collective-permute-start(bf16[3,256,384]{2,1,0:T(8,128)(2,1)S(1)} %get-tuple-element.242), channel_id=1, source_target_pairs={{0,2},{1,3},{2,0},{3,1},{4,6},{5,7},{6,4},{7,5},{8,10},{9,11},{10,... | collective-permute-start | bytes 1769480 | tf_op jit(solution)/shard_map/ppermute | solution.py:29
  488.0 40.3 %collective-permute-start.63 = (bf16[3,512,384]{2,1,0:T(8,128)(2,1)S(1)}, bf16[3,512,384]{2,1,0:T(8,128)(2,1)S(1)}, u32[]{:S(2)}, u32[]{:S(2)}) collective-permute-start(bf16[3,512,384]{2,1,0:T(8,128)(2,1)S(1)} %pad_maximum_fusion.13), channel_id=1, source_target_pairs={{0,4},{4,0},{8,12},{12,8},{16,20},{20,16},{24,28},{28,24},{1,5},{5... | collective-permute-start | bytes 3538952 | tf_op jit(solution)/shard_map/ppermute | solution.py:29
  489.0 39.3 %collective-permute-start.64 = (bf16[3,512,384]{2,1,0:T(8,128)(2,1)S(1)}, bf16[3,512,384]{2,1,0:T(8,128)(2,1)S(1)}, u32[]{:S(2)}, u32[]{:S(2)}) collective-permute-start(bf16[3,512,384]{2,1,0:T(8,128)(2,1)S(1)} %pad_maximum_fusion.14), channel_id=1, source_target_pairs={{0,2},{1,3},{2,0},{3,1},{4,6},{5,7},{6,4},{7,5},{8,10},{9,11},{10,... | collective-permute-start | bytes 3538952 | tf_op jit(solution)/shard_map/ppermute | solution.py:29
  489.8 36.9 %collective-permute-start.60 = (bf16[4,256,256]{2,1,0:T(8,128)(2,1)S(1)}, bf16[4,256,256]{2,1,0:T(8,128)(2,1)S(1)}, u32[]{:S(2)}, u32[]{:S(2)}) collective-permute-start(bf16[4,256,256]{2,1,0:T(8,128)(2,1)S(1)} %get-tuple-element.244), channel_id=1, source_target_pairs={{0,2},{1,3},{2,0},{3,1},{4,6},{5,7},{6,4},{7,5},{8,10},{9,11},{10,... | collective-permute-start | bytes 1572872 | tf_op jit(solution)/shard_map/ppermute | solution.py:29
  500.2 26.9 %collective-permute-start.62 = (bf16[3,256,384]{2,1,0:T(8,128)(2,1)S(1)}, bf16[3,256,384]{2,1,0:T(8,128)(2,1)S(1)}, u32[]{:S(2)}, u32[]{:S(2)}) collective-permute-start(bf16[3,256,384]{2,1,0:T(8,128)(2,1)S(1)} %add_convert_fusion.1), channel_id=1, source_target_pairs={{0,16},{4,20},{8,24},{12,28},{16,0},{20,4},{24,8},{28,12},{1,17},{... | collective-permute-start | bytes 1769480 | tf_op jit(solution)/shard_map/ppermute | solution.py:29
  500.7 29.0 %collective-permute-start.65 = (bf16[3,128,384]{2,1,0:T(8,128)(2,1)S(1)}, bf16[3,128,384]{2,1,0:T(8,128)(2,1)S(1)}, u32[]{:S(2)}, u32[]{:S(2)}) collective-permute-start(bf16[3,128,384]{2,1,0:T(8,128)(2,1)S(1)} %add_convert_fusion.30), channel_id=1, source_target_pairs={{0,8},{4,12},{8,0},{12,4},{16,24},{20,28},{24,16},{28,20},{1,9},{5... | collective-permute-start | bytes 884744 | tf_op jit(solution)/shard_map/ppermute | solution.py:29
  529.7 29.5 %collective-permute-start.66 = (bf16[4,512,256]{2,1,0:T(8,128)(2,1)S(1)}, bf16[4,512,256]{2,1,0:T(8,128)(2,1)S(1)}, u32[]{:S(2)}, u32[]{:S(2)}) collective-permute-start(bf16[4,512,256]{2,1,0:T(8,128)(2,1)S(1)} %pad_maximum_fusion.16), channel_id=1, source_target_pairs={{0,4},{4,0},{8,12},{12,8},{16,20},{20,16},{24,28},{28,24},{1,5},{5... | collective-permute-start | bytes 3145736 | tf_op jit(solution)/shard_map/ppermute | solution.py:29
  531.2 28.6 %collective-permute-start.67 = (bf16[4,512,256]{2,1,0:T(8,128)(2,1)S(1)}, bf16[4,512,256]{2,1,0:T(8,128)(2,1)S(1)}, u32[]{:S(2)}, u32[]{:S(2)}) collective-permute-start(bf16[4,512,256]{2,1,0:T(8,128)(2,1)S(1)} %pad_maximum_fusion.17), channel_id=1, source_target_pairs={{0,2},{1,3},{2,0},{3,1},{4,6},{5,7},{6,4},{7,5},{8,10},{9,11},{10,... | collective-permute-start | bytes 3145736 | tf_op jit(solution)/shard_map/ppermute | solution.py:29
  532.0 26.0 %collective-permute-start.68 = (bf16[3,256,384]{2,1,0:T(8,128)(2,1)S(1)}, bf16[3,256,384]{2,1,0:T(8,128)(2,1)S(1)}, u32[]{:S(2)}, u32[]{:S(2)}) collective-permute-start(bf16[3,256,384]{2,1,0:T(8,128)(2,1)S(1)} %add_convert_fusion), channel_id=1, source_target_pairs={{0,16},{4,20},{8,24},{12,28},{16,0},{20,4},{24,8},{28,12},{1,17},{... | collective-permute-start | bytes 1769480 | tf_op jit(solution)/shard_map/ppermute | solution.py:29
  532.5 36.3 %collective-permute-start.73 = (f32[5,1024]{1,0:T(8,128)S(1)}, f32[5,1024]{1,0:T(8,128)S(1)}, u32[]{:S(2)}, u32[]{:S(2)}) collective-permute-start(f32[5,1024]{1,0:T(8,128)S(1)} %maximum_maximum_fusion.1), channel_id=1, source_target_pairs={{0,1},{1,0},{2,3},{3,2},{4,5},{5,4},{6,7},{7,6},{8,9},{9,8},{10,11... | collective-permute-start | bytes 61448 | tf_op jit(solution)/shard_map/ppermute | solution.py:29
  532.6 36.3 %collective-permute-start.74 = (f32[5,1024]{1,0:T(8,128)S(1)}, f32[5,1024]{1,0:T(8,128)S(1)}, u32[]{:S(2)}, u32[]{:S(2)}) collective-permute-start(f32[5,1024]{1,0:T(8,128)S(1)} %maximum_maximum_fusion.1), channel_id=1, source_target_pairs={{0,2},{1,3},{2,0},{3,1},{4,6},{5,7},{6,4},{7,5},{8,10},{9,11},{10,... | collective-permute-start | bytes 61448 | tf_op jit(solution)/shard_map/ppermute | solution.py:29
  566.9 25.1 %collective-permute-start.70 = (bf16[4,256,256]{2,1,0:T(8,128)(2,1)S(1)}, bf16[4,256,256]{2,1,0:T(8,128)(2,1)S(1)}, u32[]{:S(2)}, u32[]{:S(2)}) collective-permute-start(bf16[4,256,256]{2,1,0:T(8,128)(2,1)S(1)} %add_convert_fusion.21), channel_id=1, source_target_pairs={{0,16},{4,20},{8,24},{12,28},{16,0},{20,4},{24,8},{28,12},{1,17},{... | collective-permute-start | bytes 1572872 | tf_op jit(solution)/shard_map/ppermute | solution.py:29
  (185 other events, 1808.6 us)

commit v5 on v4

--- a/solution.py
+++ b/solution.py
@@ -64,25 +64,6 @@
 
 def plus(left, right):
     return (left.astype(F32) + right.astype(F32)).astype(BF)
-
-
-def corner_sends(far, far_in, wide):
-    far_high, far_in_high = halves(far, wide)[1], halves(far_in, wide)[1]
-    first, second = [plus(a, b) for a, b in zip(halves(far_high, wide), halves(far_in_high, wide))]
-    return [(first, "dp", 1), (second, "tensor", 2)]
-
-
-def side_sends(near, near_in, far, far_in, corner, wide):
-    to_x, to_y = corner
-    far_low, far_in_low = halves(far, wide)[0], halves(far_in, wide)[0]
-    near_high, near_in_high = halves(near, wide)[1], halves(near_in, wide)[1]
-    far_parts = [a.astype(F32) + b.astype(F32) for a, b in zip(halves(far_low, wide), halves(far_in_low, wide))]
-    near_parts = [
-        a.astype(F32) + b.astype(F32) for a, b in zip(halves(near_high, wide), halves(near_in_high, wide))
-    ]
-    by_y = join([(far_parts[0] + to_x.astype(F32)).astype(BF), far_parts[1].astype(BF)], wide)
-    by_x = join([near_parts[0].astype(BF), (near_parts[1] + to_y.astype(F32)).astype(BF)], wide)
-    return [(by_x, "dp", 1), (by_y, "tensor", 2)]
 
 
 def rotate_left(values, count):
@@ -207,24 +188,28 @@
     return jnp.dot(left, right, preferred_element_type=F32)
 
 
-def ffn_kernel(first, h, ht, c, ct, wa, wb, *rest):
-    ga, gb, branch, back, act, dgate, dup = rest[-7:]
-    half = wa.shape[2]
-    wg, wu, wd = [jnp.concatenate([wa[k], wb[k]], 1) for k in range(3)]
+def ffn_kernel(first, h, ht, c, ct, *rest):
+    pieces, rest = rest[:8], rest[8:]
+    grads, (branch, back, w, act, dgate, dup) = rest[-14:-6], rest[-6:]
+    deep, half = pieces[0].shape[1:]
+    spots = [
+        (pl.ds(i % 4 * deep, deep), pl.ds(i // 4 * half, half)) for i in range(8)
+    ]
     rows = h.shape[0]
-    tall = rows // 2
-    if first:
-
-        @pl.when(pl.program_id(0) == 0)
-        def _():
-            branch[...] = jnp.zeros_like(branch)
-            back[...] = jnp.zeros_like(back)
-
+    tall = 384
+
+    @pl.when(pl.program_id(0) == 0)
+    def _():
+        for i, total in enumerate((branch, back)):
+            total[...] = jnp.zeros_like(total) if first else rest[i][...]
+
+    for piece, (deep_span, span) in zip(pieces, spots):
+        w[:, deep_span, span] = piece[...]
     for start in range(0, rows, tall):
         span = pl.ds(start, tall)
-        gate = nn(h[span, :], wg)
-        up = nn(h[span, :], wu)
-        da = nn(c[span, :], wd)
+        gate = nn(h[span, :], w[0])
+        up = nn(h[span, :], w[1])
+        da = nn(c[span, :], w[2])
         sigma = 1.0 / (1.0 + jnp.exp(-gate))
         silu = gate * sigma
         act[span, :] = (silu * up).astype(BF)
@@ -232,28 +217,31 @@
         dgate[span, :] = (da * up * (sigma + silu * (1.0 - sigma))).astype(BF)
     for k, (left, right) in enumerate(((ht, dgate), (ht, dup), (ct, act))):
         grad = nn(left[...], right[...]).astype(BF)
-        ga[k] = grad[:, :half]
-        gb[k] = grad[:, half:]
-    branch[...] += nt(act[...], wd)
-    back[...] += nt(dgate[...], wg) + nt(dup[...], wu)
-
-
-def ffn(h, ht, c, ct, wa, wb, sums, deps):
+        for i, out in enumerate(grads):
+            out[k] = grad[i % 4 * deep : (i % 4 + 1) * deep, i // 4 * half : (i // 4 + 1) * half]
+    for start in range(0, rows, tall):
+        span = pl.ds(start, tall)
+        branch[span, :] += nt(act[span, :], w[2])
+        back[span, :] += nt(dgate[span, :], w[0]) + nt(dup[span, :], w[1])
+
+
+def ffn(h, ht, c, ct, pieces, sums):
     rows, width = h.shape
-    cols = wa.shape[2]
+    planes, deep, cols = pieces[0].shape
     tile = 128
-    block = pl.BlockSpec((3, width, tile), lambda j: (0, 0, j))
+    block = pl.BlockSpec((planes, deep, tile), lambda j: (0, 0, j))
     vmem = pl.BlockSpec(memory_space=pltpu.VMEM)
-    grad = jax.ShapeDtypeStruct(wa.shape, BF)
+    grad = jax.ShapeDtypeStruct(pieces[0].shape, BF)
     part = jax.ShapeDtypeStruct((rows, width), F32)
-    return pl.pallas_call(
+    out = pl.pallas_call(
         functools.partial(ffn_kernel, not sums),
         grid=(cols // tile,),
-        out_shape=(grad, grad, part, part),
-        in_specs=[vmem] * 4 + [block, block] + [vmem] * len(sums) + [ANY] * len(deps),
-        out_specs=(block, block, vmem, vmem),
-        input_output_aliases={6: 2, 7: 3} if sums else {},
-        scratch_shapes=[pltpu.VMEM((rows, 2 * tile), BF)] * 3,
+        out_shape=(grad,) * 8 + (part, part),
+        in_specs=[vmem] * 4 + [block] * 8 + [vmem] * len(sums),
+        out_specs=(block,) * 8 + (vmem, vmem),
+        input_output_aliases={12: 8, 13: 9} if sums else {},
+        scratch_shapes=[pltpu.VMEM((planes, width, 2 * tile), BF)]
+        + [pltpu.VMEM((rows, 2 * tile), BF)] * 3,
         compiler_params=params(),
         cost_estimate=pl.CostEstimate(
             flops=36 * rows * width * cols,
@@ -261,7 +249,8 @@
             transcendentals=2 * rows * cols,
         ),
         name="ffn",
-    )(h, ht, c, ct, wa, wb, *sums, *deps)
+    )(h, ht, c, ct, *pieces, *sums)
+    return out[:8], out[8:]
 
 
 def middle_kernel(order, middle, scale, gain, cot, *rest):
@@ -502,51 +491,55 @@
         cols = slice(i * ffn_cols, (i + 1) * ffn_cols)
         own.append(join([gate_up[:, :, cols].astype(BF), down_proj[cols].T.astype(BF)[None]], 0))
 
-    def deepen(places, others, axis="dp", bit=None, along=wide):
+    def deepen(places, others, axis, bit, along):
         got = phase(others, [(own[i], axis, bit) for i in places])
         for i, part in zip(places, got):
             own[i] = join([own[i], part], along)
         return got
 
-    def near_block(i, side):
-        return join([own[i], side[0]], wide)
-
-    def corner_of(side):
-        by_x, by_y = side
-        return [(halves(by_y, wide)[0], "dp", 1), (halves(by_x, wide)[1], "tensor", 2)]
-
-    def far_block(side, corner):
-        return join([side[1], *corner], wide)
-
-    def sides_of(i):
-        return [(own[i], "dp", 1), (own[i], "tensor", 2)]
+    def first_rows(places, others):
+        for bit in z_bits[:-1]:
+            others = deepen(places, others, "dp", bit, wide)
+        for bit in t_bits:
+            others = deepen(places, others, "tensor", bit, cut)
+        return others
+
+    def by_x(value):
+        return (value, "dp", 1)
+
+    def by_y(value):
+        return (value, "tensor", 2)
+
+    def by_z(value):
+        return (value, "dp", z_bits[-1])
 
     def other_core(value):
         return swap(value, "tensor", 1)
+
+    xa, xb, ya, yb, zb, da, db = ({} for _ in range(7))
+
+    def pieces_of(i):
+        return [own[i], zb[i], xa[i], xb[i], ya[i], yb[i], da[i], db[i]]
 
     small = jnp.concatenate([norm_gains, conv_kernel], 0)[:, None, :]
     before = lax.ppermute(
         tokens[rows - HALO :], "tensor", [(i, i + 1) for i in range(t_size - 1)]
     )
     small_t = phase([], [(small, "tensor", code) for code in range(1, t_size)])
-    last = []
-    for bit in z_bits[:-1]:
-        last = deepen([0, 1], last, bit=bit)
+    last = first_rows([0, 1], [])
     small = join([small, *small_t], 1)
     small_x = phase([*last, small], [(small, "dp", 1)])
-    later = last
-    last = deepen([0], last, bit=z_bits[-1])
-    for bit in z_bits[:-1]:
-        later = deepen(range(2, PARTS + 1), later, bit=bit)
-    for bit in t_bits:
-        last = deepen([0], last, "tensor", bit, cut)
+    xa[0], ya[0], zb[0] = got = phase(last, [by_x(own[0]), by_y(own[0]), by_z(own[0])])
+    later = first_rows(range(2, PARTS + 1), last)
     small = join([small, *small_x], 1)
-    small_z = phase([*last, small], [(small, "dp", code) for code in range(2, dp_size, 2)])
-    side = {0: None}
-    side[0] = phase([*last, *later], sides_of(0))
-    last = deepen([1], [*last, *later], bit=z_bits[-1])
-    for bit in t_bits:
-        last = deepen(range(1, PARTS + 1), last, "tensor", bit, cut)
+    small_z = phase([*got, small], [(small, "dp", code) for code in range(2, dp_size, 2)])
+    xb[0], yb[0], da[0], ya[1], zb[1] = got = phase(
+        got, [by_x(zb[0]), by_y(zb[0]), by_x(ya[0]), by_y(own[1]), by_z(own[1])]
+    )
+    x_ext, cot = arrange(order, tokens, before, cotangent)
+    db[0], xa[1], zb[2], cot_other = phase(
+        [*got[:3], *later], [by_y(xb[0]), by_x(own[1]), by_z(own[2]), (cot, "tensor", 1)]
+    )
     small = join([small, *small_z], 1)
 
     small = small.reshape(small.shape[0], dp_size, t_size, small.shape[2])
@@ -576,18 +569,15 @@
         padded = jnp.concatenate([mask, jnp.zeros((HALO, 1), F32)], 0)
         masks.append(lax.dynamic_slice_in_dim(padded, t_index * rows, rows + HALO, 0))
 
-    x_ext, cot = arrange(order, tokens, before, cotangent)
     extended = x_ext.astype(F32)
     scale_ext = rms_scale(extended)
     normed_ext = (extended * scale_ext * gains[0]).astype(BF)
     values, scale_one, normed_one = extended[HALO:], scale_ext[HALO:], normed_ext[HALO:]
-    corner = {0: phase([*side[0], *last], corner_of(side[0]))}
-    near = near_block(0, side[0])
-    near_core = other_core(near)
-    later = phase([*side[0], *last], [(own[2], "dp", z_bits[-1])])
-    side[1] = phase(corner[0], sides_of(1))
-    far = far_block(side[0], corner[0])
-    wm = [near, near_core, far, other_core(far)]
+    near, far = join(pieces_of(0)[:4], wide), join(pieces_of(0)[4:], wide)
+    wm = [near, other_core(near), far, other_core(far)]
+    got = phase(
+        [db[0], xa[1], zb[1], ya[1]], [by_x(zb[1]), by_y(zb[1]), by_x(ya[1]), by_y(own[2])]
+    )
     wm_all = jnp.concatenate(wm, 2)
     win_all, wout_all = wm_all[:3], wm_all[3]
     projected = mm("td,kdc->ktc", normed_ext, win_all)
@@ -601,94 +591,62 @@
             product_ext, HALO - shift, rows
         )
     gated = (part_c * convolved).astype(BF)
+    (gated,) = ordered([gated], got)
     middle = values + mm("tc,dc->td", gated, wout_all)
     scale_two = rms_scale(middle)
     normed_two = (middle * scale_two * gains[1]).astype(BF)
 
-    norm_t, cot_t = normed_two.T, cot.T
-    sums = []
-    grads, core_grads, near_in, far_in = {}, {}, {}, {}
-
-    def run(weights, other):
+    normed_other = other_core(normed_two)
+    h, c = join([normed_two, normed_other], 0), join([cot, cot_other], 0)
+    ht, ct = h.T, c.T
+    sums, grads = [], {}
+    xb[1], yb[1], da[1], ya[2] = got = ordered(got, [normed_two])
+    (zb[2],) = ordered([zb[2]], [normed_two])
+    db[1], xa[2], zb[3] = phase(got, [by_y(xb[1]), by_x(own[2]), by_z(own[3])])
+
+    def run(i):
         nonlocal sums
-        grad, grad_core, *sums = ffn(normed_two, norm_t, cot, cot_t, weights, other, sums, [])
-        return grad, grad_core
-
-    *side[1], later = ordered([*side[1], *later], [normed_two])
-    own[2] = join([own[2], later], wide)
-    last = [own[2]]
-    w_far = {}
-    for i in range(1, PARTS + 1):
-        sends = corner_of(side[i])
-        if i < PARTS:
-            sends += sides_of(i + 1)
-        else:
-            sends += corner_sends(grads[1][1], far_in[1], wide)
-        if i + 2 <= PARTS:
-            sends.append((own[i + 2], "dp", z_bits[-1]))
-        if i > 2:
-            last = [*last, near_in[i - 2]]
-        got = phase(last, sends)
-        near = near_block(i, side[i])
-        near_core = other_core(near)
-        corner[i] = got[:2]
-        if i > 1:
-            g_far, g_far_core = run(*w_far[i - 1])
-            far_in[i - 1] = other_core(g_far_core)
-            grads[i - 1] = (g_near, g_far)
-            corner[i] = ordered(corner[i], [g_far])
-        far = far_block(side[i], corner[i])
-        w_far[i] = (far, other_core(far))
-        (near,) = ordered([near], corner[i])
-        g_near, g_near_core = run(near, near_core)
-        near_in[i] = other_core(g_near_core)
-        rest = ordered(got[2:], [g_near])
-        last = [*corner[i], *rest]
-        if i < PARTS:
-            side[i + 1] = rest[:2]
-        else:
-            back_corner = {1: rest[:2]}
-        if i + 2 <= PARTS:
-            own[i + 2] = join([own[i + 2], rest[2]], wide)
-
-    def back_sides(i):
-        return side_sends(grads[i][0], near_in[i], grads[i][1], far_in[i], back_corner[i], wide)
-
-    def back_corners(i):
-        return corner_sends(grads[i][1], far_in[i], wide)
-
-    got = phase([*last, near_in[PARTS - 1]], back_sides(1) + back_corners(2))
-    g_far, g_far_core = run(*w_far[PARTS])
-    far_in[PARTS] = other_core(g_far_core)
-    grads[PARTS] = (g_near, g_far)
+        grads[i], sums = ffn(h, ht, c, ct, pieces_of(i), list(sums))
+        return grads[i]
+
+    got = phase([db[1], xa[2], zb[2]], [by_x(zb[2]), by_y(zb[2]), by_x(ya[2]), by_y(own[3])])
+    xb[2], yb[2], da[2], ya[3] = got = ordered(got, run(1)[:1])
+    db[2], xa[3] = got = phase(got, [by_y(xb[2]), by_x(own[3])])
+
+    axa, axb, aya, ayb, ada, adb = ({} for _ in range(6))
+
+    def sum_xb(i):
+        return by_x(plus(grads[i][3], adb[i]))
+
+    def sum_ya(i):
+        return by_y(plus(grads[i][4], ada[i]))
+
+    got = phase([*got, zb[3]], [by_x(zb[3]), by_y(zb[3]), by_x(ya[3]), by_y(grads[1][5])])
+    xb[3], yb[3], da[3], ayb[1] = got = ordered(got, run(2)[:1])
+    db[3], ada[1] = got = phase(got, [by_y(xb[3]), by_x(grads[1][6])])
+    (db[3],) = ordered([db[3]], [ada[1]])
+    got = phase(
+        got, [by_x(grads[1][2]), by_y(grads[1][7]), by_x(grads[2][6]), by_y(grads[2][7])]
+    )
+    axa[1], adb[1], ada[2], adb[2] = got = ordered(got, run(3)[:1])
+    branch, back = ordered(sums, got)
+    branch_in, back_in = [other_core(value[rows:].astype(BF)) for value in (branch, back)]
+    deps = got
+    got = phase(got, [sum_xb(1), sum_ya(1), by_x(grads[2][2]), by_y(grads[2][5])])
     block_out, middle_grad, mixed_grad, gain_two_grad = middle_back(
-        order, middle, scale_two, gains[1:2], cot, sums[:1], sums[1:], []
-    )
-    back_side = {1: got[:2]}
-    back_corner[2] = got[2:]
-
-    terms = {}
-
-    def last_terms(i):
-        terms[i] = [halves(grads[i][0], wide)[0], halves(near_in[i], wide)[0], *back_side[i]]
-
-    def fold_send(i, axis, bit, along):
-        return (fold(terms[i], along), axis, bit)
-
-    def folded(i, got, along):
-        terms[i] = [halves(term, along)[0] for term in terms[i]] + [got]
-
-    steps = [("tensor", bit, cut) for bit in reversed(t_bits)]
-    steps += [("dp", bit, wide) for bit in reversed(z_bits)]
-
-    def advance(work, others, extra=()):
-        sends = [fold_send(i, *steps[step]) for i, step in work]
-        got = phase(others, [*extra, *sends])
-        for (i, step), value in zip(work, got[len(extra) :]):
-            folded(i, value, steps[step][2])
-        return got
+        order, middle, scale_two, gains[1:2], cot, [branch, branch_in], [back, back_in], deps
+    )
 
     gated_grad = mm("td,dc->tc", mixed_grad, wout_all)
+    axb[1], aya[1], axa[2], ayb[2] = got = ordered(got, [gated_grad])
+    (gated_grad,) = ordered([gated_grad], got)
+
+    def sum_b(i):
+        return by_z(functools.reduce(jnp.add, [v.astype(F32) for v in (grads[i][1], axb[i], ayb[i])]).astype(BF))
+
+    got = phase(
+        got, [sum_xb(2), sum_ya(2), by_x(grads[3][6]), by_y(grads[3][7]), sum_b(1)]
+    )
     conv_grad = gated_grad * part_c
     after_rel = lax.ppermute(
         conv_grad[:8], "tensor", [(i + 1, i) for i in range(t_size - 1)]
@@ -716,29 +674,47 @@
         )
         product_grad = product_grad + kernel[shift] * shift_rows(masked, shift, rows)
     proj_grad = jnp.stack([product_grad * part_x, c_grad, product_grad * part_b], 0).astype(BF)
-    last_terms(1)
-    (proj_grad,) = ordered([proj_grad], got)
-    last = [*got, mixed_grad, near_in[PARTS]]
-    extra = back_sides(2) + back_corners(3)
-    for i in range(4, PARTS + 1):
-        extra += back_corners(i)
-    got = advance([(1, 0)], last, extra)
-    back_side[2], back_corner[3] = got[:2], got[2:4]
-    last_terms(2)
-    last = got
-
+    zs = {}
+    axb[2], aya[2], ada[3], adb[3], zs[1] = got = ordered(got, [proj_grad])
     one_t, mixed_t = normed_one.T, mixed_grad.T
+    got = phase(
+        got, [by_x(grads[3][2]), sum_xb(3), by_y(grads[3][5]), sum_ya(3), sum_b(2)]
+    )
     m_near_core, m_far_core = mixer_grad(one_t, mixed_t, proj_grad, gated, 1, 3, [])
-    far_in[0], near_in[0] = other_core(m_far_core), other_core(m_near_core)
-    m_near, m_far = mixer_grad(one_t, mixed_t, proj_grad, gated, 0, 2, [])
-    grads[0] = (m_near, m_far)
-    got = advance([(1, 1), (2, 0)], [*last, m_far], back_sides(3))
-    back_side[3] = got[:2]
-    last_terms(3)
-    back_corner[0] = phase([*last, m_far], back_corners(0))
-    last = [*got, *back_corner[0]]
-
-    (late,) = ordered([proj_grad], [m_far])
+    m_in = [other_core(m_far_core), other_core(m_near_core)]
+    m_near, m_far = mixer_grad(one_t, mixed_t, proj_grad, gated, 0, 2, [axb[2], aya[2], ada[3], adb[3]])
+    axa[3], axb[3], ayb[3], aya[3], zs[2] = got = ordered(got, [m_far])
+    deep = m_near.shape[wide] // 4
+    grads[0] = [
+        plus(
+            lax.slice_in_dim(value, i * deep, (i + 1) * deep, axis=wide),
+            lax.slice_in_dim(other, i * deep, (i + 1) * deep, axis=wide),
+        )
+        for value, other in ((m_near, m_in[1]), (m_far, m_in[0]))
+        for i in range(4)
+    ]
+
+    terms, steps = {}, [("tensor", bit, cut) for bit in reversed(t_bits)]
+    steps += [("dp", bit, wide) for bit in reversed(z_bits[:-1])]
+
+    def sum_a(i):
+        terms[i] = [grads[i][0], axa[i], aya[i], zs[i]]
+
+    def fold_send(i, step):
+        axis, bit, along = steps[step]
+        return (fold(terms[i], along), axis, bit)
+
+    def folded(i, step, got):
+        along = steps[step][2]
+        terms[i] = [halves(term, along)[0] for term in terms[i]] + [got]
+
+    sum_a(1)
+    got = phase(
+        got, [by_x(grads[0][6]), by_x(grads[0][2]), by_y(grads[0][7]), by_y(grads[0][5]), sum_b(3)]
+    )
+    ada[0], axa[0], adb[0], ayb[0], zs[3] = last = got
+
+    (late,) = ordered([proj_grad], grads[0][:1])
     normed_one_grad = mm("ktc,kdc->td", late, win_all)
     grad_input, gain_one_grad = input_back(
         order, x_ext[HALO:], scale_one, gains[:1], middle_grad, normed_one_grad
@@ -767,17 +743,24 @@
     def small_step(value, others, axis, codes):
         return functools.reduce(jnp.add, [value, *phase(others, [(value, axis, code) for code in codes])])
 
-    stages = len(steps)
+    sum_a(2)
+    sum_a(3)
     total_small = small_step(total_small, last, "tensor", range(1, t_size))
-    work = [(1, 2), (2, 1), (3, 0)]
-    got = advance([(i, step) for i, step in work if step < stages], last, back_sides(0))
-    back_side[0] = got[:2]
-    last_terms(0)
-    total_small = small_step(total_small, got, "dp", [1])
-    for late_step in range(stages):
-        work = [(1, 3 + late_step), (2, 2 + late_step), (3, 1 + late_step), (0, late_step)]
-        got = advance([(i, step) for i, step in work if step < stages], got)
-    total_small = small_step(total_small, got[:1], "dp", range(2, dp_size, 2))
+    got = phase(last, [sum_xb(0), sum_ya(0), *[fold_send(i, 0) for i in range(1, PARTS + 1)]])
+    axb[0], aya[0] = got[:2]
+    for i in range(1, PARTS + 1):
+        folded(i, 0, got[i + 1])
+    total_small = small_step(total_small, got[:2], "dp", [1])
+    (zs[0],) = phase(got[:2], [sum_b(0)])
+    for step in range(1, len(steps)):
+        got = phase(got, [fold_send(i, step) for i in range(1, PARTS + 1)])
+        for i in range(1, PARTS + 1):
+            folded(i, step, got[i - 1])
+    sum_a(0)
+    total_small = small_step(total_small, [zs[0]], "dp", range(2, dp_size, 2))
+    for step in range(len(steps)):
+        (got,) = phase([], [fold_send(0, step)])
+        folded(0, step, got)
     own_width = norm_gains.shape[1]
     own_small = lax.dynamic_slice_in_dim(
         total_small, (dp_index * t_size + t_index) * own_width, own_width, 1

time: 614 us -> 607 us (0.989)
  other arithmetic: 95.5 us -> 69.1 us
  starting transfers between devices: 71.5 us -> 92.1 us
  Pallas kernels: 113 us -> 120 us
    concatenate x24 -> x7, other arithmetic: 27.9 us -> 5.49 us  [join(): return jnp.concatenate(parts, axis)]
    ppermute x78 -> x86, starting transfers between devices: 67.9 us -> 89.4 us  [swap(): return lax.ppermute(values, axis, [(i, i ^ bit) for i in range(size)])]
    convert_element_type x8 -> x4, other arithmetic: 13 us -> 4.5 us  [sum_b(): functools.reduce(jnp.add, [v.astype(F32) for v in (grads[i][1], axb[i], a...]
    transpose x1 -> x2, other arithmetic: 1.59 us -> 10.1 us  [local(): ht, ct = (h.T, c.T)]
    convert_element_type x8 -> x4, other arithmetic: 9.6 us -> 2.76 us  [fold(): functools.reduce(jnp.add, [halves(part, wide)[1].astype(F32) for part in...]
    concatenate x6, local copies, waits for them, and re-layouts: 5.61 us -> 12 us  [join(): return jnp.concatenate(parts, axis)]
    pallas_call x6 -> x3, Pallas kernels: 87.5 us -> 93 us  [ffn(): pl.pallas_call(functools.partial(ffn_kernel, not sums), grid=(cols // til...]
    unnamed x329 -> x347, local copies, waits for them, and re-layouts: 60.9 us -> 55.7 us
  transfers between devices with their start and end apart: 80 -> 88, of which waited for: 24 -> 33; matrix products, arithmetic and copies ran while one was open for 26% -> 20% of each run, Pallas kernels for 18% -> 20%
where the time goes in v5:
time: 607 us; the launch traced here: 603 us
  waiting for transfers between devices  203 us (33%)
  Pallas kernels  120 us (20%)
  starting transfers between devices  92.1 us (15%)
  local copies, waits for them, and re-layouts  90.7 us (15%)
  other arithmetic  69.1 us (11%)
  matrix products  19.3 us (3%)
  between operations  8.22 us (1%)
    ppermute x86, waiting for transfers between devices, swap(): return lax.ppermute(values, axis, [(i, i ^ bit) for i in range(size)])  203 us
    pallas_call x3, Pallas kernels, ffn(): pl.pallas_call(functools.partial(ffn_kernel, not sums), grid=(cols // til...  93 us
    ppermute x86, starting transfers between devices, swap(): return lax.ppermute(values, axis, [(i, i ^ bit) for i in range(size)])  89.4 us
    unnamed x347, local copies, waits for them, and re-layouts  55.7 us
    dot_general x4, matrix products, mm(): return jnp.einsum(spec, left, right, preferred_element_type=F32).astype(out)  19.3 us
  transfers between devices with their start and end apart: 88, of which 33 were waited for; matrix products, arithmetic and copies ran while one was open for 20% of the time, Pallas kernels for 20%

profile of v5, /device:TPU:0, one launch (start us, length us, event | category | flops | bytes accessed | tf_op | source)
XLA Modules:
  0.0 602.6 jit_solution(683865075355316854)
XLA Ops:
  4.3 3.0 collective-permute-start.1
  48.5 3.8 collective-permute-done.17
  53.9 8.0 %collective-permute-done.10 = bf16[3,128,384]{2,1,0:T(8,128)(2,1)S(1)} collective-permute-done((bf16[3,128,384]{2,1,0:T(8,128)(2,1)S(1)}, bf16[3,128,384]{2,1,0:T(8,128)(2,1)S(1)}, u32[]{:S(2)}, u32[]{:S(2)}) %collective-permute-start.10) | collective-permute-done | bytes 294944 | tf_op jit(solution)/shard_map/ppermute | solution.py:29
  74.4 3.8 collective-permute-start.20
  81.9 4.6 collective-permute-done.9
  91.7 12.6 %collective-permute-done.12 = bf16[4,256,256]{2,1,0:T(8,128)(2,1)} collective-permute-done((bf16[4,256,256]{2,1,0:T(8,128)(2,1)S(1)}, bf16[4,256,256]{2,1,0:T(8,128)(2,1)}, u32[]{:S(2)}, u32[]{:S(2)}) %collective-permute-start.12) | collective-permute-done | bytes 524320 | tf_op jit(solution)/shard_map/ppermute | solution.py:29
  108.2 3.2 multiply_convert_fusion
  113.3 9.2 %collective-permute-done.23.rest_2_ = bf16[3,256,384]{2,1,0:T(8,128)(2,1)S(1)} collective-permute-done((bf16[3,256,384]{2,1,0:T(8,128)(2,1)S(1)}, bf16[3,256,384]{2,1,0:T(8,128)(2,1)S(1)}, u32[]{:S(2)}, u32[]{:S(2)}) %collective-permute-start.23) | collective-permute-done | bytes 589856 | tf_op jit(solution)/shard_map/ppermute | solution.py:29
  126.5 8.3 %fusion.16 = f32[3,784,1024]{2,1,0:T(8,128)S(1)} fusion(bf16[4,1024,256]{2,1,0:T(8,128)(2,1)} %collective-permute-done.13, bf16[4,1024,256]{2,1,0:T(8,128)(2,1)} %constant_dynamic-update-slice_fusion.5, bf16[4,1024,256]{2,1,0:T(8,128)(2,1)} %collective-permute-done.7, bf16[4,1024,256]{2,1,0:T(8,128)(2,1)} %constant_dynamic-update-slice_fusion, ...), kind=kOutput, calls=%fused_computation.19 | convolution fusion | flops 4966055936 | bytes 19628032 | tf_op jit(solution)/shard_map/td,kdc->ktc/dot_general | solution.py:118
  135.8 2.8 copy-done.89
  138.6 2.9 multiply_convert_fusion.3
  141.5 8.7 %collective-permute-done.26.rest_6_ = bf16[3,256,384]{2,1,0:T(8,128)(2,1)S(1)} collective-permute-done((bf16[3,256,384]{2,1,0:T(8,128)(2,1)}, bf16[3,256,384]{2,1,0:T(8,128)(2,1)S(1)}, u32[]{:S(2)}, u32[]{:S(2)}) %collective-permute-start.26) | collective-permute-done | bytes 589856 | tf_op jit(solution)/shard_map/ppermute | solution.py:29
  165.2 5.0 fusion.60
  170.2 4.6 copy.75.c
  174.8 13.8 %collective-permute-done.31.rest_1_ = bf16[3,256,384]{2,1,0:T(8,128)(2,1)} collective-permute-done((bf16[3,256,384]{2,1,0:T(8,128)(2,1)}, bf16[3,256,384]{2,1,0:T(8,128)(2,1)}, u32[]{:S(2)}, u32[]{:S(2)}) %collective-permute-start.31) | collective-permute-done | bytes 589856 | tf_op jit(solution)/shard_map/ppermute | solution.py:29
  192.7 5.1 fusion.61
  197.8 4.7 copy.74.h
  214.3 29.3 %ffn.3 = (bf16[3,256,384]{2,1,0:T(8,128)(2,1)S(1)}, bf16[3,256,384]{2,1,0:T(8,128)(2,1)S(1)}, bf16[3,256,384]{2,1,0:T(8,128)(2,1)S(1)}, bf16[3,256,384]{2,1,0:T(...) custom-call(bf16[1536,1024]{1,0:T(8,128)(2,1)S(1)} %copy-done.10, ...), custom_call_target="tpu_custom_call" | custom-call | flops 21743271936 | bytes 9437184 | tf_op jit(solution)/shard_map/ffn/pallas_call | solution.py:236
  248.0 12.3 %collective-permute-done.39.rest_7_ = bf16[3,256,384]{2,1,0:T(8,128)(2,1)S(1)} collective-permute-done((bf16[3,256,384]{2,1,0:T(8,128)(2,1)}, bf16[3,256,384]{2,1,0:T(8,128)(2,1)S(1)}, u32[]{:S(2)}, u32[]{:S(2)}) %collective-permute-start.39) | collective-permute-done | bytes 589856 | tf_op jit(solution)/shard_map/ppermute | solution.py:29
  265.2 32.1 %ffn.4 = (bf16[3,256,384]{2,1,0:T(8,128)(2,1)S(1)}, bf16[3,256,384]{2,1,0:T(8,128)(2,1)S(1)}, bf16[3,256,384]{2,1,0:T(8,128)(2,1)S(1)}, bf16[3,256,384]{2,1,0:T(...) custom-call(bf16[1536,1024]{1,0:T(8,128)(2,1)S(1)} %copy-done.10, ...), custom_call_target="tpu_custom_call", output_to_operand_aliasing={{8}: (12, {}), {9}: (13, {})} | custom-call | flops 21743271936 | bytes 9437184 | tf_op jit(solution)/shard_map/ffn/pallas_call | solution.py:236
  303.5 11.3 %collective-permute-done.45 = bf16[3,256,384]{2,1,0:T(8,128)(2,1)S(1)} collective-permute-done((bf16[3,256,384]{2,1,0:T(8,128)(2,1)S(1)}, bf16[3,256,384]{2,1,0:T(8,128)(2,1)S(1)}, u32[]{:S(2)}, u32[]{:S(2)}) %collective-permute-start.45) | collective-permute-done | bytes 589856 | tf_op jit(solution)/shard_map/ppermute | solution.py:29
  319.8 31.7 %ffn.5 = (bf16[3,256,384]{2,1,0:T(8,128)(2,1)S(1)}, bf16[3,256,384]{2,1,0:T(8,128)(2,1)S(1)}, bf16[3,256,384]{2,1,0:T(8,128)(2,1)S(1)}, bf16[3,256,384]{2,1,0:T(...) custom-call(bf16[1536,1024]{1,0:T(8,128)(2,1)S(1)} %copy-done.10, ...), custom_call_target="tpu_custom_call", output_to_operand_aliasing={{8}: (12, {}), {9}: (13, {})} | custom-call | flops 21743271936 | bytes 9437184 | tf_op jit(solution)/shard_map/ffn/pallas_call | solution.py:236
  360.8 3.3 slice.618
  364.6 3.4 slice_bitcast_fusion.6.ht
  368.0 3.5 copy.76.refs_1_
  385.5 2.8 copy-done.5
  388.3 6.4 %middle_back.1 = (bf16[768,1024]{1,0:T(8,128)(2,1)}, f32[768,1024]{1,0:T(8,128)S(1)}, bf16[768,1024]{1,0:T(8,128)(2,1)S(1)}, f32[1,1024]{1,0:T(1,128)S(1)}) custom-call(s32[8]{0:T(128)S(1)} %broadcast_xor_fusion.order.refs_0_, f32[768,1024]{1,0:T(8,128)S(1)} %copy-done.2, f32[768,1]{1,0:T(8,128)S(1)} %rsqrt.21.refs_2_, ...), custom_call_target="tpu_custom_call" | custom-call | flops 23592960 | bytes 23592960 | tf_op jit(solution)/shard_map/middle_back/pallas_call | solution.py:319
  396.5 6.0 collective-permute-done.54
  403.9 4.1 fusion.32
  420.2 2.8 broadcast_multiply_fusion.1
  424.1 4.8 multiply_reduce_fusion.1
  433.1 4.5 mixer_grad.3
  438.2 4.3 collective-permute-done.59.rest_2_
  443.4 3.0 collective-permute-done.61
  450.4 13.5 %collective-permute-done.64 = bf16[3,256,384]{2,1,0:T(8,128)(2,1)S(1)} collective-permute-done((bf16[3,256,384]{2,1,0:T(8,128)(2,1)S(1)}, bf16[3,256,384]{2,1,0:T(8,128)(2,1)S(1)}, u32[]{:S(2)}, u32[]{:S(2)}) %collective-permute-start.64) | collective-permute-done | bytes 589856 | tf_op jit(solution)/shard_map/ppermute | solution.py:29
  464.7 9.6 %collective-permute-done.65 = bf16[3,256,384]{2,1,0:T(8,128)(2,1)S(1)} collective-permute-done((bf16[3,256,384]{2,1,0:T(8,128)(2,1)S(1)}, bf16[3,256,384]{2,1,0:T(8,128)(2,1)S(1)}, u32[]{:S(2)}, u32[]{:S(2)}) %collective-permute-start.65) | collective-permute-done | bytes 589856 | tf_op jit(solution)/shard_map/ppermute | solution.py:29
  474.9 4.5 mixer_grad.2
  479.4 21.5 %collective-permute-done.68 = bf16[3,256,384]{2,1,0:T(8,128)(2,1)S(1)} collective-permute-done((bf16[3,256,384]{2,1,0:T(8,128)(2,1)S(1)}, bf16[3,256,384]{2,1,0:T(8,128)(2,1)S(1)}, u32[]{:S(2)}, u32[]{:S(2)}) %collective-permute-start.68) | collective-permute-done | bytes 589856 | tf_op jit(solution)/shard_map/ppermute | solution.py:29
  507.7 9.0 %collective-permute-done.71 = bf16[4,256,256]{2,1,0:T(8,128)(2,1)S(1)} collective-permute-done((bf16[4,256,256]{2,1,0:T(8,128)(2,1)S(1)}, bf16[4,256,256]{2,1,0:T(8,128)(2,1)S(1)}, u32[]{:S(2)}, u32[]{:S(2)}) %collective-permute-start.71) | collective-permute-done | bytes 524320 | tf_op jit(solution)/shard_map/ppermute | solution.py:29
  519.8 9.6 %collective-permute-done.72 = bf16[3,256,384]{2,1,0:T(8,128)(2,1)S(1)} collective-permute-done((bf16[3,256,384]{2,1,0:T(8,128)(2,1)S(1)}, bf16[3,256,384]{2,1,0:T(8,128)(2,1)S(1)}, u32[]{:S(2)}, u32[]{:S(2)}) %collective-permute-start.72) | collective-permute-done | bytes 589856 | tf_op jit(solution)/shard_map/ppermute | solution.py:29
  536.0 6.3 %collective-permute-done.80 = bf16[3,128,384]{2,1,0:T(8,128)(2,1)} collective-permute-done((bf16[3,128,384]{2,1,0:T(8,128)(2,1)}, bf16[3,128,384]{2,1,0:T(8,128)(2,1)}, u32[]{:S(2)}, u32[]{:S(2)}) %collective-permute-start.80) | collective-permute-done | bytes 294944 | tf_op jit(solution)/shard_map/ppermute | solution.py:29
  546.8 7.3 %fusion.28.upstream = f32[768,1024]{1,0:T(8,128)S(1)} fusion(bf16[3,768,1024]{2,1,0:T(8,128)(2,1)S(1)} %bitcast.128, bf16[4,1024,256]{2,1,0:T(8,128)(2,1)} %collective-permute-done.13, bf16[4,1024,256]{2,1,0:T(8,128)(2,1)S(1)} %copy-done.99, bf16[4,1024,256]{2,1,0:T(8,128)(2,1)} %collective-permute-done.7, ...), kind=kOutput, calls=%fused_computation.53 | convolution fusion | flops 4857004032 | bytes 16252928 | tf_op jit(solution)/shard_map/ktc,kdc->td/dot_general | solution.py:118
  554.2 4.5 input_back.1
  561.3 2.9 collective-permute-start.76
  565.8 4.3 update.3
  570.2 17.4 %collective-permute-done.76 = bf16[4,256,256]{2,1,0:T(8,128)(2,1)S(1)} collective-permute-done((bf16[4,256,256]{2,1,0:T(8,128)(2,1)S(1)}, bf16[4,256,256]{2,1,0:T(8,128)(2,1)S(1)}, u32[]{:S(2)}, u32[]{:S(2)}) %collective-permute-start.76) | collective-permute-done | bytes 524320 | tf_op jit(solution)/shard_map/ppermute | solution.py:29
  587.6 3.2 collective-permute-start.86
  593.2 3.8 collective-permute-done.87
  (601 shorter events, 207.5 us)
Async XLA Ops:
  4.3 30.0 %collective-permute-start.1 = (bf16[4,128,256]{2,1,0:T(8,128)(2,1)}, bf16[4,128,256]{2,1,0:T(8,128)(2,1)}, u32[]{:S(2)}, u32[]{:S(2)}) collective-permute-start(bf16[4,128,256]{2,1,0:T(8,128)(2,1)} %get-tuple-element.190), channel_id=1, source_target_pairs={{0,8},{4,12},{8,0},{12,4},{16,24},{20,28},{24,16},{28,20},{1,9},{5... | collective-permute-start | bytes 786440 | tf_op jit(solution)/shard_map/ppermute | solution.py:29
  7.3 28.0 %collective-permute-start.2 = (bf16[3,128,384]{2,1,0:T(8,128)(2,1)}, bf16[3,128,384]{2,1,0:T(8,128)(2,1)}, u32[]{:S(2)}, u32[]{:S(2)}) collective-permute-start(bf16[3,128,384]{2,1,0:T(8,128)(2,1)} %pad_maximum_fusion.7), channel_id=1, source_target_pairs={{0,8},{4,12},{8,0},{12,4},{16,24},{20,28},{24,16},{28,20},{1,9},{5... | collective-permute-start | bytes 884744 | tf_op jit(solution)/shard_map/ppermute | solution.py:29
  35.3 27.5 %collective-permute-start.3 = (bf16[4,256,256]{2,1,0:T(8,128)(2,1)S(1)}, bf16[4,256,256]{2,1,0:T(8,128)(2,1)S(1)}, u32[]{:S(2)}, u32[]{:S(2)}) collective-permute-start(bf16[4,256,256]{2,1,0:T(8,128)(2,1)S(1)} %pad_maximum_fusion.6), channel_id=1, source_target_pairs={{0,16},{4,20},{8,24},{12,28},{16,0},{20,4},{24,8},{28,12},{1,17},{... | collective-permute-start | bytes 1572872 | tf_op jit(solution)/shard_map/ppermute | solution.py:29
  38.0 24.8 %collective-permute-start.4 = (bf16[4,256,256]{2,1,0:T(8,128)(2,1)S(1)}, bf16[4,256,256]{2,1,0:T(8,128)(2,1)S(1)}, u32[]{:S(2)}, u32[]{:S(2)}) collective-permute-start(bf16[4,256,256]{2,1,0:T(8,128)(2,1)S(1)} %pad_maximum_fusion.6), channel_id=1, source_target_pairs={{0,4},{4,0},{8,12},{12,8},{16,20},{20,16},{24,28},{28,24},{1,5},{5... | collective-permute-start | bytes 1572872 | tf_op jit(solution)/shard_map/ppermute | solution.py:29
  39.5 23.3 %collective-permute-start.5 = (bf16[4,256,256]{2,1,0:T(8,128)(2,1)S(1)}, bf16[4,256,256]{2,1,0:T(8,128)(2,1)S(1)}, u32[]{:S(2)}, u32[]{:S(2)}) collective-permute-start(bf16[4,256,256]{2,1,0:T(8,128)(2,1)S(1)} %pad_maximum_fusion.6), channel_id=1, source_target_pairs={{0,2},{1,3},{2,0},{3,1},{4,6},{5,7},{6,4},{7,5},{8,10},{9,11},{10,... | collective-permute-start | bytes 1572872 | tf_op jit(solution)/shard_map/ppermute | solution.py:29
  52.3 28.8 %collective-permute-start.11 = (bf16[3,128,384]{2,1,0:T(8,128)(2,1)S(1)}, bf16[3,128,384]{2,1,0:T(8,128)(2,1)S(1)}, u32[]{:S(2)}, u32[]{:S(2)}) collective-permute-start(bf16[3,128,384]{2,1,0:T(8,128)(2,1)S(1)} %copy-done.142), channel_id=1, source_target_pairs={{0,8},{4,12},{8,0},{12,4},{16,24},{20,28},{24,16},{28,20},{1,9},{5... | collective-permute-start | bytes 884744 | tf_op jit(solution)/shard_map/ppermute | solution.py:29
  80.1 32.9 %collective-permute-start.21 = (bf16[3,256,384]{2,1,0:T(8,128)(2,1)S(1)}, bf16[3,256,384]{2,1,0:T(8,128)(2,1)}, u32[]{:S(2)}, u32[]{:S(2)}) collective-permute-start(bf16[3,256,384]{2,1,0:T(8,128)(2,1)S(1)} %pad_maximum_fusion.3.rest_0_), channel_id=1, source_target_pairs={{0,16},{4,20},{8,24},{12,28},{16,0},{20,4},{24,8},{28,12},{1,17},{... | collective-permute-start | bytes 1769480 | tf_op jit(solution)/shard_map/ppermute | solution.py:29
  81.1 32.1 %collective-permute-start.22 = (bf16[3,256,384]{2,1,0:T(8,128)(2,1)S(1)}, bf16[3,256,384]{2,1,0:T(8,128)(2,1)}, u32[]{:S(2)}, u32[]{:S(2)}) collective-permute-start(bf16[3,256,384]{2,1,0:T(8,128)(2,1)S(1)} %pad_maximum_fusion.3.rest_0_), channel_id=1, source_target_pairs={{0,2},{1,3},{2,0},{3,1},{4,6},{5,7},{6,4},{7,5},{8,10},{9,11},{10,... | collective-permute-start | bytes 1769480 | tf_op jit(solution)/shard_map/ppermute | solution.py:29
  88.9 36.3 %collective-permute-start.7 = (bf16[4,1024,256]{2,1,0:T(8,128)(2,1)}, bf16[4,1024,256]{2,1,0:T(8,128)(2,1)}, u32[]{:S(2)}, u32[]{:S(2)}) collective-permute-start(bf16[4,1024,256]{2,1,0:T(8,128)(2,1)} %constant_dynamic-update-slice_fusion), channel_id=1, source_target_pairs={{0,1},{1,0},{2,3},{3,2},{4,5},{5,4},{6,7},{7,6},{8,9},{9,8},{10,11... | collective-permute-start | bytes 6291464 | tf_op jit(solution)/shard_map/ppermute | solution.py:29
  113.0 52.2 %collective-permute-start.29 = (bf16[768,1024]{0,1:T(8,128)(2,1)}, bf16[768,1024]{0,1:T(8,128)(2,1)}, u32[]{:S(2)}, u32[]{:S(2)}) collective-permute-start(bf16[768,1024]{0,1:T(8,128)(2,1)} %copy.68), channel_id=1, source_target_pairs={{0,1},{1,0},{2,3},{3,2},{4,5},{5,4},{6,7},{7,6},{8,9},{9,8},{10,11... | collective-permute-start | bytes 4718600 | tf_op jit(solution)/shard_map/ppermute | solution.py:29
  125.2 25.1 %collective-permute-start.26 = (bf16[3,256,384]{2,1,0:T(8,128)(2,1)}, bf16[3,256,384]{2,1,0:T(8,128)(2,1)S(1)}, u32[]{:S(2)}, u32[]{:S(2)}) collective-permute-start(bf16[3,256,384]{2,1,0:T(8,128)(2,1)} %collective-permute-done.22.rest_4_), channel_id=1, source_target_pairs={{0,4},{4,0},{8,12},{12,8},{16,20},{20,16},{24,28},{28,24},{1,5},{5... | collective-permute-start | bytes 1769480 | tf_op jit(solution)/shard_map/ppermute | solution.py:29
  125.7 25.8 %collective-permute-start.27 = (bf16[3,256,384]{2,1,0:T(8,128)(2,1)}, bf16[3,256,384]{2,1,0:T(8,128)(2,1)S(1)}, u32[]{:S(2)}, u32[]{:S(2)}) collective-permute-start(bf16[3,256,384]{2,1,0:T(8,128)(2,1)} %pad_maximum_fusion.4.rest_0_), channel_id=1, source_target_pairs={{0,2},{1,3},{2,0},{3,1},{4,6},{5,7},{6,4},{7,5},{8,10},{9,11},{10,... | collective-permute-start | bytes 1769480 | tf_op jit(solution)/shard_map/ppermute | solution.py:29
  158.1 33.8 %collective-permute-start.28 = (bf16[768,1024]{0,1:T(8,128)(2,1)}, bf16[768,1024]{0,1:T(8,128)(2,1)}, u32[]{:S(2)}, u32[]{:S(2)}) collective-permute-start(bf16[768,1024]{0,1:T(8,128)(2,1)} %multiply_convert_fusion.2), channel_id=1, source_target_pairs={{0,1},{1,0},{2,3},{3,2},{4,5},{5,4},{6,7},{7,6},{8,9},{9,8},{10,11... | collective-permute-start | bytes 4718600 | tf_op jit(solution)/shard_map/ppermute | solution.py:29
  159.0 29.6 %collective-permute-start.31 = (bf16[3,256,384]{2,1,0:T(8,128)(2,1)}, bf16[3,256,384]{2,1,0:T(8,128)(2,1)}, u32[]{:S(2)}, u32[]{:S(2)}) collective-permute-start(bf16[3,256,384]{2,1,0:T(8,128)(2,1)} %pad_maximum_fusion.4.rest_0_), channel_id=1, source_target_pairs={{0,16},{4,20},{8,24},{12,28},{16,0},{20,4},{24,8},{28,12},{1,17},{... | collective-permute-start | bytes 1769480 | tf_op jit(solution)/shard_map/ppermute | solution.py:29
  161.2 27.4 %collective-permute-start.32 = (bf16[3,256,384]{2,1,0:T(8,128)(2,1)}, bf16[3,256,384]{2,1,0:T(8,128)(2,1)}, u32[]{:S(2)}, u32[]{:S(2)}) collective-permute-start(bf16[3,256,384]{2,1,0:T(8,128)(2,1)} %collective-permute-done.24.rest_3_), channel_id=1, source_target_pairs={{0,2},{1,3},{2,0},{3,1},{4,6},{5,7},{6,4},{7,5},{8,10},{9,11},{10,... | collective-permute-start | bytes 1769480 | tf_op jit(solution)/shard_map/ppermute | solution.py:29
  162.9 25.7 %collective-permute-start.33 = (bf16[3,256,384]{2,1,0:T(8,128)(2,1)}, bf16[3,256,384]{2,1,0:T(8,128)(2,1)}, u32[]{:S(2)}, u32[]{:S(2)}) collective-permute-start(bf16[3,256,384]{2,1,0:T(8,128)(2,1)} %pad_maximum_fusion.4.rest_0_), channel_id=1, source_target_pairs={{0,4},{4,0},{8,12},{12,8},{16,20},{20,16},{24,28},{28,24},{1,5},{5... | collective-permute-start | bytes 1769480 | tf_op jit(solution)/shard_map/ppermute | solution.py:29
  188.6 59.4 %collective-permute-start.30 = (bf16[3,256,384]{2,1,0:T(8,128)(2,1)}, bf16[3,256,384]{2,1,0:T(8,128)(2,1)}, u32[]{:S(2)}, u32[]{:S(2)}) collective-permute-start(bf16[3,256,384]{2,1,0:T(8,128)(2,1)} %pad_maximum_fusion.5.rest_0_), channel_id=1, source_target_pairs={{0,16},{4,20},{8,24},{12,28},{16,0},{20,4},{24,8},{28,12},{1,17},{... | collective-permute-start | bytes 1769480 | tf_op jit(solution)/shard_map/ppermute | solution.py:29
  188.6 57.6 %collective-permute-start.34 = (bf16[3,256,384]{2,1,0:T(8,128)(2,1)}, bf16[3,256,384]{2,1,0:T(8,128)(2,1)}, u32[]{:S(2)}, u32[]{:S(2)}) collective-permute-start(bf16[3,256,384]{2,1,0:T(8,128)(2,1)} %collective-permute-done.31.rest_1_), channel_id=1, source_target_pairs={{0,4},{4,0},{8,12},{12,8},{16,20},{20,16},{24,28},{28,24},{1,5},{5... | collective-permute-start | bytes 1769480 | tf_op jit(solution)/shard_map/ppermute | solution.py:29
  189.2 57.0 %collective-permute-start.35 = (bf16[3,256,384]{2,1,0:T(8,128)(2,1)}, bf16[3,256,384]{2,1,0:T(8,128)(2,1)}, u32[]{:S(2)}, u32[]{:S(2)}) collective-permute-start(bf16[3,256,384]{2,1,0:T(8,128)(2,1)} %collective-permute-done.31.rest_1_), channel_id=1, source_target_pairs={{0,2},{1,3},{2,0},{3,1},{4,6},{5,7},{6,4},{7,5},{8,10},{9,11},{10,... | collective-permute-start | bytes 1769480 | tf_op jit(solution)/shard_map/ppermute | solution.py:29
  190.4 55.8 %collective-permute-start.36 = (bf16[3,256,384]{2,1,0:T(8,128)(2,1)}, bf16[3,256,384]{2,1,0:T(8,128)(2,1)}, u32[]{:S(2)}, u32[]{:S(2)}) collective-permute-start(bf16[3,256,384]{2,1,0:T(8,128)(2,1)} %copy-done.79), channel_id=1, source_target_pairs={{0,4},{4,0},{8,12},{12,8},{16,20},{20,16},{24,28},{28,24},{1,5},{5... | collective-permute-start | bytes 1769480 | tf_op jit(solution)/shard_map/ppermute | solution.py:29
  192.0 54.2 %collective-permute-start.37 = (bf16[3,256,384]{2,1,0:T(8,128)(2,1)}, bf16[3,256,384]{2,1,0:T(8,128)(2,1)}, u32[]{:S(2)}, u32[]{:S(2)}) collective-permute-start(bf16[3,256,384]{2,1,0:T(8,128)(2,1)} %pad_maximum_fusion.5.rest_0_), channel_id=1, source_target_pairs={{0,2},{1,3},{2,0},{3,1},{4,6},{5,7},{6,4},{7,5},{8,10},{9,11},{10,... | collective-permute-start | bytes 1769480 | tf_op jit(solution)/shard_map/ppermute | solution.py:29
  261.1 41.0 %collective-permute-start.40 = (bf16[3,256,384]{2,1,0:T(8,128)(2,1)}, bf16[3,256,384]{2,1,0:T(8,128)(2,1)S(1)}, u32[]{:S(2)}, u32[]{:S(2)}) collective-permute-start(bf16[3,256,384]{2,1,0:T(8,128)(2,1)} %collective-permute-done.30.rest_1_), channel_id=1, source_target_pairs={{0,4},{4,0},{8,12},{12,8},{16,20},{20,16},{24,28},{28,24},{1,5},{5... | collective-permute-start | bytes 1769480 | tf_op jit(solution)/shard_map/ppermute | solution.py:29
  261.6 40.6 %collective-permute-start.41 = (bf16[3,256,384]{2,1,0:T(8,128)(2,1)}, bf16[3,256,384]{2,1,0:T(8,128)(2,1)S(1)}, u32[]{:S(2)}, u32[]{:S(2)}) collective-permute-start(bf16[3,256,384]{2,1,0:T(8,128)(2,1)} %collective-permute-done.30.rest_1_), channel_id=1, source_target_pairs={{0,2},{1,3},{2,0},{3,1},{4,6},{5,7},{6,4},{7,5},{8,10},{9,11},{10,... | collective-permute-start | bytes 1769480 | tf_op jit(solution)/shard_map/ppermute | solution.py:29
  262.4 39.7 %collective-permute-start.42 = (bf16[3,256,384]{2,1,0:T(8,128)(2,1)}, bf16[3,256,384]{2,1,0:T(8,128)(2,1)S(1)}, u32[]{:S(2)}, u32[]{:S(2)}) collective-permute-start(bf16[3,256,384]{2,1,0:T(8,128)(2,1)} %collective-permute-done.37.rest_4_), channel_id=1, source_target_pairs={{0,4},{4,0},{8,12},{12,8},{16,20},{20,16},{24,28},{28,24},{1,5},{5... | collective-permute-start | bytes 1769480 | tf_op jit(solution)/shard_map/ppermute | solution.py:29
  263.9 38.3 %collective-permute-start.43 = (bf16[3,256,384]{2,1,0:T(8,128)(2,1)S(1)}, bf16[3,256,384]{2,1,0:T(8,128)(2,1)S(1)}, u32[]{:S(2)}, u32[]{:S(2)}) collective-permute-start(bf16[3,256,384]{2,1,0:T(8,128)(2,1)S(1)} %get-tuple-element.242), channel_id=1, source_target_pairs={{0,2},{1,3},{2,0},{3,1},{4,6},{5,7},{6,4},{7,5},{8,10},{9,11},{10,... | collective-permute-start | bytes 1769480 | tf_op jit(solution)/shard_map/ppermute | solution.py:29
  315.7 42.3 %collective-permute-start.46 = (bf16[3,256,384]{2,1,0:T(8,128)(2,1)S(1)}, bf16[3,256,384]{2,1,0:T(8,128)(2,1)S(1)}, u32[]{:S(2)}, u32[]{:S(2)}) collective-permute-start(bf16[3,256,384]{2,1,0:T(8,128)(2,1)S(1)} %get-tuple-element.262), channel_id=1, source_target_pairs={{0,4},{4,0},{8,12},{12,8},{16,20},{20,16},{24,28},{28,24},{1,5},{5... | collective-permute-start | bytes 1769480 | tf_op jit(solution)/shard_map/ppermute | solution.py:29
  316.6 42.3 %collective-permute-start.47 = (bf16[3,256,384]{2,1,0:T(8,128)(2,1)S(1)}, bf16[3,256,384]{2,1,0:T(8,128)(2,1)}, u32[]{:S(2)}, u32[]{:S(2)}) collective-permute-start(bf16[3,256,384]{2,1,0:T(8,128)(2,1)S(1)} %get-tuple-element.263), channel_id=1, source_target_pairs={{0,2},{1,3},{2,0},{3,1},{4,6},{5,7},{6,4},{7,5},{8,10},{9,11},{10,... | collective-permute-start | bytes 1769480 | tf_op jit(solution)/shard_map/ppermute | solution.py:29
  317.4 41.5 %collective-permute-start.48 = (bf16[3,256,384]{2,1,0:T(8,128)(2,1)S(1)}, bf16[3,256,384]{2,1,0:T(8,128)(2,1)}, u32[]{:S(2)}, u32[]{:S(2)}) collective-permute-start(bf16[3,256,384]{2,1,0:T(8,128)(2,1)S(1)} %get-tuple-element.264), channel_id=1, source_target_pairs={{0,4},{4,0},{8,12},{12,8},{16,20},{20,16},{24,28},{28,24},{1,5},{5... | collective-permute-start | bytes 1769480 | tf_op jit(solution)/shard_map/ppermute | solution.py:29
  318.5 40.4 %collective-permute-start.49 = (bf16[3,256,384]{2,1,0:T(8,128)(2,1)S(1)}, bf16[3,256,384]{2,1,0:T(8,128)(2,1)}, u32[]{:S(2)}, u32[]{:S(2)}) collective-permute-start(bf16[3,256,384]{2,1,0:T(8,128)(2,1)S(1)} %get-tuple-element.265), channel_id=1, source_target_pairs={{0,2},{1,3},{2,0},{3,1},{4,6},{5,7},{6,4},{7,5},{8,10},{9,11},{10,... | collective-permute-start | bytes 1769480 | tf_op jit(solution)/shard_map/ppermute | solution.py:29
  376.3 26.3 %collective-permute-start.54 = (bf16[3,256,384]{2,1,0:T(8,128)(2,1)S(1)}, bf16[3,256,384]{2,1,0:T(8,128)(2,1)S(1)}, u32[]{:S(2)}, u32[]{:S(2)}) collective-permute-start(bf16[3,256,384]{2,1,0:T(8,128)(2,1)S(1)} %copy-done.78), channel_id=1, source_target_pairs={{0,4},{4,0},{8,12},{12,8},{16,20},{20,16},{24,28},{28,24},{1,5},{5... | collective-permute-start | bytes 1769480 | tf_op jit(solution)/shard_map/ppermute | solution.py:29
  379.4 23.6 %collective-permute-start.55 = (bf16[3,256,384]{2,1,0:T(8,128)(2,1)S(1)}, bf16[3,256,384]{2,1,0:T(8,128)(2,1)S(1)}, u32[]{:S(2)}, u32[]{:S(2)}) collective-permute-start(bf16[3,256,384]{2,1,0:T(8,128)(2,1)S(1)} %copy-done.76), channel_id=1, source_target_pairs={{0,2},{1,3},{2,0},{3,1},{4,6},{5,7},{6,4},{7,5},{8,10},{9,11},{10,... | collective-permute-start | bytes 1769480 | tf_op jit(solution)/shard_map/ppermute | solution.py:29
  413.5 24.1 %collective-permute-start.57 = (bf16[3,256,384]{2,1,0:T(8,128)(2,1)}, bf16[3,256,384]{2,1,0:T(8,128)(2,1)S(1)}, u32[]{:S(2)}, u32[]{:S(2)}) collective-permute-start(bf16[3,256,384]{2,1,0:T(8,128)(2,1)} %add_convert_fusion.6), channel_id=1, source_target_pairs={{0,4},{4,0},{8,12},{12,8},{16,20},{20,16},{24,28},{28,24},{1,5},{5... | collective-permute-start | bytes 1769480 | tf_op jit(solution)/shard_map/ppermute | solution.py:29
  414.8 22.9 %collective-permute-start.58 = (bf16[3,256,384]{2,1,0:T(8,128)(2,1)}, bf16[3,256,384]{2,1,0:T(8,128)(2,1)S(1)}, u32[]{:S(2)}, u32[]{:S(2)}) collective-permute-start(bf16[3,256,384]{2,1,0:T(8,128)(2,1)} %add_convert_fusion.5), channel_id=1, source_target_pairs={{0,2},{1,3},{2,0},{3,1},{4,6},{5,7},{6,4},{7,5},{8,10},{9,11},{10,... | collective-permute-start | bytes 1769480 | tf_op jit(solution)/shard_map/ppermute | solution.py:29
  415.8 26.7 %collective-permute-start.59 = (bf16[3,256,384]{2,1,0:T(8,128)(2,1)}, bf16[3,256,384]{2,1,0:T(8,128)(2,1)S(1)}, u32[]{:S(2)}, u32[]{:S(2)}) collective-permute-start(bf16[3,256,384]{2,1,0:T(8,128)(2,1)} %copy-done.74), channel_id=1, source_target_pairs={{0,4},{4,0},{8,12},{12,8},{16,20},{20,16},{24,28},{28,24},{1,5},{5... | collective-permute-start | bytes 1769480 | tf_op jit(solution)/shard_map/ppermute | solution.py:29
  416.7 26.7 %collective-permute-start.60 = (bf16[3,256,384]{2,1,0:T(8,128)(2,1)}, bf16[3,256,384]{2,1,0:T(8,128)(2,1)S(1)}, u32[]{:S(2)}, u32[]{:S(2)}) collective-permute-start(bf16[3,256,384]{2,1,0:T(8,128)(2,1)} %copy-done.73), channel_id=1, source_target_pairs={{0,2},{1,3},{2,0},{3,1},{4,6},{5,7},{6,4},{7,5},{8,10},{9,11},{10,... | collective-permute-start | bytes 1769480 | tf_op jit(solution)/shard_map/ppermute | solution.py:29
  417.7 28.7 %collective-permute-start.61 = (bf16[3,256,384]{2,1,0:T(8,128)(2,1)}, bf16[3,256,384]{2,1,0:T(8,128)(2,1)S(1)}, u32[]{:S(2)}, u32[]{:S(2)}) collective-permute-start(bf16[3,256,384]{2,1,0:T(8,128)(2,1)} %add_convert_fusion.4), channel_id=1, source_target_pairs={{0,16},{4,20},{8,24},{12,28},{16,0},{20,4},{24,8},{28,12},{1,17},{... | collective-permute-start | bytes 1769480 | tf_op jit(solution)/shard_map/ppermute | solution.py:29
  437.6 64.1 %collective-permute-start.62 = (bf16[4,1024,256]{2,1,0:T(8,128)(2,1)S(1)}, bf16[4,1024,256]{2,1,0:T(8,128)(2,1)S(1)}, u32[]{:S(2)}, u32[]{:S(2)}) collective-permute-start(bf16[4,1024,256]{2,1,0:T(8,128)(2,1)S(1)} %get-tuple-element.304), channel_id=1, source_target_pairs={{0,1},{1,0},{2,3},{3,2},{4,5},{5,4},{6,7},{7,6},{8,9},{9,8},{10,11... | collective-permute-start | bytes 6291464 | tf_op jit(solution)/shard_map/ppermute | solution.py:29
  437.7 63.5 %collective-permute-start.63 = (bf16[4,1024,256]{2,1,0:T(8,128)(2,1)S(1)}, bf16[4,1024,256]{2,1,0:T(8,128)(2,1)S(1)}, u32[]{:S(2)}, u32[]{:S(2)}) collective-permute-start(bf16[4,1024,256]{2,1,0:T(8,128)(2,1)S(1)} %get-tuple-element.308), channel_id=1, source_target_pairs={{0,1},{1,0},{2,3},{3,2},{4,5},{5,4},{6,7},{7,6},{8,9},{9,8},{10,11... | collective-permute-start | bytes 6291464 | tf_op jit(solution)/shard_map/ppermute | solution.py:29
  448.8 25.5 %collective-permute-start.65 = (bf16[3,256,384]{2,1,0:T(8,128)(2,1)S(1)}, bf16[3,256,384]{2,1,0:T(8,128)(2,1)S(1)}, u32[]{:S(2)}, u32[]{:S(2)}) collective-permute-start(bf16[3,256,384]{2,1,0:T(8,128)(2,1)S(1)} %add_convert_fusion.3), channel_id=1, source_target_pairs={{0,4},{4,0},{8,12},{12,8},{16,20},{20,16},{24,28},{28,24},{1,5},{5... | collective-permute-start | bytes 1769480 | tf_op jit(solution)/shard_map/ppermute | solution.py:29
  449.7 29.7 %collective-permute-start.66 = (bf16[3,256,384]{2,1,0:T(8,128)(2,1)S(1)}, bf16[3,256,384]{2,1,0:T(8,128)(2,1)S(1)}, u32[]{:S(2)}, u32[]{:S(2)}) collective-permute-start(bf16[3,256,384]{2,1,0:T(8,128)(2,1)S(1)} %copy-done.70), channel_id=1, source_target_pairs={{0,2},{1,3},{2,0},{3,1},{4,6},{5,7},{6,4},{7,5},{8,10},{9,11},{10,... | collective-permute-start | bytes 1769480 | tf_op jit(solution)/shard_map/ppermute | solution.py:29
  474.3 26.6 %collective-permute-start.68 = (bf16[3,256,384]{2,1,0:T(8,128)(2,1)S(1)}, bf16[3,256,384]{2,1,0:T(8,128)(2,1)S(1)}, u32[]{:S(2)}, u32[]{:S(2)}) collective-permute-start(bf16[3,256,384]{2,1,0:T(8,128)(2,1)S(1)} %add_convert_fusion.1), channel_id=1, source_target_pairs={{0,16},{4,20},{8,24},{12,28},{16,0},{20,4},{24,8},{28,12},{1,17},{... | collective-permute-start | bytes 1769480 | tf_op jit(solution)/shard_map/ppermute | solution.py:29
  504.0 25.4 %collective-permute-start.72 = (bf16[3,256,384]{2,1,0:T(8,128)(2,1)S(1)}, bf16[3,256,384]{2,1,0:T(8,128)(2,1)S(1)}, u32[]{:S(2)}, u32[]{:S(2)}) collective-permute-start(bf16[3,256,384]{2,1,0:T(8,128)(2,1)S(1)} %add_convert_fusion), channel_id=1, source_target_pairs={{0,16},{4,20},{8,24},{12,28},{16,0},{20,4},{24,8},{28,12},{1,17},{... | collective-permute-start | bytes 1769480 | tf_op jit(solution)/shard_map/ppermute | solution.py:29
  504.9 25.4 %collective-permute-start.69 = (bf16[4,256,256]{2,1,0:T(8,128)(2,1)S(1)}, bf16[4,256,256]{2,1,0:T(8,128)(2,1)S(1)}, u32[]{:S(2)}, u32[]{:S(2)}) collective-permute-start(bf16[4,256,256]{2,1,0:T(8,128)(2,1)S(1)} %add_convert_fusion.17), channel_id=1, source_target_pairs={{0,4},{4,0},{8,12},{12,8},{16,20},{20,16},{24,28},{28,24},{1,5},{5... | collective-permute-start | bytes 1572872 | tf_op jit(solution)/shard_map/ppermute | solution.py:29
  505.9 25.3 %collective-permute-start.73 = (bf16[4,256,256]{2,1,0:T(8,128)(2,1)S(1)}, bf16[4,256,256]{2,1,0:T(8,128)(2,1)S(1)}, u32[]{:S(2)}, u32[]{:S(2)}) collective-permute-start(bf16[4,256,256]{2,1,0:T(8,128)(2,1)S(1)} %get-tuple-element.330), channel_id=1, source_target_pairs={{0,2},{1,3},{2,0},{3,1},{4,6},{5,7},{6,4},{7,5},{8,10},{9,11},{10,... | collective-permute-start | bytes 1572872 | tf_op jit(solution)/shard_map/ppermute | solution.py:29
  533.6 26.5 %collective-permute-start.74 = (bf16[4,256,256]{2,1,0:T(8,128)(2,1)}, bf16[4,256,256]{2,1,0:T(8,128)(2,1)S(1)}, u32[]{:S(2)}, u32[]{:S(2)}) collective-permute-start(bf16[4,256,256]{2,1,0:T(8,128)(2,1)} %add_convert_fusion.11), channel_id=1, source_target_pairs={{0,2},{1,3},{2,0},{3,1},{4,6},{5,7},{6,4},{7,5},{8,10},{9,11},{10,... | collective-permute-start | bytes 1572872 | tf_op jit(solution)/shard_map/ppermute | solution.py:29
  533.9 27.4 %collective-permute-start.79 = (bf16[3,128,384]{2,1,0:T(8,128)(2,1)}, bf16[3,128,384]{2,1,0:T(8,128)(2,1)S(1)}, u32[]{:S(2)}, u32[]{:S(2)}) collective-permute-start(bf16[3,128,384]{2,1,0:T(8,128)(2,1)} %add_convert_fusion.21), channel_id=1, source_target_pairs={{0,8},{4,12},{8,0},{12,4},{16,24},{20,28},{24,16},{28,20},{1,9},{5... | collective-permute-start | bytes 884744 | tf_op jit(solution)/shard_map/ppermute | solution.py:29
  535.5 29.9 %collective-permute-start.78 = (bf16[3,128,384]{2,1,0:T(8,128)(2,1)S(1)}, bf16[3,128,384]{2,1,0:T(8,128)(2,1)S(1)}, u32[]{:S(2)}, u32[]{:S(2)}) collective-permute-start(bf16[3,128,384]{2,1,0:T(8,128)(2,1)S(1)} %copy-done.139), channel_id=1, source_target_pairs={{0,8},{4,12},{8,0},{12,4},{16,24},{20,28},{24,16},{28,20},{1,9},{5... | collective-permute-start | bytes 884744 | tf_op jit(solution)/shard_map/ppermute | solution.py:29
  561.3 26.3 %collective-permute-start.76 = (bf16[4,256,256]{2,1,0:T(8,128)(2,1)S(1)}, bf16[4,256,256]{2,1,0:T(8,128)(2,1)S(1)}, u32[]{:S(2)}, u32[]{:S(2)}) collective-permute-start(bf16[4,256,256]{2,1,0:T(8,128)(2,1)S(1)} %get-tuple-element.333), channel_id=1, source_target_pairs={{0,16},{4,20},{8,24},{12,28},{16,0},{20,4},{24,8},{28,12},{1,17},{... | collective-permute-start | bytes 1572872 | tf_op jit(solution)/shard_map/ppermute | solution.py:29
  (203 other events, 2416.0 us)

commit v6 on v5

--- a/solution.py
+++ b/solution.py
@@ -188,14 +188,15 @@
     return jnp.dot(left, right, preferred_element_type=F32)
 
 
-def ffn_kernel(first, h, ht, c, ct, *rest):
+def ffn_kernel(first, h_own, h_other, ht_own, ht_other, c, ct, *rest):
     pieces, rest = rest[:8], rest[8:]
     grads, (branch, back, w, act, dgate, dup) = rest[-14:-6], rest[-6:]
     deep, half = pieces[0].shape[1:]
     spots = [
         (pl.ds(i % 4 * deep, deep), pl.ds(i // 4 * half, half)) for i in range(8)
     ]
-    rows = h.shape[0]
+    rows = c.shape[0]
+    own = rows // 2
     tall = 384
 
     @pl.when(pl.program_id(0) == 0)
@@ -207,16 +208,21 @@
         w[:, deep_span, span] = piece[...]
     for start in range(0, rows, tall):
         span = pl.ds(start, tall)
-        gate = nn(h[span, :], w[0])
-        up = nn(h[span, :], w[1])
+        h = h_own[span, :] if start < own else h_other[pl.ds(start - own, tall), :]
+        gate = nn(h, w[0])
+        up = nn(h, w[1])
         da = nn(c[span, :], w[2])
         sigma = 1.0 / (1.0 + jnp.exp(-gate))
         silu = gate * sigma
         act[span, :] = (silu * up).astype(BF)
         dup[span, :] = (da * silu).astype(BF)
         dgate[span, :] = (da * up * (sigma + silu * (1.0 - sigma))).astype(BF)
-    for k, (left, right) in enumerate(((ht, dgate), (ht, dup), (ct, act))):
-        grad = nn(left[...], right[...]).astype(BF)
+    for k, right in enumerate((dgate, dup, act)):
+        if k < 2:
+            grad = nn(ht_own[...], right[:own, :]) + nn(ht_other[...], right[own:, :])
+        else:
+            grad = nn(ct[...], right[...])
+        grad = grad.astype(BF)
         for i, out in enumerate(grads):
             out[k] = grad[i % 4 * deep : (i % 4 + 1) * deep, i // 4 * half : (i // 4 + 1) * half]
     for start in range(0, rows, tall):
@@ -225,8 +231,8 @@
         back[span, :] += nt(dgate[span, :], w[0]) + nt(dup[span, :], w[1])
 
 
-def ffn(h, ht, c, ct, pieces, sums):
-    rows, width = h.shape
+def ffn(tokens, pieces, sums):
+    rows, width = tokens[4].shape
     planes, deep, cols = pieces[0].shape
     tile = 128
     block = pl.BlockSpec((planes, deep, tile), lambda j: (0, 0, j))
@@ -237,9 +243,9 @@
         functools.partial(ffn_kernel, not sums),
         grid=(cols // tile,),
         out_shape=(grad,) * 8 + (part, part),
-        in_specs=[vmem] * 4 + [block] * 8 + [vmem] * len(sums),
+        in_specs=[vmem] * 6 + [block] * 8 + [vmem] * len(sums),
         out_specs=(block,) * 8 + (vmem, vmem),
-        input_output_aliases={12: 8, 13: 9} if sums else {},
+        input_output_aliases={14: 8, 15: 9} if sums else {},
         scratch_shapes=[pltpu.VMEM((planes, width, 2 * tile), BF)]
         + [pltpu.VMEM((rows, 2 * tile), BF)] * 3,
         compiler_params=params(),
@@ -249,7 +255,7 @@
             transcendentals=2 * rows * cols,
         ),
         name="ffn",
-    )(h, ht, c, ct, *pieces, *sums)
+    )(*tokens, *pieces, *sums)
     return out[:8], out[8:]
 
 
@@ -534,11 +540,11 @@
     small = join([small, *small_x], 1)
     small_z = phase([*got, small], [(small, "dp", code) for code in range(2, dp_size, 2)])
     xb[0], yb[0], da[0], ya[1], zb[1] = got = phase(
-        got, [by_x(zb[0]), by_y(zb[0]), by_x(ya[0]), by_y(own[1]), by_z(own[1])]
-    )
-    x_ext, cot = arrange(order, tokens, before, cotangent)
+        [*got, *later], [by_x(zb[0]), by_y(zb[0]), by_x(ya[0]), by_y(own[1]), by_z(own[1])]
+    )
+    x_ext, cot = arrange(order, *ordered([tokens, before, cotangent], last))
     db[0], xa[1], zb[2], cot_other = phase(
-        [*got[:3], *later], [by_y(xb[0]), by_x(own[1]), by_z(own[2]), (cot, "tensor", 1)]
+        got[:3], [by_y(xb[0]), by_x(own[1]), by_z(own[2]), (cot, "tensor", 1)]
     )
     small = join([small, *small_z], 1)
 
@@ -572,11 +578,15 @@
     extended = x_ext.astype(F32)
     scale_ext = rms_scale(extended)
     normed_ext = (extended * scale_ext * gains[0]).astype(BF)
+    c = join([cot, cot_other], 0)
+    ct = c.T
+    (normed_ext,) = ordered([normed_ext], [c, ct])
     values, scale_one, normed_one = extended[HALO:], scale_ext[HALO:], normed_ext[HALO:]
     near, far = join(pieces_of(0)[:4], wide), join(pieces_of(0)[4:], wide)
     wm = [near, other_core(near), far, other_core(far)]
     got = phase(
-        [db[0], xa[1], zb[1], ya[1]], [by_x(zb[1]), by_y(zb[1]), by_x(ya[1]), by_y(own[2])]
+        [db[0], xa[1], zb[1], ya[1], zb[2]],
+        [by_x(zb[1]), by_y(zb[1]), by_x(ya[1]), by_y(own[2]), by_z(own[3])],
     )
     wm_all = jnp.concatenate(wm, 2)
     win_all, wout_all = wm_all[:3], wm_all[3]
@@ -597,19 +607,17 @@
     normed_two = (middle * scale_two * gains[1]).astype(BF)
 
     normed_other = other_core(normed_two)
-    h, c = join([normed_two, normed_other], 0), join([cot, cot_other], 0)
-    ht, ct = h.T, c.T
+    tokens_both = (normed_two, normed_other, normed_two.T, normed_other.T, c, ct)
     sums, grads = [], {}
-    xb[1], yb[1], da[1], ya[2] = got = ordered(got, [normed_two])
-    (zb[2],) = ordered([zb[2]], [normed_two])
-    db[1], xa[2], zb[3] = phase(got, [by_y(xb[1]), by_x(own[2]), by_z(own[3])])
+    xb[1], yb[1], da[1], ya[2], zb[3] = got = ordered(got, [normed_two])
+    db[1], xa[2] = got = phase(got, [by_y(xb[1]), by_x(own[2])])
 
     def run(i):
         nonlocal sums
-        grads[i], sums = ffn(h, ht, c, ct, pieces_of(i), list(sums))
+        grads[i], sums = ffn(tokens_both, pieces_of(i), list(sums))
         return grads[i]
 
-    got = phase([db[1], xa[2], zb[2]], [by_x(zb[2]), by_y(zb[2]), by_x(ya[2]), by_y(own[3])])
+    got = phase(got, [by_x(zb[2]), by_y(zb[2]), by_x(ya[2]), by_y(own[3])])
     xb[2], yb[2], da[2], ya[3] = got = ordered(got, run(1)[:1])
     db[2], xa[3] = got = phase(got, [by_y(xb[2]), by_x(own[3])])
 
@@ -621,10 +629,11 @@
     def sum_ya(i):
         return by_y(plus(grads[i][4], ada[i]))
 
-    got = phase([*got, zb[3]], [by_x(zb[3]), by_y(zb[3]), by_x(ya[3]), by_y(grads[1][5])])
+    got = phase(got, [by_x(zb[3]), by_y(zb[3]), by_x(ya[3]), by_y(grads[1][5])])
     xb[3], yb[3], da[3], ayb[1] = got = ordered(got, run(2)[:1])
     db[3], ada[1] = got = phase(got, [by_y(xb[3]), by_x(grads[1][6])])
-    (db[3],) = ordered([db[3]], [ada[1]])
+    one_t = normed_one.T
+    (db[3],) = ordered([db[3]], [ada[1], one_t])
     got = phase(
         got, [by_x(grads[1][2]), by_y(grads[1][7]), by_x(grads[2][6]), by_y(grads[2][7])]
     )
@@ -676,13 +685,14 @@
     proj_grad = jnp.stack([product_grad * part_x, c_grad, product_grad * part_b], 0).astype(BF)
     zs = {}
     axb[2], aya[2], ada[3], adb[3], zs[1] = got = ordered(got, [proj_grad])
-    one_t, mixed_t = normed_one.T, mixed_grad.T
+    mixed_t = mixed_grad.T
+    m_near_core, m_far_core = mixer_grad(one_t, mixed_t, proj_grad, gated, 1, 3, [axb[2], aya[2], ada[3], adb[3]])
+    m_in = [other_core(m_far_core), other_core(m_near_core)]
     got = phase(
-        got, [by_x(grads[3][2]), sum_xb(3), by_y(grads[3][5]), sum_ya(3), sum_b(2)]
-    )
-    m_near_core, m_far_core = mixer_grad(one_t, mixed_t, proj_grad, gated, 1, 3, [])
-    m_in = [other_core(m_far_core), other_core(m_near_core)]
-    m_near, m_far = mixer_grad(one_t, mixed_t, proj_grad, gated, 0, 2, [axb[2], aya[2], ada[3], adb[3]])
+        [*got, *m_in],
+        [by_x(grads[3][2]), sum_xb(3), by_y(grads[3][5]), sum_ya(3), sum_b(2)],
+    )
+    m_near, m_far = mixer_grad(one_t, mixed_t, proj_grad, gated, 0, 2, m_in)
     axa[3], axb[3], ayb[3], aya[3], zs[2] = got = ordered(got, [m_far])
     deep = m_near.shape[wide] // 4
     grads[0] = [
@@ -746,7 +756,7 @@
     sum_a(2)
     sum_a(3)
     total_small = small_step(total_small, last, "tensor", range(1, t_size))
-    got = phase(last, [sum_xb(0), sum_ya(0), *[fold_send(i, 0) for i in range(1, PARTS + 1)]])
+    got = phase([*last, gain_one_grad], [sum_xb(0), sum_ya(0), *[fold_send(i, 0) for i in range(1, PARTS + 1)]])
     axb[0], aya[0] = got[:2]
     for i in range(1, PARTS + 1):
         folded(i, 0, got[i + 1])

time: 607 us -> 598 us (0.985)
  waiting for transfers between devices: 203 us -> 194 us
  starting transfers between devices: 92.1 us -> 83.7 us
  other arithmetic: 69.1 us -> 77.4 us
    ppermute x86, waiting for transfers between devices: 203 us -> 194 us  [swap(): return lax.ppermute(values, axis, [(i, i ^ bit) for i in range(size)])]
    ppermute x86, starting transfers between devices: 89.4 us -> 80.9 us  [swap(): return lax.ppermute(values, axis, [(i, i ^ bit) for i in range(size)])]
    convert_element_type x10, other arithmetic: 9.76 us -> 17.1 us  [plus(): return (left.astype(F32) + right.astype(F32)).astype(BF)]
    unnamed x347 -> x321, local copies, waits for them, and re-layouts: 55.7 us -> 54.5 us
  transfers between devices with their start and end apart: 88 -> 88, of which waited for: 33 -> 35; matrix products, arithmetic and copies ran while one was open for 20% -> 22% of each run, Pallas kernels for 20% -> 19%
where the time goes in v6:
time: 598 us; the launch traced here: 593 us
  waiting for transfers between devices  194 us (32%)
  Pallas kernels  121 us (20%)
  local copies, waits for them, and re-layouts  89.9 us (15%)
  starting transfers between devices  83.7 us (14%)
  other arithmetic  77.4 us (13%)
  matrix products  18.5 us (3%)
  between operations  8.11 us (1%)
    ppermute x86, waiting for transfers between devices, swap(): return lax.ppermute(values, axis, [(i, i ^ bit) for i in range(size)])  194 us
    pallas_call x3, Pallas kernels, ffn(): pl.pallas_call(functools.partial(ffn_kernel, not sums), grid=(cols // til...  93 us
    ppermute x86, starting transfers between devices, swap(): return lax.ppermute(values, axis, [(i, i ^ bit) for i in range(size)])  80.9 us
    unnamed x321, local copies, waits for them, and re-layouts  54.5 us
    dot_general x4, matrix products, mm(): return jnp.einsum(spec, left, right, preferred_element_type=F32).astype(out)  18.5 us
    convert_element_type x10, other arithmetic, plus(): return (left.astype(F32) + right.astype(F32)).astype(BF)  17.1 us
  transfers between devices with their start and end apart: 88, of which 35 were waited for; matrix products, arithmetic and copies ran while one was open for 22% of the time, Pallas kernels for 19%

profile of v6, /device:TPU:0, one launch (start us, length us, event | category | flops | bytes accessed | tf_op | source)
XLA Modules:
  0.0 592.8 jit_solution(6434340832046995745)
XLA Ops:
  3.5 3.0 collective-permute-start.1
  38.0 2.9 copy.67
  51.0 6.2 %collective-permute-done.7 = bf16[3,128,384]{2,1,0:T(8,128)(2,1)S(1)} collective-permute-done((bf16[3,128,384]{2,1,0:T(8,128)(2,1)}, bf16[3,128,384]{2,1,0:T(8,128)(2,1)S(1)}, u32[]{:S(2)}, u32[]{:S(2)}) %collective-permute-start.7) | collective-permute-done | bytes 294944 | tf_op jit(solution)/shard_map/ppermute | solution.py:29
  69.0 3.6 collective-permute-done.18
  72.6 2.6 collective-permute-start.19
  75.2 12.5 %collective-permute-done.19 = f32[5,8,32]{2,0,1:T(8,128)S(1)} collective-permute-done((f32[5,8,32]{2,0,1:T(8,128)S(1)}, f32[5,8,32]{2,0,1:T(8,128)S(1)}, u32[]{:S(2)}, u32[]{:S(2)}) %collective-permute-start.19) | collective-permute-done | bytes 5152 | tf_op jit(solution)/shard_map/ppermute | solution.py:29
  89.4 4.1 collective-permute-done.20
  103.8 15.1 %collective-permute-done.12 = bf16[4,256,256]{2,1,0:T(8,128)(2,1)} collective-permute-done((bf16[4,256,256]{2,1,0:T(8,128)(2,1)}, bf16[4,256,256]{2,1,0:T(8,128)(2,1)}, u32[]{:S(2)}, u32[]{:S(2)}) %collective-permute-start.12) | collective-permute-done | bytes 524320 | tf_op jit(solution)/shard_map/ppermute | solution.py:29
  124.7 12.2 %collective-permute-done.24.rest_2_ = bf16[3,256,384]{2,1,0:T(8,128)(2,1)S(1)} collective-permute-done((bf16[3,256,384]{2,1,0:T(8,128)(2,1)S(1)}, bf16[3,256,384]{2,1,0:T(8,128)(2,1)S(1)}, u32[]{:S(2)}, u32[]{:S(2)}) %collective-permute-start.24) | collective-permute-done | bytes 589856 | tf_op jit(solution)/shard_map/ppermute | solution.py:29
  137.7 13.0 %collective-permute-done.25.rest_1_ = bf16[3,256,384]{2,1,0:T(8,128)(2,1)} collective-permute-done((bf16[3,256,384]{2,1,0:T(8,128)(2,1)}, bf16[3,256,384]{2,1,0:T(8,128)(2,1)}, u32[]{:S(2)}, u32[]{:S(2)}) %collective-permute-start.25) | collective-permute-done | bytes 589856 | tf_op jit(solution)/shard_map/ppermute | solution.py:29
  154.5 4.4 fusion.60
  159.2 7.7 %fusion.16 = f32[3,784,1024]{2,1,0:T(8,128)S(1)} fusion(bf16[4,1024,256]{2,1,0:T(8,128)(2,1)} %collective-permute-done.13, bf16[4,1024,256]{2,1,0:T(8,128)(2,1)} %constant_dynamic-update-slice_fusion.5, bf16[4,1024,256]{2,1,0:T(8,128)(2,1)} %collective-permute-done.9, bf16[4,1024,256]{2,1,0:T(8,128)(2,1)} %constant_dynamic-update-slice_fusion, ...), kind=kOutput, calls=%fused_computation.19 | convolution fusion | flops 4966055936 | bytes 19628032 | tf_op jit(solution)/shard_map/td,kdc->ktc/dot_general | solution.py:118
  167.9 2.8 copy-done.93
  170.7 2.9 multiply_convert_fusion.3
  173.6 5.0 collective-permute-done.28.rest_6_
  179.0 7.9 %collective-permute-done.30.rest_1_ = bf16[3,256,384]{2,1,0:T(8,128)(2,1)S(1)} collective-permute-done((bf16[3,256,384]{2,1,0:T(8,128)(2,1)}, bf16[3,256,384]{2,1,0:T(8,128)(2,1)S(1)}, u32[]{:S(2)}, u32[]{:S(2)}) %collective-permute-start.30) | collective-permute-done | bytes 589856 | tf_op jit(solution)/shard_map/ppermute | solution.py:29
  195.1 4.9 copy.81.c
  200.0 2.6 copy.79.h_own
  202.6 3.4 fusion.73.ht_own
  206.0 3.6 collective-permute-done.32.rest_7_
  229.4 29.2 %ffn.3 = (bf16[3,256,384]{2,1,0:T(8,128)(2,1)S(1)}, bf16[3,256,384]{2,1,0:T(8,128)(2,1)S(1)}, bf16[3,256,384]{2,1,0:T(8,128)(2,1)S(1)}, bf16[3,256,384]{2,1,0:T(...) custom-call(bf16[768,1024]{1,0:T(8,128)(2,1)S(1)} %copy-done.33, ...), custom_call_target="tpu_custom_call" | custom-call | flops 21743271936 | bytes 9437184 | tf_op jit(solution)/shard_map/ffn/pallas_call | solution.py:242
  263.4 12.2 %collective-permute-done.39.rest_7_ = bf16[3,256,384]{2,1,0:T(8,128)(2,1)S(1)} collective-permute-done((bf16[3,256,384]{2,1,0:T(8,128)(2,1)}, bf16[3,256,384]{2,1,0:T(8,128)(2,1)S(1)}, u32[]{:S(2)}, u32[]{:S(2)}) %collective-permute-start.39) | collective-permute-done | bytes 589856 | tf_op jit(solution)/shard_map/ppermute | solution.py:29
  280.6 32.1 %ffn.4 = (bf16[3,256,384]{2,1,0:T(8,128)(2,1)S(1)}, bf16[3,256,384]{2,1,0:T(8,128)(2,1)S(1)}, bf16[3,256,384]{2,1,0:T(8,128)(2,1)S(1)}, bf16[3,256,384]{2,1,0:T(...) custom-call(bf16[768,1024]{1,0:T(8,128)(2,1)S(1)} %copy-done.33, ...), custom_call_target="tpu_custom_call", output_to_operand_aliasing={{8}: (14, {}), {9}: (15, {})} | custom-call | flops 21743271936 | bytes 9437184 | tf_op jit(solution)/shard_map/ffn/pallas_call | solution.py:242
  316.1 11.2 %collective-permute-done.45 = bf16[3,256,384]{2,1,0:T(8,128)(2,1)S(1)} collective-permute-done((bf16[3,256,384]{2,1,0:T(8,128)(2,1)S(1)}, bf16[3,256,384]{2,1,0:T(8,128)(2,1)S(1)}, u32[]{:S(2)}, u32[]{:S(2)}) %collective-permute-start.45) | collective-permute-done | bytes 589856 | tf_op jit(solution)/shard_map/ppermute | solution.py:29
  331.3 31.7 %ffn.5 = (bf16[3,256,384]{2,1,0:T(8,128)(2,1)S(1)}, bf16[3,256,384]{2,1,0:T(8,128)(2,1)S(1)}, bf16[3,256,384]{2,1,0:T(8,128)(2,1)S(1)}, bf16[3,256,384]{2,1,0:T(...) custom-call(bf16[768,1024]{1,0:T(8,128)(2,1)S(1)} %copy-done.33, ...), custom_call_target="tpu_custom_call", output_to_operand_aliasing={{8}: (14, {}), {9}: (15, {})} | custom-call | flops 21743271936 | bytes 9437184 | tf_op jit(solution)/shard_map/ffn/pallas_call | solution.py:242
  372.5 3.3 slice.617
  376.4 3.6 copy.82.refs_1_
  391.2 2.8 copy-done.8
  394.0 2.8 copy-done.9
  396.8 6.4 %middle_back.1 = (bf16[768,1024]{1,0:T(8,128)(2,1)}, f32[768,1024]{1,0:T(8,128)S(1)}, bf16[768,1024]{1,0:T(8,128)(2,1)S(1)}, f32[1,1024]{1,0:T(1,128)S(1)}) custom-call(s32[8]{0:T(128)S(1)} %broadcast_xor_fusion.order.refs_0_, f32[768,1024]{1,0:T(8,128)S(1)} %copy-done.6, f32[768,1]{1,0:T(8,128)S(1)} %rsqrt.21.refs_2_, ...), custom_call_target="tpu_custom_call" | custom-call | flops 23592960 | bytes 23592960 | tf_op jit(solution)/shard_map/middle_back/pallas_call | solution.py:325
  405.6 5.4 collective-permute-done.54
  412.4 4.3 fusion.32
  427.4 2.8 broadcast_multiply_fusion.1
  431.2 4.0 multiply_reduce_fusion.1
  435.2 2.6 fusion.34
  440.2 12.0 %collective-permute-done.59.rest_2_ = bf16[3,256,384]{2,1,0:T(8,128)(2,1)S(1)} collective-permute-done((bf16[3,256,384]{2,1,0:T(8,128)(2,1)}, bf16[3,256,384]{2,1,0:T(8,128)(2,1)S(1)}, u32[]{:S(2)}, u32[]{:S(2)}) %collective-permute-start.59) | collective-permute-done | bytes 589856 | tf_op jit(solution)/shard_map/ppermute | solution.py:29
  455.2 5.5 mixer_grad.2
  465.4 2.9 collective-permute-done.63.rest_1_
  472.4 4.5 mixer_grad.3
  479.2 2.9 add_convert_fusion.15
  484.7 11.8 %collective-permute-done.65 = bf16[3,256,384]{2,1,0:T(8,128)(2,1)S(1)} collective-permute-done((bf16[3,256,384]{2,1,0:T(8,128)(2,1)S(1)}, bf16[3,256,384]{2,1,0:T(8,128)(2,1)S(1)}, u32[]{:S(2)}, u32[]{:S(2)}) %collective-permute-start.65) | collective-permute-done | bytes 589856 | tf_op jit(solution)/shard_map/ppermute | solution.py:29
  506.7 8.9 %collective-permute-done.70 = bf16[4,256,256]{2,1,0:T(8,128)(2,1)S(1)} collective-permute-done((bf16[4,256,256]{2,1,0:T(8,128)(2,1)S(1)}, bf16[4,256,256]{2,1,0:T(8,128)(2,1)S(1)}, u32[]{:S(2)}, u32[]{:S(2)}) %collective-permute-start.70) | collective-permute-done | bytes 524320 | tf_op jit(solution)/shard_map/ppermute | solution.py:29
  518.1 7.1 %fusion.28.upstream = f32[768,1024]{1,0:T(8,128)S(1)} fusion(bf16[3,768,1024]{2,1,0:T(8,128)(2,1)S(1)} %copy-done.1, bf16[4,1024,256]{2,1,0:T(8,128)(2,1)} %collective-permute-done.13, bf16[4,1024,256]{2,1,0:T(8,128)(2,1)S(1)} %copy-done.105, bf16[4,1024,256]{2,1,0:T(8,128)(2,1)} %collective-permute-done.9, bf16[4,1024,256]{2,1,0:T(8,128)(2,1)S(1)} %copy-done.107), kind=kOutput, calls=%fused_computation.52 | convolution fusion | flops 4857004032 | bytes 16252928 | tf_op jit(solution)/shard_map/ktc,kdc->td/dot_general | solution.py:118
  525.3 4.5 input_back.1
  543.3 7.2 %collective-permute-done.75 = bf16[4,256,256]{2,1,0:T(8,128)(2,1)S(1)} collective-permute-done((bf16[4,256,256]{2,1,0:T(8,128)(2,1)}, bf16[4,256,256]{2,1,0:T(8,128)(2,1)S(1)}, u32[]{:S(2)}, u32[]{:S(2)}) %collective-permute-start.75) | collective-permute-done | bytes 524320 | tf_op jit(solution)/shard_map/ppermute | solution.py:29
  555.4 4.3 update.3
  559.7 18.0 %collective-permute-done.76 = bf16[4,256,256]{2,1,0:T(8,128)(2,1)S(1)} collective-permute-done((bf16[4,256,256]{2,1,0:T(8,128)(2,1)S(1)}, bf16[4,256,256]{2,1,0:T(8,128)(2,1)S(1)}, u32[]{:S(2)}, u32[]{:S(2)}) %collective-permute-start.76) | collective-permute-done | bytes 524320 | tf_op jit(solution)/shard_map/ppermute | solution.py:29
  583.3 2.8 collective-permute-done.87
  (575 shorter events, 217.8 us)
Async XLA Ops:
  7.3 25.9 %collective-permute-start = (bf16[16,1024]{1,0:T(8,128)(2,1)S(1)}, bf16[16,1024]{1,0:T(8,128)(2,1)S(1)}, u32[]{:S(2)}, u32[]{:S(2)}) collective-permute-start(bf16[16,1024]{1,0:T(8,128)(2,1)S(1)} %slice.353), channel_id=1, source_target_pairs={{0,1},{1,2},{2,3},{4,5},{5,6},{6,7},{8,9},{9,10},{10,11},{12,13},{... | collective-permute-start | bytes 98312 | tf_op jit(solution)/shard_map/ppermute | solution.py:531
  25.5 23.6 %collective-permute-start.6 = (bf16[3,128,384]{2,1,0:T(8,128)(2,1)}, bf16[3,128,384]{2,1,0:T(8,128)(2,1)}, u32[]{:S(2)}, u32[]{:S(2)}) collective-permute-start(bf16[3,128,384]{2,1,0:T(8,128)(2,1)} %get-tuple-element.202), channel_id=1, source_target_pairs={{0,8},{4,12},{8,0},{12,4},{16,24},{20,28},{24,16},{28,20},{1,9},{5... | collective-permute-start | bytes 884744 | tf_op jit(solution)/shard_map/ppermute | solution.py:29
  27.0 31.0 %collective-permute-start.3 = (bf16[4,256,256]{2,1,0:T(8,128)(2,1)}, bf16[4,256,256]{2,1,0:T(8,128)(2,1)}, u32[]{:S(2)}, u32[]{:S(2)}) collective-permute-start(bf16[4,256,256]{2,1,0:T(8,128)(2,1)} %pad_maximum_fusion.5), channel_id=1, source_target_pairs={{0,16},{4,20},{8,24},{12,28},{16,0},{20,4},{24,8},{28,12},{1,17},{... | collective-permute-start | bytes 1572872 | tf_op jit(solution)/shard_map/ppermute | solution.py:29
  29.6 28.4 %collective-permute-start.4 = (bf16[4,256,256]{2,1,0:T(8,128)(2,1)}, bf16[4,256,256]{2,1,0:T(8,128)(2,1)}, u32[]{:S(2)}, u32[]{:S(2)}) collective-permute-start(bf16[4,256,256]{2,1,0:T(8,128)(2,1)} %pad_maximum_fusion.5), channel_id=1, source_target_pairs={{0,4},{4,0},{8,12},{12,8},{16,20},{20,16},{24,28},{28,24},{1,5},{5... | collective-permute-start | bytes 1572872 | tf_op jit(solution)/shard_map/ppermute | solution.py:29
  31.1 26.9 %collective-permute-start.5 = (bf16[4,256,256]{2,1,0:T(8,128)(2,1)}, bf16[4,256,256]{2,1,0:T(8,128)(2,1)}, u32[]{:S(2)}, u32[]{:S(2)}) collective-permute-start(bf16[4,256,256]{2,1,0:T(8,128)(2,1)} %pad_maximum_fusion.5), channel_id=1, source_target_pairs={{0,2},{1,3},{2,0},{3,1},{4,6},{5,7},{6,4},{7,5},{8,10},{9,11},{10,... | collective-permute-start | bytes 1572872 | tf_op jit(solution)/shard_map/ppermute | solution.py:29
  58.0 36.8 %collective-permute-start.10 = (bf16[4,256,256]{2,1,0:T(8,128)(2,1)}, bf16[4,256,256]{2,1,0:T(8,128)(2,1)}, u32[]{:S(2)}, u32[]{:S(2)}) collective-permute-start(bf16[4,256,256]{2,1,0:T(8,128)(2,1)} %collective-permute-done.3), channel_id=1, source_target_pairs={{0,2},{1,3},{2,0},{3,1},{4,6},{5,7},{6,4},{7,5},{8,10},{9,11},{10,... | collective-permute-start | bytes 1572872 | tf_op jit(solution)/shard_map/ppermute | solution.py:29
  59.4 35.4 %collective-permute-start.11 = (bf16[4,256,256]{2,1,0:T(8,128)(2,1)}, bf16[4,256,256]{2,1,0:T(8,128)(2,1)}, u32[]{:S(2)}, u32[]{:S(2)}) collective-permute-start(bf16[4,256,256]{2,1,0:T(8,128)(2,1)} %collective-permute-done.5), channel_id=1, source_target_pairs={{0,4},{4,0},{8,12},{12,8},{16,20},{20,16},{24,28},{28,24},{1,5},{5... | collective-permute-start | bytes 1572872 | tf_op jit(solution)/shard_map/ppermute | solution.py:29
  60.9 33.9 %collective-permute-start.8 = (bf16[4,256,256]{2,1,0:T(8,128)(2,1)}, bf16[4,256,256]{2,1,0:T(8,128)(2,1)}, u32[]{:S(2)}, u32[]{:S(2)}) collective-permute-start(bf16[4,256,256]{2,1,0:T(8,128)(2,1)} %collective-permute-done.3), channel_id=1, source_target_pairs={{0,4},{4,0},{8,12},{12,8},{16,20},{20,16},{24,28},{28,24},{1,5},{5... | collective-permute-start | bytes 1572872 | tf_op jit(solution)/shard_map/ppermute | solution.py:29
  61.4 59.6 %collective-permute-start.22 = (bf16[3,256,384]{2,1,0:T(8,128)(2,1)S(1)}, bf16[3,256,384]{2,1,0:T(8,128)(2,1)S(1)}, u32[]{:S(2)}, u32[]{:S(2)}) collective-permute-start(bf16[3,256,384]{2,1,0:T(8,128)(2,1)S(1)} %pad_maximum_fusion.2.rest_0_), channel_id=1, source_target_pairs={{0,16},{4,20},{8,24},{12,28},{16,0},{20,4},{24,8},{28,12},{1,17},{... | collective-permute-start | bytes 1769480 | tf_op jit(solution)/shard_map/ppermute | solution.py:29
  93.4 29.2 %collective-permute-start.23 = (bf16[3,256,384]{2,1,0:T(8,128)(2,1)S(1)}, bf16[3,256,384]{2,1,0:T(8,128)(2,1)}, u32[]{:S(2)}, u32[]{:S(2)}) collective-permute-start(bf16[3,256,384]{2,1,0:T(8,128)(2,1)S(1)} %pad_maximum_fusion.2.rest_0_), channel_id=1, source_target_pairs={{0,2},{1,3},{2,0},{3,1},{4,6},{5,7},{6,4},{7,5},{8,10},{9,11},{10,... | collective-permute-start | bytes 1769480 | tf_op jit(solution)/shard_map/ppermute | solution.py:29
  94.8 24.0 %collective-permute-start.12 = (bf16[4,256,256]{2,1,0:T(8,128)(2,1)}, bf16[4,256,256]{2,1,0:T(8,128)(2,1)}, u32[]{:S(2)}, u32[]{:S(2)}) collective-permute-start(bf16[4,256,256]{2,1,0:T(8,128)(2,1)} %collective-permute-done.8), channel_id=1, source_target_pairs={{0,2},{1,3},{2,0},{3,1},{4,6},{5,7},{6,4},{7,5},{8,10},{9,11},{10,... | collective-permute-start | bytes 1572872 | tf_op jit(solution)/shard_map/ppermute | solution.py:29
  97.9 61.0 %collective-permute-start.9 = (bf16[4,1024,256]{2,1,0:T(8,128)(2,1)}, bf16[4,1024,256]{2,1,0:T(8,128)(2,1)}, u32[]{:S(2)}, u32[]{:S(2)}) collective-permute-start(bf16[4,1024,256]{2,1,0:T(8,128)(2,1)} %constant_dynamic-update-slice_fusion), channel_id=1, source_target_pairs={{0,1},{1,0},{2,3},{3,2},{4,5},{5,4},{6,7},{7,6},{8,9},{9,8},{10,11... | collective-permute-start | bytes 6291464 | tf_op jit(solution)/shard_map/ppermute | solution.py:29
  99.5 53.5 %collective-permute-start.21 = (bf16[768,1024]{0,1:T(8,128)(2,1)}, bf16[768,1024]{0,1:T(8,128)(2,1)}, u32[]{:S(2)}, u32[]{:S(2)}) collective-permute-start(bf16[768,1024]{0,1:T(8,128)(2,1)} %copy.69), channel_id=1, source_target_pairs={{0,1},{1,0},{2,3},{3,2},{4,5},{5,4},{6,7},{7,6},{8,9},{9,8},{10,11... | collective-permute-start | bytes 4718600 | tf_op jit(solution)/shard_map/ppermute | solution.py:29
  120.8 38.4 %collective-permute-start.13 = (bf16[4,1024,256]{2,1,0:T(8,128)(2,1)}, bf16[4,1024,256]{2,1,0:T(8,128)(2,1)}, u32[]{:S(2)}, u32[]{:S(2)}) collective-permute-start(bf16[4,1024,256]{2,1,0:T(8,128)(2,1)} %constant_dynamic-update-slice_fusion.5), channel_id=1, source_target_pairs={{0,1},{1,0},{2,3},{3,2},{4,5},{5,4},{6,7},{7,6},{8,9},{9,8},{10,11... | collective-permute-start | bytes 6291464 | tf_op jit(solution)/shard_map/ppermute | solution.py:29
  122.6 28.1 %collective-permute-start.25 = (bf16[3,256,384]{2,1,0:T(8,128)(2,1)}, bf16[3,256,384]{2,1,0:T(8,128)(2,1)}, u32[]{:S(2)}, u32[]{:S(2)}) collective-permute-start(bf16[3,256,384]{2,1,0:T(8,128)(2,1)} %pad_maximum_fusion.3.rest_0_), channel_id=1, source_target_pairs={{0,16},{4,20},{8,24},{12,28},{16,0},{20,4},{24,8},{28,12},{1,17},{... | collective-permute-start | bytes 1769480 | tf_op jit(solution)/shard_map/ppermute | solution.py:29
  150.7 22.9 %collective-permute-start.26 = (bf16[3,256,384]{2,1,0:T(8,128)(2,1)S(1)}, bf16[3,256,384]{2,1,0:T(8,128)(2,1)}, u32[]{:S(2)}, u32[]{:S(2)}) collective-permute-start(bf16[3,256,384]{2,1,0:T(8,128)(2,1)S(1)} %collective-permute-done.22.rest_1_), channel_id=1, source_target_pairs={{0,4},{4,0},{8,12},{12,8},{16,20},{20,16},{24,28},{28,24},{1,5},{5... | collective-permute-start | bytes 1769480 | tf_op jit(solution)/shard_map/ppermute | solution.py:29
  151.2 22.4 %collective-permute-start.27 = (bf16[3,256,384]{2,1,0:T(8,128)(2,1)S(1)}, bf16[3,256,384]{2,1,0:T(8,128)(2,1)S(1)}, u32[]{:S(2)}, u32[]{:S(2)}) collective-permute-start(bf16[3,256,384]{2,1,0:T(8,128)(2,1)S(1)} %collective-permute-done.22.rest_1_), channel_id=1, source_target_pairs={{0,2},{1,3},{2,0},{3,1},{4,6},{5,7},{6,4},{7,5},{8,10},{9,11},{10,... | collective-permute-start | bytes 1769480 | tf_op jit(solution)/shard_map/ppermute | solution.py:29
  153.0 25.6 %collective-permute-start.28 = (bf16[3,256,384]{2,1,0:T(8,128)(2,1)}, bf16[3,256,384]{2,1,0:T(8,128)(2,1)S(1)}, u32[]{:S(2)}, u32[]{:S(2)}) collective-permute-start(bf16[3,256,384]{2,1,0:T(8,128)(2,1)} %collective-permute-done.23.rest_4_), channel_id=1, source_target_pairs={{0,4},{4,0},{8,12},{12,8},{16,20},{20,16},{24,28},{28,24},{1,5},{5... | collective-permute-start | bytes 1769480 | tf_op jit(solution)/shard_map/ppermute | solution.py:29
  159.2 27.7 %collective-permute-start.30 = (bf16[3,256,384]{2,1,0:T(8,128)(2,1)}, bf16[3,256,384]{2,1,0:T(8,128)(2,1)S(1)}, u32[]{:S(2)}, u32[]{:S(2)}) collective-permute-start(bf16[3,256,384]{2,1,0:T(8,128)(2,1)} %pad_maximum_fusion.4.rest_0_), channel_id=1, source_target_pairs={{0,16},{4,20},{8,24},{12,28},{16,0},{20,4},{24,8},{28,12},{1,17},{... | collective-permute-start | bytes 1769480 | tf_op jit(solution)/shard_map/ppermute | solution.py:29
  193.5 20.9 %collective-permute-start.31 = (bf16[768,1024]{0,1:T(8,128)(2,1)}, bf16[768,1024]{0,1:T(8,128)(2,1)S(1)}, u32[]{:S(2)}, u32[]{:S(2)}) collective-permute-start(bf16[768,1024]{0,1:T(8,128)(2,1)} %multiply_convert_fusion.2), channel_id=1, source_target_pairs={{0,1},{1,0},{2,3},{3,2},{4,5},{5,4},{6,7},{7,6},{8,9},{9,8},{10,11... | collective-permute-start | bytes 4718600 | tf_op jit(solution)/shard_map/ppermute | solution.py:29
  210.3 51.5 %collective-permute-start.34 = (bf16[3,256,384]{2,1,0:T(8,128)(2,1)}, bf16[3,256,384]{2,1,0:T(8,128)(2,1)}, u32[]{:S(2)}, u32[]{:S(2)}) collective-permute-start(bf16[3,256,384]{2,1,0:T(8,128)(2,1)} %collective-permute-done.25.rest_1_), channel_id=1, source_target_pairs={{0,4},{4,0},{8,12},{12,8},{16,20},{20,16},{24,28},{28,24},{1,5},{5... | collective-permute-start | bytes 1769480 | tf_op jit(solution)/shard_map/ppermute | solution.py:29
  210.9 51.0 %collective-permute-start.35 = (bf16[3,256,384]{2,1,0:T(8,128)(2,1)}, bf16[3,256,384]{2,1,0:T(8,128)(2,1)}, u32[]{:S(2)}, u32[]{:S(2)}) collective-permute-start(bf16[3,256,384]{2,1,0:T(8,128)(2,1)} %collective-permute-done.25.rest_1_), channel_id=1, source_target_pairs={{0,2},{1,3},{2,0},{3,1},{4,6},{5,7},{6,4},{7,5},{8,10},{9,11},{10,... | collective-permute-start | bytes 1769480 | tf_op jit(solution)/shard_map/ppermute | solution.py:29
  211.8 50.0 %collective-permute-start.36 = (bf16[3,256,384]{2,1,0:T(8,128)(2,1)}, bf16[3,256,384]{2,1,0:T(8,128)(2,1)}, u32[]{:S(2)}, u32[]{:S(2)}) collective-permute-start(bf16[3,256,384]{2,1,0:T(8,128)(2,1)} %collective-permute-done.29.rest_4_), channel_id=1, source_target_pairs={{0,4},{4,0},{8,12},{12,8},{16,20},{20,16},{24,28},{28,24},{1,5},{5... | collective-permute-start | bytes 1769480 | tf_op jit(solution)/shard_map/ppermute | solution.py:29
  213.3 48.5 %collective-permute-start.37 = (bf16[3,256,384]{2,1,0:T(8,128)(2,1)}, bf16[3,256,384]{2,1,0:T(8,128)(2,1)}, u32[]{:S(2)}, u32[]{:S(2)}) collective-permute-start(bf16[3,256,384]{2,1,0:T(8,128)(2,1)} %pad_maximum_fusion.4.rest_0_), channel_id=1, source_target_pairs={{0,2},{1,3},{2,0},{3,1},{4,6},{5,7},{6,4},{7,5},{8,10},{9,11},{10,... | collective-permute-start | bytes 1769480 | tf_op jit(solution)/shard_map/ppermute | solution.py:29
  276.6 37.0 %collective-permute-start.40 = (bf16[3,256,384]{2,1,0:T(8,128)(2,1)S(1)}, bf16[3,256,384]{2,1,0:T(8,128)(2,1)S(1)}, u32[]{:S(2)}, u32[]{:S(2)}) collective-permute-start(bf16[3,256,384]{2,1,0:T(8,128)(2,1)S(1)} %copy-done.84), channel_id=1, source_target_pairs={{0,4},{4,0},{8,12},{12,8},{16,20},{20,16},{24,28},{28,24},{1,5},{5... | collective-permute-start | bytes 1769480 | tf_op jit(solution)/shard_map/ppermute | solution.py:29
  277.1 36.5 %collective-permute-start.41 = (bf16[3,256,384]{2,1,0:T(8,128)(2,1)S(1)}, bf16[3,256,384]{2,1,0:T(8,128)(2,1)S(1)}, u32[]{:S(2)}, u32[]{:S(2)}) collective-permute-start(bf16[3,256,384]{2,1,0:T(8,128)(2,1)S(1)} %copy-done.84), channel_id=1, source_target_pairs={{0,2},{1,3},{2,0},{3,1},{4,6},{5,7},{6,4},{7,5},{8,10},{9,11},{10,... | collective-permute-start | bytes 1769480 | tf_op jit(solution)/shard_map/ppermute | solution.py:29
  278.2 35.5 %collective-permute-start.42 = (bf16[3,256,384]{2,1,0:T(8,128)(2,1)}, bf16[3,256,384]{2,1,0:T(8,128)(2,1)S(1)}, u32[]{:S(2)}, u32[]{:S(2)}) collective-permute-start(bf16[3,256,384]{2,1,0:T(8,128)(2,1)} %collective-permute-done.37.rest_4_), channel_id=1, source_target_pairs={{0,4},{4,0},{8,12},{12,8},{16,20},{20,16},{24,28},{28,24},{1,5},{5... | collective-permute-start | bytes 1769480 | tf_op jit(solution)/shard_map/ppermute | solution.py:29
  279.7 34.0 %collective-permute-start.43 = (bf16[3,256,384]{2,1,0:T(8,128)(2,1)S(1)}, bf16[3,256,384]{2,1,0:T(8,128)(2,1)S(1)}, u32[]{:S(2)}, u32[]{:S(2)}) collective-permute-start(bf16[3,256,384]{2,1,0:T(8,128)(2,1)S(1)} %get-tuple-element.250), channel_id=1, source_target_pairs={{0,2},{1,3},{2,0},{3,1},{4,6},{5,7},{6,4},{7,5},{8,10},{9,11},{10,... | collective-permute-start | bytes 1769480 | tf_op jit(solution)/shard_map/ppermute | solution.py:29
  327.2 41.6 %collective-permute-start.46 = (bf16[3,256,384]{2,1,0:T(8,128)(2,1)S(1)}, bf16[3,256,384]{2,1,0:T(8,128)(2,1)S(1)}, u32[]{:S(2)}, u32[]{:S(2)}) collective-permute-start(bf16[3,256,384]{2,1,0:T(8,128)(2,1)S(1)} %get-tuple-element.270), channel_id=1, source_target_pairs={{0,4},{4,0},{8,12},{12,8},{16,20},{20,16},{24,28},{28,24},{1,5},{5... | collective-permute-start | bytes 1769480 | tf_op jit(solution)/shard_map/ppermute | solution.py:29
  329.0 42.0 %collective-permute-start.47 = (bf16[3,256,384]{2,1,0:T(8,128)(2,1)S(1)}, bf16[3,256,384]{2,1,0:T(8,128)(2,1)}, u32[]{:S(2)}, u32[]{:S(2)}) collective-permute-start(bf16[3,256,384]{2,1,0:T(8,128)(2,1)S(1)} %get-tuple-element.271), channel_id=1, source_target_pairs={{0,2},{1,3},{2,0},{3,1},{4,6},{5,7},{6,4},{7,5},{8,10},{9,11},{10,... | collective-permute-start | bytes 1769480 | tf_op jit(solution)/shard_map/ppermute | solution.py:29
  330.0 41.0 %collective-permute-start.48 = (bf16[3,256,384]{2,1,0:T(8,128)(2,1)S(1)}, bf16[3,256,384]{2,1,0:T(8,128)(2,1)}, u32[]{:S(2)}, u32[]{:S(2)}) collective-permute-start(bf16[3,256,384]{2,1,0:T(8,128)(2,1)S(1)} %get-tuple-element.272), channel_id=1, source_target_pairs={{0,4},{4,0},{8,12},{12,8},{16,20},{20,16},{24,28},{28,24},{1,5},{5... | collective-permute-start | bytes 1769480 | tf_op jit(solution)/shard_map/ppermute | solution.py:29
  330.3 40.7 %collective-permute-start.49 = (bf16[3,256,384]{2,1,0:T(8,128)(2,1)S(1)}, bf16[3,256,384]{2,1,0:T(8,128)(2,1)}, u32[]{:S(2)}, u32[]{:S(2)}) collective-permute-start(bf16[3,256,384]{2,1,0:T(8,128)(2,1)S(1)} %get-tuple-element.273), channel_id=1, source_target_pairs={{0,2},{1,3},{2,0},{3,1},{4,6},{5,7},{6,4},{7,5},{8,10},{9,11},{10,... | collective-permute-start | bytes 1769480 | tf_op jit(solution)/shard_map/ppermute | solution.py:29
  383.0 22.6 %collective-permute-start.52 = (bf16[3,256,384]{2,1,0:T(8,128)(2,1)S(1)}, bf16[3,256,384]{2,1,0:T(8,128)(2,1)S(1)}, u32[]{:S(2)}, u32[]{:S(2)}) collective-permute-start(bf16[3,256,384]{2,1,0:T(8,128)(2,1)S(1)} %add_convert_fusion.8), channel_id=1, source_target_pairs={{0,4},{4,0},{8,12},{12,8},{16,20},{20,16},{24,28},{28,24},{1,5},{5... | collective-permute-start | bytes 1769480 | tf_op jit(solution)/shard_map/ppermute | solution.py:29
  384.8 20.8 %collective-permute-start.53 = (bf16[3,256,384]{2,1,0:T(8,128)(2,1)S(1)}, bf16[3,256,384]{2,1,0:T(8,128)(2,1)S(1)}, u32[]{:S(2)}, u32[]{:S(2)}) collective-permute-start(bf16[3,256,384]{2,1,0:T(8,128)(2,1)S(1)} %add_convert_fusion.7), channel_id=1, source_target_pairs={{0,2},{1,3},{2,0},{3,1},{4,6},{5,7},{6,4},{7,5},{8,10},{9,11},{10,... | collective-permute-start | bytes 1769480 | tf_op jit(solution)/shard_map/ppermute | solution.py:29
  385.8 25.1 %collective-permute-start.54 = (bf16[3,256,384]{2,1,0:T(8,128)(2,1)}, bf16[3,256,384]{2,1,0:T(8,128)(2,1)S(1)}, u32[]{:S(2)}, u32[]{:S(2)}) collective-permute-start(bf16[3,256,384]{2,1,0:T(8,128)(2,1)} %copy-done.80), channel_id=1, source_target_pairs={{0,4},{4,0},{8,12},{12,8},{16,20},{20,16},{24,28},{28,24},{1,5},{5... | collective-permute-start | bytes 1769480 | tf_op jit(solution)/shard_map/ppermute | solution.py:29
  388.1 24.3 %collective-permute-start.55 = (bf16[3,256,384]{2,1,0:T(8,128)(2,1)}, bf16[3,256,384]{2,1,0:T(8,128)(2,1)S(1)}, u32[]{:S(2)}, u32[]{:S(2)}) collective-permute-start(bf16[3,256,384]{2,1,0:T(8,128)(2,1)} %copy-done.79), channel_id=1, source_target_pairs={{0,2},{1,3},{2,0},{3,1},{4,6},{5,7},{6,4},{7,5},{8,10},{9,11},{10,... | collective-permute-start | bytes 1769480 | tf_op jit(solution)/shard_map/ppermute | solution.py:29
  425.5 26.8 %collective-permute-start.59 = (bf16[3,256,384]{2,1,0:T(8,128)(2,1)}, bf16[3,256,384]{2,1,0:T(8,128)(2,1)S(1)}, u32[]{:S(2)}, u32[]{:S(2)}) collective-permute-start(bf16[3,256,384]{2,1,0:T(8,128)(2,1)} %copy-done.78), channel_id=1, source_target_pairs={{0,4},{4,0},{8,12},{12,8},{16,20},{20,16},{24,28},{28,24},{1,5},{5... | collective-permute-start | bytes 1769480 | tf_op jit(solution)/shard_map/ppermute | solution.py:29
  427.0 25.8 %collective-permute-start.60 = (bf16[3,256,384]{2,1,0:T(8,128)(2,1)}, bf16[3,256,384]{2,1,0:T(8,128)(2,1)S(1)}, u32[]{:S(2)}, u32[]{:S(2)}) collective-permute-start(bf16[3,256,384]{2,1,0:T(8,128)(2,1)} %copy-done.77), channel_id=1, source_target_pairs={{0,2},{1,3},{2,0},{3,1},{4,6},{5,7},{6,4},{7,5},{8,10},{9,11},{10,... | collective-permute-start | bytes 1769480 | tf_op jit(solution)/shard_map/ppermute | solution.py:29
  427.4 27.8 %collective-permute-start.61 = (bf16[3,256,384]{2,1,0:T(8,128)(2,1)}, bf16[3,256,384]{2,1,0:T(8,128)(2,1)S(1)}, u32[]{:S(2)}, u32[]{:S(2)}) collective-permute-start(bf16[3,256,384]{2,1,0:T(8,128)(2,1)} %add_convert_fusion.4), channel_id=1, source_target_pairs={{0,16},{4,20},{8,24},{12,28},{16,0},{20,4},{24,8},{28,12},{1,17},{... | collective-permute-start | bytes 1769480 | tf_op jit(solution)/shard_map/ppermute | solution.py:29
  468.8 27.7 %collective-permute-start.65 = (bf16[3,256,384]{2,1,0:T(8,128)(2,1)S(1)}, bf16[3,256,384]{2,1,0:T(8,128)(2,1)S(1)}, u32[]{:S(2)}, u32[]{:S(2)}) collective-permute-start(bf16[3,256,384]{2,1,0:T(8,128)(2,1)S(1)} %add_convert_fusion.3), channel_id=1, source_target_pairs={{0,4},{4,0},{8,12},{12,8},{16,20},{20,16},{24,28},{28,24},{1,5},{5... | collective-permute-start | bytes 1769480 | tf_op jit(solution)/shard_map/ppermute | solution.py:29
  470.3 26.2 %collective-permute-start.66 = (bf16[3,256,384]{2,1,0:T(8,128)(2,1)}, bf16[3,256,384]{2,1,0:T(8,128)(2,1)S(1)}, u32[]{:S(2)}, u32[]{:S(2)}) collective-permute-start(bf16[3,256,384]{2,1,0:T(8,128)(2,1)} %copy-done.75), channel_id=1, source_target_pairs={{0,2},{1,3},{2,0},{3,1},{4,6},{5,7},{6,4},{7,5},{8,10},{9,11},{10,... | collective-permute-start | bytes 1769480 | tf_op jit(solution)/shard_map/ppermute | solution.py:29
  472.0 26.0 %collective-permute-start.67 = (bf16[3,256,384]{2,1,0:T(8,128)(2,1)S(1)}, bf16[3,256,384]{2,1,0:T(8,128)(2,1)S(1)}, u32[]{:S(2)}, u32[]{:S(2)}) collective-permute-start(bf16[3,256,384]{2,1,0:T(8,128)(2,1)S(1)} %add_convert_fusion.2), channel_id=1, source_target_pairs={{0,2},{1,3},{2,0},{3,1},{4,6},{5,7},{6,4},{7,5},{8,10},{9,11},{10,... | collective-permute-start | bytes 1769480 | tf_op jit(solution)/shard_map/ppermute | solution.py:29
  472.3 27.5 %collective-permute-start.68 = (bf16[3,256,384]{2,1,0:T(8,128)(2,1)S(1)}, bf16[3,256,384]{2,1,0:T(8,128)(2,1)S(1)}, u32[]{:S(2)}, u32[]{:S(2)}) collective-permute-start(bf16[3,256,384]{2,1,0:T(8,128)(2,1)S(1)} %add_convert_fusion.1), channel_id=1, source_target_pairs={{0,16},{4,20},{8,24},{12,28},{16,0},{20,4},{24,8},{28,12},{1,17},{... | collective-permute-start | bytes 1769480 | tf_op jit(solution)/shard_map/ppermute | solution.py:29
  502.8 29.8 %collective-permute-start.72 = (bf16[3,256,384]{2,1,0:T(8,128)(2,1)}, bf16[3,256,384]{2,1,0:T(8,128)(2,1)S(1)}, u32[]{:S(2)}, u32[]{:S(2)}) collective-permute-start(bf16[3,256,384]{2,1,0:T(8,128)(2,1)} %add_convert_fusion), channel_id=1, source_target_pairs={{0,16},{4,20},{8,24},{12,28},{16,0},{20,4},{24,8},{28,12},{1,17},{... | collective-permute-start | bytes 1769480 | tf_op jit(solution)/shard_map/ppermute | solution.py:29
  502.8 30.8 %collective-permute-start.69 = (bf16[4,256,256]{2,1,0:T(8,128)(2,1)}, bf16[4,256,256]{2,1,0:T(8,128)(2,1)}, u32[]{:S(2)}, u32[]{:S(2)}) collective-permute-start(bf16[4,256,256]{2,1,0:T(8,128)(2,1)} %add_convert_fusion.17), channel_id=1, source_target_pairs={{0,4},{4,0},{8,12},{12,8},{16,20},{20,16},{24,28},{28,24},{1,5},{5... | collective-permute-start | bytes 1572872 | tf_op jit(solution)/shard_map/ppermute | solution.py:29
  503.3 27.1 %collective-permute-start.71 = (bf16[4,256,256]{2,1,0:T(8,128)(2,1)}, bf16[4,256,256]{2,1,0:T(8,128)(2,1)}, u32[]{:S(2)}, u32[]{:S(2)}) collective-permute-start(bf16[4,256,256]{2,1,0:T(8,128)(2,1)} %get-tuple-element.336), channel_id=1, source_target_pairs={{0,4},{4,0},{8,12},{12,8},{16,20},{20,16},{24,28},{28,24},{1,5},{5... | collective-permute-start | bytes 1572872 | tf_op jit(solution)/shard_map/ppermute | solution.py:29
  504.8 28.7 %collective-permute-start.73 = (bf16[4,256,256]{2,1,0:T(8,128)(2,1)}, bf16[4,256,256]{2,1,0:T(8,128)(2,1)}, u32[]{:S(2)}, u32[]{:S(2)}) collective-permute-start(bf16[4,256,256]{2,1,0:T(8,128)(2,1)} %get-tuple-element.338), channel_id=1, source_target_pairs={{0,2},{1,3},{2,0},{3,1},{4,6},{5,7},{6,4},{7,5},{8,10},{9,11},{10,... | collective-permute-start | bytes 1572872 | tf_op jit(solution)/shard_map/ppermute | solution.py:29
  552.2 25.5 %collective-permute-start.76 = (bf16[4,256,256]{2,1,0:T(8,128)(2,1)S(1)}, bf16[4,256,256]{2,1,0:T(8,128)(2,1)S(1)}, u32[]{:S(2)}, u32[]{:S(2)}) collective-permute-start(bf16[4,256,256]{2,1,0:T(8,128)(2,1)S(1)} %add_convert_fusion.9), channel_id=1, source_target_pairs={{0,16},{4,20},{8,24},{12,28},{16,0},{20,4},{24,8},{28,12},{1,17},{... | collective-permute-start | bytes 1572872 | tf_op jit(solution)/shard_map/ppermute | solution.py:29
  (190 other events, 2360.3 us)

commit v7 on v6

--- a/solution.py
+++ b/solution.py
@@ -188,65 +188,72 @@
     return jnp.dot(left, right, preferred_element_type=F32)
 
 
-def ffn_kernel(first, h_own, h_other, ht_own, ht_other, c, ct, *rest):
-    pieces, rest = rest[:8], rest[8:]
-    grads, (branch, back, w, act, dgate, dup) = rest[-14:-6], rest[-6:]
+def ffn_kernel(first, final, *refs):
+    tokens, pieces, rest = refs[:8], refs[8:16], refs[16:]
+    h, ht, c, ct = tokens[:2], tokens[2:4], tokens[4:6], tokens[6:]
+    branch, w, act, dgate, dup = rest[-5:]
+    back, outs = rest[-6], rest[: -6] if first else rest[1:-6]
+    grads, branch_own, branch_other = outs[:8], outs[8], outs[9]
     deep, half = pieces[0].shape[1:]
     spots = [
         (pl.ds(i % 4 * deep, deep), pl.ds(i // 4 * half, half)) for i in range(8)
     ]
-    rows = c.shape[0]
-    own = rows // 2
+    own = h[0].shape[0]
     tall = 384
 
     @pl.when(pl.program_id(0) == 0)
     def _():
-        for i, total in enumerate((branch, back)):
-            total[...] = jnp.zeros_like(total) if first else rest[i][...]
+        branch[...] = jnp.zeros_like(branch)
+        back[...] = jnp.zeros_like(back) if first else rest[0][...]
 
     for piece, (deep_span, span) in zip(pieces, spots):
         w[:, deep_span, span] = piece[...]
-    for start in range(0, rows, tall):
-        span = pl.ds(start, tall)
-        h = h_own[span, :] if start < own else h_other[pl.ds(start - own, tall), :]
-        gate = nn(h, w[0])
-        up = nn(h, w[1])
-        da = nn(c[span, :], w[2])
+    for start in range(0, 2 * own, tall):
+        span, part = pl.ds(start, tall), pl.ds(start % own, tall)
+        gate = nn(h[start // own][part, :], w[0])
+        up = nn(h[start // own][part, :], w[1])
+        da = nn(c[start // own][part, :], w[2])
         sigma = 1.0 / (1.0 + jnp.exp(-gate))
         silu = gate * sigma
         act[span, :] = (silu * up).astype(BF)
         dup[span, :] = (da * silu).astype(BF)
         dgate[span, :] = (da * up * (sigma + silu * (1.0 - sigma))).astype(BF)
-    for k, right in enumerate((dgate, dup, act)):
-        if k < 2:
-            grad = nn(ht_own[...], right[:own, :]) + nn(ht_other[...], right[own:, :])
-        else:
-            grad = nn(ct[...], right[...])
-        grad = grad.astype(BF)
+    for k, (left, right) in enumerate(((ht, dgate), (ht, dup), (ct, act))):
+        grad = (nn(left[0][...], right[:own, :]) + nn(left[1][...], right[own:, :])).astype(BF)
         for i, out in enumerate(grads):
             out[k] = grad[i % 4 * deep : (i % 4 + 1) * deep, i // 4 * half : (i // 4 + 1) * half]
-    for start in range(0, rows, tall):
+    for start in range(0, 2 * own, tall):
         span = pl.ds(start, tall)
         branch[span, :] += nt(act[span, :], w[2])
         back[span, :] += nt(dgate[span, :], w[0]) + nt(dup[span, :], w[1])
 
-
-def ffn(tokens, pieces, sums):
-    rows, width = tokens[4].shape
+    @pl.when(pl.program_id(0) == pl.num_programs(0) - 1)
+    def _():
+        branch_own[...] = branch[:own, :].astype(BF)
+        branch_other[...] = branch[own:, :].astype(BF)
+        if final:
+            outs[10][...] = back[own:, :].astype(BF)
+
+
+def ffn(tokens, pieces, sums, final):
+    own, width = tokens[0].shape
+    rows = 2 * own
     planes, deep, cols = pieces[0].shape
     tile = 128
     block = pl.BlockSpec((planes, deep, tile), lambda j: (0, 0, j))
     vmem = pl.BlockSpec(memory_space=pltpu.VMEM)
-    grad = jax.ShapeDtypeStruct(pieces[0].shape, BF)
+    grad = pltpu.HBM(pieces[0].shape, BF)
     part = jax.ShapeDtypeStruct((rows, width), F32)
+    other = [pltpu.HBM((own, width), BF)] * (3 if final else 2)
+    count = 8 + len(other)
     out = pl.pallas_call(
-        functools.partial(ffn_kernel, not sums),
+        functools.partial(ffn_kernel, not sums, final),
         grid=(cols // tile,),
-        out_shape=(grad,) * 8 + (part, part),
-        in_specs=[vmem] * 6 + [block] * 8 + [vmem] * len(sums),
-        out_specs=(block,) * 8 + (vmem, vmem),
-        input_output_aliases={14: 8, 15: 9} if sums else {},
-        scratch_shapes=[pltpu.VMEM((planes, width, 2 * tile), BF)]
+        out_shape=(*[grad] * 8, *other, part),
+        in_specs=[vmem] * 8 + [block] * 8 + [vmem] * len(sums),
+        out_specs=(*[block] * 8, *[whole((own, width))] * len(other), vmem),
+        input_output_aliases={16: count} if sums else {},
+        scratch_shapes=[pltpu.VMEM((rows, width), F32), pltpu.VMEM((planes, width, 2 * tile), BF)]
         + [pltpu.VMEM((rows, 2 * tile), BF)] * 3,
         compiler_params=params(),
         cost_estimate=pl.CostEstimate(
@@ -256,13 +263,12 @@
         ),
         name="ffn",
     )(*tokens, *pieces, *sums)
-    return out[:8], out[8:]
+    return out[:8], out[8:10], out[10:-1], out[-1:]
 
 
 def middle_kernel(order, middle, scale, gain, cot, *rest):
     block_out, grad, grad_low, gain_grad = rest[-4:]
-    half = (len(rest) - 4) // 2
-    branches, backs = rest[:half], rest[half : 2 * half]
+    branches, backs = rest[: len(rest) - 6], rest[-6:-4]
     x2, r2, up = middle[...], scale[...], backs[0][...].astype(F32)
     for ref in backs[1:]:
         up = up + ref[...].astype(F32)
@@ -317,10 +323,10 @@
     rows, width = middle.shape
     tile = 128
     smem, row, column, single = row_specs(tile, width)
-    count = len(branches)
+    count = 5 + len(branches) + len(backs)
 
     def kernel(*refs):
-        middle_kernel(*refs[: 5 + 2 * count], *refs[5 + 2 * count + len(deps) :])
+        middle_kernel(*refs[:count], *refs[count + len(deps) :])
 
     return pl.pallas_call(
         kernel,
@@ -331,11 +337,11 @@
             jax.ShapeDtypeStruct((rows, width), BF),
             jax.ShapeDtypeStruct((1, width), F32),
         ),
-        in_specs=[smem, row, column, single, row] + [row] * (2 * count) + [ANY] * len(deps),
+        in_specs=[smem, row, column, single, row] + [row] * (count - 5) + [ANY] * len(deps),
         out_specs=(row, row, row, single),
         compiler_params=params(),
         cost_estimate=pl.CostEstimate(
-            flops=30 * rows * width, bytes_accessed=(14 + 8 * count) * rows * width, transcendentals=0
+            flops=30 * rows * width, bytes_accessed=(4 + 2 * count) * rows * width, transcendentals=0
         ),
         name="middle_back",
     )(order, middle, scale, gain, cot, *branches, *backs, *deps)
@@ -527,18 +533,19 @@
     def pieces_of(i):
         return [own[i], zb[i], xa[i], xb[i], ya[i], yb[i], da[i], db[i]]
 
-    small = jnp.concatenate([norm_gains, conv_kernel], 0)[:, None, :]
+    small = jnp.concatenate([norm_gains, conv_kernel], 0)[:, None, None, None, None, :]
+    small_z = phase([], [(small, "dp", code) for code in range(2, dp_size, 2)])
     before = lax.ppermute(
         tokens[rows - HALO :], "tensor", [(i, i + 1) for i in range(t_size - 1)]
     )
-    small_t = phase([], [(small, "tensor", code) for code in range(1, t_size)])
-    last = first_rows([0, 1], [])
-    small = join([small, *small_t], 1)
-    small_x = phase([*last, small], [(small, "dp", 1)])
+    last = first_rows([0, 1], small_z)
+    small = join([small, *small_z], 1)
+    small = join([small, swap(small, "dp", 1)], 2)
+    small = join([small, *[swap(small, "tensor", code) for code in range(2, t_size, 2)]], 3)
+    small = join([small, swap(small, "tensor", 1)], 4)
+    last = [*last, small, before]
     xa[0], ya[0], zb[0] = got = phase(last, [by_x(own[0]), by_y(own[0]), by_z(own[0])])
     later = first_rows(range(2, PARTS + 1), last)
-    small = join([small, *small_x], 1)
-    small_z = phase([*got, small], [(small, "dp", code) for code in range(2, dp_size, 2)])
     xb[0], yb[0], da[0], ya[1], zb[1] = got = phase(
         [*got, *later], [by_x(zb[0]), by_y(zb[0]), by_x(ya[0]), by_y(own[1]), by_z(own[1])]
     )
@@ -546,9 +553,7 @@
     db[0], xa[1], zb[2], cot_other = phase(
         got[:3], [by_y(xb[0]), by_x(own[1]), by_z(own[2]), (cot, "tensor", 1)]
     )
-    small = join([small, *small_z], 1)
-
-    small = small.reshape(small.shape[0], dp_size, t_size, small.shape[2])
+    small = small.reshape(small.shape[0], dp_size, t_size, small.shape[-1])
     for axis, index, size_axis in ((1, dp_index, dp_size), (2, t_index, t_size)):
         for i in range(size_axis.bit_length() - 1):
             shape = small.shape
@@ -578,9 +583,8 @@
     extended = x_ext.astype(F32)
     scale_ext = rms_scale(extended)
     normed_ext = (extended * scale_ext * gains[0]).astype(BF)
-    c = join([cot, cot_other], 0)
-    ct = c.T
-    (normed_ext,) = ordered([normed_ext], [c, ct])
+    ct, ct_other = cot.T, cot_other.T
+    (normed_ext,) = ordered([normed_ext], [ct, ct_other])
     values, scale_one, normed_one = extended[HALO:], scale_ext[HALO:], normed_ext[HALO:]
     near, far = join(pieces_of(0)[:4], wide), join(pieces_of(0)[4:], wide)
     wm = [near, other_core(near), far, other_core(far)]
@@ -607,14 +611,17 @@
     normed_two = (middle * scale_two * gains[1]).astype(BF)
 
     normed_other = other_core(normed_two)
-    tokens_both = (normed_two, normed_other, normed_two.T, normed_other.T, c, ct)
-    sums, grads = [], {}
+    tokens_both = (normed_two, normed_other, normed_two.T, normed_other.T)
+    tokens_both += (cot, cot_other, ct, ct_other)
+    sums, grads, back_other, branch_own, branch_other = [], {}, [], [], []
     xb[1], yb[1], da[1], ya[2], zb[3] = got = ordered(got, [normed_two])
     db[1], xa[2] = got = phase(got, [by_y(xb[1]), by_x(own[2])])
 
     def run(i):
-        nonlocal sums
-        grads[i], sums = ffn(tokens_both, pieces_of(i), list(sums))
+        nonlocal sums, back_other
+        grads[i], branches, back_other, sums = ffn(tokens_both, pieces_of(i), list(sums), i == PARTS)
+        branch_own.append(branches[0])
+        branch_other.append(branches[1])
         return grads[i]
 
     got = phase(got, [by_x(zb[2]), by_y(zb[2]), by_x(ya[2]), by_y(own[3])])
@@ -638,12 +645,15 @@
         got, [by_x(grads[1][2]), by_y(grads[1][7]), by_x(grads[2][6]), by_y(grads[2][7])]
     )
     axa[1], adb[1], ada[2], adb[2] = got = ordered(got, run(3)[:1])
-    branch, back = ordered(sums, got)
-    branch_in, back_in = [other_core(value[rows:].astype(BF)) for value in (branch, back)]
+    back_other, back = ordered([*back_other, *sums], got)
+    back_in = other_core(back_other)
+    branch_in = other_core(
+        functools.reduce(jnp.add, [value.astype(F32) for value in branch_other]).astype(BF)
+    )
     deps = got
     got = phase(got, [sum_xb(1), sum_ya(1), by_x(grads[2][2]), by_y(grads[2][5])])
     block_out, middle_grad, mixed_grad, gain_two_grad = middle_back(
-        order, middle, scale_two, gains[1:2], cot, [branch, branch_in], [back, back_in], deps
+        order, middle, scale_two, gains[1:2], cot, [*branch_own, branch_in], [back, back_in], deps
     )
 
     gated_grad = mm("td,dc->tc", mixed_grad, wout_all)

time: 598 us -> 599 us (level)
  waiting for transfers between devices: 194 us -> 216 us
  local copies, waits for them, and re-layouts: 89.9 us -> 74.7 us
    ppermute x86 -> x85, waiting for transfers between devices: 194 us -> 216 us  [swap(): return lax.ppermute(values, axis, [(i, i ^ bit) for i in range(size)])]
    unnamed x321 -> x296, local copies, waits for them, and re-layouts: 54.5 us -> 44.8 us
    ppermute x86 -> x85, starting transfers between devices: 80.9 us -> 81.3 us  [swap(): return lax.ppermute(values, axis, [(i, i ^ bit) for i in range(size)])]
  transfers between devices with their start and end apart: 88 -> 87, of which waited for: 35 -> 42; matrix products, arithmetic and copies ran while one was open for 22% -> 21% of each run, Pallas kernels for 19% -> 19%
where the time goes in v7:
time: 599 us; the launch traced here: 594 us
  waiting for transfers between devices  216 us (36%)
  Pallas kernels  118 us (20%)
  starting transfers between devices  83.9 us (14%)
  local copies, waits for them, and re-layouts  74.7 us (12%)
  other arithmetic  74.5 us (12%)
  matrix products  18.9 us (3%)
  between operations  8.1 us (1%)
    ppermute x85, waiting for transfers between devices, swap(): return lax.ppermute(values, axis, [(i, i ^ bit) for i in range(size)])  216 us
    pallas_call x3, Pallas kernels, ffn(): pl.pallas_call(functools.partial(ffn_kernel, not sums, final), grid=(cols...  89.6 us
    ppermute x85, starting transfers between devices, swap(): return lax.ppermute(values, axis, [(i, i ^ bit) for i in range(size)])  81.3 us
    unnamed x296, local copies, waits for them, and re-layouts  44.8 us
    dot_general x4, matrix products, mm(): return jnp.einsum(spec, left, right, preferred_element_type=F32).astype(out)  18.9 us
    convert_element_type x10, other arithmetic, plus(): return (left.astype(F32) + right.astype(F32)).astype(BF)  17.1 us
  transfers between devices with their start and end apart: 87, of which 42 were waited for; matrix products, arithmetic and copies ran while one was open for 21% of the time, Pallas kernels for 19%

profile of v7, /device:TPU:0, one launch (start us, length us, event | category | flops | bytes accessed | tf_op | source)
XLA Modules:
  0.0 593.7 jit_solution(12781609695158311828)
XLA Ops:
  1.4 3.0 collective-permute-start.1
  29.0 7.2 %collective-permute-done.4 = bf16[4,128,256]{2,1,0:T(8,128)(2,1)S(1)} collective-permute-done((bf16[4,128,256]{2,1,0:T(8,128)(2,1)}, bf16[4,128,256]{2,1,0:T(8,128)(2,1)S(1)}, u32[]{:S(2)}, u32[]{:S(2)}) %collective-permute-start.4) | collective-permute-done | bytes 262176 | tf_op jit(solution)/shard_map/ppermute | solution.py:29
  37.0 4.9 collective-permute-done.5
  51.8 14.8 %collective-permute-done.12 = bf16[3,128,384]{2,1,0:T(8,128)(2,1)S(1)} collective-permute-done((bf16[3,128,384]{2,1,0:T(8,128)(2,1)}, bf16[3,128,384]{2,1,0:T(8,128)(2,1)S(1)}, u32[]{:S(2)}, u32[]{:S(2)}) %collective-permute-start.12) | collective-permute-done | bytes 294944 | tf_op jit(solution)/shard_map/ppermute | solution.py:29
  66.6 5.9 collective-permute-done.13
  83.3 4.4 collective-permute-done.14
  87.8 7.4 %collective-permute-done.17 = bf16[4,256,256]{2,1,0:T(8,128)(2,1)} collective-permute-done((bf16[4,256,256]{2,1,0:T(8,128)(2,1)}, bf16[4,256,256]{2,1,0:T(8,128)(2,1)}, u32[]{:S(2)}, u32[]{:S(2)}) %collective-permute-start.17) | collective-permute-done | bytes 524320 | tf_op jit(solution)/shard_map/ppermute | solution.py:29
  112.1 3.7 collective-permute-start.21
  119.1 3.7 copy.65
  122.8 3.7 convert_element_type.365
  126.9 15.4 %collective-permute-done.21.refs_9_ = bf16[3,256,384]{2,1,0:T(8,128)(2,1)} collective-permute-done((bf16[3,256,384]{2,1,0:T(8,128)(2,1)}, bf16[3,256,384]{2,1,0:T(8,128)(2,1)}, u32[]{:S(2)}, u32[]{:S(2)}) %collective-permute-start.21) | collective-permute-done | bytes 589856 | tf_op jit(solution)/shard_map/ppermute | solution.py:29
  144.3 12.7 %collective-permute-done.23.refs_10_ = bf16[3,256,384]{2,1,0:T(8,128)(2,1)S(1)} collective-permute-done((bf16[3,256,384]{2,1,0:T(8,128)(2,1)S(1)}, bf16[3,256,384]{2,1,0:T(8,128)(2,1)S(1)}, u32[]{:S(2)}, u32[]{:S(2)}) %collective-permute-start.23) | collective-permute-done | bytes 589856 | tf_op jit(solution)/shard_map/ppermute | solution.py:29
  157.8 13.3 %collective-permute-done.24.refs_9_ = bf16[3,256,384]{2,1,0:T(8,128)(2,1)} collective-permute-done((bf16[3,256,384]{2,1,0:T(8,128)(2,1)}, bf16[3,256,384]{2,1,0:T(8,128)(2,1)}, u32[]{:S(2)}, u32[]{:S(2)}) %collective-permute-start.24) | collective-permute-done | bytes 589856 | tf_op jit(solution)/shard_map/ppermute | solution.py:29
  175.2 7.7 %fusion.16 = f32[3,784,1024]{2,1,0:T(8,128)S(1)} fusion(bf16[4,1024,256]{2,1,0:T(8,128)(2,1)} %collective-permute-done.19, bf16[4,1024,256]{2,1,0:T(8,128)(2,1)} %constant_dynamic-update-slice_fusion.5, bf16[4,1024,256]{2,1,0:T(8,128)(2,1)} %collective-permute-done.15, bf16[4,1024,256]{2,1,0:T(8,128)(2,1)} %constant_dynamic-update-slice_fusion, ...), kind=kOutput, calls=%fused_computation.19 | convolution fusion | flops 4966055936 | bytes 19628032 | tf_op jit(solution)/shard_map/td,kdc->ktc/dot_general | solution.py:118
  183.9 2.8 copy-done.73
  186.7 2.8 multiply_convert_fusion.3
  189.5 8.1 %collective-permute-done.27.refs_14_ = bf16[3,256,384]{2,1,0:T(8,128)(2,1)S(1)} collective-permute-done((bf16[3,256,384]{2,1,0:T(8,128)(2,1)}, bf16[3,256,384]{2,1,0:T(8,128)(2,1)S(1)}, u32[]{:S(2)}, u32[]{:S(2)}) %collective-permute-start.27) | collective-permute-done | bytes 589856 | tf_op jit(solution)/shard_map/ppermute | solution.py:29
  212.9 2.6 copy.71.refs_0_
  215.5 3.4 fusion.72.refs_2_
  218.9 5.7 collective-permute-done.31.refs_15_
  228.6 2.6 copy.72.refs_1_
  244.0 29.2 %ffn.3 = (bf16[3,256,384]{2,1,0:T(8,128)(2,1)}, bf16[3,256,384]{2,1,0:T(8,128)(2,1)}, bf16[3,256,384]{2,1,0:T(8,128)(2,1)}, bf16[3,256,384]{2,1,0:T(8,128)(2,1)}...) custom-call(bf16[768,1024]{1,0:T(8,128)(2,1)S(1)} %copy-done.39, ...), custom_call_target="tpu_custom_call" | custom-call | flops 21743271936 | bytes 9437184 | tf_op jit(solution)/shard_map/ffn/pallas_call | solution.py:249
  276.5 10.8 %collective-permute-done.37.refs_15_ = bf16[3,256,384]{2,1,0:T(8,128)(2,1)S(1)} collective-permute-done((bf16[3,256,384]{2,1,0:T(8,128)(2,1)}, bf16[3,256,384]{2,1,0:T(8,128)(2,1)S(1)}, u32[]{:S(2)}, u32[]{:S(2)}) %collective-permute-start.37) | collective-permute-done | bytes 589856 | tf_op jit(solution)/shard_map/ppermute | solution.py:29
  292.8 29.9 %ffn.4 = (bf16[3,256,384]{2,1,0:T(8,128)(2,1)}, bf16[3,256,384]{2,1,0:T(8,128)(2,1)}, bf16[3,256,384]{2,1,0:T(8,128)(2,1)}, bf16[3,256,384]{2,1,0:T(8,128)(2,1)}...) custom-call(bf16[768,1024]{1,0:T(8,128)(2,1)S(1)} %copy-done.39, ...), custom_call_target="tpu_custom_call", output_to_operand_aliasing={{10}: (16, {})} | custom-call | flops 21743271936 | bytes 9437184 | tf_op jit(solution)/shard_map/ffn/pallas_call | solution.py:249
  325.5 10.0 %collective-permute-done.44 = bf16[3,256,384]{2,1,0:T(8,128)(2,1)S(1)} collective-permute-done((bf16[3,256,384]{2,1,0:T(8,128)(2,1)S(1)}, bf16[3,256,384]{2,1,0:T(8,128)(2,1)S(1)}, u32[]{:S(2)}, u32[]{:S(2)}) %collective-permute-start.44) | collective-permute-done | bytes 589856 | tf_op jit(solution)/shard_map/ppermute | solution.py:29
  341.7 30.4 %ffn.5 = (bf16[3,256,384]{2,1,0:T(8,128)(2,1)}, bf16[3,256,384]{2,1,0:T(8,128)(2,1)}, bf16[3,256,384]{2,1,0:T(8,128)(2,1)}, bf16[3,256,384]{2,1,0:T(8,128)(2,1)}...) custom-call(bf16[768,1024]{1,0:T(8,128)(2,1)S(1)} %copy-done.40, ...), custom_call_target="tpu_custom_call", output_to_operand_aliasing={{11}: (16, {})} | custom-call | flops 21743271936 | bytes 9437184 | tf_op jit(solution)/shard_map/ffn/pallas_call | solution.py:249
  372.1 4.8 add_convert_fusion
  378.5 3.5 copy.80.refs_1_
  393.6 2.8 copy-done.10
  399.2 6.6 %middle_back.1 = (bf16[768,1024]{1,0:T(8,128)(2,1)}, f32[768,1024]{1,0:T(8,128)S(1)}, bf16[768,1024]{1,0:T(8,128)(2,1)S(1)}, f32[1,1024]{1,0:T(1,128)S(1)}) custom-call(s32[8]{0:T(128)S(1)} %broadcast_xor_fusion.order.refs_0_, f32[768,1024]{1,0:T(8,128)S(1)} %copy-done.7, f32[768,1]{1,0:T(8,128)S(1)} %rsqrt.21.refs_2_, ...), custom_call_target="tpu_custom_call" | custom-call | flops 23592960 | bytes 20447232 | tf_op jit(solution)/shard_map/middle_back/pallas_call | solution.py:331
  408.2 4.9 collective-permute-done.53
  414.1 4.1 fusion.32
  429.0 2.8 broadcast_multiply_fusion.1
  432.7 4.0 multiply_reduce_fusion.1
  436.8 2.6 fusion.34
  442.9 10.9 %collective-permute-done.58.rest_2_ = bf16[3,256,384]{2,1,0:T(8,128)(2,1)S(1)} collective-permute-done((bf16[3,256,384]{2,1,0:T(8,128)(2,1)}, bf16[3,256,384]{2,1,0:T(8,128)(2,1)S(1)}, u32[]{:S(2)}, u32[]{:S(2)}) %collective-permute-start.58) | collective-permute-done | bytes 589856 | tf_op jit(solution)/shard_map/ppermute | solution.py:29
  456.4 5.5 mixer_grad.2
  466.6 2.9 collective-permute-done.62.rest_1_
  473.6 4.5 mixer_grad.3
  480.5 2.9 add_convert_fusion.16
  485.9 11.8 %collective-permute-done.64 = bf16[3,256,384]{2,1,0:T(8,128)(2,1)S(1)} collective-permute-done((bf16[3,256,384]{2,1,0:T(8,128)(2,1)S(1)}, bf16[3,256,384]{2,1,0:T(8,128)(2,1)S(1)}, u32[]{:S(2)}, u32[]{:S(2)}) %collective-permute-start.64) | collective-permute-done | bytes 589856 | tf_op jit(solution)/shard_map/ppermute | solution.py:29
  507.5 9.0 %collective-permute-done.69 = bf16[4,256,256]{2,1,0:T(8,128)(2,1)S(1)} collective-permute-done((bf16[4,256,256]{2,1,0:T(8,128)(2,1)S(1)}, bf16[4,256,256]{2,1,0:T(8,128)(2,1)S(1)}, u32[]{:S(2)}, u32[]{:S(2)}) %collective-permute-start.69) | collective-permute-done | bytes 524320 | tf_op jit(solution)/shard_map/ppermute | solution.py:29
  518.8 7.6 %fusion.28.upstream = f32[768,1024]{1,0:T(8,128)S(1)} fusion(bf16[3,768,1024]{2,1,0:T(8,128)(2,1)S(1)} %copy-done.1, bf16[4,1024,256]{2,1,0:T(8,128)(2,1)} %collective-permute-done.19, bf16[4,1024,256]{2,1,0:T(8,128)(2,1)} %constant_dynamic-update-slice_fusion.5, bf16[4,1024,256]{2,1,0:T(8,128)(2,1)} %collective-permute-done.15, ...), kind=kOutput, calls=%fused_computation.50 | convolution fusion | flops 4857004032 | bytes 16252928 | tf_op jit(solution)/shard_map/ktc,kdc->td/dot_general | solution.py:118
  526.3 4.5 input_back.1
  545.1 7.9 %collective-permute-done.74 = bf16[4,256,256]{2,1,0:T(8,128)(2,1)} collective-permute-done((bf16[4,256,256]{2,1,0:T(8,128)(2,1)}, bf16[4,256,256]{2,1,0:T(8,128)(2,1)}, u32[]{:S(2)}, u32[]{:S(2)}) %collective-permute-start.74) | collective-permute-done | bytes 524320 | tf_op jit(solution)/shard_map/ppermute | solution.py:29
  558.7 4.3 update.3
  563.1 17.2 %collective-permute-done.75 = bf16[4,256,256]{2,1,0:T(8,128)(2,1)S(1)} collective-permute-done((bf16[4,256,256]{2,1,0:T(8,128)(2,1)S(1)}, bf16[4,256,256]{2,1,0:T(8,128)(2,1)S(1)}, u32[]{:S(2)}, u32[]{:S(2)}) %collective-permute-start.75) | collective-permute-done | bytes 524320 | tf_op jit(solution)/shard_map/ppermute | solution.py:29
  585.1 3.6 collective-permute-done.86
  (547 shorter events, 210.8 us)
Async XLA Ops:
  7.8 29.2 %collective-permute-start = (bf16[16,1024]{1,0:T(8,128)(2,1)S(1)}, bf16[16,1024]{1,0:T(8,128)(2,1)S(1)}, u32[]{:S(2)}, u32[]{:S(2)}) collective-permute-start(bf16[16,1024]{1,0:T(8,128)(2,1)S(1)} %slice.345), channel_id=1, source_target_pairs={{0,1},{1,2},{2,3},{4,5},{5,6},{6,7},{8,9},{9,10},{10,11},{12,13},{... | collective-permute-start | bytes 98312 | tf_op jit(solution)/shard_map/ppermute | solution.py:538
  41.9 30.5 %collective-permute-start.10 = (bf16[4,256,256]{2,1,0:T(8,128)(2,1)}, bf16[4,256,256]{2,1,0:T(8,128)(2,1)S(1)}, u32[]{:S(2)}, u32[]{:S(2)}) collective-permute-start(bf16[4,256,256]{2,1,0:T(8,128)(2,1)} %pad_maximum_fusion.4), channel_id=1, source_target_pairs={{0,4},{4,0},{8,12},{12,8},{16,20},{20,16},{24,28},{28,24},{1,5},{5... | collective-permute-start | bytes 1572872 | tf_op jit(solution)/shard_map/ppermute | solution.py:29
  43.4 29.1 %collective-permute-start.11 = (bf16[4,256,256]{2,1,0:T(8,128)(2,1)}, bf16[4,256,256]{2,1,0:T(8,128)(2,1)}, u32[]{:S(2)}, u32[]{:S(2)}) collective-permute-start(bf16[4,256,256]{2,1,0:T(8,128)(2,1)} %pad_maximum_fusion.4), channel_id=1, source_target_pairs={{0,2},{1,3},{2,0},{3,1},{4,6},{5,7},{6,4},{7,5},{8,10},{9,11},{10,... | collective-permute-start | bytes 1572872 | tf_op jit(solution)/shard_map/ppermute | solution.py:29
  45.1 27.4 %collective-permute-start.9 = (bf16[4,256,256]{2,1,0:T(8,128)(2,1)}, bf16[4,256,256]{2,1,0:T(8,128)(2,1)}, u32[]{:S(2)}, u32[]{:S(2)}) collective-permute-start(bf16[4,256,256]{2,1,0:T(8,128)(2,1)} %pad_maximum_fusion.4), channel_id=1, source_target_pairs={{0,16},{4,20},{8,24},{12,28},{16,0},{20,4},{24,8},{28,12},{1,17},{... | collective-permute-start | bytes 1572872 | tf_op jit(solution)/shard_map/ppermute | solution.py:29
  47.8 18.8 %collective-permute-start.12 = (bf16[3,128,384]{2,1,0:T(8,128)(2,1)}, bf16[3,128,384]{2,1,0:T(8,128)(2,1)S(1)}, u32[]{:S(2)}, u32[]{:S(2)}) collective-permute-start(bf16[3,128,384]{2,1,0:T(8,128)(2,1)} %get-tuple-element.205), channel_id=1, source_target_pairs={{0,8},{4,12},{8,0},{12,4},{16,24},{20,28},{24,16},{28,20},{1,9},{5... | collective-permute-start | bytes 884744 | tf_op jit(solution)/shard_map/ppermute | solution.py:29
  49.6 22.9 %collective-permute-start.13 = (bf16[3,128,384]{2,1,0:T(8,128)(2,1)}, bf16[3,128,384]{2,1,0:T(8,128)(2,1)S(1)}, u32[]{:S(2)}, u32[]{:S(2)}) collective-permute-start(bf16[3,128,384]{2,1,0:T(8,128)(2,1)} %get-tuple-element.206), channel_id=1, source_target_pairs={{0,8},{4,12},{8,0},{12,4},{16,24},{20,28},{24,16},{28,20},{1,9},{5... | collective-permute-start | bytes 884744 | tf_op jit(solution)/shard_map/ppermute | solution.py:29
  73.4 21.8 %collective-permute-start.17 = (bf16[4,256,256]{2,1,0:T(8,128)(2,1)}, bf16[4,256,256]{2,1,0:T(8,128)(2,1)}, u32[]{:S(2)}, u32[]{:S(2)}) collective-permute-start(bf16[4,256,256]{2,1,0:T(8,128)(2,1)} %collective-permute-done.11), channel_id=1, source_target_pairs={{0,4},{4,0},{8,12},{12,8},{16,20},{20,16},{24,28},{28,24},{1,5},{5... | collective-permute-start | bytes 1572872 | tf_op jit(solution)/shard_map/ppermute | solution.py:29
  100.0 73.4 %collective-permute-start.15 = (bf16[4,1024,256]{2,1,0:T(8,128)(2,1)}, bf16[4,1024,256]{2,1,0:T(8,128)(2,1)}, u32[]{:S(2)}, u32[]{:S(2)}) collective-permute-start(bf16[4,1024,256]{2,1,0:T(8,128)(2,1)} %constant_dynamic-update-slice_fusion), channel_id=1, source_target_pairs={{0,1},{1,0},{2,3},{3,2},{4,5},{5,4},{6,7},{7,6},{8,9},{9,8},{10,11... | collective-permute-start | bytes 6291464 | tf_op jit(solution)/shard_map/ppermute | solution.py:29
  106.3 68.8 %collective-permute-start.19 = (bf16[4,1024,256]{2,1,0:T(8,128)(2,1)}, bf16[4,1024,256]{2,1,0:T(8,128)(2,1)}, u32[]{:S(2)}, u32[]{:S(2)}) collective-permute-start(bf16[4,1024,256]{2,1,0:T(8,128)(2,1)} %constant_dynamic-update-slice_fusion.5), channel_id=1, source_target_pairs={{0,1},{1,0},{2,3},{3,2},{4,5},{5,4},{6,7},{7,6},{8,9},{9,8},{10,11... | collective-permute-start | bytes 6291464 | tf_op jit(solution)/shard_map/ppermute | solution.py:29
  110.3 62.5 %collective-permute-start.20 = (bf16[768,1024]{0,1:T(8,128)(2,1)}, bf16[768,1024]{0,1:T(8,128)(2,1)S(1)}, u32[]{:S(2)}, u32[]{:S(2)}) collective-permute-start(bf16[768,1024]{0,1:T(8,128)(2,1)} %copy.68), channel_id=1, source_target_pairs={{0,1},{1,0},{2,3},{3,2},{4,5},{5,4},{6,7},{7,6},{8,9},{9,8},{10,11... | collective-permute-start | bytes 4718600 | tf_op jit(solution)/shard_map/ppermute | solution.py:29
  112.1 30.2 %collective-permute-start.21 = (bf16[3,256,384]{2,1,0:T(8,128)(2,1)}, bf16[3,256,384]{2,1,0:T(8,128)(2,1)}, u32[]{:S(2)}, u32[]{:S(2)}) collective-permute-start(bf16[3,256,384]{2,1,0:T(8,128)(2,1)} %pad_maximum_fusion.1.refs_8_), channel_id=1, source_target_pairs={{0,16},{4,20},{8,24},{12,28},{16,0},{20,4},{24,8},{28,12},{1,17},{... | collective-permute-start | bytes 1769480 | tf_op jit(solution)/shard_map/ppermute | solution.py:29
  115.8 27.0 %collective-permute-start.22 = (bf16[3,256,384]{2,1,0:T(8,128)(2,1)}, bf16[3,256,384]{2,1,0:T(8,128)(2,1)}, u32[]{:S(2)}, u32[]{:S(2)}) collective-permute-start(bf16[3,256,384]{2,1,0:T(8,128)(2,1)} %pad_maximum_fusion.1.refs_8_), channel_id=1, source_target_pairs={{0,2},{1,3},{2,0},{3,1},{4,6},{5,7},{6,4},{7,5},{8,10},{9,11},{10,... | collective-permute-start | bytes 1769480 | tf_op jit(solution)/shard_map/ppermute | solution.py:29
  142.8 28.3 %collective-permute-start.24 = (bf16[3,256,384]{2,1,0:T(8,128)(2,1)}, bf16[3,256,384]{2,1,0:T(8,128)(2,1)}, u32[]{:S(2)}, u32[]{:S(2)}) collective-permute-start(bf16[3,256,384]{2,1,0:T(8,128)(2,1)} %pad_maximum_fusion.2.refs_8_), channel_id=1, source_target_pairs={{0,16},{4,20},{8,24},{12,28},{16,0},{20,4},{24,8},{28,12},{1,17},{... | collective-permute-start | bytes 1769480 | tf_op jit(solution)/shard_map/ppermute | solution.py:29
  171.1 18.4 %collective-permute-start.25 = (bf16[3,256,384]{2,1,0:T(8,128)(2,1)}, bf16[3,256,384]{2,1,0:T(8,128)(2,1)}, u32[]{:S(2)}, u32[]{:S(2)}) collective-permute-start(bf16[3,256,384]{2,1,0:T(8,128)(2,1)} %collective-permute-done.21.refs_9_), channel_id=1, source_target_pairs={{0,4},{4,0},{8,12},{12,8},{16,20},{20,16},{24,28},{28,24},{1,5},{5... | collective-permute-start | bytes 1769480 | tf_op jit(solution)/shard_map/ppermute | solution.py:29
  172.6 16.9 %collective-permute-start.26 = (bf16[3,256,384]{2,1,0:T(8,128)(2,1)}, bf16[3,256,384]{2,1,0:T(8,128)(2,1)S(1)}, u32[]{:S(2)}, u32[]{:S(2)}) collective-permute-start(bf16[3,256,384]{2,1,0:T(8,128)(2,1)} %collective-permute-done.21.refs_9_), channel_id=1, source_target_pairs={{0,2},{1,3},{2,0},{3,1},{4,6},{5,7},{6,4},{7,5},{8,10},{9,11},{10,... | collective-permute-start | bytes 1769480 | tf_op jit(solution)/shard_map/ppermute | solution.py:29
  172.9 24.8 %collective-permute-start.27 = (bf16[3,256,384]{2,1,0:T(8,128)(2,1)}, bf16[3,256,384]{2,1,0:T(8,128)(2,1)S(1)}, u32[]{:S(2)}, u32[]{:S(2)}) collective-permute-start(bf16[3,256,384]{2,1,0:T(8,128)(2,1)} %collective-permute-done.22.refs_12_), channel_id=1, source_target_pairs={{0,4},{4,0},{8,12},{12,8},{16,20},{20,16},{24,28},{28,24},{1,5},{5... | collective-permute-start | bytes 1769480 | tf_op jit(solution)/shard_map/ppermute | solution.py:29
  173.4 25.6 %collective-permute-start.28 = (bf16[3,256,384]{2,1,0:T(8,128)(2,1)}, bf16[3,256,384]{2,1,0:T(8,128)(2,1)}, u32[]{:S(2)}, u32[]{:S(2)}) collective-permute-start(bf16[3,256,384]{2,1,0:T(8,128)(2,1)} %pad_maximum_fusion.2.refs_8_), channel_id=1, source_target_pairs={{0,2},{1,3},{2,0},{3,1},{4,6},{5,7},{6,4},{7,5},{8,10},{9,11},{10,... | collective-permute-start | bytes 1769480 | tf_op jit(solution)/shard_map/ppermute | solution.py:29
  175.1 26.4 %collective-permute-start.29 = (bf16[3,256,384]{2,1,0:T(8,128)(2,1)}, bf16[3,256,384]{2,1,0:T(8,128)(2,1)S(1)}, u32[]{:S(2)}, u32[]{:S(2)}) collective-permute-start(bf16[3,256,384]{2,1,0:T(8,128)(2,1)} %pad_maximum_fusion.3.refs_8_), channel_id=1, source_target_pairs={{0,16},{4,20},{8,24},{12,28},{16,0},{20,4},{24,8},{28,12},{1,17},{... | collective-permute-start | bytes 1769480 | tf_op jit(solution)/shard_map/ppermute | solution.py:29
  208.5 20.2 %collective-permute-start.30 = (bf16[768,1024]{0,1:T(8,128)(2,1)}, bf16[768,1024]{0,1:T(8,128)(2,1)}, u32[]{:S(2)}, u32[]{:S(2)}) collective-permute-start(bf16[768,1024]{0,1:T(8,128)(2,1)} %multiply_convert_fusion.2), channel_id=1, source_target_pairs={{0,1},{1,0},{2,3},{3,2},{4,5},{5,4},{6,7},{7,6},{8,9},{9,8},{10,11... | collective-permute-start | bytes 4718600 | tf_op jit(solution)/shard_map/ppermute | solution.py:29
  224.6 48.6 %collective-permute-start.33 = (bf16[3,256,384]{2,1,0:T(8,128)(2,1)}, bf16[3,256,384]{2,1,0:T(8,128)(2,1)}, u32[]{:S(2)}, u32[]{:S(2)}) collective-permute-start(bf16[3,256,384]{2,1,0:T(8,128)(2,1)} %collective-permute-done.24.refs_9_), channel_id=1, source_target_pairs={{0,4},{4,0},{8,12},{12,8},{16,20},{20,16},{24,28},{28,24},{1,5},{5... | collective-permute-start | bytes 1769480 | tf_op jit(solution)/shard_map/ppermute | solution.py:29
  226.1 47.1 %collective-permute-start.34 = (bf16[3,256,384]{2,1,0:T(8,128)(2,1)}, bf16[3,256,384]{2,1,0:T(8,128)(2,1)}, u32[]{:S(2)}, u32[]{:S(2)}) collective-permute-start(bf16[3,256,384]{2,1,0:T(8,128)(2,1)} %collective-permute-done.24.refs_9_), channel_id=1, source_target_pairs={{0,2},{1,3},{2,0},{3,1},{4,6},{5,7},{6,4},{7,5},{8,10},{9,11},{10,... | collective-permute-start | bytes 1769480 | tf_op jit(solution)/shard_map/ppermute | solution.py:29
  227.8 45.5 %collective-permute-start.35 = (bf16[3,256,384]{2,1,0:T(8,128)(2,1)}, bf16[3,256,384]{2,1,0:T(8,128)(2,1)}, u32[]{:S(2)}, u32[]{:S(2)}) collective-permute-start(bf16[3,256,384]{2,1,0:T(8,128)(2,1)} %collective-permute-done.28.refs_12_), channel_id=1, source_target_pairs={{0,4},{4,0},{8,12},{12,8},{16,20},{20,16},{24,28},{28,24},{1,5},{5... | collective-permute-start | bytes 1769480 | tf_op jit(solution)/shard_map/ppermute | solution.py:29
  228.3 45.0 %collective-permute-start.36 = (bf16[3,256,384]{2,1,0:T(8,128)(2,1)}, bf16[3,256,384]{2,1,0:T(8,128)(2,1)}, u32[]{:S(2)}, u32[]{:S(2)}) collective-permute-start(bf16[3,256,384]{2,1,0:T(8,128)(2,1)} %pad_maximum_fusion.3.refs_8_), channel_id=1, source_target_pairs={{0,2},{1,3},{2,0},{3,1},{4,6},{5,7},{6,4},{7,5},{8,10},{9,11},{10,... | collective-permute-start | bytes 1769480 | tf_op jit(solution)/shard_map/ppermute | solution.py:29
  288.7 34.1 %collective-permute-start.39 = (bf16[3,256,384]{2,1,0:T(8,128)(2,1)S(1)}, bf16[3,256,384]{2,1,0:T(8,128)(2,1)S(1)}, u32[]{:S(2)}, u32[]{:S(2)}) collective-permute-start(bf16[3,256,384]{2,1,0:T(8,128)(2,1)S(1)} %copy-done.64), channel_id=1, source_target_pairs={{0,4},{4,0},{8,12},{12,8},{16,20},{20,16},{24,28},{28,24},{1,5},{5... | collective-permute-start | bytes 1769480 | tf_op jit(solution)/shard_map/ppermute | solution.py:29
  290.2 32.6 %collective-permute-start.40 = (bf16[3,256,384]{2,1,0:T(8,128)(2,1)S(1)}, bf16[3,256,384]{2,1,0:T(8,128)(2,1)S(1)}, u32[]{:S(2)}, u32[]{:S(2)}) collective-permute-start(bf16[3,256,384]{2,1,0:T(8,128)(2,1)S(1)} %copy-done.64), channel_id=1, source_target_pairs={{0,2},{1,3},{2,0},{3,1},{4,6},{5,7},{6,4},{7,5},{8,10},{9,11},{10,... | collective-permute-start | bytes 1769480 | tf_op jit(solution)/shard_map/ppermute | solution.py:29
  290.5 32.3 %collective-permute-start.41 = (bf16[3,256,384]{2,1,0:T(8,128)(2,1)}, bf16[3,256,384]{2,1,0:T(8,128)(2,1)S(1)}, u32[]{:S(2)}, u32[]{:S(2)}) collective-permute-start(bf16[3,256,384]{2,1,0:T(8,128)(2,1)} %collective-permute-done.36.refs_12_), channel_id=1, source_target_pairs={{0,4},{4,0},{8,12},{12,8},{16,20},{20,16},{24,28},{28,24},{1,5},{5... | collective-permute-start | bytes 1769480 | tf_op jit(solution)/shard_map/ppermute | solution.py:29
  291.1 31.8 %collective-permute-start.42 = (bf16[3,256,384]{2,1,0:T(8,128)(2,1)}, bf16[3,256,384]{2,1,0:T(8,128)(2,1)S(1)}, u32[]{:S(2)}, u32[]{:S(2)}) collective-permute-start(bf16[3,256,384]{2,1,0:T(8,128)(2,1)} %get-tuple-element.249), channel_id=1, source_target_pairs={{0,2},{1,3},{2,0},{3,1},{4,6},{5,7},{6,4},{7,5},{8,10},{9,11},{10,... | collective-permute-start | bytes 1769480 | tf_op jit(solution)/shard_map/ppermute | solution.py:29
  337.6 39.4 %collective-permute-start.46 = (bf16[3,256,384]{2,1,0:T(8,128)(2,1)S(1)}, bf16[3,256,384]{2,1,0:T(8,128)(2,1)S(1)}, u32[]{:S(2)}, u32[]{:S(2)}) collective-permute-start(bf16[3,256,384]{2,1,0:T(8,128)(2,1)S(1)} %copy-done.137), channel_id=1, source_target_pairs={{0,4},{4,0},{8,12},{12,8},{16,20},{20,16},{24,28},{28,24},{1,5},{5... | collective-permute-start | bytes 1769480 | tf_op jit(solution)/shard_map/ppermute | solution.py:29
  337.9 39.9 %collective-permute-start.47 = (bf16[3,256,384]{2,1,0:T(8,128)(2,1)S(1)}, bf16[3,256,384]{2,1,0:T(8,128)(2,1)}, u32[]{:S(2)}, u32[]{:S(2)}) collective-permute-start(bf16[3,256,384]{2,1,0:T(8,128)(2,1)S(1)} %copy-done.136), channel_id=1, source_target_pairs={{0,2},{1,3},{2,0},{3,1},{4,6},{5,7},{6,4},{7,5},{8,10},{9,11},{10,... | collective-permute-start | bytes 1769480 | tf_op jit(solution)/shard_map/ppermute | solution.py:29
  338.3 39.5 %collective-permute-start.48 = (bf16[3,256,384]{2,1,0:T(8,128)(2,1)}, bf16[3,256,384]{2,1,0:T(8,128)(2,1)}, u32[]{:S(2)}, u32[]{:S(2)}) collective-permute-start(bf16[3,256,384]{2,1,0:T(8,128)(2,1)} %get-tuple-element.272), channel_id=1, source_target_pairs={{0,4},{4,0},{8,12},{12,8},{16,20},{20,16},{24,28},{28,24},{1,5},{5... | collective-permute-start | bytes 1769480 | tf_op jit(solution)/shard_map/ppermute | solution.py:29
  339.9 37.8 %collective-permute-start.49 = (bf16[3,256,384]{2,1,0:T(8,128)(2,1)}, bf16[3,256,384]{2,1,0:T(8,128)(2,1)}, u32[]{:S(2)}, u32[]{:S(2)}) collective-permute-start(bf16[3,256,384]{2,1,0:T(8,128)(2,1)} %get-tuple-element.273), channel_id=1, source_target_pairs={{0,2},{1,3},{2,0},{3,1},{4,6},{5,7},{6,4},{7,5},{8,10},{9,11},{10,... | collective-permute-start | bytes 1769480 | tf_op jit(solution)/shard_map/ppermute | solution.py:29
  385.1 23.2 %collective-permute-start.51 = (bf16[3,256,384]{2,1,0:T(8,128)(2,1)S(1)}, bf16[3,256,384]{2,1,0:T(8,128)(2,1)S(1)}, u32[]{:S(2)}, u32[]{:S(2)}) collective-permute-start(bf16[3,256,384]{2,1,0:T(8,128)(2,1)S(1)} %add_convert_fusion.9), channel_id=1, source_target_pairs={{0,4},{4,0},{8,12},{12,8},{16,20},{20,16},{24,28},{28,24},{1,5},{5... | collective-permute-start | bytes 1769480 | tf_op jit(solution)/shard_map/ppermute | solution.py:29
  385.5 22.7 %collective-permute-start.52 = (bf16[3,256,384]{2,1,0:T(8,128)(2,1)S(1)}, bf16[3,256,384]{2,1,0:T(8,128)(2,1)S(1)}, u32[]{:S(2)}, u32[]{:S(2)}) collective-permute-start(bf16[3,256,384]{2,1,0:T(8,128)(2,1)S(1)} %add_convert_fusion.8), channel_id=1, source_target_pairs={{0,2},{1,3},{2,0},{3,1},{4,6},{5,7},{6,4},{7,5},{8,10},{9,11},{10,... | collective-permute-start | bytes 1769480 | tf_op jit(solution)/shard_map/ppermute | solution.py:29
  385.8 27.3 %collective-permute-start.53 = (bf16[3,256,384]{2,1,0:T(8,128)(2,1)}, bf16[3,256,384]{2,1,0:T(8,128)(2,1)S(1)}, u32[]{:S(2)}, u32[]{:S(2)}) collective-permute-start(bf16[3,256,384]{2,1,0:T(8,128)(2,1)} %get-tuple-element.290), channel_id=1, source_target_pairs={{0,4},{4,0},{8,12},{12,8},{16,20},{20,16},{24,28},{28,24},{1,5},{5... | collective-permute-start | bytes 1769480 | tf_op jit(solution)/shard_map/ppermute | solution.py:29
  389.7 23.5 %collective-permute-start.54 = (bf16[3,256,384]{2,1,0:T(8,128)(2,1)}, bf16[3,256,384]{2,1,0:T(8,128)(2,1)S(1)}, u32[]{:S(2)}, u32[]{:S(2)}) collective-permute-start(bf16[3,256,384]{2,1,0:T(8,128)(2,1)} %get-tuple-element.291), channel_id=1, source_target_pairs={{0,2},{1,3},{2,0},{3,1},{4,6},{5,7},{6,4},{7,5},{8,10},{9,11},{10,... | collective-permute-start | bytes 1769480 | tf_op jit(solution)/shard_map/ppermute | solution.py:29
  426.4 16.4 %collective-permute-start.57 = (bf16[3,256,384]{2,1,0:T(8,128)(2,1)}, bf16[3,256,384]{2,1,0:T(8,128)(2,1)S(1)}, u32[]{:S(2)}, u32[]{:S(2)}) collective-permute-start(bf16[3,256,384]{2,1,0:T(8,128)(2,1)} %add_convert_fusion.6), channel_id=1, source_target_pairs={{0,2},{1,3},{2,0},{3,1},{4,6},{5,7},{6,4},{7,5},{8,10},{9,11},{10,... | collective-permute-start | bytes 1769480 | tf_op jit(solution)/shard_map/ppermute | solution.py:29
  427.7 26.1 %collective-permute-start.58 = (bf16[3,256,384]{2,1,0:T(8,128)(2,1)}, bf16[3,256,384]{2,1,0:T(8,128)(2,1)S(1)}, u32[]{:S(2)}, u32[]{:S(2)}) collective-permute-start(bf16[3,256,384]{2,1,0:T(8,128)(2,1)} %get-tuple-element.304), channel_id=1, source_target_pairs={{0,4},{4,0},{8,12},{12,8},{16,20},{20,16},{24,28},{28,24},{1,5},{5... | collective-permute-start | bytes 1769480 | tf_op jit(solution)/shard_map/ppermute | solution.py:29
  428.3 27.1 %collective-permute-start.59 = (bf16[3,256,384]{2,1,0:T(8,128)(2,1)}, bf16[3,256,384]{2,1,0:T(8,128)(2,1)S(1)}, u32[]{:S(2)}, u32[]{:S(2)}) collective-permute-start(bf16[3,256,384]{2,1,0:T(8,128)(2,1)} %get-tuple-element.305), channel_id=1, source_target_pairs={{0,2},{1,3},{2,0},{3,1},{4,6},{5,7},{6,4},{7,5},{8,10},{9,11},{10,... | collective-permute-start | bytes 1769480 | tf_op jit(solution)/shard_map/ppermute | solution.py:29
  428.9 27.5 %collective-permute-start.60 = (bf16[3,256,384]{2,1,0:T(8,128)(2,1)}, bf16[3,256,384]{2,1,0:T(8,128)(2,1)S(1)}, u32[]{:S(2)}, u32[]{:S(2)}) collective-permute-start(bf16[3,256,384]{2,1,0:T(8,128)(2,1)} %add_convert_fusion.5), channel_id=1, source_target_pairs={{0,16},{4,20},{8,24},{12,28},{16,0},{20,4},{24,8},{28,12},{1,17},{... | collective-permute-start | bytes 1769480 | tf_op jit(solution)/shard_map/ppermute | solution.py:29
  471.1 26.6 %collective-permute-start.64 = (bf16[3,256,384]{2,1,0:T(8,128)(2,1)S(1)}, bf16[3,256,384]{2,1,0:T(8,128)(2,1)S(1)}, u32[]{:S(2)}, u32[]{:S(2)}) collective-permute-start(bf16[3,256,384]{2,1,0:T(8,128)(2,1)S(1)} %add_convert_fusion.4), channel_id=1, source_target_pairs={{0,4},{4,0},{8,12},{12,8},{16,20},{20,16},{24,28},{28,24},{1,5},{5... | collective-permute-start | bytes 1769480 | tf_op jit(solution)/shard_map/ppermute | solution.py:29
  471.5 26.2 %collective-permute-start.65 = (bf16[3,256,384]{2,1,0:T(8,128)(2,1)}, bf16[3,256,384]{2,1,0:T(8,128)(2,1)S(1)}, u32[]{:S(2)}, u32[]{:S(2)}) collective-permute-start(bf16[3,256,384]{2,1,0:T(8,128)(2,1)} %get-tuple-element.326), channel_id=1, source_target_pairs={{0,2},{1,3},{2,0},{3,1},{4,6},{5,7},{6,4},{7,5},{8,10},{9,11},{10,... | collective-permute-start | bytes 1769480 | tf_op jit(solution)/shard_map/ppermute | solution.py:29
  471.9 27.3 %collective-permute-start.66 = (bf16[3,256,384]{2,1,0:T(8,128)(2,1)S(1)}, bf16[3,256,384]{2,1,0:T(8,128)(2,1)S(1)}, u32[]{:S(2)}, u32[]{:S(2)}) collective-permute-start(bf16[3,256,384]{2,1,0:T(8,128)(2,1)S(1)} %add_convert_fusion.3), channel_id=1, source_target_pairs={{0,2},{1,3},{2,0},{3,1},{4,6},{5,7},{6,4},{7,5},{8,10},{9,11},{10,... | collective-permute-start | bytes 1769480 | tf_op jit(solution)/shard_map/ppermute | solution.py:29
  473.6 27.8 %collective-permute-start.67 = (bf16[3,256,384]{2,1,0:T(8,128)(2,1)S(1)}, bf16[3,256,384]{2,1,0:T(8,128)(2,1)S(1)}, u32[]{:S(2)}, u32[]{:S(2)}) collective-permute-start(bf16[3,256,384]{2,1,0:T(8,128)(2,1)S(1)} %add_convert_fusion.2), channel_id=1, source_target_pairs={{0,16},{4,20},{8,24},{12,28},{16,0},{20,4},{24,8},{28,12},{1,17},{... | collective-permute-start | bytes 1769480 | tf_op jit(solution)/shard_map/ppermute | solution.py:29
  502.9 30.6 %collective-permute-start.71 = (bf16[3,256,384]{2,1,0:T(8,128)(2,1)S(1)}, bf16[3,256,384]{2,1,0:T(8,128)(2,1)S(1)}, u32[]{:S(2)}, u32[]{:S(2)}) collective-permute-start(bf16[3,256,384]{2,1,0:T(8,128)(2,1)S(1)} %add_convert_fusion.1), channel_id=1, source_target_pairs={{0,16},{4,20},{8,24},{12,28},{16,0},{20,4},{24,8},{28,12},{1,17},{... | collective-permute-start | bytes 1769480 | tf_op jit(solution)/shard_map/ppermute | solution.py:29
  502.9 31.6 %collective-permute-start.68 = (bf16[4,256,256]{2,1,0:T(8,128)(2,1)}, bf16[4,256,256]{2,1,0:T(8,128)(2,1)S(1)}, u32[]{:S(2)}, u32[]{:S(2)}) collective-permute-start(bf16[4,256,256]{2,1,0:T(8,128)(2,1)} %add_convert_fusion.18), channel_id=1, source_target_pairs={{0,4},{4,0},{8,12},{12,8},{16,20},{20,16},{24,28},{28,24},{1,5},{5... | collective-permute-start | bytes 1572872 | tf_op jit(solution)/shard_map/ppermute | solution.py:29
  504.5 27.0 %collective-permute-start.70 = (bf16[4,256,256]{2,1,0:T(8,128)(2,1)}, bf16[4,256,256]{2,1,0:T(8,128)(2,1)S(1)}, u32[]{:S(2)}, u32[]{:S(2)}) collective-permute-start(bf16[4,256,256]{2,1,0:T(8,128)(2,1)} %get-tuple-element.336), channel_id=1, source_target_pairs={{0,4},{4,0},{8,12},{12,8},{16,20},{20,16},{24,28},{28,24},{1,5},{5... | collective-permute-start | bytes 1572872 | tf_op jit(solution)/shard_map/ppermute | solution.py:29
  504.9 30.3 %collective-permute-start.72 = (bf16[4,256,256]{2,1,0:T(8,128)(2,1)}, bf16[4,256,256]{2,1,0:T(8,128)(2,1)S(1)}, u32[]{:S(2)}, u32[]{:S(2)}) collective-permute-start(bf16[4,256,256]{2,1,0:T(8,128)(2,1)} %get-tuple-element.338), channel_id=1, source_target_pairs={{0,2},{1,3},{2,0},{3,1},{4,6},{5,7},{6,4},{7,5},{8,10},{9,11},{10,... | collective-permute-start | bytes 1572872 | tf_op jit(solution)/shard_map/ppermute | solution.py:29
  554.8 25.5 %collective-permute-start.75 = (bf16[4,256,256]{2,1,0:T(8,128)(2,1)S(1)}, bf16[4,256,256]{2,1,0:T(8,128)(2,1)S(1)}, u32[]{:S(2)}, u32[]{:S(2)}) collective-permute-start(bf16[4,256,256]{2,1,0:T(8,128)(2,1)S(1)} %add_convert_fusion.10), channel_id=1, source_target_pairs={{0,16},{4,20},{8,24},{12,28},{16,0},{20,4},{24,8},{28,12},{1,17},{... | collective-permute-start | bytes 1572872 | tf_op jit(solution)/shard_map/ppermute | solution.py:29
  (180 other events, 2594.4 us)

commit v8 on v7

--- a/solution.py
+++ b/solution.py
@@ -550,9 +550,8 @@
         [*got, *later], [by_x(zb[0]), by_y(zb[0]), by_x(ya[0]), by_y(own[1]), by_z(own[1])]
     )
     x_ext, cot = arrange(order, *ordered([tokens, before, cotangent], last))
-    db[0], xa[1], zb[2], cot_other = phase(
-        got[:3], [by_y(xb[0]), by_x(own[1]), by_z(own[2]), (cot, "tensor", 1)]
-    )
+    db[0], xa[1], cot_other = phase(got, [by_y(xb[0]), by_x(own[1]), (cot, "tensor", 1)])
+    (db[0],) = ordered([db[0]], [xa[1], cot_other])
     small = small.reshape(small.shape[0], dp_size, t_size, small.shape[-1])
     for axis, index, size_axis in ((1, dp_index, dp_size), (2, t_index, t_size)):
         for i in range(size_axis.bit_length() - 1):
@@ -589,8 +588,8 @@
     near, far = join(pieces_of(0)[:4], wide), join(pieces_of(0)[4:], wide)
     wm = [near, other_core(near), far, other_core(far)]
     got = phase(
-        [db[0], xa[1], zb[1], ya[1], zb[2]],
-        [by_x(zb[1]), by_y(zb[1]), by_x(ya[1]), by_y(own[2]), by_z(own[3])],
+        [db[0], xa[1]],
+        [by_x(zb[1]), by_y(zb[1]), by_x(ya[1]), by_y(own[2]), by_z(own[2])],
     )
     wm_all = jnp.concatenate(wm, 2)
     win_all, wout_all = wm_all[:3], wm_all[3]
@@ -614,7 +613,7 @@
     tokens_both = (normed_two, normed_other, normed_two.T, normed_other.T)
     tokens_both += (cot, cot_other, ct, ct_other)
     sums, grads, back_other, branch_own, branch_other = [], {}, [], [], []
-    xb[1], yb[1], da[1], ya[2], zb[3] = got = ordered(got, [normed_two])
+    xb[1], yb[1], da[1], ya[2], zb[2] = got = ordered(got, [normed_two])
     db[1], xa[2] = got = phase(got, [by_y(xb[1]), by_x(own[2])])
 
     def run(i):
@@ -624,8 +623,8 @@
         branch_other.append(branches[1])
         return grads[i]
 
-    got = phase(got, [by_x(zb[2]), by_y(zb[2]), by_x(ya[2]), by_y(own[3])])
-    xb[2], yb[2], da[2], ya[3] = got = ordered(got, run(1)[:1])
+    got = phase(got, [by_x(zb[2]), by_y(zb[2]), by_x(ya[2]), by_y(own[3]), by_z(own[3])])
+    xb[2], yb[2], da[2], ya[3], zb[3] = got = ordered(got, run(1)[:1])
     db[2], xa[3] = got = phase(got, [by_y(xb[2]), by_x(own[3])])
 
     axa, axb, aya, ayb, ada, adb = ({} for _ in range(6))
@@ -641,19 +640,25 @@
     db[3], ada[1] = got = phase(got, [by_y(xb[3]), by_x(grads[1][6])])
     one_t = normed_one.T
     (db[3],) = ordered([db[3]], [ada[1], one_t])
+    early = plus(branch_other[0], branch_other[1])
     got = phase(
-        got, [by_x(grads[1][2]), by_y(grads[1][7]), by_x(grads[2][6]), by_y(grads[2][7])]
-    )
-    axa[1], adb[1], ada[2], adb[2] = got = ordered(got, run(3)[:1])
+        got,
+        [
+            by_x(grads[1][2]),
+            by_y(grads[1][7]),
+            by_x(grads[2][6]),
+            by_y(grads[2][7]),
+            (early, "tensor", 1),
+        ],
+    )
+    axa[1], adb[1], ada[2], adb[2], early = got = ordered(got, run(3)[:1])
     back_other, back = ordered([*back_other, *sums], got)
     back_in = other_core(back_other)
-    branch_in = other_core(
-        functools.reduce(jnp.add, [value.astype(F32) for value in branch_other]).astype(BF)
-    )
+    branch_in = other_core(branch_other[2])
     deps = got
     got = phase(got, [sum_xb(1), sum_ya(1), by_x(grads[2][2]), by_y(grads[2][5])])
     block_out, middle_grad, mixed_grad, gain_two_grad = middle_back(
-        order, middle, scale_two, gains[1:2], cot, [*branch_own, branch_in], [back, back_in], deps
+        order, middle, scale_two, gains[1:2], cot, [*branch_own, early, branch_in], [back, back_in], deps
     )
 
     gated_grad = mm("td,dc->tc", mixed_grad, wout_all)

time: 599 us -> 547 us (0.913)
  waiting for transfers between devices: 216 us -> 162 us
    ppermute x85 -> x86, waiting for transfers between devices: 216 us -> 162 us  [swap(): return lax.ppermute(values, axis, [(i, i ^ bit) for i in range(size)])]
    ppermute x85 -> x86, starting transfers between devices: 81.3 us -> 76.3 us  [swap(): return lax.ppermute(values, axis, [(i, i ^ bit) for i in range(size)])]
    convert_element_type x10 -> x11, other arithmetic: 17.1 us -> 18.6 us  [plus(): return (left.astype(F32) + right.astype(F32)).astype(BF)]
  transfers between devices with their start and end apart: 87 -> 88, of which waited for: 42 -> 40; matrix products, arithmetic and copies ran while one was open for 21% -> 23% of each run, Pallas kernels for 19% -> 20%
where the time goes in v8:
time: 547 us; the launch traced here: 542 us
  waiting for transfers between devices  162 us (30%)
  Pallas kernels  117 us (21%)
  starting transfers between devices  80 us (15%)
  local copies, waits for them, and re-layouts  79.8 us (15%)
  other arithmetic  76 us (14%)
  matrix products  18.7 us (3%)
  between operations  8.14 us (1%)
    ppermute x86, waiting for transfers between devices, swap(): return lax.ppermute(values, axis, [(i, i ^ bit) for i in range(size)])  162 us
    pallas_call x3, Pallas kernels, ffn(): pl.pallas_call(functools.partial(ffn_kernel, not sums, final), grid=(cols...  89 us
    ppermute x86, starting transfers between devices, swap(): return lax.ppermute(values, axis, [(i, i ^ bit) for i in range(size)])  76.3 us
    unnamed x296, local copies, waits for them, and re-layouts  48.9 us
    dot_general x4, matrix products, mm(): return jnp.einsum(spec, left, right, preferred_element_type=F32).astype(out)  18.7 us
    convert_element_type x11, other arithmetic, plus(): return (left.astype(F32) + right.astype(F32)).astype(BF)  18.6 us
  transfers between devices with their start and end apart: 88, of which 40 were waited for; matrix products, arithmetic and copies ran while one was open for 23% of the time, Pallas kernels for 20%

profile of v8, /device:TPU:0, one launch (start us, length us, event | category | flops | bytes accessed | tf_op | source)
XLA Modules:
  0.0 541.7 jit_solution(5896044882291662760)
XLA Ops:
  1.4 3.1 collective-permute-start.1
  4.5 2.6 collective-permute-start.2
  9.8 2.7 collective-permute-done.3
  34.0 14.7 %collective-permute-done.12 = bf16[3,128,384]{2,1,0:T(8,128)(2,1)S(1)} collective-permute-done((bf16[3,128,384]{2,1,0:T(8,128)(2,1)S(1)}, bf16[3,128,384]{2,1,0:T(8,128)(2,1)S(1)}, u32[]{:S(2)}, u32[]{:S(2)}) %collective-permute-start.12) | collective-permute-done | bytes 294944 | tf_op jit(solution)/shard_map/ppermute | solution.py:29
  48.7 5.5 %collective-permute-done.13 = bf16[3,128,384]{2,1,0:T(8,128)(2,1)S(1)} collective-permute-done((bf16[3,128,384]{2,1,0:T(8,128)(2,1)S(1)}, bf16[3,128,384]{2,1,0:T(8,128)(2,1)S(1)}, u32[]{:S(2)}, u32[]{:S(2)}) %collective-permute-start.13) | collective-permute-done | bytes 294944 | tf_op jit(solution)/shard_map/ppermute | solution.py:29
  71.6 7.6 %collective-permute-done.16 = bf16[4,256,256]{2,1,0:T(8,128)(2,1)} collective-permute-done((bf16[4,256,256]{2,1,0:T(8,128)(2,1)}, bf16[4,256,256]{2,1,0:T(8,128)(2,1)}, u32[]{:S(2)}, u32[]{:S(2)}) %collective-permute-start.16) | collective-permute-done | bytes 524320 | tf_op jit(solution)/shard_map/ppermute | solution.py:29
  79.3 3.6 collective-permute-done.19.refs_9_
  102.5 5.1 collective-permute-done.20
  111.5 3.7 copy.65
  115.2 3.6 convert_element_type.362
  125.4 7.7 %fusion.16 = f32[3,784,1024]{2,1,0:T(8,128)S(1)} fusion(bf16[4,1024,256]{2,1,0:T(8,128)(2,1)} %collective-permute-done.23, bf16[4,1024,256]{2,1,0:T(8,128)(2,1)} %constant_dynamic-update-slice_fusion.5, bf16[4,1024,256]{2,1,0:T(8,128)(2,1)} %collective-permute-done.15, bf16[4,1024,256]{2,1,0:T(8,128)(2,1)S(1)} %copy-done.87, ...), kind=kOutput, calls=%fused_computation.19 | convolution fusion | flops 4966055936 | bytes 19628032 | tf_op jit(solution)/shard_map/td,kdc->ktc/dot_general | solution.py:118
  134.1 2.8 copy-done.77
  136.9 2.8 multiply_convert_fusion.3
  139.7 10.2 %collective-permute-done.26.refs_14_ = bf16[3,256,384]{2,1,0:T(8,128)(2,1)S(1)} collective-permute-done((bf16[3,256,384]{2,1,0:T(8,128)(2,1)}, bf16[3,256,384]{2,1,0:T(8,128)(2,1)S(1)}, u32[]{:S(2)}, u32[]{:S(2)}) %collective-permute-start.26) | collective-permute-done | bytes 589856 | tf_op jit(solution)/shard_map/ppermute | solution.py:29
  161.6 2.6 copy.73.refs_5_
  164.2 2.6 copy.71.refs_0_
  166.8 3.4 fusion.72.refs_2_
  170.2 5.0 collective-permute-done.30.refs_15_
  179.3 2.8 copy.72.refs_1_
  193.8 28.9 %ffn.3 = (bf16[3,256,384]{2,1,0:T(8,128)(2,1)}, bf16[3,256,384]{2,1,0:T(8,128)(2,1)}, bf16[3,256,384]{2,1,0:T(8,128)(2,1)}, bf16[3,256,384]{2,1,0:T(8,128)(2,1)}...) custom-call(bf16[768,1024]{1,0:T(8,128)(2,1)S(1)} %copy-done.47, ...), custom_call_target="tpu_custom_call" | custom-call | flops 21743271936 | bytes 9437184 | tf_op jit(solution)/shard_map/ffn/pallas_call | solution.py:249
  225.7 11.1 %collective-permute-done.37.refs_15_ = bf16[3,256,384]{2,1,0:T(8,128)(2,1)S(1)} collective-permute-done((bf16[3,256,384]{2,1,0:T(8,128)(2,1)}, bf16[3,256,384]{2,1,0:T(8,128)(2,1)S(1)}, u32[]{:S(2)}, u32[]{:S(2)}) %collective-permute-start.37) | collective-permute-done | bytes 589856 | tf_op jit(solution)/shard_map/ppermute | solution.py:29
  242.1 30.0 %ffn.4 = (bf16[3,256,384]{2,1,0:T(8,128)(2,1)}, bf16[3,256,384]{2,1,0:T(8,128)(2,1)}, bf16[3,256,384]{2,1,0:T(8,128)(2,1)}, bf16[3,256,384]{2,1,0:T(8,128)(2,1)}...) custom-call(bf16[768,1024]{1,0:T(8,128)(2,1)S(1)} %copy-done.47, ...), custom_call_target="tpu_custom_call", output_to_operand_aliasing={{10}: (16, {})} | custom-call | flops 21743271936 | bytes 9437184 | tf_op jit(solution)/shard_map/ffn/pallas_call | solution.py:249
  277.1 6.2 %collective-permute-done.44 = bf16[3,256,384]{2,1,0:T(8,128)(2,1)S(1)} collective-permute-done((bf16[3,256,384]{2,1,0:T(8,128)(2,1)S(1)}, bf16[3,256,384]{2,1,0:T(8,128)(2,1)S(1)}, u32[]{:S(2)}, u32[]{:S(2)}) %collective-permute-start.44) | collective-permute-done | bytes 589856 | tf_op jit(solution)/shard_map/ppermute | solution.py:29
  288.4 30.1 %ffn.5 = (bf16[3,256,384]{2,1,0:T(8,128)(2,1)}, bf16[3,256,384]{2,1,0:T(8,128)(2,1)}, bf16[3,256,384]{2,1,0:T(8,128)(2,1)}, bf16[3,256,384]{2,1,0:T(8,128)(2,1)}...) custom-call(bf16[768,1024]{1,0:T(8,128)(2,1)S(1)} %copy-done.48, ...), custom_call_target="tpu_custom_call", output_to_operand_aliasing={{11}: (16, {})} | custom-call | flops 21743271936 | bytes 9437184 | tf_op jit(solution)/shard_map/ffn/pallas_call | solution.py:249
  324.5 3.5 copy.80.refs_1_
  339.5 2.8 copy-done.12
  348.7 6.7 %middle_back.1 = (bf16[768,1024]{1,0:T(8,128)(2,1)}, f32[768,1024]{1,0:T(8,128)S(1)}, bf16[768,1024]{1,0:T(8,128)(2,1)S(1)}, f32[1,1024]{1,0:T(1,128)S(1)}) custom-call(s32[8]{0:T(128)S(1)} %broadcast_xor_fusion.order.refs_0_, f32[768,1024]{1,0:T(8,128)S(1)} %copy-done.7, f32[768,1]{1,0:T(8,128)S(1)} %rsqrt.21.refs_2_, ...), custom_call_target="tpu_custom_call" | custom-call | flops 23592960 | bytes 22020096 | tf_op jit(solution)/shard_map/middle_back/pallas_call | solution.py:331
  359.8 4.1 fusion.32
  369.0 2.6 copy.82
  378.0 2.8 broadcast_multiply_fusion.1
  381.8 4.0 multiply_reduce_fusion.1
  385.8 2.6 fusion.34
  389.2 11.2 %collective-permute-done.59.rest_2_ = bf16[3,256,384]{2,1,0:T(8,128)(2,1)S(1)} collective-permute-done((bf16[3,256,384]{2,1,0:T(8,128)(2,1)}, bf16[3,256,384]{2,1,0:T(8,128)(2,1)S(1)}, u32[]{:S(2)}, u32[]{:S(2)}) %collective-permute-start.59) | collective-permute-done | bytes 589856 | tf_op jit(solution)/shard_map/ppermute | solution.py:29
  401.8 2.9 collective-permute-done.61
  404.6 5.4 %mixer_grad.2 = (bf16[4,1024,256]{2,1,0:T(8,128)(2,1)}, bf16[4,1024,256]{2,1,0:T(8,128)(2,1)}) custom-call(bf16[1024,768]{1,0:T(8,128)(2,1)S(1)} %slice_bitcast_fusion.6.ht, bf16[1024,768]{1,0:T(8,128)(2,1)S(1)} %bitcast.124, bf16[3,768,1024]{2,1,0:T(8,128)(2,1)S(1)} %pad_maximum_fusion.pa.pb, bf16[3,768,1024]{2,1,0:T(8,128)(2,1)S(1)} %pad_maximum_fusion.pa.pb, ...), custom_call_target="tpu_custom_call" | custom-call | flops 3221225472 | bytes 10485760 | tf_op jit(solution)/shard_map/mixer_grad/pallas_call | solution.py:404
  414.8 2.9 collective-permute-done.63.rest_1_
  421.7 4.5 mixer_grad.3
  427.8 2.9 add_convert_fusion.16
  430.7 3.4 collective-permute-done.64
  434.1 11.8 %collective-permute-done.65 = bf16[3,256,384]{2,1,0:T(8,128)(2,1)S(1)} collective-permute-done((bf16[3,256,384]{2,1,0:T(8,128)(2,1)S(1)}, bf16[3,256,384]{2,1,0:T(8,128)(2,1)S(1)}, u32[]{:S(2)}, u32[]{:S(2)}) %collective-permute-start.65) | collective-permute-done | bytes 589856 | tf_op jit(solution)/shard_map/ppermute | solution.py:29
  457.4 7.0 %collective-permute-done.70 = bf16[4,256,256]{2,1,0:T(8,128)(2,1)S(1)} collective-permute-done((bf16[4,256,256]{2,1,0:T(8,128)(2,1)S(1)}, bf16[4,256,256]{2,1,0:T(8,128)(2,1)S(1)}, u32[]{:S(2)}, u32[]{:S(2)}) %collective-permute-start.70) | collective-permute-done | bytes 524320 | tf_op jit(solution)/shard_map/ppermute | solution.py:29
  466.8 7.3 %fusion.28.upstream = f32[768,1024]{1,0:T(8,128)S(1)} fusion(bf16[3,768,1024]{2,1,0:T(8,128)(2,1)S(1)} %copy-done.1, bf16[4,1024,256]{2,1,0:T(8,128)(2,1)} %collective-permute-done.23, bf16[4,1024,256]{2,1,0:T(8,128)(2,1)} %constant_dynamic-update-slice_fusion.5, bf16[4,1024,256]{2,1,0:T(8,128)(2,1)} %collective-permute-done.15, ...), kind=kOutput, calls=%fused_computation.50 | convolution fusion | flops 4857004032 | bytes 16252928 | tf_op jit(solution)/shard_map/ktc,kdc->td/dot_general | solution.py:118
  474.1 4.5 input_back.1
  493.0 7.9 %collective-permute-done.75 = bf16[4,256,256]{2,1,0:T(8,128)(2,1)} collective-permute-done((bf16[4,256,256]{2,1,0:T(8,128)(2,1)}, bf16[4,256,256]{2,1,0:T(8,128)(2,1)}, u32[]{:S(2)}, u32[]{:S(2)}) %collective-permute-start.75) | collective-permute-done | bytes 524320 | tf_op jit(solution)/shard_map/ppermute | solution.py:29
  508.4 4.3 update.3
  512.8 15.5 %collective-permute-done.76 = bf16[4,256,256]{2,1,0:T(8,128)(2,1)S(1)} collective-permute-done((bf16[4,256,256]{2,1,0:T(8,128)(2,1)S(1)}, bf16[4,256,256]{2,1,0:T(8,128)(2,1)S(1)}, u32[]{:S(2)}, u32[]{:S(2)}) %collective-permute-start.76) | collective-permute-done | bytes 524320 | tf_op jit(solution)/shard_map/ppermute | solution.py:29
  528.2 2.7 collective-permute-start.86
  533.0 4.0 collective-permute-done.87
  (548 shorter events, 207.9 us)
Async XLA Ops:
  26.8 27.4 %collective-permute-start.10 = (bf16[4,256,256]{2,1,0:T(8,128)(2,1)}, bf16[4,256,256]{2,1,0:T(8,128)(2,1)S(1)}, u32[]{:S(2)}, u32[]{:S(2)}) collective-permute-start(bf16[4,256,256]{2,1,0:T(8,128)(2,1)} %pad_maximum_fusion.4), channel_id=1, source_target_pairs={{0,4},{4,0},{8,12},{12,8},{16,20},{20,16},{24,28},{28,24},{1,5},{5... | collective-permute-start | bytes 1572872 | tf_op jit(solution)/shard_map/ppermute | solution.py:29
  27.7 26.5 %collective-permute-start.11 = (bf16[4,256,256]{2,1,0:T(8,128)(2,1)}, bf16[4,256,256]{2,1,0:T(8,128)(2,1)}, u32[]{:S(2)}, u32[]{:S(2)}) collective-permute-start(bf16[4,256,256]{2,1,0:T(8,128)(2,1)} %pad_maximum_fusion.4), channel_id=1, source_target_pairs={{0,2},{1,3},{2,0},{3,1},{4,6},{5,7},{6,4},{7,5},{8,10},{9,11},{10,... | collective-permute-start | bytes 1572872 | tf_op jit(solution)/shard_map/ppermute | solution.py:29
  29.3 24.9 %collective-permute-start.9 = (bf16[4,256,256]{2,1,0:T(8,128)(2,1)}, bf16[4,256,256]{2,1,0:T(8,128)(2,1)}, u32[]{:S(2)}, u32[]{:S(2)}) collective-permute-start(bf16[4,256,256]{2,1,0:T(8,128)(2,1)} %pad_maximum_fusion.4), channel_id=1, source_target_pairs={{0,16},{4,20},{8,24},{12,28},{16,0},{20,4},{24,8},{28,12},{1,17},{... | collective-permute-start | bytes 1572872 | tf_op jit(solution)/shard_map/ppermute | solution.py:29
  30.0 18.7 %collective-permute-start.12 = (bf16[3,128,384]{2,1,0:T(8,128)(2,1)S(1)}, bf16[3,128,384]{2,1,0:T(8,128)(2,1)S(1)}, u32[]{:S(2)}, u32[]{:S(2)}) collective-permute-start(bf16[3,128,384]{2,1,0:T(8,128)(2,1)S(1)} %get-tuple-element.209), channel_id=1, source_target_pairs={{0,8},{4,12},{8,0},{12,4},{16,24},{20,28},{24,16},{28,20},{1,9},{5... | collective-permute-start | bytes 884744 | tf_op jit(solution)/shard_map/ppermute | solution.py:29
  31.8 22.4 %collective-permute-start.13 = (bf16[3,128,384]{2,1,0:T(8,128)(2,1)S(1)}, bf16[3,128,384]{2,1,0:T(8,128)(2,1)S(1)}, u32[]{:S(2)}, u32[]{:S(2)}) collective-permute-start(bf16[3,128,384]{2,1,0:T(8,128)(2,1)S(1)} %get-tuple-element.210), channel_id=1, source_target_pairs={{0,8},{4,12},{8,0},{12,4},{16,24},{20,28},{24,16},{28,20},{1,9},{5... | collective-permute-start | bytes 884744 | tf_op jit(solution)/shard_map/ppermute | solution.py:29
  54.2 25.1 %collective-permute-start.18 = (bf16[3,256,384]{2,1,0:T(8,128)(2,1)}, bf16[3,256,384]{2,1,0:T(8,128)(2,1)}, u32[]{:S(2)}, u32[]{:S(2)}) collective-permute-start(bf16[3,256,384]{2,1,0:T(8,128)(2,1)} %pad_maximum_fusion.1.refs_8_), channel_id=1, source_target_pairs={{0,2},{1,3},{2,0},{3,1},{4,6},{5,7},{6,4},{7,5},{8,10},{9,11},{10,... | collective-permute-start | bytes 1769480 | tf_op jit(solution)/shard_map/ppermute | solution.py:29
  56.0 26.9 %collective-permute-start.19 = (bf16[3,256,384]{2,1,0:T(8,128)(2,1)}, bf16[3,256,384]{2,1,0:T(8,128)(2,1)}, u32[]{:S(2)}, u32[]{:S(2)}) collective-permute-start(bf16[3,256,384]{2,1,0:T(8,128)(2,1)} %pad_maximum_fusion.1.refs_8_), channel_id=1, source_target_pairs={{0,16},{4,20},{8,24},{12,28},{16,0},{20,4},{24,8},{28,12},{1,17},{... | collective-permute-start | bytes 1769480 | tf_op jit(solution)/shard_map/ppermute | solution.py:29
  57.5 21.7 %collective-permute-start.16 = (bf16[4,256,256]{2,1,0:T(8,128)(2,1)}, bf16[4,256,256]{2,1,0:T(8,128)(2,1)}, u32[]{:S(2)}, u32[]{:S(2)}) collective-permute-start(bf16[4,256,256]{2,1,0:T(8,128)(2,1)} %collective-permute-done.9), channel_id=1, source_target_pairs={{0,2},{1,3},{2,0},{3,1},{4,6},{5,7},{6,4},{7,5},{8,10},{9,11},{10,... | collective-permute-start | bytes 1572872 | tf_op jit(solution)/shard_map/ppermute | solution.py:29
  58.1 21.2 %collective-permute-start.17 = (bf16[4,256,256]{2,1,0:T(8,128)(2,1)}, bf16[4,256,256]{2,1,0:T(8,128)(2,1)}, u32[]{:S(2)}, u32[]{:S(2)}) collective-permute-start(bf16[4,256,256]{2,1,0:T(8,128)(2,1)} %collective-permute-done.11), channel_id=1, source_target_pairs={{0,4},{4,0},{8,12},{12,8},{16,20},{20,16},{24,28},{28,24},{1,5},{5... | collective-permute-start | bytes 1572872 | tf_op jit(solution)/shard_map/ppermute | solution.py:29
  84.7 24.1 %collective-permute-start.22 = (bf16[768,1024]{0,1:T(8,128)(2,1)}, bf16[768,1024]{0,1:T(8,128)(2,1)S(1)}, u32[]{:S(2)}, u32[]{:S(2)}) collective-permute-start(bf16[768,1024]{0,1:T(8,128)(2,1)} %copy.66), channel_id=1, source_target_pairs={{0,1},{1,0},{2,3},{3,2},{4,5},{5,4},{6,7},{7,6},{8,9},{9,8},{10,11... | collective-permute-start | bytes 4718600 | tf_op jit(solution)/shard_map/ppermute | solution.py:29
  98.8 24.9 %collective-permute-start.15 = (bf16[4,1024,256]{2,1,0:T(8,128)(2,1)}, bf16[4,1024,256]{2,1,0:T(8,128)(2,1)}, u32[]{:S(2)}, u32[]{:S(2)}) collective-permute-start(bf16[4,1024,256]{2,1,0:T(8,128)(2,1)} %constant_dynamic-update-slice_fusion), channel_id=1, source_target_pairs={{0,1},{1,0},{2,3},{3,2},{4,5},{5,4},{6,7},{7,6},{8,9},{9,8},{10,11... | collective-permute-start | bytes 6291464 | tf_op jit(solution)/shard_map/ppermute | solution.py:29
  121.3 18.4 %collective-permute-start.24 = (bf16[3,256,384]{2,1,0:T(8,128)(2,1)}, bf16[3,256,384]{2,1,0:T(8,128)(2,1)}, u32[]{:S(2)}, u32[]{:S(2)}) collective-permute-start(bf16[3,256,384]{2,1,0:T(8,128)(2,1)} %collective-permute-done.19.refs_9_), channel_id=1, source_target_pairs={{0,4},{4,0},{8,12},{12,8},{16,20},{20,16},{24,28},{28,24},{1,5},{5... | collective-permute-start | bytes 1769480 | tf_op jit(solution)/shard_map/ppermute | solution.py:29
  121.8 17.9 %collective-permute-start.25 = (bf16[3,256,384]{2,1,0:T(8,128)(2,1)}, bf16[3,256,384]{2,1,0:T(8,128)(2,1)S(1)}, u32[]{:S(2)}, u32[]{:S(2)}) collective-permute-start(bf16[3,256,384]{2,1,0:T(8,128)(2,1)} %collective-permute-done.19.refs_9_), channel_id=1, source_target_pairs={{0,2},{1,3},{2,0},{3,1},{4,6},{5,7},{6,4},{7,5},{8,10},{9,11},{10,... | collective-permute-start | bytes 1769480 | tf_op jit(solution)/shard_map/ppermute | solution.py:29
  122.6 27.3 %collective-permute-start.26 = (bf16[3,256,384]{2,1,0:T(8,128)(2,1)}, bf16[3,256,384]{2,1,0:T(8,128)(2,1)S(1)}, u32[]{:S(2)}, u32[]{:S(2)}) collective-permute-start(bf16[3,256,384]{2,1,0:T(8,128)(2,1)} %collective-permute-done.18.refs_12_), channel_id=1, source_target_pairs={{0,4},{4,0},{8,12},{12,8},{16,20},{20,16},{24,28},{28,24},{1,5},{5... | collective-permute-start | bytes 1769480 | tf_op jit(solution)/shard_map/ppermute | solution.py:29
  123.7 26.6 %collective-permute-start.27 = (bf16[3,256,384]{2,1,0:T(8,128)(2,1)}, bf16[3,256,384]{2,1,0:T(8,128)(2,1)}, u32[]{:S(2)}, u32[]{:S(2)}) collective-permute-start(bf16[3,256,384]{2,1,0:T(8,128)(2,1)} %pad_maximum_fusion.2.refs_8_), channel_id=1, source_target_pairs={{0,2},{1,3},{2,0},{3,1},{4,6},{5,7},{6,4},{7,5},{8,10},{9,11},{10,... | collective-permute-start | bytes 1769480 | tf_op jit(solution)/shard_map/ppermute | solution.py:29
  125.4 27.2 %collective-permute-start.28 = (bf16[3,256,384]{2,1,0:T(8,128)(2,1)}, bf16[3,256,384]{2,1,0:T(8,128)(2,1)}, u32[]{:S(2)}, u32[]{:S(2)}) collective-permute-start(bf16[3,256,384]{2,1,0:T(8,128)(2,1)} %pad_maximum_fusion.2.refs_8_), channel_id=1, source_target_pairs={{0,16},{4,20},{8,24},{12,28},{16,0},{20,4},{24,8},{28,12},{1,17},{... | collective-permute-start | bytes 1769480 | tf_op jit(solution)/shard_map/ppermute | solution.py:29
  159.1 20.2 %collective-permute-start.29 = (bf16[768,1024]{0,1:T(8,128)(2,1)}, bf16[768,1024]{0,1:T(8,128)(2,1)}, u32[]{:S(2)}, u32[]{:S(2)}) collective-permute-start(bf16[768,1024]{0,1:T(8,128)(2,1)} %multiply_convert_fusion.2), channel_id=1, source_target_pairs={{0,1},{1,0},{2,3},{3,2},{4,5},{5,4},{6,7},{7,6},{8,9},{9,8},{10,11... | collective-permute-start | bytes 4718600 | tf_op jit(solution)/shard_map/ppermute | solution.py:29
  175.3 47.5 %collective-permute-start.32 = (bf16[3,256,384]{2,1,0:T(8,128)(2,1)}, bf16[3,256,384]{2,1,0:T(8,128)(2,1)}, u32[]{:S(2)}, u32[]{:S(2)}) collective-permute-start(bf16[3,256,384]{2,1,0:T(8,128)(2,1)} %collective-permute-done.28.refs_9_), channel_id=1, source_target_pairs={{0,4},{4,0},{8,12},{12,8},{16,20},{20,16},{24,28},{28,24},{1,5},{5... | collective-permute-start | bytes 1769480 | tf_op jit(solution)/shard_map/ppermute | solution.py:29
  176.5 46.3 %collective-permute-start.33 = (bf16[3,256,384]{2,1,0:T(8,128)(2,1)}, bf16[3,256,384]{2,1,0:T(8,128)(2,1)}, u32[]{:S(2)}, u32[]{:S(2)}) collective-permute-start(bf16[3,256,384]{2,1,0:T(8,128)(2,1)} %collective-permute-done.28.refs_9_), channel_id=1, source_target_pairs={{0,2},{1,3},{2,0},{3,1},{4,6},{5,7},{6,4},{7,5},{8,10},{9,11},{10,... | collective-permute-start | bytes 1769480 | tf_op jit(solution)/shard_map/ppermute | solution.py:29
  178.2 44.6 %collective-permute-start.34 = (bf16[3,256,384]{2,1,0:T(8,128)(2,1)}, bf16[3,256,384]{2,1,0:T(8,128)(2,1)}, u32[]{:S(2)}, u32[]{:S(2)}) collective-permute-start(bf16[3,256,384]{2,1,0:T(8,128)(2,1)} %collective-permute-done.27.refs_12_), channel_id=1, source_target_pairs={{0,4},{4,0},{8,12},{12,8},{16,20},{20,16},{24,28},{28,24},{1,5},{5... | collective-permute-start | bytes 1769480 | tf_op jit(solution)/shard_map/ppermute | solution.py:29
  179.0 43.8 %collective-permute-start.35 = (bf16[3,256,384]{2,1,0:T(8,128)(2,1)}, bf16[3,256,384]{2,1,0:T(8,128)(2,1)}, u32[]{:S(2)}, u32[]{:S(2)}) collective-permute-start(bf16[3,256,384]{2,1,0:T(8,128)(2,1)} %pad_maximum_fusion.3.refs_8_), channel_id=1, source_target_pairs={{0,2},{1,3},{2,0},{3,1},{4,6},{5,7},{6,4},{7,5},{8,10},{9,11},{10,... | collective-permute-start | bytes 1769480 | tf_op jit(solution)/shard_map/ppermute | solution.py:29
  179.3 43.4 %collective-permute-start.36 = (bf16[3,256,384]{2,1,0:T(8,128)(2,1)}, bf16[3,256,384]{2,1,0:T(8,128)(2,1)}, u32[]{:S(2)}, u32[]{:S(2)}) collective-permute-start(bf16[3,256,384]{2,1,0:T(8,128)(2,1)} %pad_maximum_fusion.3.refs_8_), channel_id=1, source_target_pairs={{0,16},{4,20},{8,24},{12,28},{16,0},{20,4},{24,8},{28,12},{1,17},{... | collective-permute-start | bytes 1769480 | tf_op jit(solution)/shard_map/ppermute | solution.py:29
  238.0 34.1 %collective-permute-start.39 = (bf16[3,256,384]{2,1,0:T(8,128)(2,1)}, bf16[3,256,384]{2,1,0:T(8,128)(2,1)S(1)}, u32[]{:S(2)}, u32[]{:S(2)}) collective-permute-start(bf16[3,256,384]{2,1,0:T(8,128)(2,1)} %collective-permute-done.36.refs_9_), channel_id=1, source_target_pairs={{0,4},{4,0},{8,12},{12,8},{16,20},{20,16},{24,28},{28,24},{1,5},{5... | collective-permute-start | bytes 1769480 | tf_op jit(solution)/shard_map/ppermute | solution.py:29
  239.2 32.9 %collective-permute-start.40 = (bf16[3,256,384]{2,1,0:T(8,128)(2,1)}, bf16[3,256,384]{2,1,0:T(8,128)(2,1)S(1)}, u32[]{:S(2)}, u32[]{:S(2)}) collective-permute-start(bf16[3,256,384]{2,1,0:T(8,128)(2,1)} %collective-permute-done.36.refs_9_), channel_id=1, source_target_pairs={{0,2},{1,3},{2,0},{3,1},{4,6},{5,7},{6,4},{7,5},{8,10},{9,11},{10,... | collective-permute-start | bytes 1769480 | tf_op jit(solution)/shard_map/ppermute | solution.py:29
  239.8 32.4 %collective-permute-start.41 = (bf16[3,256,384]{2,1,0:T(8,128)(2,1)}, bf16[3,256,384]{2,1,0:T(8,128)(2,1)S(1)}, u32[]{:S(2)}, u32[]{:S(2)}) collective-permute-start(bf16[3,256,384]{2,1,0:T(8,128)(2,1)} %collective-permute-done.35.refs_12_), channel_id=1, source_target_pairs={{0,4},{4,0},{8,12},{12,8},{16,20},{20,16},{24,28},{28,24},{1,5},{5... | collective-permute-start | bytes 1769480 | tf_op jit(solution)/shard_map/ppermute | solution.py:29
  240.6 31.6 %collective-permute-start.42 = (bf16[3,256,384]{2,1,0:T(8,128)(2,1)}, bf16[3,256,384]{2,1,0:T(8,128)(2,1)S(1)}, u32[]{:S(2)}, u32[]{:S(2)}) collective-permute-start(bf16[3,256,384]{2,1,0:T(8,128)(2,1)} %get-tuple-element.255), channel_id=1, source_target_pairs={{0,2},{1,3},{2,0},{3,1},{4,6},{5,7},{6,4},{7,5},{8,10},{9,11},{10,... | collective-permute-start | bytes 1769480 | tf_op jit(solution)/shard_map/ppermute | solution.py:29
  284.3 37.7 %collective-permute-start.49 = (bf16[768,1024]{1,0:T(8,128)(2,1)S(1)}, bf16[768,1024]{1,0:T(8,128)(2,1)S(1)}, u32[]{:S(2)}, u32[]{:S(2)}) collective-permute-start(bf16[768,1024]{1,0:T(8,128)(2,1)S(1)} %add_convert_fusion), channel_id=1, source_target_pairs={{0,1},{1,0},{2,3},{3,2},{4,5},{5,4},{6,7},{7,6},{8,9},{9,8},{10,11... | collective-permute-start | bytes 4718600 | tf_op jit(solution)/shard_map/ppermute | solution.py:29
  284.3 36.8 %collective-permute-start.45 = (bf16[3,256,384]{2,1,0:T(8,128)(2,1)S(1)}, bf16[3,256,384]{2,1,0:T(8,128)(2,1)S(1)}, u32[]{:S(2)}, u32[]{:S(2)}) collective-permute-start(bf16[3,256,384]{2,1,0:T(8,128)(2,1)S(1)} %copy-done.137), channel_id=1, source_target_pairs={{0,4},{4,0},{8,12},{12,8},{16,20},{20,16},{24,28},{28,24},{1,5},{5... | collective-permute-start | bytes 1769480 | tf_op jit(solution)/shard_map/ppermute | solution.py:29
  285.1 36.8 %collective-permute-start.46 = (bf16[3,256,384]{2,1,0:T(8,128)(2,1)S(1)}, bf16[3,256,384]{2,1,0:T(8,128)(2,1)S(1)}, u32[]{:S(2)}, u32[]{:S(2)}) collective-permute-start(bf16[3,256,384]{2,1,0:T(8,128)(2,1)S(1)} %copy-done.136), channel_id=1, source_target_pairs={{0,2},{1,3},{2,0},{3,1},{4,6},{5,7},{6,4},{7,5},{8,10},{9,11},{10,... | collective-permute-start | bytes 1769480 | tf_op jit(solution)/shard_map/ppermute | solution.py:29
  286.0 36.0 %collective-permute-start.47 = (bf16[3,256,384]{2,1,0:T(8,128)(2,1)}, bf16[3,256,384]{2,1,0:T(8,128)(2,1)S(1)}, u32[]{:S(2)}, u32[]{:S(2)}) collective-permute-start(bf16[3,256,384]{2,1,0:T(8,128)(2,1)} %get-tuple-element.275), channel_id=1, source_target_pairs={{0,4},{4,0},{8,12},{12,8},{16,20},{20,16},{24,28},{28,24},{1,5},{5... | collective-permute-start | bytes 1769480 | tf_op jit(solution)/shard_map/ppermute | solution.py:29
  287.2 34.7 %collective-permute-start.48 = (bf16[3,256,384]{2,1,0:T(8,128)(2,1)}, bf16[3,256,384]{2,1,0:T(8,128)(2,1)S(1)}, u32[]{:S(2)}, u32[]{:S(2)}) collective-permute-start(bf16[3,256,384]{2,1,0:T(8,128)(2,1)} %get-tuple-element.276), channel_id=1, source_target_pairs={{0,2},{1,3},{2,0},{3,1},{4,6},{5,7},{6,4},{7,5},{8,10},{9,11},{10,... | collective-permute-start | bytes 1769480 | tf_op jit(solution)/shard_map/ppermute | solution.py:29
  331.1 26.7 %collective-permute-start.52 = (bf16[3,256,384]{2,1,0:T(8,128)(2,1)S(1)}, bf16[3,256,384]{2,1,0:T(8,128)(2,1)}, u32[]{:S(2)}, u32[]{:S(2)}) collective-permute-start(bf16[3,256,384]{2,1,0:T(8,128)(2,1)S(1)} %add_convert_fusion.9), channel_id=1, source_target_pairs={{0,4},{4,0},{8,12},{12,8},{16,20},{20,16},{24,28},{28,24},{1,5},{5... | collective-permute-start | bytes 1769480 | tf_op jit(solution)/shard_map/ppermute | solution.py:29
  332.0 25.8 %collective-permute-start.53 = (bf16[3,256,384]{2,1,0:T(8,128)(2,1)S(1)}, bf16[3,256,384]{2,1,0:T(8,128)(2,1)}, u32[]{:S(2)}, u32[]{:S(2)}) collective-permute-start(bf16[3,256,384]{2,1,0:T(8,128)(2,1)S(1)} %add_convert_fusion.8), channel_id=1, source_target_pairs={{0,2},{1,3},{2,0},{3,1},{4,6},{5,7},{6,4},{7,5},{8,10},{9,11},{10,... | collective-permute-start | bytes 1769480 | tf_op jit(solution)/shard_map/ppermute | solution.py:29
  332.9 26.5 %collective-permute-start.54 = (bf16[3,256,384]{2,1,0:T(8,128)(2,1)}, bf16[3,256,384]{2,1,0:T(8,128)(2,1)}, u32[]{:S(2)}, u32[]{:S(2)}) collective-permute-start(bf16[3,256,384]{2,1,0:T(8,128)(2,1)} %get-tuple-element.298), channel_id=1, source_target_pairs={{0,4},{4,0},{8,12},{12,8},{16,20},{20,16},{24,28},{28,24},{1,5},{5... | collective-permute-start | bytes 1769480 | tf_op jit(solution)/shard_map/ppermute | solution.py:29
  336.1 23.7 %collective-permute-start.55 = (bf16[3,256,384]{2,1,0:T(8,128)(2,1)}, bf16[3,256,384]{2,1,0:T(8,128)(2,1)}, u32[]{:S(2)}, u32[]{:S(2)}) collective-permute-start(bf16[3,256,384]{2,1,0:T(8,128)(2,1)} %get-tuple-element.299), channel_id=1, source_target_pairs={{0,2},{1,3},{2,0},{3,1},{4,6},{5,7},{6,4},{7,5},{8,10},{9,11},{10,... | collective-permute-start | bytes 1769480 | tf_op jit(solution)/shard_map/ppermute | solution.py:29
  371.6 17.5 %collective-permute-start.57 = (bf16[3,256,384]{2,1,0:T(8,128)(2,1)}, bf16[3,256,384]{2,1,0:T(8,128)(2,1)S(1)}, u32[]{:S(2)}, u32[]{:S(2)}) collective-permute-start(bf16[3,256,384]{2,1,0:T(8,128)(2,1)} %add_convert_fusion.7), channel_id=1, source_target_pairs={{0,4},{4,0},{8,12},{12,8},{16,20},{20,16},{24,28},{28,24},{1,5},{5... | collective-permute-start | bytes 1769480 | tf_op jit(solution)/shard_map/ppermute | solution.py:29
  374.3 26.1 %collective-permute-start.59 = (bf16[3,256,384]{2,1,0:T(8,128)(2,1)}, bf16[3,256,384]{2,1,0:T(8,128)(2,1)S(1)}, u32[]{:S(2)}, u32[]{:S(2)}) collective-permute-start(bf16[3,256,384]{2,1,0:T(8,128)(2,1)} %get-tuple-element.312), channel_id=1, source_target_pairs={{0,4},{4,0},{8,12},{12,8},{16,20},{20,16},{24,28},{28,24},{1,5},{5... | collective-permute-start | bytes 1769480 | tf_op jit(solution)/shard_map/ppermute | solution.py:29
  375.1 26.7 %collective-permute-start.60 = (bf16[3,256,384]{2,1,0:T(8,128)(2,1)}, bf16[3,256,384]{2,1,0:T(8,128)(2,1)S(1)}, u32[]{:S(2)}, u32[]{:S(2)}) collective-permute-start(bf16[3,256,384]{2,1,0:T(8,128)(2,1)} %get-tuple-element.313), channel_id=1, source_target_pairs={{0,2},{1,3},{2,0},{3,1},{4,6},{5,7},{6,4},{7,5},{8,10},{9,11},{10,... | collective-permute-start | bytes 1769480 | tf_op jit(solution)/shard_map/ppermute | solution.py:29
  375.6 29.0 %collective-permute-start.61 = (bf16[3,256,384]{2,1,0:T(8,128)(2,1)}, bf16[3,256,384]{2,1,0:T(8,128)(2,1)S(1)}, u32[]{:S(2)}, u32[]{:S(2)}) collective-permute-start(bf16[3,256,384]{2,1,0:T(8,128)(2,1)} %add_convert_fusion.5), channel_id=1, source_target_pairs={{0,16},{4,20},{8,24},{12,28},{16,0},{20,4},{24,8},{28,12},{1,17},{... | collective-permute-start | bytes 1769480 | tf_op jit(solution)/shard_map/ppermute | solution.py:29
  418.9 27.0 %collective-permute-start.65 = (bf16[3,256,384]{2,1,0:T(8,128)(2,1)S(1)}, bf16[3,256,384]{2,1,0:T(8,128)(2,1)S(1)}, u32[]{:S(2)}, u32[]{:S(2)}) collective-permute-start(bf16[3,256,384]{2,1,0:T(8,128)(2,1)S(1)} %add_convert_fusion.4), channel_id=1, source_target_pairs={{0,4},{4,0},{8,12},{12,8},{16,20},{20,16},{24,28},{28,24},{1,5},{5... | collective-permute-start | bytes 1769480 | tf_op jit(solution)/shard_map/ppermute | solution.py:29
  419.7 26.2 %collective-permute-start.66 = (bf16[3,256,384]{2,1,0:T(8,128)(2,1)}, bf16[3,256,384]{2,1,0:T(8,128)(2,1)S(1)}, u32[]{:S(2)}, u32[]{:S(2)}) collective-permute-start(bf16[3,256,384]{2,1,0:T(8,128)(2,1)} %get-tuple-element.334), channel_id=1, source_target_pairs={{0,2},{1,3},{2,0},{3,1},{4,6},{5,7},{6,4},{7,5},{8,10},{9,11},{10,... | collective-permute-start | bytes 1769480 | tf_op jit(solution)/shard_map/ppermute | solution.py:29
  420.6 26.8 %collective-permute-start.67 = (bf16[3,256,384]{2,1,0:T(8,128)(2,1)S(1)}, bf16[3,256,384]{2,1,0:T(8,128)(2,1)S(1)}, u32[]{:S(2)}, u32[]{:S(2)}) collective-permute-start(bf16[3,256,384]{2,1,0:T(8,128)(2,1)S(1)} %add_convert_fusion.3), channel_id=1, source_target_pairs={{0,2},{1,3},{2,0},{3,1},{4,6},{5,7},{6,4},{7,5},{8,10},{9,11},{10,... | collective-permute-start | bytes 1769480 | tf_op jit(solution)/shard_map/ppermute | solution.py:29
  421.7 27.7 %collective-permute-start.68 = (bf16[3,256,384]{2,1,0:T(8,128)(2,1)S(1)}, bf16[3,256,384]{2,1,0:T(8,128)(2,1)S(1)}, u32[]{:S(2)}, u32[]{:S(2)}) collective-permute-start(bf16[3,256,384]{2,1,0:T(8,128)(2,1)S(1)} %add_convert_fusion.2), channel_id=1, source_target_pairs={{0,16},{4,20},{8,24},{12,28},{16,0},{20,4},{24,8},{28,12},{1,17},{... | collective-permute-start | bytes 1769480 | tf_op jit(solution)/shard_map/ppermute | solution.py:29
  452.4 29.1 %collective-permute-start.72 = (bf16[3,256,384]{2,1,0:T(8,128)(2,1)S(1)}, bf16[3,256,384]{2,1,0:T(8,128)(2,1)S(1)}, u32[]{:S(2)}, u32[]{:S(2)}) collective-permute-start(bf16[3,256,384]{2,1,0:T(8,128)(2,1)S(1)} %add_convert_fusion.1), channel_id=1, source_target_pairs={{0,16},{4,20},{8,24},{12,28},{16,0},{20,4},{24,8},{28,12},{1,17},{... | collective-permute-start | bytes 1769480 | tf_op jit(solution)/shard_map/ppermute | solution.py:29
  452.4 30.0 %collective-permute-start.69 = (bf16[4,256,256]{2,1,0:T(8,128)(2,1)S(1)}, bf16[4,256,256]{2,1,0:T(8,128)(2,1)S(1)}, u32[]{:S(2)}, u32[]{:S(2)}) collective-permute-start(bf16[4,256,256]{2,1,0:T(8,128)(2,1)S(1)} %add_convert_fusion.18), channel_id=1, source_target_pairs={{0,4},{4,0},{8,12},{12,8},{16,20},{20,16},{24,28},{28,24},{1,5},{5... | collective-permute-start | bytes 1572872 | tf_op jit(solution)/shard_map/ppermute | solution.py:29
  452.8 26.5 %collective-permute-start.71 = (bf16[4,256,256]{2,1,0:T(8,128)(2,1)}, bf16[4,256,256]{2,1,0:T(8,128)(2,1)}, u32[]{:S(2)}, u32[]{:S(2)}) collective-permute-start(bf16[4,256,256]{2,1,0:T(8,128)(2,1)} %get-tuple-element.344), channel_id=1, source_target_pairs={{0,4},{4,0},{8,12},{12,8},{16,20},{20,16},{24,28},{28,24},{1,5},{5... | collective-permute-start | bytes 1572872 | tf_op jit(solution)/shard_map/ppermute | solution.py:29
  454.4 28.8 %collective-permute-start.73 = (bf16[4,256,256]{2,1,0:T(8,128)(2,1)}, bf16[4,256,256]{2,1,0:T(8,128)(2,1)S(1)}, u32[]{:S(2)}, u32[]{:S(2)}) collective-permute-start(bf16[4,256,256]{2,1,0:T(8,128)(2,1)} %get-tuple-element.346), channel_id=1, source_target_pairs={{0,2},{1,3},{2,0},{3,1},{4,6},{5,7},{6,4},{7,5},{8,10},{9,11},{10,... | collective-permute-start | bytes 1572872 | tf_op jit(solution)/shard_map/ppermute | solution.py:29
  502.7 25.5 %collective-permute-start.76 = (bf16[4,256,256]{2,1,0:T(8,128)(2,1)S(1)}, bf16[4,256,256]{2,1,0:T(8,128)(2,1)S(1)}, u32[]{:S(2)}, u32[]{:S(2)}) collective-permute-start(bf16[4,256,256]{2,1,0:T(8,128)(2,1)S(1)} %add_convert_fusion.10), channel_id=1, source_target_pairs={{0,16},{4,20},{8,24},{12,28},{16,0},{20,4},{24,8},{28,12},{1,17},{... | collective-permute-start | bytes 1572872 | tf_op jit(solution)/shard_map/ppermute | solution.py:29
  (180 other events, 2337.5 us)
